TPU v7x, 32 devices: a whole 2x2x4 slice. The times are simulated.
32 devices in a mesh: gx: 2 (over core), gy: 4 (over y, x), grp: 4 (over z).
Axes of the slice: x: 2, y: 2, z: 4, core: 2. Of those that a mesh axis runs over, the one named last changes fastest.
Arguments:
- field_in: bfloat16 [4, 16, 64, 1024], P('grp', 'gx', 'gy'), may hold values from -6 to 6
- first_weight: bfloat16 [3, 3, 3, 64, 64], replicated, may hold values from -0.15625 to 0.15625
- second_weight: bfloat16 [3, 3, 3, 64, 64], replicated, may hold values from -0.15625 to 0.15625
- cotangent: bfloat16 [4, 16, 64, 1024], P('grp', 'gx', 'gy'), may hold values from -6 to 6
Outputs:
- field_out: bfloat16 [4, 16, 64, 1024], P('grp', 'gx', 'gy')
- first_grad: float32 [3, 3, 3, 64, 64], replicated
- second_grad: float32 [3, 3, 3, 64, 64], replicated
All inputs are finite; a program needn't handle non-finite values.
Results may differ from a plain program's by a relative error of at most 0.0095.
Values may be sent and summed in bfloat16 or wider, within the bound.
No kernel may reach another device: no remote copies, remote signals or barrier semaphores. Data moves between devices by JAX's collectives and lax.ppermute only.
A program may use at most 64 MiB of HBM per device.

v0:
```python
import math

import jax
import jax.numpy as jnp
from jax import lax
from jax.sharding import PartitionSpec as P

C = 64
NZ = 16


def extended(cells, sides, width):
    for axis, dim in sides:
        count = lax.axis_size(axis)
        ends = count - 1
        head = lax.slice_in_dim(cells, 0, width, axis=dim)
        tail = lax.slice_in_dim(cells, cells.shape[dim] - width, cells.shape[dim], axis=dim)
        cells = jnp.concatenate(
            [
                lax.ppermute(tail, axis, [(i, (i + 1) % count) for i in range(ends)]),
                cells,
                lax.ppermute(head, axis, [((i + 1) % count, i) for i in range(ends)]),
            ],
            axis=dim,
        )
    return cells


def conv_local(padded, weight):
    return lax.conv_general_dilated(
        padded,
        weight,
        (1, 1, 1),
        ((0, 0), (0, 0), (1, 1)),
        dimension_numbers=("NHWDC", "HWDIO", "NHWDC"),
        preferred_element_type=jnp.float32,
    )


def kernel_local(padded, grad_out):
    result = lax.conv_general_dilated(
        padded,
        grad_out,
        (1, 1, 1),
        ((0, 0), (0, 0), (1, 1)),
        dimension_numbers=("CHWDN", "IHWDO", "NHWDC"),
        preferred_element_type=jnp.float32,
    )
    return jnp.transpose(result, (1, 2, 3, 0, 4))


def as_cells(field):
    return field.reshape(field.shape[0], field.shape[1], field.shape[2], NZ, C)


def reduce_grad(local):
    return lax.psum(local, ("gx", "gy", "grp"))


def shards(field_in, first_weight, second_weight, cotangent):
    total = (
        field_in.shape[0]
        * field_in.shape[1]
        * field_in.shape[2]
        * NZ
        * lax.axis_size("gx")
        * lax.axis_size("gy")
        * lax.axis_size("grp")
    )
    factor = 1.0 / math.sqrt(total)
    padded_in = extended(field_in, (("gx", 1), ("gy", 2)), 1)
    pre_first = conv_local(as_cells(padded_in), first_weight)
    hidden = jax.nn.silu(pre_first).astype(jnp.bfloat16)
    flat_hidden = hidden.reshape(field_in.shape)
    padded_hidden = extended(flat_hidden, (("gx", 1), ("gy", 2)), 1)
    output = conv_local(as_cells(padded_hidden), second_weight).astype(jnp.bfloat16)
    padded_grad = extended(cotangent, (("gx", 1), ("gy", 2)), 1)
    grad_cells = as_cells(cotangent)
    second_local = kernel_local(as_cells(padded_hidden), grad_cells) * factor
    second_grad = reduce_grad(second_local)
    flipped = jnp.swapaxes(second_weight[::-1, ::-1, ::-1], 3, 4)
    hidden_grad = conv_local(as_cells(padded_grad), flipped)
    sigma = jax.nn.sigmoid(pre_first)
    pre_grad = (hidden_grad * sigma * (1.0 + pre_first * (1.0 - sigma))).astype(jnp.bfloat16)
    first_local = kernel_local(as_cells(padded_in), pre_grad) * factor
    first_grad = reduce_grad(first_local)
    return (output.reshape(field_in.shape), first_grad, second_grad)


def solution(mesh):
    return jax.shard_map(
        shards,
        mesh=mesh,
        in_specs=(P("grp", "gx", "gy", None), P(), P(), P("grp", "gx", "gy", None)),
        out_specs=(P("grp", "gx", "gy", None), P(), P()),
        check_vma=False,
    )
```

profile of v0, /device:TPU:0, one launch (start us, length us, event | category | flops | bytes accessed | tf_op | source)
XLA Modules:
  0.0 267.5 jit_solution(5499933623690740506)
XLA Ops:
  8.1 2.3 collective-permute-start
  10.5 1.3 collective-permute-start.1
  12.5 3.0 %collective-permute-start.8 = (bf16[1,1,16,1024]{3,2,1,0:T(8,128)(2,1)S(1)}, bf16[1,1,16,1024]{3,2,1,0:T(8,128)(2,1)S(1)}, u32[]{:S(2)}, u32[]{:S(2)}) collective-permute-start(bf16[1,1,16,1024]{3,2,1,0:T(8,128)(2,1)S(1)} %get-tuple-element.18), channel_id=1, source_target_pairs={{0,16},{1,17},{2,18},{3,19},{4,20},{5,21},{6,22},{7,23},{8,24},{9,... | collective-permute-start | bytes 98312 | tf_op jit(solution)/shard_map/ppermute | solution.py:20
  15.6 1.3 collective-permute-start.9
  16.9 3.5 %reshape.92 = bf16[1,8,16,16,64]{4,0,3,2,1:T(2,128)(2,1)} reshape(bf16[1,8,16,1024]{3,2,1,0:T(8,128)(2,1)} %param.7) | data formatting | bytes 524288 | tf_op jit(solution)/shard_map/reshape | solution.py:53
  20.5 1.3 collective-permute-start.3
  21.8 4.9 %collective-permute-start.2 = (bf16[1,10,1,1024]{3,2,1,0:T(2,128)(2,1)S(1)}, bf16[1,10,1,1024]{3,2,1,0:T(2,128)(2,1)S(1)}, u32[]{:S(2)}, u32[]{:S(2)}) collective-permute-start(bf16[1,10,1,1024]{3,2,1,0:T(2,128)(2,1)S(1)} %get-tuple-element.15), channel_id=1, source_target_pairs={{0,4},{4,8},{8,12},{1,5},{5,9},{9,13},{2,6},{6,10},{10,14},{3,7},{... | collective-permute-start | bytes 61448 | tf_op jit(solution)/shard_map/ppermute | solution.py:20
  28.8 6.1 %collective-permute-start.10 = (bf16[1,10,1,1024]{3,2,1,0:T(2,128)(2,1)}, bf16[1,10,1,1024]{3,2,1,0:T(2,128)(2,1)}, u32[]{:S(2)}, u32[]{:S(2)}) collective-permute-start(bf16[1,10,1,1024]{3,2,1,0:T(2,128)(2,1)} %get-tuple-element.11), channel_id=1, source_target_pairs={{0,4},{4,8},{8,12},{1,5},{5,9},{9,13},{2,6},{6,10},{10,14},{3,7},{... | collective-permute-start | bytes 61448 | tf_op jit(solution)/shard_map/ppermute | solution.py:20
  35.6 1.5 fusion.78
  37.7 2.2 fusion.77
  39.9 2.1 fusion.76
  42.0 2.8 %reshape.34 = bf16[10,18,1,8,3,64]{5,4,3,1,0,2:T(4,128)(2,1)S(1)} reshape(bf16[10,18,1,24,64]{4,3,1,0,2:T(8,128)(2,1)} %get-tuple-element.10) | data formatting | bytes 1105920 | tf_op jit(solution)/shard_map/conv_general_dilated | solution.py:30
  45.5 4.3 %multiply_convert_fusion.1 = (bf16[8,16,8,3,64]{4,2,3,1,0:T(8,128)(2,1)S(1)}, f32[8,16,8,3,64]{4,2,3,1,0:T(8,128)}) fusion(pred[8,3]{0,1:T(4,128)(4,1)S(1)} %copy-done.17, bf16[3,3,3,64,64]{4,3,2,1,0:T(8,128)(2,1)S(1)} %copy-done, bf16[10,18,1,7,2,64]{5,3,4,1,0,2:T(8,128)(2,1)S(1)} %slice.59, bf16[10,18,1,8,3,64]{5,3,4,1,0,2:T(8,128)(2,1)S(1)} %copy.27), kind=kOutput, calls=%fused_computation.34 | convolution fusion | flops 683421696 | bytes 2276376 | tf_op jit(solution)/shard_map/conv_general_dilated | solution.py:30
  51.2 1.4 fusion.83
  52.6 2.8 %collective-permute-start.4 = (bf16[1,1,16,1024]{3,2,1,0:T(8,128)(2,1)}, bf16[1,1,16,1024]{3,2,1,0:T(8,128)(2,1)}, u32[]{:S(2)}, u32[]{:S(2)}) collective-permute-start(bf16[1,1,16,1024]{3,2,1,0:T(8,128)(2,1)} %get-tuple-element.20), channel_id=1, source_target_pairs={{0,16},{1,17},{2,18},{3,19},{4,20},{5,21},{6,22},{7,23},{8,24},{9,... | collective-permute-start | bytes 98312 | tf_op jit(solution)/shard_map/ppermute | solution.py:20
  55.4 1.5 collective-permute-start.5
  59.3 1.9 fusion.49
  69.1 4.6 %collective-permute-start.6 = (bf16[1,10,1,1024]{3,2,1,0:T(2,128)(2,1)S(1)}, bf16[1,10,1,1024]{3,2,1,0:T(2,128)(2,1)S(1)}, u32[]{:S(2)}, u32[]{:S(2)}) collective-permute-start(bf16[1,10,1,1024]{3,2,1,0:T(2,128)(2,1)S(1)} %get-tuple-element.13), channel_id=1, source_target_pairs={{0,4},{4,8},{8,12},{1,5},{5,9},{9,13},{2,6},{6,10},{10,14},{3,7},{... | collective-permute-start | bytes 61448 | tf_op jit(solution)/shard_map/ppermute | solution.py:20
  73.7 27.2 %fusion.39 = f32[3,3,3,64,64]{4,3,2,1,0:T(8,128)} fusion(bf16[10,18,8,3,64,1]{4,2,5,3,1,0:T(8,128)(2,1)} %get-tuple-element.25, bf16[10,18,8,3,64,1]{4,2,5,3,1,0:T(8,128)(2,1)S(1)} %copy-done.9, bf16[10,18,8,3,64,1]{4,2,5,3,1,0:T(8,128)(2,1)} %get-tuple-element.26, f32[8,16,8,3,64]{4,2,3,1,0:T(8,128)} %get-tuple-element.24, ...), kind=kOutput, calls=%fused_computation.38 | convolution fusion | flops 1365848064 | bytes 3984408 | tf_op jit(solution)/shard_map/transpose | solution.py:49
  102.6 2.7 %reshape.91 = bf16[1,10,18,16,64]{4,0,3,2,1:T(2,128)(2,1)} reshape(bf16[1,10,18,1024]{3,2,1,0:T(8,128)(2,1)S(1)} %pad_maximum_fusion.1) | data formatting | bytes 737280 | tf_op jit(solution)/shard_map/reshape | solution.py:53
  108.6 13.9 %convolution_multiply_fusion = f32[3,3,3,64,64]{4,3,2,1,0:T(8,128)} fusion(bf16[1,10,18,16,64]{4,0,3,2,1:T(2,128)(2,1)S(1)} %copy-done.6, bf16[1,8,16,16,64]{4,0,3,2,1:T(2,128)(2,1)S(1)} %copy-done.10), kind=kOutput, calls=%fused_computation.37 | convolution fusion | flops 434221056 | bytes 1073152 | tf_op jit(solution)/shard_map/transpose | solution.py:49
  123.9 4.2 %select_convert_fusion = bf16[8,16,8,3,64]{4,2,3,1,0:T(8,128)(2,1)S(1)} fusion(bf16[3,3,3,64,64]{4,3,2,1,0:T(8,128)(2,1)S(1)} %copy-done.16, bf16[10,18,1,7,2,64]{5,3,4,1,0,2:T(8,128)(2,1)} %slice.65, bf16[10,18,1,8,3,64]{5,3,4,1,0,2:T(8,128)(2,1)S(1)} %copy-done.2, pred[8,3]{0,1:T(4,128)(4,1)S(1)} %copy-done.18), kind=kOutput, calls=%fused_computation.33 | convolution fusion | flops 682635264 | bytes 1489944 | tf_op jit(solution)/shard_map/conv_general_dilated | solution.py:30
  129.5 127.7 %all-reduce.3.cloned.1.call-done = (f32[3,3,3,64,64]{4,3,2,1,0:T(8,128)}, f32[3,3,3,64,64]{4,3,2,1,0:T(8,128)}) async-done(((f32[3,3,3,64,64]{4,3,2,1,0:T(8,128)}, f32[3,3,3,64,64]{4,3,2,1,0:T(8,128)}), (f32[3,3,3,64,64]{4,3,2,1,0:T(8,128)}, f32[3,3,3,64,64]{4,3,2,1,0:T(8,128)})) %all-reduce.3.cloned.1.call-update) | async-done | bytes 884752 | tf_op jit(solution)/shard_map/psum | solution.py:57
  257.2 2.3 copy.56
  (100 shorter events, 25.9 us)
Async XLA Ops:
  7.2 38.1 %copy-start = (bf16[3,3,3,64,64]{4,3,2,1,0:T(8,128)(2,1)S(1)}, bf16[3,3,3,64,64]{4,3,2,1,0:T(8,128)(2,1)}, u32[]{:S(2)}) copy-start(bf16[3,3,3,64,64]{4,3,2,1,0:T(8,128)(2,1)} %param.5) | copy-start | bytes 663556
  7.2 13.2 %copy-start.15 = (bf16[1,8,16,1024]{3,2,1,0:T(8,128)(2,1)S(1)}, bf16[1,8,16,1024]{3,2,1,0:T(8,128)(2,1)}, u32[]{:S(2)}) copy-start(bf16[1,8,16,1024]{3,2,1,0:T(8,128)(2,1)} %param.4) | copy-start | bytes 786436
  7.2 19.5 %copy-start.7 = (bf16[1,8,16,1024]{3,2,1,0:T(8,128)(2,1)S(1)}, bf16[1,8,16,1024]{3,2,1,0:T(8,128)(2,1)}, u32[]{:S(2)}) copy-start(bf16[1,8,16,1024]{3,2,1,0:T(8,128)(2,1)} %param.7) | copy-start | bytes 786436
  7.2 250.0 %all-reduce.3.cloned.1.call-start = ((), (), s32[]{:S(2)}) async-start(), calls=%async_computation | async-start | bytes 3538944 | tf_op jit(solution)/shard_map/psum | solution.py:57
  8.1 12.2 %collective-permute-start = (bf16[1,1,16,1024]{3,2,1,0:T(8,128)(2,1)S(1)}, bf16[1,1,16,1024]{3,2,1,0:T(8,128)(2,1)S(1)}, u32[]{:S(2)}, u32[]{:S(2)}) collective-permute-start(bf16[1,1,16,1024]{3,2,1,0:T(8,128)(2,1)S(1)} %get-tuple-element.22), channel_id=1, source_target_pairs={{0,16},{1,17},{2,18},{3,19},{4,20},{5,21},{6,22},{7,23},{8,24},{9,... | collective-permute-start | bytes 98312 | tf_op jit(solution)/shard_map/ppermute | solution.py:20
  10.5 9.9 %collective-permute-start.1 = (bf16[1,1,16,1024]{3,2,1,0:T(8,128)(2,1)S(1)}, bf16[1,1,16,1024]{3,2,1,0:T(8,128)(2,1)S(1)}, u32[]{:S(2)}, u32[]{:S(2)}) collective-permute-start(bf16[1,1,16,1024]{3,2,1,0:T(8,128)(2,1)S(1)} %get-tuple-element.21), channel_id=1, source_target_pairs={{16,0},{17,1},{18,2},{19,3},{20,4},{21,5},{22,6},{23,7},{24,8},{25... | collective-permute-start | bytes 98312 | tf_op jit(solution)/shard_map/ppermute | solution.py:22
  12.5 14.1 %collective-permute-start.8 = (bf16[1,1,16,1024]{3,2,1,0:T(8,128)(2,1)S(1)}, bf16[1,1,16,1024]{3,2,1,0:T(8,128)(2,1)S(1)}, u32[]{:S(2)}, u32[]{:S(2)}) collective-permute-start(bf16[1,1,16,1024]{3,2,1,0:T(8,128)(2,1)S(1)} %get-tuple-element.18), channel_id=1, source_target_pairs={{0,16},{1,17},{2,18},{3,19},{4,20},{5,21},{6,22},{7,23},{8,24},{9,... | collective-permute-start | bytes 98312 | tf_op jit(solution)/shard_map/ppermute | solution.py:20
  15.6 11.1 %collective-permute-start.9 = (bf16[1,1,16,1024]{3,2,1,0:T(8,128)(2,1)S(1)}, bf16[1,1,16,1024]{3,2,1,0:T(8,128)(2,1)S(1)}, u32[]{:S(2)}, u32[]{:S(2)}) collective-permute-start(bf16[1,1,16,1024]{3,2,1,0:T(8,128)(2,1)S(1)} %get-tuple-element.17), channel_id=1, source_target_pairs={{16,0},{17,1},{18,2},{19,3},{20,4},{21,5},{22,6},{23,7},{24,8},{25... | collective-permute-start | bytes 98312 | tf_op jit(solution)/shard_map/ppermute | solution.py:22
  20.5 14.4 %collective-permute-start.3 = (bf16[1,10,1,1024]{3,2,1,0:T(2,128)(2,1)S(1)}, bf16[1,10,1,1024]{3,2,1,0:T(2,128)(2,1)S(1)}, u32[]{:S(2)}, u32[]{:S(2)}) collective-permute-start(bf16[1,10,1,1024]{3,2,1,0:T(2,128)(2,1)S(1)} %get-tuple-element.16), channel_id=1, source_target_pairs={{4,0},{8,4},{12,8},{5,1},{9,5},{13,9},{6,2},{10,6},{14,10},{7,3},{... | collective-permute-start | bytes 61448 | tf_op jit(solution)/shard_map/ppermute | solution.py:22
  21.8 13.1 %collective-permute-start.2 = (bf16[1,10,1,1024]{3,2,1,0:T(2,128)(2,1)S(1)}, bf16[1,10,1,1024]{3,2,1,0:T(2,128)(2,1)S(1)}, u32[]{:S(2)}, u32[]{:S(2)}) collective-permute-start(bf16[1,10,1,1024]{3,2,1,0:T(2,128)(2,1)S(1)} %get-tuple-element.15), channel_id=1, source_target_pairs={{0,4},{4,8},{8,12},{1,5},{5,9},{9,13},{2,6},{6,10},{10,14},{3,7},{... | collective-permute-start | bytes 61448 | tf_op jit(solution)/shard_map/ppermute | solution.py:20
  26.7 8.1 %copy-start.13 = (bf16[1,10,16,1024]{3,2,1,0:T(8,128)(2,1)}, bf16[1,10,16,1024]{3,2,1,0:T(8,128)(2,1)S(1)}, u32[]{:S(2)}) copy-start(bf16[1,10,16,1024]{3,2,1,0:T(8,128)(2,1)S(1)} %constant_dynamic-update-slice_fusion.6) | copy-start | bytes 983044
  27.5 33.7 %collective-permute-start.11 = (bf16[1,10,1,1024]{3,2,1,0:T(2,128)(2,1)}, bf16[1,10,1,1024]{3,2,1,0:T(2,128)(2,1)}, u32[]{:S(2)}, u32[]{:S(2)}) collective-permute-start(bf16[1,10,1,1024]{3,2,1,0:T(2,128)(2,1)} %get-tuple-element.12), channel_id=1, source_target_pairs={{4,0},{8,4},{12,8},{5,1},{9,5},{13,9},{6,2},{10,6},{14,10},{7,3},{... | collective-permute-start | bytes 61448 | tf_op jit(solution)/shard_map/ppermute | solution.py:22
  28.8 32.4 %collective-permute-start.10 = (bf16[1,10,1,1024]{3,2,1,0:T(2,128)(2,1)}, bf16[1,10,1,1024]{3,2,1,0:T(2,128)(2,1)}, u32[]{:S(2)}, u32[]{:S(2)}) collective-permute-start(bf16[1,10,1,1024]{3,2,1,0:T(2,128)(2,1)} %get-tuple-element.11), channel_id=1, source_target_pairs={{0,4},{4,8},{8,12},{1,5},{5,9},{9,13},{2,6},{6,10},{10,14},{3,7},{... | collective-permute-start | bytes 61448 | tf_op jit(solution)/shard_map/ppermute | solution.py:20
  50.0 8.1 %copy-start.4 = (bf16[10,18,1,8,2,64]{5,4,3,1,0,2:T(2,128)(2,1)S(1)}, bf16[10,18,1,8,2,64]{5,4,3,1,0,2:T(2,128)(2,1)}, u32[]{:S(2)}) copy-start(bf16[10,18,1,8,2,64]{5,4,3,1,0,2:T(2,128)(2,1)} %get-tuple-element.6) | copy-start | bytes 1105924
  50.2 8.1 %copy-start.3 = (bf16[10,18,1,8,2,64]{5,4,3,1,0,2:T(2,128)(2,1)S(1)}, bf16[10,18,1,8,2,64]{5,4,3,1,0,2:T(2,128)(2,1)}, u32[]{:S(2)}) copy-start(bf16[10,18,1,8,2,64]{5,4,3,1,0,2:T(2,128)(2,1)} %get-tuple-element.5) | copy-start | bytes 1105924
  52.6 13.5 %collective-permute-start.4 = (bf16[1,1,16,1024]{3,2,1,0:T(8,128)(2,1)}, bf16[1,1,16,1024]{3,2,1,0:T(8,128)(2,1)}, u32[]{:S(2)}, u32[]{:S(2)}) collective-permute-start(bf16[1,1,16,1024]{3,2,1,0:T(8,128)(2,1)} %get-tuple-element.20), channel_id=1, source_target_pairs={{0,16},{1,17},{2,18},{3,19},{4,20},{5,21},{6,22},{7,23},{8,24},{9,... | collective-permute-start | bytes 98312 | tf_op jit(solution)/shard_map/ppermute | solution.py:20
  55.4 11.6 %collective-permute-start.5 = (bf16[1,1,16,1024]{3,2,1,0:T(8,128)(2,1)}, bf16[1,1,16,1024]{3,2,1,0:T(8,128)(2,1)S(1)}, u32[]{:S(2)}, u32[]{:S(2)}) collective-permute-start(bf16[1,1,16,1024]{3,2,1,0:T(8,128)(2,1)} %get-tuple-element.19), channel_id=1, source_target_pairs={{16,0},{17,1},{18,2},{19,3},{20,4},{21,5},{22,6},{23,7},{24,8},{25... | collective-permute-start | bytes 98312 | tf_op jit(solution)/shard_map/ppermute | solution.py:22
  59.3 1.9 copy-start.14
  65.9 7.8 %copy-start.9 = (bf16[10,18,8,3,64,1]{4,2,5,3,1,0:T(8,128)(2,1)S(1)}, bf16[10,18,8,3,64,1]{4,2,5,3,1,0:T(8,128)(2,1)}, u32[]{:S(2)}) copy-start(bf16[10,18,8,3,64,1]{4,2,5,3,1,0:T(8,128)(2,1)} %copy.38) | copy-start | bytes 1658884
  67.8 33.1 %collective-permute-start.7 = (bf16[1,10,1,1024]{3,2,1,0:T(2,128)(2,1)S(1)}, bf16[1,10,1,1024]{3,2,1,0:T(2,128)(2,1)S(1)}, u32[]{:S(2)}, u32[]{:S(2)}) collective-permute-start(bf16[1,10,1,1024]{3,2,1,0:T(2,128)(2,1)S(1)} %get-tuple-element.14), channel_id=1, source_target_pairs={{4,0},{8,4},{12,8},{5,1},{9,5},{13,9},{6,2},{10,6},{14,10},{7,3},{... | collective-permute-start | bytes 61448 | tf_op jit(solution)/shard_map/ppermute | solution.py:22
  69.1 31.8 %collective-permute-start.6 = (bf16[1,10,1,1024]{3,2,1,0:T(2,128)(2,1)S(1)}, bf16[1,10,1,1024]{3,2,1,0:T(2,128)(2,1)S(1)}, u32[]{:S(2)}, u32[]{:S(2)}) collective-permute-start(bf16[1,10,1,1024]{3,2,1,0:T(2,128)(2,1)S(1)} %get-tuple-element.13), channel_id=1, source_target_pairs={{0,4},{4,8},{8,12},{1,5},{5,9},{9,13},{2,6},{6,10},{10,14},{3,7},{... | collective-permute-start | bytes 61448 | tf_op jit(solution)/shard_map/ppermute | solution.py:20
  106.4 2.3 copy-start.6
  106.4 2.3 copy-start.10
  257.2 2.3 copy-start.11
  (8 other events, 8.7 us)
Sparse Core Ops, SparseCore 0:
  122.9 134.2 all-reduce.2
where the time goes:
time: 271 us; the launch traced here: 267 us
  waiting for transfers between devices  128 us (47%)
  matrix products  49.5 us (18%)
  local copies, waits for them, and re-layouts  39.1 us (14%)
  starting transfers between devices  31.7 us (12%)
  between operations  14.8 us (5%)
  other arithmetic  4.27 us (2%)
    psum x1, waiting for transfers between devices, reduce_grad(): return lax.psum(local, ('gx', 'gy', 'grp'))  128 us
    transpose x2, matrix products, kernel_local(): return jnp.transpose(result, (1, 2, 3, 0, 4))  41.1 us
    ppermute x6, starting transfers between devices, extended(): lax.ppermute(tail, axis, [(i, (i + 1) % count) for i in range(ends)])  23.7 us
    reshape x13, local copies, waits for them, and re-layouts, as_cells(): return field.reshape(field.shape[0], field.shape[1], field.shape[2], NZ, C)  16.8 us
    unnamed x50, local copies, waits for them, and re-layouts  9.48 us
    conv_general_dilated x2, matrix products, conv_local(): lax.conv_general_dilated(padded, weight, (1, 1, 1), ((0, 0), (0, 0), (1,...  8.46 us
    ppermute x6, starting transfers between devices, extended(): lax.ppermute(head, axis, [((i + 1) % count, i) for i in range(ends)])  7.99 us
    conv_general_dilated x9, local copies, waits for them, and re-layouts, conv_local(): lax.conv_general_dilated(padded, weight, (1, 1, 1), ((0, 0), (0, 0), (1,...  6.24 us
  transfers between devices with their start and end apart: 13, of which 1 were waited for; matrix products, arithmetic and copies ran while one was open for 24% of the time, Pallas kernels for 0%

commit v1 on v0

v1 whole, which is shorter than its diff:
```python
import functools
import math

import jax
import jax.numpy as jnp
from jax import lax
from jax.experimental import pallas as pl
from jax.experimental.pallas import tpu as pltpu
from jax.sharding import PartitionSpec as P

C = 64
NZ = 16
BF16 = jnp.bfloat16
F32 = jnp.float32
TAPS = [(dx, dy) for dx in range(3) for dy in range(3)]
BLOCKS = 14


def swap(array):
    return lax.ppermute(array, "gx", [(0, 1), (1, 0)])


def shift(array, step):
    count = lax.axis_size("gy")
    return lax.ppermute(array, "gy", [(i, i + step) for i in range(count) if 0 <= i + step < count])


def dot(a, b):
    return jnp.dot(a, b, preferred_element_type=F32)


def dot_nt(a, b):
    return lax.dot_general(a, b, (((1,), (1,)), ((), ())), preferred_element_type=F32)


def band(taps):
    zero = jnp.zeros((C, C), BF16)
    left = jnp.concatenate(list(taps) + [zero], axis=0)
    right = jnp.concatenate([zero] + list(taps), axis=0)
    return jnp.concatenate([left, right], axis=1)


def band_flipped(taps):
    zero = jnp.zeros((C, C), BF16)
    back = list(taps)[::-1]
    upper = jnp.concatenate(back + [zero], axis=1)
    lower = jnp.concatenate([zero] + back, axis=1)
    return jnp.concatenate([upper, lower], axis=0)


def shifted_rows(scratch, target, width):
    rows = target.shape[2]
    target[0, :, :, pl.ds(width, scratch.shape[2])] = scratch[:, 7:7 + rows, :].astype(BF16)
    target[2, :, :, pl.ds(width, scratch.shape[2])] = scratch[:, 9:9 + rows, :].astype(BF16)


def weight_gradient(rows_t, taps_of, total):
    result = []
    for dx, dy in TAPS:
        full = dot(rows_t, taps_of(dx, dy)) * total
        result.append(full[0:C, 0:3 * C] + full[C:2 * C, C:4 * C])
    return result


def packed(pieces):
    blocks = [piece[:, 0:2 * C] for piece in pieces]
    for pair in range(0, 9, 2):
        second = pieces[pair + 1][:, 2 * C:3 * C] if pair + 1 < 9 else jnp.zeros((C, C), F32)
        blocks.append(jnp.concatenate([pieces[pair][:, 2 * C:3 * C], second], axis=1))
    return blocks


def layers(factor, gx_count, gy_count, field, cot, side, sent_head, sent_tail, from_prev, from_next, w1, w2,
           out, keep, send, fd, cd, hd, fs, cs, hs, es, eh, pf, w1b, w2b, wfb):
    nx, ny, width = field.shape
    pairs = NZ // 2
    lane = 2 * C
    gx = lax.axis_index("gx")
    gy = lax.axis_index("gy")
    low = (gx > 0).astype(F32)
    high = (gx < gx_count - 1).astype(F32)
    prev = (gy > 0).astype(F32)
    after = (gy < gy_count - 1).astype(F32)

    for t in range(9):
        w1b[t * 4 * C:(t + 1) * 4 * C, :] = band([w1[3 * t + z] for z in range(3)])
        w2b[t * 4 * C:(t + 1) * 4 * C, :] = band([w2[3 * t + z] for z in range(3)])
        wfb[:, t * 4 * C:(t + 1) * 4 * C] = band_flipped([w2[3 * (8 - t) + z] for z in range(3)])

    fs[2:2 + nx, 8:8 + ny, :] = field[...].astype(F32)
    fs[0:2, 8:8 + ny, :] = side[0:2].astype(F32) * low
    fs[2 + nx:4 + nx, 8:8 + ny, :] = side[0:2].astype(F32) * high
    cs[1:1 + nx, 8:8 + ny, :] = cot[...].astype(F32)
    cs[0:1, 8:8 + ny, :] = side[2:3].astype(F32) * low
    cs[1 + nx:2 + nx, 8:8 + ny, :] = side[2:3].astype(F32) * high

    rows_prev = from_prev[...].astype(F32) * prev
    rows_next = from_next[...].astype(F32) * after
    for x in range(nx + 4):
        fs[x, 7:8, :] = rows_prev[1, x:x + 1, :]
        fs[x, 8 + ny:9 + ny, :] = rows_next[0, x:x + 1, :]
    for x in range(nx + 2):
        cs[x, 7:8, :] = rows_prev[2, x + 1:x + 2, :]
        cs[x, 8 + ny:9 + ny, :] = rows_next[2, x + 1:x + 2, :]

    for copies in (fd, cd):
        copies[:, :, :, 0:lane] = jnp.zeros(copies.shape[:3] + (lane,), BF16)
        copies[:, :, :, lane + width:] = jnp.zeros(copies.shape[:3] + (lane,), BF16)
    for scratch, copies in ((fs, fd), (cs, cd)):
        shifted_rows(scratch, copies, lane)
        copies[1, :, :, lane:lane + width] = scratch[:, 8:8 + ny, :].astype(BF16)

    es[...] = jnp.zeros(es.shape, F32)
    for index, rows in enumerate((
        rows_prev[0], rows_prev[1], sent_head[0].astype(F32),
        sent_tail[1].astype(F32), rows_next[0], rows_next[1],
    )):
        es[index, 0:nx + 4, :] = rows
    eh[:, :, :, 0:lane] = jnp.zeros((9, 2, 16, lane), BF16)
    eh[:, :, :, lane + width:] = jnp.zeros((9, 2, 16, lane), BF16)
    for t, (dx, dy) in enumerate(TAPS):
        for end in range(2):
            eh[t, end, :, lane:lane + width] = es[3 * end + dy, dx:dx + 16, :].astype(BF16)

    depth = nx + 2
    main = depth * ny
    x_of = lax.broadcasted_iota(jnp.int32, (depth, ny, lane), 0)
    mask = jnp.where(x_of == 0, low, jnp.where(x_of == depth - 1, high, 1.0))
    end_of = lax.broadcasted_iota(jnp.int32, (2, 16, lane), 0)
    row_of = lax.broadcasted_iota(jnp.int32, (2, 16, lane), 1)
    end_mask = jnp.where(row_of == 0, low, jnp.where(row_of == depth - 1, high, 1.0)) * jnp.where(end_of == 0, prev, after)
    lane_of = lax.broadcasted_iota(jnp.int32, (1, 1, lane), 2)
    for p in range(pairs + 1):
        span = slice(lane * p, lane * (p + 2))
        here = slice(lane * p, lane * (p + 1))
        block = jnp.concatenate(
            [
                jnp.concatenate([fd[dy, dx:dx + depth, :, span].reshape(main, 2 * lane) for dx, dy in TAPS], axis=1),
                jnp.concatenate([eh[t, :, :, span].reshape(32, 2 * lane) for t in range(9)], axis=1),
            ],
            axis=0,
        )
        pre = dot(block, w1b[...])
        hidden = pre * jax.nn.sigmoid(pre)
        hidden_main = hidden[:main].reshape(depth, ny, lane) * mask
        hidden_ends = hidden[main:].reshape(2, 16, lane) * end_mask
        if p == 0:
            hidden_main = jnp.where(lane_of >= C, hidden_main, 0.0)
            hidden_ends = jnp.where(lane_of >= C, hidden_ends, 0.0)
        if p == pairs:
            hidden_main = jnp.where(lane_of < C, hidden_main, 0.0)
            hidden_ends = jnp.where(lane_of < C, hidden_ends, 0.0)
        pf[p] = pre[ny:ny + nx * ny]
        hs[:, 8:8 + ny, here] = hidden_main
        hd[1, :, :, here] = hidden_main.astype(BF16)
        for x in range(depth):
            hs[x, 7:8, here] = hidden_ends[0, x:x + 1, :]
            hs[x, 8 + ny:9 + ny, here] = hidden_ends[1, x:x + 1, :]
    shifted_rows(hs, hd, 0)

    cells = nx * ny

    def hidden_span(dx, dy, p):
        return hd[dy, dx:dx + nx, :, lane * p:lane * (p + 2)].reshape(cells, 2 * lane)

    def field_span(dx, dy, p):
        return fd[dy, dx + 1:dx + 1 + nx, :, lane * p:lane * (p + 2)].reshape(cells, 2 * lane)

    def cot_span(dx, dy, p):
        return cd[dy, dx:dx + nx, :, lane * p:lane * (p + 2)].reshape(cells, 2 * lane)

    cot_t = jnp.concatenate(
        [cot[:, :, lane * p:lane * (p + 1)].reshape(cells, lane).T for p in range(pairs)], axis=1)
    second = packed(weight_gradient(
        cot_t,
        lambda dx, dy: jnp.concatenate([hidden_span(dx, dy, p) for p in range(pairs)], axis=0),
        factor))

    grads_t = []
    for p in range(pairs + 1):
        grad = dot_nt(jnp.concatenate([cot_span(dx, dy, p) for dx, dy in TAPS], axis=1), wfb[...])
        pre = pf[p]
        sigma = jax.nn.sigmoid(pre)
        grad = grad * sigma * (1.0 + pre * (1.0 - sigma))
        if p == 0:
            grad = jnp.where(lane_of[0] >= C, grad, 0.0)
        if p == pairs:
            grad = jnp.where(lane_of[0] < C, grad, 0.0)
        grads_t.append(grad.astype(BF16).T)
    first = packed(weight_gradient(
        jnp.concatenate(grads_t, axis=1),
        lambda dx, dy: jnp.concatenate([field_span(dx, dy, p) for p in range(pairs + 1)], axis=0),
        factor))

    for index in range(BLOCKS):
        rows = slice(index * C, (index + 1) * C)
        keep[rows, :] = jnp.where(gx == 0, first[index], second[index])
        send[rows, :] = jnp.where(gx == 0, second[index], first[index]).astype(BF16)
    if keep.shape[0] > BLOCKS * C:
        rest = (keep.shape[0] - BLOCKS * C, lane)
        keep[BLOCKS * C:, :] = jnp.zeros(rest, F32)
        send[BLOCKS * C:, :] = jnp.zeros(rest, BF16)

    for p in range(pairs):
        block = jnp.concatenate([hidden_span(dx, dy, p) for dx, dy in TAPS], axis=1)
        out[:, :, lane * p:lane * (p + 1)] = dot(block, w2b[...]).astype(BF16).reshape(nx, ny, lane)


def unpack(mine, other, first, second):
    gx = lax.axis_index("gx")
    a = mine[...].astype(F32)
    b = other[...].astype(F32)
    for out, rows in ((first, jnp.where(gx == 0, a, b)), (second, jnp.where(gx == 0, b, a))):
        for t in range(9):
            turned = rows[t * C:(t + 1) * C].T
            out[3 * t] = turned[0:C]
            out[3 * t + 1] = turned[C:2 * C]
        for pair in range(5):
            turned = rows[(9 + pair) * C:(10 + pair) * C].T
            out[6 * pair + 2] = turned[0:C]
            if pair < 4:
                out[6 * pair + 5] = turned[C:2 * C]


def vmem(count):
    return [pl.BlockSpec(memory_space=pltpu.VMEM)] * count


def shards(field_in, first_weight, second_weight, cotangent):
    nx, ny, width = field_in.shape[1:]
    gx_count, gy_count, grp_count = (lax.axis_size(axis) for axis in ("gx", "gy", "grp"))
    total = field_in.shape[0] * nx * ny * NZ * gx_count * gy_count * grp_count
    factor = 1.0 / math.sqrt(total)
    ranks = gy_count * grp_count
    rows = -(-BLOCKS * C // (16 * ranks)) * 16 * ranks
    gx = lax.axis_index("gx")
    field = field_in[0]
    cot = cotangent[0]

    side = swap(jnp.concatenate(
        [
            jnp.where(gx == 0, field[nx - 2:nx], field[0:2]),
            jnp.where(gx == 0, cot[nx - 1:nx], cot[0:1]),
        ],
        axis=0,
    ))
    low = jnp.where(gx == 0, jnp.zeros_like(side), side)
    high = jnp.where(gx == 0, side, jnp.zeros_like(side))

    def edge(first_row, cot_row):
        fields = jnp.concatenate([a[:, first_row:first_row + 2] for a in (low[0:2], field, high[0:2])], axis=0)
        cots = jnp.concatenate([a[:, cot_row:cot_row + 1] for a in (low[2:3], cot, high[2:3])], axis=0)
        cots = jnp.pad(cots, ((1, 1), (0, 0), (0, 0)))
        return jnp.transpose(jnp.concatenate([fields, cots], axis=1), (1, 0, 2))

    head = edge(0, 0)
    tail = edge(ny - 2, ny - 1)
    from_prev = shift(tail, 1)
    from_next = shift(head, -1)

    lane = 2 * C
    wide = width + 2 * lane
    out, keep, send = pl.pallas_call(
        functools.partial(layers, factor, gx_count, gy_count),
        out_shape=[
            jax.ShapeDtypeStruct((nx, ny, width), BF16),
            jax.ShapeDtypeStruct((rows, lane), F32),
            jax.ShapeDtypeStruct((rows, lane), BF16),
        ],
        in_specs=vmem(9),
        out_specs=vmem(3),
        scratch_shapes=[
            pltpu.VMEM((3, nx + 4, ny, wide), BF16),
            pltpu.VMEM((3, nx + 2, ny, wide), BF16),
            pltpu.VMEM((3, nx + 2, ny, width + lane), BF16),
            pltpu.VMEM((nx + 4, ny + 16, width), F32),
            pltpu.VMEM((nx + 2, ny + 16, width), F32),
            pltpu.VMEM((nx + 2, ny + 16, width + lane), F32),
            pltpu.VMEM((6, 24, width), F32),
            pltpu.VMEM((9, 2, 16, wide), BF16),
            pltpu.VMEM((NZ // 2 + 1, nx * ny, lane), F32),
            pltpu.VMEM((9 * 4 * C, lane), BF16),
            pltpu.VMEM((9 * 4 * C, lane), BF16),
            pltpu.VMEM((lane, 9 * 4 * C), BF16),
        ],
        compiler_params=pltpu.CompilerParams(vmem_limit_bytes=56 * 1024 * 1024),
        name="layers",
    )(field, cot, side, head, tail, from_prev, from_next,
      first_weight.reshape(27, C, C), second_weight.reshape(27, C, C))

    both = (keep + swap(send).astype(F32)).astype(BF16).reshape(ranks, rows // ranks, lane)
    terms = lax.all_to_all(both, ("gy", "grp"), 0, 0)
    mine = jnp.sum(terms.astype(F32), axis=0).astype(BF16)
    mine = lax.all_to_all(jnp.broadcast_to(mine[None], terms.shape), ("gy", "grp"), 0, 0).reshape(rows, lane)
    other = swap(mine)
    first, second = pl.pallas_call(
        unpack,
        out_shape=[jax.ShapeDtypeStruct((27, C, C), F32)] * 2,
        in_specs=vmem(2),
        out_specs=vmem(2),
        name="unpack",
    )(mine, other)
    shape = (3, 3, 3, C, C)
    return out[None], first.reshape(shape), second.reshape(shape)


def solution(mesh):
    return jax.shard_map(
        shards,
        mesh=mesh,
        in_specs=(P("grp", "gx", "gy", None), P(), P(), P("grp", "gx", "gy", None)),
        out_specs=(P("grp", "gx", "gy", None), P(), P()),
        check_vma=False,
    )
```

time: 271 us -> 64.2 us (0.24); the launches traced: 267 us -> 63.7 us
  waiting for transfers between devices: 128 us -> 5.58 us
  matrix products: 49.5 us -> 0 us
  local copies, waits for them, and re-layouts: 39.1 us -> 3.6 us
  blocking collectives: 0 us -> 32.5 us
  starting transfers between devices: 31.7 us -> 7.2 us
  between operations: 14.8 us -> 0.79 us
  Pallas kernels: 0 us -> 11.6 us
    psum x1 -> x0, waiting for transfers between devices: 128 us -> none  [reduce_grad(): return lax.psum(local, ('gx', 'gy', 'grp'))]
    transpose x2 -> x0, matrix products: 41.1 us -> none  [kernel_local(): return jnp.transpose(result, (1, 2, 3, 0, 4))]
    all_to_all x0 -> x2, blocking collectives: none -> 32.5 us  [the longest x1 19.7 us: shards(): terms = lax.all_to_all(both, ('gy', 'grp'), 0, 0)]
    ppermute x12 -> x5, starting transfers between devices: 31.6 us -> 7.2 us  [the longest x2 6.68 us: shift(): lax.ppermute(array, 'gy', [(i, i + step) for i in range(count) if 0 <= i...]
    reshape x15 -> x0, local copies, waits for them, and re-layouts: 18.9 us -> none  [the longest x13 16.8 us: as_cells(): return field.reshape(field.shape[0], field.shape[1], field.shape[2], NZ, C)]
    pallas_call x0 -> x2, Pallas kernels: none -> 11.6 us  [the longest x1 9.16 us: shards(): pl.pallas_call(functools.partial(layers, factor, gx_count, gy_count), out...]
    conv_general_dilated x2 -> x0, matrix products: 8.46 us -> none  [conv_local(): lax.conv_general_dilated(padded, weight, (1, 1, 1), ((0, 0), (0, 0), (1,...]
    unnamed x50 -> x16, local copies, waits for them, and re-layouts: 9.48 us -> 2.76 us
  transfers between devices with their start and end apart: 13 -> 5, of which waited for: 1 -> 5; matrix products, arithmetic and copies ran while one was open for 24% -> 1% of each run, Pallas kernels for 0% -> 0%
where the time goes in v1:
time: 64.2 us; the launch traced here: 63.7 us
  blocking collectives  32.5 us (51%)
  Pallas kernels  11.6 us (18%)
  starting transfers between devices  7.2 us (11%)
  waiting for transfers between devices  5.58 us (9%)
  local copies, waits for them, and re-layouts  3.6 us (6%)
  other arithmetic  2.43 us (4%)
  between operations  0.79 us (1%)
    all_to_all x1, blocking collectives, shards(): terms = lax.all_to_all(both, ('gy', 'grp'), 0, 0)  19.7 us
    all_to_all x1, blocking collectives, shards(): lax.all_to_all(jnp.broadcast_to(mine[None], terms.shape), ('gy', 'grp'),...  12.8 us
    pallas_call x1, Pallas kernels, shards(): pl.pallas_call(functools.partial(layers, factor, gx_count, gy_count), out...  9.16 us
    ppermute x2, starting transfers between devices, shift(): lax.ppermute(array, 'gy', [(i, i + step) for i in range(count) if 0 <= i...  6.68 us
    ppermute x3, waiting for transfers between devices, swap(): return lax.ppermute(array, 'gx', [(0, 1), (1, 0)])  3.92 us
    unnamed x16, local copies, waits for them, and re-layouts  2.76 us
    pallas_call x1, Pallas kernels, shards(): pl.pallas_call(unpack, out_shape=[jax.ShapeDtypeStruct((27, C, C), F32)]...  2.45 us
    ppermute x2, waiting for transfers between devices, shift(): lax.ppermute(array, 'gy', [(i, i + step) for i in range(count) if 0 <= i...  1.65 us
  transfers between devices with their start and end apart: 5, of which 5 were waited for; matrix products, arithmetic and copies ran while one was open for 1% of the time, Pallas kernels for 0%

profile of v1, /device:TPU:0, one launch (start us, length us, event | category | flops | bytes accessed | tf_op | source)
XLA Modules:
  0.0 63.7 jit_solution(10016480255760506852)
XLA Ops:
  0.6 0.8 %select_bitcast_fusion = bf16[1,16,1024]{2,1,0:T(8,128)(2,1)S(1)} fusion(bf16[1,8,16,1024]{3,2,1,0:T(8,128)(2,1)} %param.7, pred[]{:T(512)S(6)} %eq.2), kind=kLoop, calls=%fused_computation.17 | loop fusion | flops 16384 | bytes 98305 | tf_op jit(solution)/shard_map/jit(_where)/select_n | solution.py:243
  1.4 0.1 copy.18
  1.5 1.1 %copy.28 = bf16[1,8,16,1024]{3,1,2,0:T(8,128)(2,1)S(1)} copy(bf16[1,8,16,1024]{3,2,1,0:T(8,128)(2,1)} %param.4) | data formatting | bytes 524288 | tf_op args[0]
  2.6 0.1 fusion
  2.7 0.1 pad_maximum_fusion
  2.9 0.5 collective-permute-start
  3.4 0.2 copy-done
  3.5 0.1 copy.27
  3.7 0.6 %collective-permute-done = bf16[3,16,1024]{2,0,1:T(4,128)(2,1)S(1)} collective-permute-done((bf16[3,16,1024]{2,0,1:T(4,128)(2,1)S(1)}, bf16[3,16,1024]{2,0,1:T(4,128)(2,1)S(1)}, u32[]{:S(2)}, u32[]{:S(2)}) %collective-permute-start) | collective-permute-done | bytes 98336 | tf_op jit(solution)/shard_map/ppermute | solution.py:20
  4.4 0.1 broadcast_select_fusion.1
  4.6 1.3 %collective-permute-start.2 = (bf16[3,12,1024]{2,1,0:T(8,128)(2,1)S(1)}, bf16[3,12,1024]{2,1,0:T(8,128)(2,1)S(1)}, u32[]{:S(2)}, u32[]{:S(2)}) collective-permute-start(bf16[3,12,1024]{2,1,0:T(8,128)(2,1)S(1)} %maximum_bitcast_fusion.sent_head), channel_id=1, source_target_pairs={{4,0},{8,4},{12,8},{5,1},{9,5},{13,9},{6,2},{10,6},{14,10},{7,3},{... | collective-permute-start | bytes 221192 | tf_op jit(solution)/shard_map/ppermute | solution.py:25
  6.0 5.4 %collective-permute-start.1 = (bf16[3,12,1024]{2,1,0:T(8,128)(2,1)S(1)}, bf16[3,12,1024]{2,1,0:T(8,128)(2,1)S(1)}, u32[]{:S(2)}, u32[]{:S(2)}) collective-permute-start(bf16[3,12,1024]{2,1,0:T(8,128)(2,1)S(1)} %maximum_bitcast_fusion.1.sent_tail), channel_id=1, source_target_pairs={{0,4},{4,8},{8,12},{1,5},{5,9},{9,13},{2,6},{6,10},{10,14},{3,7},{... | collective-permute-start | bytes 221192 | tf_op jit(solution)/shard_map/ppermute | solution.py:25
  11.4 0.7 %copy.21.side = bf16[3,16,1024]{2,1,0:T(8,128)(2,1)} copy(bf16[3,16,1024]{2,0,1:T(4,128)(2,1)S(1)} %collective-permute-done) | data formatting | bytes 196608 | tf_op jit(solution)/shard_map/ppermute | solution.py:20
  12.1 0.4 collective-permute-done.2.from_next
  12.5 1.3 %collective-permute-done.1.from_prev = bf16[3,12,1024]{2,1,0:T(8,128)(2,1)S(1)} collective-permute-done((bf16[3,12,1024]{2,1,0:T(8,128)(2,1)S(1)}, bf16[3,12,1024]{2,1,0:T(8,128)(2,1)S(1)}, u32[]{:S(2)}, u32[]{:S(2)}) %collective-permute-start.1) | collective-permute-done | bytes 73760 | tf_op jit(solution)/shard_map/ppermute | solution.py:25
  13.8 0.6 copy-done.6
  14.4 9.2 %layers.1 = (bf16[8,16,1024]{2,1,0:T(8,128)(2,1)}, f32[1024,128]{1,0:T(8,128)}, bf16[1024,128]{1,0:T(8,128)(2,1)}) custom-call(bf16[8,16,1024]{2,1,0:T(8,128)(2,1)} %bitcast.27, bf16[8,16,1024]{2,1,0:T(8,128)(2,1)} %bitcast.23, bf16[3,16,1024]{2,1,0:T(8,128)(2,1)} %copy.21.side, bf16[3,12,1024]{2,1,0:T(8,128)(2,1)} %copy-done.2, ...), custom_call_target="tpu_custom_call" | custom-call | tf_op jit(solution)/shard_map/layers/pallas_call | solution.py:263
  23.6 1.7 %collective-permute-done.3 = bf16[1024,128]{1,0:T(8,128)(2,1)S(1)} collective-permute-done((bf16[1024,128]{1,0:T(8,128)(2,1)}, bf16[1024,128]{1,0:T(8,128)(2,1)S(1)}, u32[]{:S(2)}, u32[]{:S(2)}) %collective-permute-start.3) | collective-permute-done | bytes 262176 | tf_op jit(solution)/shard_map/ppermute | solution.py:20
  25.3 1.1 %add_convert_fusion = bf16[1024,128]{1,0:T(8,128)(2,1)S(1)} fusion(f32[1024,128]{1,0:T(8,128)} %get-tuple-element.9, bf16[1024,128]{1,0:T(8,128)(2,1)S(1)} %collective-permute-done.3), kind=kLoop, calls=%fused_computation | loop fusion | flops 393216 | bytes 1048576 | tf_op jit(solution)/shard_map/convert_element_type | solution.py:291
  26.4 19.7 %all_to_all.10 = bf16[16,64,128]{2,1,0:T(8,128)(2,1)S(1)} all-to-all(bf16[16,64,128]{2,1,0:T(8,128)(2,1)S(1)} %bitcast.26), channel_id=1, replica_groups=mesh['gx'=2,'gy'=4,'grp'=4] {'gy','grp'}, dimensions={0} | all-to-all | bytes 524288 | tf_op jit(solution)/shard_map/all_to_all | solution.py:292
  46.2 12.8 %all_to_all.11 = bf16[16,64,128]{2,1,0:T(8,128)(2,1)S(1)} all-to-all(bf16[16,64,128]{2,1,0:T(8,128)(2,1)S(1)} %broadcast_in_dim.10), channel_id=1, replica_groups=mesh['gx'=2,'gy'=4,'grp'=4] {'gy','grp'}, dimensions={0} | all-to-all | bytes 524288 | tf_op jit(solution)/shard_map/all_to_all | solution.py:294
  59.1 1.5 %collective-permute-done.4.other = bf16[1024,128]{1,0:T(8,128)(2,1)S(1)} collective-permute-done((bf16[1024,128]{1,0:T(8,128)(2,1)S(1)}, bf16[1024,128]{1,0:T(8,128)(2,1)S(1)}, u32[]{:S(2)}, u32[]{:S(2)}) %collective-permute-start.4) | collective-permute-done | bytes 262176 | tf_op jit(solution)/shard_map/ppermute | solution.py:20
  60.6 0.7 %copy-done.4 = bf16[1024,128]{1,0:T(8,128)(2,1)} copy-done((bf16[1024,128]{1,0:T(8,128)(2,1)}, bf16[1024,128]{1,0:T(8,128)(2,1)S(1)}, u32[]{:S(2)}) %copy-start.4) | copy-done | bytes 262168
  61.3 2.4 %unpack.1 = (f32[27,64,64]{2,1,0:T(8,128)}, f32[27,64,64]{2,1,0:T(8,128)}) custom-call(bf16[1024,128]{1,0:T(8,128)(2,1)} %bitcast.25, bf16[1024,128]{1,0:T(8,128)(2,1)} %copy-done.4), custom_call_target="tpu_custom_call" | custom-call | tf_op jit(solution)/shard_map/unpack/pallas_call | solution.py:296
  (23 shorter events, 0.3 us)
Async XLA Ops:
  2.6 1.0 %copy-start = (bf16[1,8,16,1024]{3,2,1,0:T(8,128)(2,1)S(1)}, bf16[1,8,16,1024]{3,2,1,0:T(8,128)(2,1)}, u32[]{:S(2)}) copy-start(bf16[1,8,16,1024]{3,2,1,0:T(8,128)(2,1)} %param.7) | copy-start | bytes 786436
  2.9 1.5 %collective-permute-start = (bf16[3,16,1024]{2,0,1:T(4,128)(2,1)S(1)}, bf16[3,16,1024]{2,0,1:T(4,128)(2,1)S(1)}, u32[]{:S(2)}, u32[]{:S(2)}) collective-permute-start(bf16[3,16,1024]{2,0,1:T(4,128)(2,1)S(1)} %pad_maximum_fusion), channel_id=1, source_target_pairs={{0,16},{16,0},{1,17},{17,1},{2,18},{18,2},{3,19},{19,3},{4,20},{20... | collective-permute-start | bytes 294920 | tf_op jit(solution)/shard_map/ppermute | solution.py:20
  4.6 1.4 %copy-start.2 = (bf16[3,12,1024]{2,1,0:T(8,128)(2,1)}, bf16[3,12,1024]{2,1,0:T(8,128)(2,1)S(1)}, u32[]{:S(2)}) copy-start(bf16[3,12,1024]{2,1,0:T(8,128)(2,1)S(1)} %maximum_bitcast_fusion.sent_head) | copy-start | bytes 221188
  4.6 7.9 %collective-permute-start.2 = (bf16[3,12,1024]{2,1,0:T(8,128)(2,1)S(1)}, bf16[3,12,1024]{2,1,0:T(8,128)(2,1)S(1)}, u32[]{:S(2)}, u32[]{:S(2)}) collective-permute-start(bf16[3,12,1024]{2,1,0:T(8,128)(2,1)S(1)} %maximum_bitcast_fusion.sent_head), channel_id=1, source_target_pairs={{4,0},{8,4},{12,8},{5,1},{9,5},{13,9},{6,2},{10,6},{14,10},{7,3},{... | collective-permute-start | bytes 221192 | tf_op jit(solution)/shard_map/ppermute | solution.py:25
  6.0 6.1 %copy-start.3 = (bf16[3,12,1024]{2,1,0:T(8,128)(2,1)}, bf16[3,12,1024]{2,1,0:T(8,128)(2,1)S(1)}, u32[]{:S(2)}) copy-start(bf16[3,12,1024]{2,1,0:T(8,128)(2,1)S(1)} %maximum_bitcast_fusion.1.sent_tail) | copy-start | bytes 221188
  6.0 7.7 %collective-permute-start.1 = (bf16[3,12,1024]{2,1,0:T(8,128)(2,1)S(1)}, bf16[3,12,1024]{2,1,0:T(8,128)(2,1)S(1)}, u32[]{:S(2)}, u32[]{:S(2)}) collective-permute-start(bf16[3,12,1024]{2,1,0:T(8,128)(2,1)S(1)} %maximum_bitcast_fusion.1.sent_tail), channel_id=1, source_target_pairs={{0,4},{4,8},{8,12},{1,5},{5,9},{9,13},{2,6},{6,10},{10,14},{3,7},{... | collective-permute-start | bytes 221192 | tf_op jit(solution)/shard_map/ppermute | solution.py:25
  12.5 1.3 %copy-start.5 = (bf16[3,12,1024]{2,1,0:T(8,128)(2,1)}, bf16[3,12,1024]{2,1,0:T(8,128)(2,1)S(1)}, u32[]{:S(2)}) copy-start(bf16[3,12,1024]{2,1,0:T(8,128)(2,1)S(1)} %collective-permute-done.2.from_next) | copy-start | bytes 221188
  13.8 0.6 %copy-start.6 = (bf16[3,12,1024]{2,1,0:T(8,128)(2,1)}, bf16[3,12,1024]{2,1,0:T(8,128)(2,1)S(1)}, u32[]{:S(2)}) copy-start(bf16[3,12,1024]{2,1,0:T(8,128)(2,1)S(1)} %collective-permute-done.1.from_prev) | copy-start | bytes 221188
  23.6 1.7 %collective-permute-start.3 = (bf16[1024,128]{1,0:T(8,128)(2,1)}, bf16[1024,128]{1,0:T(8,128)(2,1)S(1)}, u32[]{:S(2)}, u32[]{:S(2)}) collective-permute-start(bf16[1024,128]{1,0:T(8,128)(2,1)} %get-tuple-element.10), channel_id=1, source_target_pairs={{0,16},{16,0},{1,17},{17,1},{2,18},{18,2},{3,19},{19,3},{4,20},{20... | collective-permute-start | bytes 786440 | tf_op jit(solution)/shard_map/ppermute | solution.py:20
  59.1 1.5 %copy-start.1 = (bf16[16,64,128]{2,1,0:T(8,128)(2,1)}, bf16[16,64,128]{2,1,0:T(8,128)(2,1)S(1)}, u32[]{:S(2)}) copy-start(bf16[16,64,128]{2,1,0:T(8,128)(2,1)S(1)} %all_to_all.11) | copy-start | bytes 786436
  59.1 1.5 %collective-permute-start.4 = (bf16[1024,128]{1,0:T(8,128)(2,1)S(1)}, bf16[1024,128]{1,0:T(8,128)(2,1)S(1)}, u32[]{:S(2)}, u32[]{:S(2)}) collective-permute-start(bf16[1024,128]{1,0:T(8,128)(2,1)S(1)} %bitcast.24), channel_id=1, source_target_pairs={{0,16},{16,0},{1,17},{17,1},{2,18},{18,2},{3,19},{19,3},{4,20},{20... | collective-permute-start | bytes 786440 | tf_op jit(solution)/shard_map/ppermute | solution.py:20
  60.6 0.7 %copy-start.4 = (bf16[1024,128]{1,0:T(8,128)(2,1)}, bf16[1024,128]{1,0:T(8,128)(2,1)S(1)}, u32[]{:S(2)}) copy-start(bf16[1024,128]{1,0:T(8,128)(2,1)S(1)} %collective-permute-done.4.other) | copy-start | bytes 786436

commit v2 on v1

--- a/solution.py
+++ b/solution.py
@@ -70,8 +70,41 @@
     return blocks
 
 
-def layers(factor, gx_count, gy_count, field, cot, side, sent_head, sent_tail, from_prev, from_next, w1, w2,
-           out, keep, send, fd, cd, hd, fs, cs, hs, es, eh, pf, w1b, w2b, wfb):
+def pack(field, cot, head, tail, side, rows):
+    nx, ny, width = field.shape
+    gx = lax.axis_index("gx")
+    for x in range(nx):
+        fields = field[x].astype(F32)
+        cots = cot[x].astype(F32)
+        for index, row in enumerate((fields[0:1], fields[1:2], cots[0:1], fields[ny - 2:ny - 1], fields[ny - 1:ny], cots[ny - 1:ny])):
+            rows[index, x:x + 1, :] = row
+    head[...] = rows[0:3].astype(BF16)
+    tail[...] = rows[3:6].astype(BF16)
+
+    @pl.when(gx == 0)
+    def _():
+        side[0:2] = field[nx - 2:nx]
+        side[2:3] = cot[nx - 1:nx]
+
+    @pl.when(gx != 0)
+    def _():
+        side[0:2] = field[0:2]
+        side[2:3] = cot[0:1]
+
+
+def prepare(w1, w2, cot, w1b, w2b, wfb, cot_t):
+    cells = cot.shape[0] * cot.shape[1]
+    lane = 2 * C
+    for t in range(9):
+        w1b[t * 4 * C:(t + 1) * 4 * C, :] = band([w1[3 * t + z] for z in range(3)])
+        w2b[t * 4 * C:(t + 1) * 4 * C, :] = band([w2[3 * t + z] for z in range(3)])
+        wfb[:, t * 4 * C:(t + 1) * 4 * C] = band_flipped([w2[3 * (8 - t) + z] for z in range(3)])
+    for p in range(NZ // 2):
+        cot_t[:, cells * p:cells * (p + 1)] = cot[:, :, lane * p:lane * (p + 1)].reshape(cells, lane).T
+
+
+def layers(factor, gx_count, gy_count, field, cot, side, head, tail, from_prev, from_next, corner, w1b, wfb, cot_t,
+           hd, keep, send, fd, cd, fs, cs, hs, es, ec, eh, pf):
     nx, ny, width = field.shape
     pairs = NZ // 2
     lane = 2 * C
@@ -82,11 +115,6 @@
     prev = (gy > 0).astype(F32)
     after = (gy < gy_count - 1).astype(F32)
 
-    for t in range(9):
-        w1b[t * 4 * C:(t + 1) * 4 * C, :] = band([w1[3 * t + z] for z in range(3)])
-        w2b[t * 4 * C:(t + 1) * 4 * C, :] = band([w2[3 * t + z] for z in range(3)])
-        wfb[:, t * 4 * C:(t + 1) * 4 * C] = band_flipped([w2[3 * (8 - t) + z] for z in range(3)])
-
     fs[2:2 + nx, 8:8 + ny, :] = field[...].astype(F32)
     fs[0:2, 8:8 + ny, :] = side[0:2].astype(F32) * low
     fs[2 + nx:4 + nx, 8:8 + ny, :] = side[0:2].astype(F32) * high
@@ -94,14 +122,26 @@
     cs[0:1, 8:8 + ny, :] = side[2:3].astype(F32) * low
     cs[1 + nx:2 + nx, 8:8 + ny, :] = side[2:3].astype(F32) * high
 
-    rows_prev = from_prev[...].astype(F32) * prev
-    rows_next = from_next[...].astype(F32) * after
+    es[...] = jnp.zeros(es.shape, F32)
+    ec[...] = jnp.zeros(ec.shape, F32)
+    for end, own, there, scale in ((0, from_prev, 0, prev), (1, from_next, 3, after)):
+        for target, index, source in ((es, 4 * end, 0), (es, 4 * end + 1, 1), (ec, end, 2)):
+            other = corner[there + source].astype(F32) * scale
+            target[index, 8:8 + nx, :] = own[source].astype(F32) * scale
+            target[index, 6:8, :] = other[nx - 2:nx] * low
+            target[index, 8 + nx:10 + nx, :] = other[0:2] * high
+    es[2, 8:8 + nx, :] = head[0].astype(F32)
+    es[3, 8:8 + nx, :] = tail[1].astype(F32)
+    for x in (0, 1, nx + 2, nx + 3):
+        es[2, 6 + x:7 + x, :] = fs[x, 8:9, :]
+        es[3, 6 + x:7 + x, :] = fs[x, 7 + ny:8 + ny, :]
+
     for x in range(nx + 4):
-        fs[x, 7:8, :] = rows_prev[1, x:x + 1, :]
-        fs[x, 8 + ny:9 + ny, :] = rows_next[0, x:x + 1, :]
+        fs[x, 7:8, :] = es[1, 6 + x:7 + x, :]
+        fs[x, 8 + ny:9 + ny, :] = es[4, 6 + x:7 + x, :]
     for x in range(nx + 2):
-        cs[x, 7:8, :] = rows_prev[2, x + 1:x + 2, :]
-        cs[x, 8 + ny:9 + ny, :] = rows_next[2, x + 1:x + 2, :]
+        cs[x, 7:8, :] = ec[0, 7 + x:8 + x, :]
+        cs[x, 8 + ny:9 + ny, :] = ec[1, 7 + x:8 + x, :]
 
     for copies in (fd, cd):
         copies[:, :, :, 0:lane] = jnp.zeros(copies.shape[:3] + (lane,), BF16)
@@ -110,17 +150,11 @@
         shifted_rows(scratch, copies, lane)
         copies[1, :, :, lane:lane + width] = scratch[:, 8:8 + ny, :].astype(BF16)
 
-    es[...] = jnp.zeros(es.shape, F32)
-    for index, rows in enumerate((
-        rows_prev[0], rows_prev[1], sent_head[0].astype(F32),
-        sent_tail[1].astype(F32), rows_next[0], rows_next[1],
-    )):
-        es[index, 0:nx + 4, :] = rows
     eh[:, :, :, 0:lane] = jnp.zeros((9, 2, 16, lane), BF16)
     eh[:, :, :, lane + width:] = jnp.zeros((9, 2, 16, lane), BF16)
     for t, (dx, dy) in enumerate(TAPS):
         for end in range(2):
-            eh[t, end, :, lane:lane + width] = es[3 * end + dy, dx:dx + 16, :].astype(BF16)
+            eh[t, end, :, lane:lane + width] = es[3 * end + dy, 6 + dx:22 + dx, :].astype(BF16)
 
     depth = nx + 2
     main = depth * ny
@@ -169,10 +203,8 @@
     def cot_span(dx, dy, p):
         return cd[dy, dx:dx + nx, :, lane * p:lane * (p + 2)].reshape(cells, 2 * lane)
 
-    cot_t = jnp.concatenate(
-        [cot[:, :, lane * p:lane * (p + 1)].reshape(cells, lane).T for p in range(pairs)], axis=1)
     second = packed(weight_gradient(
-        cot_t,
+        cot_t[...],
         lambda dx, dy: jnp.concatenate([hidden_span(dx, dy, p) for p in range(pairs)], axis=0),
         factor))
 
@@ -201,9 +233,34 @@
         keep[BLOCKS * C:, :] = jnp.zeros(rest, F32)
         send[BLOCKS * C:, :] = jnp.zeros(rest, BF16)
 
-    for p in range(pairs):
-        block = jnp.concatenate([hidden_span(dx, dy, p) for dx, dy in TAPS], axis=1)
+
+def output_conv(hd, w2b, out):
+    nx, ny, _ = out.shape
+    lane = 2 * C
+    for p in range(NZ // 2):
+        block = jnp.concatenate(
+            [hd[dy, dx:dx + nx, :, lane * p:lane * (p + 2)].reshape(nx * ny, 2 * lane) for dx, dy in TAPS], axis=1)
         out[:, :, lane * p:lane * (p + 1)] = dot(block, w2b[...]).astype(BF16).reshape(nx, ny, lane)
+
+
+def add_pair(keep, other, out):
+    out[...] = (keep[...] + other[...].astype(F32)).astype(BF16)
+
+
+def add_terms(terms, out):
+    total = terms[0].astype(F32)
+    for index in range(1, terms.shape[0]):
+        total = total + terms[index].astype(F32)
+    out[...] = total.astype(BF16)
+
+
+def add_and_repeat(terms, out):
+    total = terms[0].astype(F32)
+    for index in range(1, terms.shape[0]):
+        total = total + terms[index].astype(F32)
+    total = total.astype(BF16)
+    for index in range(out.shape[0]):
+        out[index] = total
 
 
 def unpack(mine, other, first, second):
@@ -222,8 +279,23 @@
                 out[6 * pair + 5] = turned[C:2 * C]
 
 
-def vmem(count):
-    return [pl.BlockSpec(memory_space=pltpu.VMEM)] * count
+def near(shape, dtype):
+    return pltpu.VMEM(shape, dtype)
+
+
+def call(body, name, inputs, outs, scratch=(), limit=16, flops=0):
+    placed = [pltpu.with_memory_space_constraint(x, pltpu.VMEM) if held else x for x, held in inputs]
+    size = sum(x.size * x.dtype.itemsize for x in placed)
+    return pl.pallas_call(
+        body,
+        out_shape=list(outs),
+        in_specs=[pl.BlockSpec(memory_space=pltpu.VMEM)] * len(placed),
+        out_specs=[pl.BlockSpec(memory_space=pltpu.VMEM)] * len(outs),
+        scratch_shapes=list(scratch),
+        compiler_params=pltpu.CompilerParams(vmem_limit_bytes=limit * 1024 * 1024),
+        cost_estimate=pl.CostEstimate(flops=flops, bytes_accessed=size, transcendentals=0),
+        name=name,
+    )(*placed)
 
 
 def shards(field_in, first_weight, second_weight, cotangent):
@@ -232,74 +304,61 @@
     total = field_in.shape[0] * nx * ny * NZ * gx_count * gy_count * grp_count
     factor = 1.0 / math.sqrt(total)
     ranks = gy_count * grp_count
-    rows = -(-BLOCKS * C // (16 * ranks)) * 16 * ranks
-    gx = lax.axis_index("gx")
+    rows = -(-BLOCKS * C // (8 * ranks)) * 8 * ranks
     field = field_in[0]
     cot = cotangent[0]
-
-    side = swap(jnp.concatenate(
-        [
-            jnp.where(gx == 0, field[nx - 2:nx], field[0:2]),
-            jnp.where(gx == 0, cot[nx - 1:nx], cot[0:1]),
-        ],
-        axis=0,
-    ))
-    low = jnp.where(gx == 0, jnp.zeros_like(side), side)
-    high = jnp.where(gx == 0, side, jnp.zeros_like(side))
-
-    def edge(first_row, cot_row):
-        fields = jnp.concatenate([a[:, first_row:first_row + 2] for a in (low[0:2], field, high[0:2])], axis=0)
-        cots = jnp.concatenate([a[:, cot_row:cot_row + 1] for a in (low[2:3], cot, high[2:3])], axis=0)
-        cots = jnp.pad(cots, ((1, 1), (0, 0), (0, 0)))
-        return jnp.transpose(jnp.concatenate([fields, cots], axis=1), (1, 0, 2))
-
-    head = edge(0, 0)
-    tail = edge(ny - 2, ny - 1)
-    from_prev = shift(tail, 1)
-    from_next = shift(head, -1)
-
     lane = 2 * C
     wide = width + 2 * lane
-    out, keep, send = pl.pallas_call(
-        functools.partial(layers, factor, gx_count, gy_count),
-        out_shape=[
-            jax.ShapeDtypeStruct((nx, ny, width), BF16),
-            jax.ShapeDtypeStruct((rows, lane), F32),
-            jax.ShapeDtypeStruct((rows, lane), BF16),
-        ],
-        in_specs=vmem(9),
-        out_specs=vmem(3),
-        scratch_shapes=[
+    pairs = NZ // 2
+    cells = nx * ny
+
+    head, tail, side = call(
+        pack, "pack", [(field, False), (cot, False)],
+        [near((3, nx, width), BF16), near((3, nx, width), BF16), near((3, ny, width), BF16)],
+        [pltpu.VMEM((6, nx, width), F32)])
+    from_next = shift(head, -1)
+    from_prev = shift(tail, 1)
+    side = swap(side)
+    corner = swap(jnp.concatenate([from_prev, from_next], axis=0))
+
+    w1b, w2b, wfb, cot_t = call(
+        prepare, "prepare",
+        [(first_weight.reshape(27, C, C), False), (second_weight.reshape(27, C, C), False), (cot, False)],
+        [near((9 * 4 * C, lane), BF16), near((9 * 4 * C, lane), BF16), near((lane, 9 * 4 * C), BF16),
+         near((lane, cells * pairs), BF16)])
+
+    hd, keep, send = call(
+        functools.partial(layers, factor, gx_count, gy_count), "layers",
+        [(field, False), (cot, False)] + [(x, True) for x in (side, head, tail, from_prev, from_next, corner, w1b, wfb, cot_t)],
+        [near((3, nx + 2, ny, width + lane), BF16), near((rows, lane), F32), near((rows, lane), BF16)],
+        [
             pltpu.VMEM((3, nx + 4, ny, wide), BF16),
             pltpu.VMEM((3, nx + 2, ny, wide), BF16),
-            pltpu.VMEM((3, nx + 2, ny, width + lane), BF16),
             pltpu.VMEM((nx + 4, ny + 16, width), F32),
             pltpu.VMEM((nx + 2, ny + 16, width), F32),
             pltpu.VMEM((nx + 2, ny + 16, width + lane), F32),
             pltpu.VMEM((6, 24, width), F32),
+            pltpu.VMEM((2, 24, width), F32),
             pltpu.VMEM((9, 2, 16, wide), BF16),
-            pltpu.VMEM((NZ // 2 + 1, nx * ny, lane), F32),
-            pltpu.VMEM((9 * 4 * C, lane), BF16),
-            pltpu.VMEM((9 * 4 * C, lane), BF16),
-            pltpu.VMEM((lane, 9 * 4 * C), BF16),
+            pltpu.VMEM((pairs + 1, cells, lane), F32),
         ],
-        compiler_params=pltpu.CompilerParams(vmem_limit_bytes=56 * 1024 * 1024),
-        name="layers",
-    )(field, cot, side, head, tail, from_prev, from_next,
-      first_weight.reshape(27, C, C), second_weight.reshape(27, C, C))
-
-    both = (keep + swap(send).astype(F32)).astype(BF16).reshape(ranks, rows // ranks, lane)
-    terms = lax.all_to_all(both, ("gy", "grp"), 0, 0)
-    mine = jnp.sum(terms.astype(F32), axis=0).astype(BF16)
-    mine = lax.all_to_all(jnp.broadcast_to(mine[None], terms.shape), ("gy", "grp"), 0, 0).reshape(rows, lane)
+        limit=32, flops=10 ** 10)
+
+    other = swap(send)
+    out, = call(
+        output_conv, "output_conv", [(hd, True), (w2b, True)],
+        [jax.ShapeDtypeStruct((nx, ny, width), BF16)], flops=2 * 10 ** 9)
+    both, = call(add_pair, "add_pair", [(keep, True), (other, True)], [near((rows, lane), BF16)])
+    terms = lax.all_to_all(both.reshape(gy_count, rows // gy_count, lane), "gy", 0, 0)
+    part, = call(add_terms, "add_gy", [(terms, True)], [near(terms.shape[1:], BF16)])
+    terms = lax.all_to_all(part.reshape(grp_count, rows // ranks, lane), "grp", 0, 0)
+    spread, = call(add_and_repeat, "add_grp", [(terms, True)], [near(terms.shape, BF16)])
+    part = lax.all_to_all(spread, "grp", 0, 0).reshape(1, rows // gy_count, lane)
+    spread = jnp.broadcast_to(part, (gy_count,) + part.shape[1:])
+    mine = lax.all_to_all(spread, "gy", 0, 0).reshape(rows, lane)
     other = swap(mine)
-    first, second = pl.pallas_call(
-        unpack,
-        out_shape=[jax.ShapeDtypeStruct((27, C, C), F32)] * 2,
-        in_specs=vmem(2),
-        out_specs=vmem(2),
-        name="unpack",
-    )(mine, other)
+    first, second = call(
+        unpack, "unpack", [(mine, True), (other, True)], [jax.ShapeDtypeStruct((27, C, C), F32)] * 2)
     shape = (3, 3, 3, C, C)
     return out[None], first.reshape(shape), second.reshape(shape)
 

time: 64.2 us -> 64.9 us (1.011)
  blocking collectives: 32.5 us -> 38.2 us
  waiting for transfers between devices: 5.58 us -> 2.78 us
  other arithmetic: 2.43 us -> 0.01 us
  Pallas kernels: 11.6 us -> 10 us
  local copies, waits for them, and re-layouts: 3.6 us -> 4.9 us
    all_to_all x2 -> x4, blocking collectives: 32.5 us -> 38.2 us  [the longest x1 11.7 us: shards(): lax.all_to_all(both.reshape(gy_count, rows // gy_count, lane), 'gy', 0, 0)]
    ppermute x3 -> x4, waiting for transfers between devices: 3.92 us -> 1.12 us  [swap(): return lax.ppermute(array, 'gx', [(0, 1), (1, 0)])]
    unnamed x16 -> x14, local copies, waits for them, and re-layouts: 2.76 us -> 4.87 us
    pallas_call x2 -> x8, Pallas kernels: 11.6 us -> 10 us  [call(): pl.pallas_call(body, out_shape=list(outs), in_specs=[pl.BlockSpec(memory_...]
    convert_element_type x1 -> x0, other arithmetic: 1.11 us -> none  [shards(): (keep + swap(send).astype(F32)).astype(BF16)]
    select_n x3 -> x0, other arithmetic: 0.99 us -> none  [the longest x1 0.78 us: shards(): jnp.where(gx == 0, cot[nx - 1:nx], cot[0:1])]
    ppermute x1 -> x0, local copies, waits for them, and re-layouts: 0.68 us -> none  [swap(): return lax.ppermute(array, 'gx', [(0, 1), (1, 0)])]
  transfers between devices with their start and end apart: 5 -> 6, of which waited for: 5 -> 2; matrix products, arithmetic and copies ran while one was open for 1% -> 0% of each run, Pallas kernels for 0% -> 4%
where the time goes in v2:
time: 64.9 us; the launch traced here: 64.3 us
  blocking collectives  38.2 us (59%)
  Pallas kernels  10 us (15%)
  starting transfers between devices  7.6 us (12%)
  local copies, waits for them, and re-layouts  4.9 us (8%)
  waiting for transfers between devices  2.78 us (4%)
  between operations  0.76 us (1%)
    all_to_all x1, blocking collectives, shards(): lax.all_to_all(both.reshape(gy_count, rows // gy_count, lane), 'gy', 0, 0)  11.7 us
    all_to_all x1, blocking collectives, shards(): lax.all_to_all(part.reshape(grp_count, rows // ranks, lane), 'grp', 0, 0)  10.4 us
    pallas_call x8, Pallas kernels, call(): pl.pallas_call(body, out_shape=list(outs), in_specs=[pl.BlockSpec(memory_...  10 us
    all_to_all x1, blocking collectives, shards(): lax.all_to_all(spread, 'grp', 0, 0).reshape(1, rows // gy_count, lane)  8.08 us
    all_to_all x1, blocking collectives, shards(): mine = lax.all_to_all(spread, 'gy', 0, 0).reshape(rows, lane)  8.01 us
    ppermute x2, starting transfers between devices, shift(): lax.ppermute(array, 'gy', [(i, i + step) for i in range(count) if 0 <= i...  6.9 us
    unnamed x14, local copies, waits for them, and re-layouts  4.87 us
    ppermute x2, waiting for transfers between devices, shift(): lax.ppermute(array, 'gy', [(i, i + step) for i in range(count) if 0 <= i...  1.65 us
  transfers between devices with their start and end apart: 6, of which 2 were waited for; matrix products, arithmetic and copies ran while one was open for 0% of the time, Pallas kernels for 4%

profile of v2, /device:TPU:0, one launch (start us, length us, event | category | flops | bytes accessed | tf_op | source)
XLA Modules:
  0.0 64.3 jit_solution(16913431143038426785)
XLA Ops:
  0.6 0.9 %copy-done = bf16[1,8,16,1024]{3,2,1,0:T(8,128)(2,1)S(1)} copy-done((bf16[1,8,16,1024]{3,2,1,0:T(8,128)(2,1)S(1)}, bf16[1,8,16,1024]{3,2,1,0:T(8,128)(2,1)}, u32[]{:S(2)}) %copy-start) | copy-done | bytes 262168
  1.6 0.9 %copy-done.5 = bf16[1,8,16,1024]{3,2,1,0:T(8,128)(2,1)S(1)} copy-done((bf16[1,8,16,1024]{3,2,1,0:T(8,128)(2,1)S(1)}, bf16[1,8,16,1024]{3,2,1,0:T(8,128)(2,1)}, u32[]{:S(2)}) %copy-start.5) | copy-done | bytes 262168
  2.5 0.1 pack.1
  2.7 1.4 %collective-permute-start.2 = (bf16[3,8,1024]{2,1,0:T(8,128)(2,1)S(1)}, bf16[3,8,1024]{2,1,0:T(8,128)(2,1)S(1)}, u32[]{:S(2)}, u32[]{:S(2)}) collective-permute-start(bf16[3,8,1024]{2,1,0:T(8,128)(2,1)S(1)} %get-tuple-element.16.head), channel_id=1, source_target_pairs={{4,0},{8,4},{12,8},{5,1},{9,5},{13,9},{6,2},{10,6},{14,10},{7,3},{... | collective-permute-start | bytes 147464 | tf_op jit(solution)/shard_map/ppermute | solution.py:25
  4.1 5.5 %collective-permute-start.1 = (bf16[3,8,1024]{2,1,0:T(8,128)(2,1)S(1)}, bf16[3,8,1024]{2,1,0:T(8,128)(2,1)S(1)}, u32[]{:S(2)}, u32[]{:S(2)}) collective-permute-start(bf16[3,8,1024]{2,1,0:T(8,128)(2,1)S(1)} %get-tuple-element.17.tail), channel_id=1, source_target_pairs={{0,4},{4,8},{8,12},{1,5},{5,9},{9,13},{2,6},{6,10},{10,14},{3,7},{... | collective-permute-start | bytes 147464 | tf_op jit(solution)/shard_map/ppermute | solution.py:25
  9.6 0.1 collective-permute-start
  9.7 0.0 collective-permute-done.2.from_next
  9.7 1.6 %collective-permute-done.1.from_prev = bf16[3,8,1024]{2,1,0:T(8,128)(2,1)S(1)} collective-permute-done((bf16[3,8,1024]{2,1,0:T(8,128)(2,1)S(1)}, bf16[3,8,1024]{2,1,0:T(8,128)(2,1)S(1)}, u32[]{:S(2)}, u32[]{:S(2)}) %collective-permute-start.1) | collective-permute-done | bytes 49184 | tf_op jit(solution)/shard_map/ppermute | solution.py:25
  11.3 0.1 collective-permute-start.3
  11.4 0.0 copy-start.1
  11.4 0.9 %copy-done.1 = bf16[1,8,16,1024]{3,2,1,0:T(8,128)(2,1)S(1)} copy-done((bf16[1,8,16,1024]{3,2,1,0:T(8,128)(2,1)S(1)}, bf16[1,8,16,1024]{3,2,1,0:T(8,128)(2,1)}, u32[]{:S(2)}) %copy-start.1) | copy-done | bytes 262168
  12.4 1.0 %copy-done.3 = bf16[3,3,3,64,64]{4,3,2,1,0:T(8,128)(2,1)S(1)} copy-done((bf16[3,3,3,64,64]{4,3,2,1,0:T(8,128)(2,1)S(1)}, bf16[3,3,3,64,64]{4,3,2,1,0:T(8,128)(2,1)}, u32[]{:S(2)}) %copy-start.3) | copy-done | bytes 221208
  13.4 1.0 %copy-done.4 = bf16[3,3,3,64,64]{4,3,2,1,0:T(8,128)(2,1)S(1)} copy-done((bf16[3,3,3,64,64]{4,3,2,1,0:T(8,128)(2,1)S(1)}, bf16[3,3,3,64,64]{4,3,2,1,0:T(8,128)(2,1)}, u32[]{:S(2)}) %copy-start.4) | copy-done | bytes 221208
  14.4 0.5 prepare.1
  14.9 5.8 %layers.1 = (bf16[3,10,16,1152]{3,2,1,0:T(8,128)(2,1)S(1)}, f32[896,128]{1,0:T(8,128)S(1)}, bf16[896,128]{1,0:T(8,128)(2,1)S(1)}) custom-call(bf16[8,16,1024]{2,1,0:T(8,128)(2,1)S(1)} %bitcast.20, bf16[8,16,1024]{2,1,0:T(8,128)(2,1)S(1)} %bitcast.13, bf16[3,16,1024]{2,1,0:T(8,128)(2,1)S(1)} %collective-permute-done.side, ...), custom_call_target="tpu_custom_call" | custom-call | flops 10000000000 | bytes 2359296 | tf_op jit(solution)/shard_map/layers/pallas_call | solution.py:289
  20.7 0.6 collective-permute-start.4
  21.3 1.1 %collective-permute-done.4.other = bf16[896,128]{1,0:T(8,128)(2,1)S(1)} collective-permute-done((bf16[896,128]{1,0:T(8,128)(2,1)S(1)}, bf16[896,128]{1,0:T(8,128)(2,1)S(1)}, u32[]{:S(2)}, u32[]{:S(2)}) %collective-permute-start.4) | collective-permute-done | bytes 229408 | tf_op jit(solution)/shard_map/ppermute | solution.py:20
  22.4 0.1 add_pair.1
  22.5 11.7 %all_to_all.20.terms = bf16[4,224,128]{2,1,0:T(8,128)(2,1)S(1)} all-to-all(bf16[4,224,128]{2,1,0:T(8,128)(2,1)S(1)} %bitcast.14), channel_id=1, replica_groups=mesh['gx'=2,'gy'=4,'grp'=4] {'gy'}, dimensions={0} | all-to-all | bytes 458752 | tf_op jit(solution)/shard_map/all_to_all | solution.py:352
  34.2 10.4 %all_to_all.21.terms = bf16[4,56,128]{2,1,0:T(8,128)(2,1)S(1)} all-to-all(bf16[4,56,128]{2,1,0:T(8,128)(2,1)S(1)} %bitcast.21), channel_id=1, replica_groups=mesh['gx'=2,'gy'=4,'grp'=4] {'grp'}, dimensions={0} | all-to-all | bytes 114688 | tf_op jit(solution)/shard_map/all_to_all | solution.py:354
  44.6 8.1 %all_to_all.22 = bf16[4,56,128]{2,1,0:T(8,128)(2,1)S(1)} all-to-all(bf16[4,56,128]{2,1,0:T(8,128)(2,1)S(1)} %add_grp.1), channel_id=1, replica_groups=mesh['gx'=2,'gy'=4,'grp'=4] {'grp'}, dimensions={0} | all-to-all | bytes 114688 | tf_op jit(solution)/shard_map/all_to_all | solution.py:356
  52.8 8.0 %all_to_all.23 = bf16[4,224,128]{2,1,0:T(8,128)(2,1)S(1)} all-to-all(bf16[4,224,128]{2,1,0:T(8,128)(2,1)S(1)} %broadcast_in_dim.12), channel_id=1, replica_groups=mesh['gx'=2,'gy'=4,'grp'=4] {'gy'}, dimensions={0} | all-to-all | bytes 458752 | tf_op jit(solution)/shard_map/all_to_all | solution.py:358
  60.8 2.1 %output_conv.1 = bf16[8,16,1024]{2,1,0:T(8,128)(2,1)} custom-call(bf16[3,10,16,1152]{3,2,1,0:T(8,128)(2,1)S(1)} %get-tuple-element.21.hd, bf16[2304,128]{1,0:T(8,128)(2,1)S(1)} %get-tuple-element.22.w2b), custom_call_target="tpu_custom_call" | custom-call | flops 2000000000 | bytes 1695744 | tf_op jit(solution)/shard_map/output_conv/pallas_call | solution.py:289
  62.9 1.4 %unpack.1 = (f32[27,64,64]{2,1,0:T(8,128)}, f32[27,64,64]{2,1,0:T(8,128)}) custom-call(bf16[896,128]{1,0:T(8,128)(2,1)S(1)} %bitcast.16, bf16[896,128]{1,0:T(8,128)(2,1)S(1)} %collective-permute-done.5.other), custom_call_target="tpu_custom_call" | custom-call | bytes 458752 | tf_op jit(solution)/shard_map/unpack/pallas_call | solution.py:289
  (16 shorter events, 0.1 us)
Async XLA Ops:
  0.6 1.0 %copy-start = (bf16[1,8,16,1024]{3,2,1,0:T(8,128)(2,1)S(1)}, bf16[1,8,16,1024]{3,2,1,0:T(8,128)(2,1)}, u32[]{:S(2)}) copy-start(bf16[1,8,16,1024]{3,2,1,0:T(8,128)(2,1)} %param.7) | copy-start | bytes 786436
  1.6 0.9 %copy-start.5 = (bf16[1,8,16,1024]{3,2,1,0:T(8,128)(2,1)S(1)}, bf16[1,8,16,1024]{3,2,1,0:T(8,128)(2,1)}, u32[]{:S(2)}) copy-start(bf16[1,8,16,1024]{3,2,1,0:T(8,128)(2,1)} %param.4) | copy-start | bytes 786436
  2.5 12.4 %copy-start.2 = (bf16[1,8,16,1024]{3,2,1,0:T(8,128)(2,1)S(1)}, bf16[1,8,16,1024]{3,2,1,0:T(8,128)(2,1)}, u32[]{:S(2)}) copy-start(bf16[1,8,16,1024]{3,2,1,0:T(8,128)(2,1)} %param.7) | copy-start | bytes 786436
  2.5 12.4 %copy-start.6 = (bf16[1,8,16,1024]{3,2,1,0:T(8,128)(2,1)S(1)}, bf16[1,8,16,1024]{3,2,1,0:T(8,128)(2,1)}, u32[]{:S(2)}) copy-start(bf16[1,8,16,1024]{3,2,1,0:T(8,128)(2,1)} %param.4) | copy-start | bytes 786436
  2.7 7.0 %collective-permute-start.2 = (bf16[3,8,1024]{2,1,0:T(8,128)(2,1)S(1)}, bf16[3,8,1024]{2,1,0:T(8,128)(2,1)S(1)}, u32[]{:S(2)}, u32[]{:S(2)}) collective-permute-start(bf16[3,8,1024]{2,1,0:T(8,128)(2,1)S(1)} %get-tuple-element.16.head), channel_id=1, source_target_pairs={{4,0},{8,4},{12,8},{5,1},{9,5},{13,9},{6,2},{10,6},{14,10},{7,3},{... | collective-permute-start | bytes 147464 | tf_op jit(solution)/shard_map/ppermute | solution.py:25
  4.1 7.2 %collective-permute-start.1 = (bf16[3,8,1024]{2,1,0:T(8,128)(2,1)S(1)}, bf16[3,8,1024]{2,1,0:T(8,128)(2,1)S(1)}, u32[]{:S(2)}, u32[]{:S(2)}) collective-permute-start(bf16[3,8,1024]{2,1,0:T(8,128)(2,1)S(1)} %get-tuple-element.17.tail), channel_id=1, source_target_pairs={{0,4},{4,8},{8,12},{1,5},{5,9},{9,13},{2,6},{6,10},{10,14},{3,7},{... | collective-permute-start | bytes 147464 | tf_op jit(solution)/shard_map/ppermute | solution.py:25
  9.6 5.3 %collective-permute-start = (bf16[3,16,1024]{2,1,0:T(8,128)(2,1)S(1)}, bf16[3,16,1024]{2,1,0:T(8,128)(2,1)S(1)}, u32[]{:S(2)}, u32[]{:S(2)}) collective-permute-start(bf16[3,16,1024]{2,1,0:T(8,128)(2,1)S(1)} %get-tuple-element.15), channel_id=1, source_target_pairs={{0,16},{16,0},{1,17},{17,1},{2,18},{18,2},{3,19},{19,3},{4,20},{20... | collective-permute-start | bytes 294920 | tf_op jit(solution)/shard_map/ppermute | solution.py:20
  11.3 3.6 %collective-permute-start.3 = (bf16[6,8,1024]{2,1,0:T(8,128)(2,1)S(1)}, bf16[6,8,1024]{2,1,0:T(8,128)(2,1)S(1)}, u32[]{:S(2)}, u32[]{:S(2)}) collective-permute-start(bf16[6,8,1024]{2,1,0:T(8,128)(2,1)S(1)} %pad_maximum_fusion), channel_id=1, source_target_pairs={{0,16},{16,0},{1,17},{17,1},{2,18},{18,2},{3,19},{19,3},{4,20},{20... | collective-permute-start | bytes 294920 | tf_op jit(solution)/shard_map/ppermute | solution.py:20
  11.4 1.0 %copy-start.1 = (bf16[1,8,16,1024]{3,2,1,0:T(8,128)(2,1)S(1)}, bf16[1,8,16,1024]{3,2,1,0:T(8,128)(2,1)}, u32[]{:S(2)}) copy-start(bf16[1,8,16,1024]{3,2,1,0:T(8,128)(2,1)} %param.7) | copy-start | bytes 786436
  12.4 1.0 %copy-start.3 = (bf16[3,3,3,64,64]{4,3,2,1,0:T(8,128)(2,1)S(1)}, bf16[3,3,3,64,64]{4,3,2,1,0:T(8,128)(2,1)}, u32[]{:S(2)}) copy-start(bf16[3,3,3,64,64]{4,3,2,1,0:T(8,128)(2,1)} %param.5) | copy-start | bytes 663556
  13.4 1.0 %copy-start.4 = (bf16[3,3,3,64,64]{4,3,2,1,0:T(8,128)(2,1)S(1)}, bf16[3,3,3,64,64]{4,3,2,1,0:T(8,128)(2,1)}, u32[]{:S(2)}) copy-start(bf16[3,3,3,64,64]{4,3,2,1,0:T(8,128)(2,1)} %param.6) | copy-start | bytes 663556
  20.7 1.7 %collective-permute-start.4 = (bf16[896,128]{1,0:T(8,128)(2,1)S(1)}, bf16[896,128]{1,0:T(8,128)(2,1)S(1)}, u32[]{:S(2)}, u32[]{:S(2)}) collective-permute-start(bf16[896,128]{1,0:T(8,128)(2,1)S(1)} %get-tuple-element.24), channel_id=1, source_target_pairs={{0,16},{16,0},{1,17},{17,1},{2,18},{18,2},{3,19},{19,3},{4,20},{20... | collective-permute-start | bytes 688136 | tf_op jit(solution)/shard_map/ppermute | solution.py:20
  60.8 2.1 %collective-permute-start.5 = (bf16[896,128]{1,0:T(8,128)(2,1)S(1)}, bf16[896,128]{1,0:T(8,128)(2,1)S(1)}, u32[]{:S(2)}, u32[]{:S(2)}) collective-permute-start(bf16[896,128]{1,0:T(8,128)(2,1)S(1)} %bitcast.15), channel_id=1, source_target_pairs={{0,16},{16,0},{1,17},{17,1},{2,18},{18,2},{3,19},{19,3},{4,20},{20... | collective-permute-start | bytes 688136 | tf_op jit(solution)/shard_map/ppermute | solution.py:20

commit v3 on v2

--- a/solution.py
+++ b/solution.py
@@ -20,11 +20,6 @@
     return lax.ppermute(array, "gx", [(0, 1), (1, 0)])
 
 
-def shift(array, step):
-    count = lax.axis_size("gy")
-    return lax.ppermute(array, "gy", [(i, i + step) for i in range(count) if 0 <= i + step < count])
-
-
 def dot(a, b):
     return jnp.dot(a, b, preferred_element_type=F32)
 
@@ -70,7 +65,15 @@
     return blocks
 
 
-def pack(field, cot, head, tail, side, rows):
+def pack(field_hbm, cot_hbm, field, cot, edge, given, rows, sems):
+    copies = [
+        pltpu.make_async_copy(source, target, sems.at[index])
+        for index, (source, target) in enumerate(((field_hbm, field), (cot_hbm, cot)))
+    ]
+    for copy in copies:
+        copy.start()
+    for copy in copies:
+        copy.wait()
     nx, ny, width = field.shape
     gx = lax.axis_index("gx")
     for x in range(nx):
@@ -78,32 +81,59 @@
         cots = cot[x].astype(F32)
         for index, row in enumerate((fields[0:1], fields[1:2], cots[0:1], fields[ny - 2:ny - 1], fields[ny - 1:ny], cots[ny - 1:ny])):
             rows[index, x:x + 1, :] = row
-    head[...] = rows[0:3].astype(BF16)
-    tail[...] = rows[3:6].astype(BF16)
+    head = rows[0:3].astype(BF16)
+    tail = rows[3:6].astype(BF16)
 
     @pl.when(gx == 0)
     def _():
-        side[0:2] = field[nx - 2:nx]
-        side[2:3] = cot[nx - 1:nx]
+        edge[...] = head
+        given[:, ny:ny + nx] = tail
+        given[0:2, 0:ny] = field[nx - 2:nx]
+        given[2:3, 0:ny] = cot[nx - 1:nx]
 
     @pl.when(gx != 0)
     def _():
-        side[0:2] = field[0:2]
-        side[2:3] = cot[0:1]
-
-
-def prepare(w1, w2, cot, w1b, w2b, wfb, cot_t):
+        edge[...] = tail
+        given[:, ny:ny + nx] = head
+        given[0:2, 0:ny] = field[0:2]
+        given[2:3, 0:ny] = cot[0:1]
+
+
+def join_edges(edge, taken, whole):
+    nx = edge.shape[1]
+    gx = lax.axis_index("gx")
+
+    @pl.when(gx == 0)
+    def _():
+        whole[:, 0:nx] = edge[...]
+        whole[:, nx:2 * nx] = taken[:, taken.shape[1] - nx:]
+
+    @pl.when(gx != 0)
+    def _():
+        whole[:, 0:nx] = taken[:, taken.shape[1] - nx:]
+        whole[:, nx:2 * nx] = edge[...]
+
+
+def prepare(w1_hbm, w2_hbm, cot, w1b, w2b, wfb, cot_t, w1, w2, sems):
+    copies = [
+        pltpu.make_async_copy(source, target, sems.at[index])
+        for index, (source, target) in enumerate(((w1_hbm, w1), (w2_hbm, w2)))
+    ]
+    for copy in copies:
+        copy.start()
     cells = cot.shape[0] * cot.shape[1]
     lane = 2 * C
+    for p in range(NZ // 2):
+        cot_t[:, cells * p:cells * (p + 1)] = cot[:, :, lane * p:lane * (p + 1)].reshape(cells, lane).T
+    for copy in copies:
+        copy.wait()
     for t in range(9):
         w1b[t * 4 * C:(t + 1) * 4 * C, :] = band([w1[3 * t + z] for z in range(3)])
         w2b[t * 4 * C:(t + 1) * 4 * C, :] = band([w2[3 * t + z] for z in range(3)])
         wfb[:, t * 4 * C:(t + 1) * 4 * C] = band_flipped([w2[3 * (8 - t) + z] for z in range(3)])
-    for p in range(NZ // 2):
-        cot_t[:, cells * p:cells * (p + 1)] = cot[:, :, lane * p:lane * (p + 1)].reshape(cells, lane).T
-
-
-def layers(factor, gx_count, gy_count, field, cot, side, head, tail, from_prev, from_next, corner, w1b, wfb, cot_t,
+
+
+def layers(factor, gx_count, gy_count, field, cot, side, near_rows, far_rows, w1b, wfb, cot_t,
            hd, keep, send, fd, cd, fs, cs, hs, es, ec, eh, pf):
     nx, ny, width = field.shape
     pairs = NZ // 2
@@ -116,23 +146,32 @@
     after = (gy < gy_count - 1).astype(F32)
 
     fs[2:2 + nx, 8:8 + ny, :] = field[...].astype(F32)
-    fs[0:2, 8:8 + ny, :] = side[0:2].astype(F32) * low
-    fs[2 + nx:4 + nx, 8:8 + ny, :] = side[0:2].astype(F32) * high
+    fs[0:2, 8:8 + ny, :] = side[0:2, 0:ny].astype(F32) * low
+    fs[2 + nx:4 + nx, 8:8 + ny, :] = side[0:2, 0:ny].astype(F32) * high
     cs[1:1 + nx, 8:8 + ny, :] = cot[...].astype(F32)
-    cs[0:1, 8:8 + ny, :] = side[2:3].astype(F32) * low
-    cs[1 + nx:2 + nx, 8:8 + ny, :] = side[2:3].astype(F32) * high
+    cs[0:1, 8:8 + ny, :] = side[2:3, 0:ny].astype(F32) * low
+    cs[1 + nx:2 + nx, 8:8 + ny, :] = side[2:3, 0:ny].astype(F32) * high
 
     es[...] = jnp.zeros(es.shape, F32)
     ec[...] = jnp.zeros(ec.shape, F32)
-    for end, own, there, scale in ((0, from_prev, 0, prev), (1, from_next, 3, after)):
-        for target, index, source in ((es, 4 * end, 0), (es, 4 * end + 1, 1), (ec, end, 2)):
-            other = corner[there + source].astype(F32) * scale
-            target[index, 8:8 + nx, :] = own[source].astype(F32) * scale
-            target[index, 6:8, :] = other[nx - 2:nx] * low
-            target[index, 8 + nx:10 + nx, :] = other[0:2] * high
-    es[2, 8:8 + nx, :] = head[0].astype(F32)
-    es[3, 8:8 + nx, :] = tail[1].astype(F32)
-    for x in (0, 1, nx + 2, nx + 3):
+
+    def place(first, last, from_row, to_row):
+        span = slice(to_row, to_row + nx + 2)
+        for target, index, source in (
+            (es, 0, first[0]), (es, 1, first[1]), (ec, 0, first[2]),
+            (es, 4, last[0]), (es, 5, last[1]), (ec, 1, last[2]),
+        ):
+            target[index, span, :] = source.astype(F32)[from_row:from_row + nx + 2]
+
+    @pl.when(gx == 0)
+    def _():
+        place(near_rows, far_rows, 0, 8)
+
+    @pl.when(gx != 0)
+    def _():
+        place(far_rows, near_rows, nx - 2, 6)
+
+    for x in range(nx + 4):
         es[2, 6 + x:7 + x, :] = fs[x, 8:9, :]
         es[3, 6 + x:7 + x, :] = fs[x, 7 + ny:8 + ny, :]
 
@@ -254,15 +293,6 @@
     out[...] = total.astype(BF16)
 
 
-def add_and_repeat(terms, out):
-    total = terms[0].astype(F32)
-    for index in range(1, terms.shape[0]):
-        total = total + terms[index].astype(F32)
-    total = total.astype(BF16)
-    for index in range(out.shape[0]):
-        out[index] = total
-
-
 def unpack(mine, other, first, second):
     gx = lax.axis_index("gx")
     a = mine[...].astype(F32)
@@ -284,12 +314,12 @@
 
 
 def call(body, name, inputs, outs, scratch=(), limit=16, flops=0):
-    placed = [pltpu.with_memory_space_constraint(x, pltpu.VMEM) if held else x for x, held in inputs]
-    size = sum(x.size * x.dtype.itemsize for x in placed)
+    placed = [pltpu.with_memory_space_constraint(x, pltpu.VMEM if held else pltpu.HBM) for x, held in inputs]
+    size = sum(x.size * x.dtype.itemsize for x, _ in inputs)
     return pl.pallas_call(
         body,
         out_shape=list(outs),
-        in_specs=[pl.BlockSpec(memory_space=pltpu.VMEM)] * len(placed),
+        in_specs=[pl.BlockSpec(memory_space=pltpu.VMEM if held else pl.ANY) for _, held in inputs],
         out_specs=[pl.BlockSpec(memory_space=pltpu.VMEM)] * len(outs),
         scratch_shapes=list(scratch),
         compiler_params=pltpu.CompilerParams(vmem_limit_bytes=limit * 1024 * 1024),
@@ -303,33 +333,32 @@
     gx_count, gy_count, grp_count = (lax.axis_size(axis) for axis in ("gx", "gy", "grp"))
     total = field_in.shape[0] * nx * ny * NZ * gx_count * gy_count * grp_count
     factor = 1.0 / math.sqrt(total)
-    ranks = gy_count * grp_count
-    rows = -(-BLOCKS * C // (8 * ranks)) * 8 * ranks
-    field = field_in[0]
-    cot = cotangent[0]
+    rows = -(-BLOCKS * C // (8 * gy_count)) * 8 * gy_count
     lane = 2 * C
     wide = width + 2 * lane
     pairs = NZ // 2
     cells = nx * ny
 
-    head, tail, side = call(
-        pack, "pack", [(field, False), (cot, False)],
-        [near((3, nx, width), BF16), near((3, nx, width), BF16), near((3, ny, width), BF16)],
-        [pltpu.VMEM((6, nx, width), F32)])
-    from_next = shift(head, -1)
-    from_prev = shift(tail, 1)
-    side = swap(side)
-    corner = swap(jnp.concatenate([from_prev, from_next], axis=0))
-
+    field, cot, edge, given = call(
+        pack, "pack", [(field_in[0], False), (cotangent[0], False)],
+        [near((nx, ny, width), BF16), near((nx, ny, width), BF16), near((3, nx, width), BF16), near((3, ny + nx, width), BF16)],
+        [pltpu.VMEM((6, nx, width), F32), pltpu.SemaphoreType.DMA((2,))])
+    side = swap(given)
+    whole, = call(join_edges, "join_edges", [(edge, True), (side, True)], [near((3, 2 * nx, width), BF16)])
+    ends = [(gy_count + j, j + 1) for j in range(gy_count - 1)]
+    near_rows = lax.ppermute(whole, ("gx", "gy"), ends + [(b, a) for a, b in ends])
     w1b, w2b, wfb, cot_t = call(
         prepare, "prepare",
-        [(first_weight.reshape(27, C, C), False), (second_weight.reshape(27, C, C), False), (cot, False)],
+        [(first_weight.reshape(27, C, C), False), (second_weight.reshape(27, C, C), False), (cot, True)],
         [near((9 * 4 * C, lane), BF16), near((9 * 4 * C, lane), BF16), near((lane, 9 * 4 * C), BF16),
-         near((lane, cells * pairs), BF16)])
+         near((lane, cells * pairs), BF16)],
+        [pltpu.VMEM((27, C, C), BF16), pltpu.VMEM((27, C, C), BF16), pltpu.SemaphoreType.DMA((2,))])
+    near_rows, w1b, w2b, wfb, cot_t = lax.optimization_barrier((near_rows, w1b, w2b, wfb, cot_t))
+    far_rows = swap(near_rows)
 
     hd, keep, send = call(
         functools.partial(layers, factor, gx_count, gy_count), "layers",
-        [(field, False), (cot, False)] + [(x, True) for x in (side, head, tail, from_prev, from_next, corner, w1b, wfb, cot_t)],
+        [(x, True) for x in (field, cot, side, near_rows, far_rows, w1b, wfb, cot_t)],
         [near((3, nx + 2, ny, width + lane), BF16), near((rows, lane), F32), near((rows, lane), BF16)],
         [
             pltpu.VMEM((3, nx + 4, ny, wide), BF16),
@@ -347,14 +376,13 @@
     other = swap(send)
     out, = call(
         output_conv, "output_conv", [(hd, True), (w2b, True)],
-        [jax.ShapeDtypeStruct((nx, ny, width), BF16)], flops=2 * 10 ** 9)
+        [near((nx, ny, width), BF16)], flops=2 * 10 ** 9)
+    other, out = lax.optimization_barrier((other, out))
     both, = call(add_pair, "add_pair", [(keep, True), (other, True)], [near((rows, lane), BF16)])
     terms = lax.all_to_all(both.reshape(gy_count, rows // gy_count, lane), "gy", 0, 0)
-    part, = call(add_terms, "add_gy", [(terms, True)], [near(terms.shape[1:], BF16)])
-    terms = lax.all_to_all(part.reshape(grp_count, rows // ranks, lane), "grp", 0, 0)
-    spread, = call(add_and_repeat, "add_grp", [(terms, True)], [near(terms.shape, BF16)])
-    part = lax.all_to_all(spread, "grp", 0, 0).reshape(1, rows // gy_count, lane)
-    spread = jnp.broadcast_to(part, (gy_count,) + part.shape[1:])
+    part, = call(add_terms, "add_terms", [(terms, True)], [near(terms.shape[1:], BF16)])
+    part = lax.psum(part, "grp")
+    spread = jnp.broadcast_to(part[None], (gy_count,) + part.shape)
     mine = lax.all_to_all(spread, "gy", 0, 0).reshape(rows, lane)
     other = swap(mine)
     first, second = call(

time: 64.9 us -> 60.9 us (0.938)
  local copies, waits for them, and re-layouts: 4.9 us -> 0.73 us
  Pallas kernels: 10 us -> 11.5 us
  starting transfers between devices: 7.6 us -> 6.66 us
    psum x0 -> x1, blocking collectives: none -> 19.9 us  [shards(): part = lax.psum(part, 'grp')]
    all_to_all x2 -> x0, blocking collectives: 18.5 us -> none  [the longest x1 10.4 us: shards(): lax.all_to_all(part.reshape(grp_count, rows // ranks, lane), 'grp', 0, 0)]
    ppermute x2 -> x1, starting transfers between devices: 6.9 us -> 0.65 us  [shards(): lax.ppermute(whole, ('gx', 'gy'), ends + [(b, a) for a, b in ends])]
    ppermute x4, starting transfers between devices: 0.7 us -> 6 us  [swap(): return lax.ppermute(array, 'gx', [(0, 1), (1, 0)])]
    unnamed x14 -> x1, local copies, waits for them, and re-layouts: 4.87 us -> 0.7 us
    ppermute x2 -> x1, waiting for transfers between devices: 1.65 us -> 0.01 us  [shards(): lax.ppermute(whole, ('gx', 'gy'), ends + [(b, a) for a, b in ends])]
    ppermute x4, waiting for transfers between devices: 1.12 us -> 2.74 us  [swap(): return lax.ppermute(array, 'gx', [(0, 1), (1, 0)])]
    pallas_call x8, Pallas kernels: 10 us -> 11.5 us  [call(): pl.pallas_call(body, out_shape=list(outs), in_specs=[pl.BlockSpec(memory_...]
  transfers between devices with their start and end apart: 6 -> 5, of which waited for: 2 -> 3; matrix products, arithmetic and copies ran while one was open for 0% -> 1% of each run, Pallas kernels for 4% -> 5%
where the time goes in v3:
time: 60.9 us; the launch traced here: 60.7 us
  blocking collectives  38.3 us (63%)
  Pallas kernels  11.5 us (19%)
  starting transfers between devices  6.66 us (11%)
  waiting for transfers between devices  2.74 us (4%)
  local copies, waits for them, and re-layouts  0.73 us (1%)
  between operations  0.71 us (1%)
    psum x1, blocking collectives, shards(): part = lax.psum(part, 'grp')  19.9 us
    pallas_call x8, Pallas kernels, call(): pl.pallas_call(body, out_shape=list(outs), in_specs=[pl.BlockSpec(memory_...  11.5 us
    all_to_all x1, blocking collectives, shards(): lax.all_to_all(both.reshape(gy_count, rows // gy_count, lane), 'gy', 0, 0)  10.4 us
    all_to_all x1, blocking collectives, shards(): mine = lax.all_to_all(spread, 'gy', 0, 0).reshape(rows, lane)  8.01 us
    ppermute x4, starting transfers between devices, swap(): return lax.ppermute(array, 'gx', [(0, 1), (1, 0)])  6 us
    ppermute x4, waiting for transfers between devices, swap(): return lax.ppermute(array, 'gx', [(0, 1), (1, 0)])  2.74 us
  transfers between devices with their start and end apart: 5, of which 3 were waited for; matrix products, arithmetic and copies ran while one was open for 1% of the time, Pallas kernels for 5%

profile of v3, /device:TPU:0, one launch (start us, length us, event | category | flops | bytes accessed | tf_op | source)
XLA Modules:
  0.0 60.7 jit_solution(29697306501852723)
XLA Ops:
  0.6 1.2 %pack.1 = (bf16[8,16,1024]{2,1,0:T(8,128)(2,1)S(1)}, bf16[8,16,1024]{2,1,0:T(8,128)(2,1)S(1)}, bf16[3,8,1024]{2,1,0:T(8,128)(2,1)S(1)}, bf16[3,24,1024]{2,1,0:T(8,128)(2,1)S(1)}) custom-call(bf16[8,16,1024]{2,1,0:T(8,128)(2,1)} %bitcast.15, bf16[8,16,1024]{2,1,0:T(8,128)(2,1)} %bitcast.16), custom_call_target="tpu_custom_call" | custom-call | bytes 524288 | tf_op jit(solution)/shard_map/pack/pallas_call | solution.py:319
  1.8 0.5 collective-permute-start
  2.3 1.0 %collective-permute-done.taken.side = bf16[3,24,1024]{2,1,0:T(8,128)(2,1)S(1)} collective-permute-done((bf16[3,24,1024]{2,1,0:T(8,128)(2,1)S(1)}, bf16[3,24,1024]{2,1,0:T(8,128)(2,1)S(1)}, u32[]{:S(2)}, u32[]{:S(2)}) %collective-permute-start) | collective-permute-done | bytes 147488 | tf_op jit(solution)/shard_map/ppermute | solution.py:20
  3.4 0.7 %collective-permute-start.1 = (bf16[3,16,1024]{2,1,0:T(8,128)(2,1)S(1)}, bf16[3,16,1024]{2,1,0:T(8,128)(2,1)S(1)}, u32[]{:S(2)}, u32[]{:S(2)}) collective-permute-start(bf16[3,16,1024]{2,1,0:T(8,128)(2,1)S(1)} %join_edges.1), channel_id=1, source_target_pairs={{16,4},{20,8},{24,12},{4,16},{8,20},{12,24},{17,5},{21,9},{25,13},... | collective-permute-start | bytes 294920 | tf_op jit(solution)/shard_map/ppermute | solution.py:349
  4.0 1.6 %prepare.1 = (bf16[2304,128]{1,0:T(8,128)(2,1)S(1)}, bf16[2304,128]{1,0:T(8,128)(2,1)S(1)}, bf16[128,2304]{1,0:T(8,128)(2,1)S(1)}, bf16[128,1024]{1,0:T(8,128)(2,1)S(1)}) custom-call(bf16[27,64,64]{2,1,0:T(8,128)(2,1)} %bitcast.13, bf16[27,64,64]{2,1,0:T(8,128)(2,1)} %bitcast.14, bf16[8,16,1024]{2,1,0:T(8,128)(2,1)S(1)} %get-tuple-element.24.cot), custom_call_target="tpu_custom_call" | custom-call | bytes 704512 | tf_op jit(solution)/shard_map/prepare/pallas_call | solution.py:319
  5.6 0.0 collective-permute-done.1.near_rows
  5.6 5.1 %collective-permute-start.2 = (bf16[3,16,1024]{2,1,0:T(8,128)(2,1)S(1)}, bf16[3,16,1024]{2,1,0:T(8,128)(2,1)S(1)}, u32[]{:S(2)}, u32[]{:S(2)}) collective-permute-start(bf16[3,16,1024]{2,1,0:T(8,128)(2,1)S(1)} %collective-permute-done.1.near_rows), channel_id=1, source_target_pairs={{0,16},{16,0},{1,17},{17,1},{2,18},{18,2},{3,19},{19,3},{4,20},{20... | collective-permute-start | bytes 294920 | tf_op jit(solution)/shard_map/ppermute | solution.py:20
  10.7 0.9 %collective-permute-done.2.far_rows = bf16[3,16,1024]{2,1,0:T(8,128)(2,1)S(1)} collective-permute-done((bf16[3,16,1024]{2,1,0:T(8,128)(2,1)S(1)}, bf16[3,16,1024]{2,1,0:T(8,128)(2,1)S(1)}, u32[]{:S(2)}, u32[]{:S(2)}) %collective-permute-start.2) | collective-permute-done | bytes 98336 | tf_op jit(solution)/shard_map/ppermute | solution.py:20
  11.6 5.8 %layers.1 = (bf16[3,10,16,1152]{3,2,1,0:T(8,128)(2,1)S(1)}, f32[896,128]{1,0:T(8,128)S(1)}, bf16[896,128]{1,0:T(8,128)(2,1)S(1)}) custom-call(bf16[8,16,1024]{2,1,0:T(8,128)(2,1)S(1)} %get-tuple-element.23.field, bf16[8,16,1024]{2,1,0:T(8,128)(2,1)S(1)} %get-tuple-element.24.cot, bf16[3,24,1024]{2,1,0:T(8,128)(2,1)S(1)} %collective-permute-done.taken.side, ...), custom_call_target="tpu_custom_call" | custom-call | flops 10000000000 | bytes 2310144 | tf_op jit(solution)/shard_map/layers/pallas_call | solution.py:319
  17.4 0.4 collective-permute-start.3
  17.9 1.4 %output_conv.1 = bf16[8,16,1024]{2,1,0:T(8,128)(2,1)S(1)} custom-call(bf16[3,10,16,1152]{3,2,1,0:T(8,128)(2,1)S(1)} %get-tuple-element.36.hd, bf16[2304,128]{1,0:T(8,128)(2,1)S(1)} %get-tuple-element.37.w2b), custom_call_target="tpu_custom_call" | custom-call | flops 2000000000 | bytes 1695744 | tf_op jit(solution)/shard_map/output_conv/pallas_call | solution.py:319
  19.3 0.0 collective-permute-done.3.other
  19.4 10.4 %all_to_all.10.terms = bf16[4,224,128]{2,1,0:T(8,128)(2,1)S(1)} all-to-all(bf16[4,224,128]{2,1,0:T(8,128)(2,1)S(1)} %bitcast.10), channel_id=1, replica_groups=mesh['gx'=2,'gy'=4,'grp'=4] {'gy'}, dimensions={0} | all-to-all | bytes 458752 | tf_op jit(solution)/shard_map/all_to_all | solution.py:382
  29.8 19.9 %psum.7 = bf16[224,128]{1,0:T(8,128)(2,1)S(1)} all-reduce(bf16[224,128]{1,0:T(8,128)(2,1)S(1)} %add_terms.1), channel_id=1, replica_groups=mesh['gx'=2,'gy'=4,'grp'=4] {'grp'}, use_global_device_ids=true, to_apply=%region_0.0 | all-reduce | flops 28672 | bytes 114688 | tf_op jit(solution)/shard_map/psum | solution.py:384
  49.8 8.0 %all_to_all.11 = bf16[4,224,128]{2,1,0:T(8,128)(2,1)S(1)} all-to-all(bf16[4,224,128]{2,1,0:T(8,128)(2,1)S(1)} %broadcast_in_dim.10), channel_id=1, replica_groups=mesh['gx'=2,'gy'=4,'grp'=4] {'gy'}, dimensions={0} | all-to-all | bytes 458752 | tf_op jit(solution)/shard_map/all_to_all | solution.py:386
  57.8 0.0 collective-permute-start.4
  57.8 0.7 %copy.7 = bf16[1,8,16,1024]{3,2,1,0:T(8,128)(2,1)} copy(bf16[1,8,16,1024]{3,2,1,0:T(8,128)(2,1)S(1)} %bitcast.9) | data formatting | bytes 524288
  58.5 0.8 %collective-permute-done.4.other = bf16[896,128]{1,0:T(8,128)(2,1)S(1)} collective-permute-done((bf16[896,128]{1,0:T(8,128)(2,1)S(1)}, bf16[896,128]{1,0:T(8,128)(2,1)S(1)}, u32[]{:S(2)}, u32[]{:S(2)}) %collective-permute-start.4) | collective-permute-done | bytes 229408 | tf_op jit(solution)/shard_map/ppermute | solution.py:20
  59.3 1.4 %unpack.1 = (f32[27,64,64]{2,1,0:T(8,128)}, f32[27,64,64]{2,1,0:T(8,128)}) custom-call(bf16[896,128]{1,0:T(8,128)(2,1)S(1)} %bitcast.12, bf16[896,128]{1,0:T(8,128)(2,1)S(1)} %collective-permute-done.4.other), custom_call_target="tpu_custom_call" | custom-call | bytes 458752 | tf_op jit(solution)/shard_map/unpack/pallas_call | solution.py:319
  (4 shorter events, 0.1 us)
Async XLA Ops:
  1.8 1.5 %collective-permute-start = (bf16[3,24,1024]{2,1,0:T(8,128)(2,1)S(1)}, bf16[3,24,1024]{2,1,0:T(8,128)(2,1)S(1)}, u32[]{:S(2)}, u32[]{:S(2)}) collective-permute-start(bf16[3,24,1024]{2,1,0:T(8,128)(2,1)S(1)} %get-tuple-element.25), channel_id=1, source_target_pairs={{0,16},{16,0},{1,17},{17,1},{2,18},{18,2},{3,19},{19,3},{4,20},{20... | collective-permute-start | bytes 442376 | tf_op jit(solution)/shard_map/ppermute | solution.py:20
  3.4 2.3 %collective-permute-start.1 = (bf16[3,16,1024]{2,1,0:T(8,128)(2,1)S(1)}, bf16[3,16,1024]{2,1,0:T(8,128)(2,1)S(1)}, u32[]{:S(2)}, u32[]{:S(2)}) collective-permute-start(bf16[3,16,1024]{2,1,0:T(8,128)(2,1)S(1)} %join_edges.1), channel_id=1, source_target_pairs={{16,4},{20,8},{24,12},{4,16},{8,20},{12,24},{17,5},{21,9},{25,13},... | collective-permute-start | bytes 294920 | tf_op jit(solution)/shard_map/ppermute | solution.py:349
  5.6 6.0 %collective-permute-start.2 = (bf16[3,16,1024]{2,1,0:T(8,128)(2,1)S(1)}, bf16[3,16,1024]{2,1,0:T(8,128)(2,1)S(1)}, u32[]{:S(2)}, u32[]{:S(2)}) collective-permute-start(bf16[3,16,1024]{2,1,0:T(8,128)(2,1)S(1)} %collective-permute-done.1.near_rows), channel_id=1, source_target_pairs={{0,16},{16,0},{1,17},{17,1},{2,18},{18,2},{3,19},{19,3},{4,20},{20... | collective-permute-start | bytes 294920 | tf_op jit(solution)/shard_map/ppermute | solution.py:20
  17.4 1.9 %collective-permute-start.3 = (bf16[896,128]{1,0:T(8,128)(2,1)S(1)}, bf16[896,128]{1,0:T(8,128)(2,1)S(1)}, u32[]{:S(2)}, u32[]{:S(2)}) collective-permute-start(bf16[896,128]{1,0:T(8,128)(2,1)S(1)} %get-tuple-element.35), channel_id=1, source_target_pairs={{0,16},{16,0},{1,17},{17,1},{2,18},{18,2},{3,19},{19,3},{4,20},{20... | collective-permute-start | bytes 688136 | tf_op jit(solution)/shard_map/ppermute | solution.py:20
  57.8 1.5 %collective-permute-start.4 = (bf16[896,128]{1,0:T(8,128)(2,1)S(1)}, bf16[896,128]{1,0:T(8,128)(2,1)S(1)}, u32[]{:S(2)}, u32[]{:S(2)}) collective-permute-start(bf16[896,128]{1,0:T(8,128)(2,1)S(1)} %bitcast.11), channel_id=1, source_target_pairs={{0,16},{16,0},{1,17},{17,1},{2,18},{18,2},{3,19},{19,3},{4,20},{20... | collective-permute-start | bytes 688136 | tf_op jit(solution)/shard_map/ppermute | solution.py:20

commit v4 on v3

--- a/solution.py
+++ b/solution.py
@@ -286,11 +286,13 @@
     out[...] = (keep[...] + other[...].astype(F32)).astype(BF16)
 
 
-def add_terms(terms, out):
+def add_and_repeat(terms, out):
     total = terms[0].astype(F32)
     for index in range(1, terms.shape[0]):
         total = total + terms[index].astype(F32)
-    out[...] = total.astype(BF16)
+    total = total.astype(BF16)
+    for index in range(out.shape[0]):
+        out[index] = total
 
 
 def unpack(mine, other, first, second):
@@ -333,7 +335,8 @@
     gx_count, gy_count, grp_count = (lax.axis_size(axis) for axis in ("gx", "gy", "grp"))
     total = field_in.shape[0] * nx * ny * NZ * gx_count * gy_count * grp_count
     factor = 1.0 / math.sqrt(total)
-    rows = -(-BLOCKS * C // (8 * gy_count)) * 8 * gy_count
+    ranks = gy_count * grp_count
+    rows = -(-BLOCKS * C // (8 * ranks)) * 8 * ranks
     lane = 2 * C
     wide = width + 2 * lane
     pairs = NZ // 2
@@ -379,11 +382,9 @@
         [near((nx, ny, width), BF16)], flops=2 * 10 ** 9)
     other, out = lax.optimization_barrier((other, out))
     both, = call(add_pair, "add_pair", [(keep, True), (other, True)], [near((rows, lane), BF16)])
-    terms = lax.all_to_all(both.reshape(gy_count, rows // gy_count, lane), "gy", 0, 0)
-    part, = call(add_terms, "add_terms", [(terms, True)], [near(terms.shape[1:], BF16)])
-    part = lax.psum(part, "grp")
-    spread = jnp.broadcast_to(part[None], (gy_count,) + part.shape)
-    mine = lax.all_to_all(spread, "gy", 0, 0).reshape(rows, lane)
+    terms = lax.all_to_all(both.reshape(ranks, rows // ranks, lane), ("gy", "grp"), 0, 0)
+    spread, = call(add_and_repeat, "add_and_repeat", [(terms, True)], [near(terms.shape, BF16)])
+    mine = lax.all_to_all(spread, ("gy", "grp"), 0, 0).reshape(rows, lane)
     other = swap(mine)
     first, second = call(
         unpack, "unpack", [(mine, True), (other, True)], [jax.ShapeDtypeStruct((27, C, C), F32)] * 2)

time: 60.9 us -> 52.7 us (0.87)
  blocking collectives: 38.3 us -> 30.2 us
    psum x1 -> x0, blocking collectives: 19.9 us -> none  [shards(): part = lax.psum(part, 'grp')]
    all_to_all x2, blocking collectives: 18.4 us -> 30.2 us  [the longest x1 18 us: shards(): lax.all_to_all(both.reshape(ranks, rows // ranks, lane), ('gy', 'grp'), 0...]
  transfers between devices with their start and end apart: 5 -> 5, of which waited for: 3 -> 3; matrix products, arithmetic and copies ran while one was open for 1% -> 1% of each run, Pallas kernels for 5% -> 6%
where the time goes in v4:
time: 52.7 us; the launch traced here: 52.5 us
  blocking collectives  30.2 us (57%)
  Pallas kernels  11.5 us (22%)
  starting transfers between devices  6.66 us (13%)
  waiting for transfers between devices  2.74 us (5%)
  local copies, waits for them, and re-layouts  0.7 us (1%)
  between operations  0.7 us (1%)
    all_to_all x1, blocking collectives, shards(): lax.all_to_all(both.reshape(ranks, rows // ranks, lane), ('gy', 'grp'), 0...  18 us
    all_to_all x1, blocking collectives, shards(): mine = lax.all_to_all(spread, ('gy', 'grp'), 0, 0).reshape(rows, lane)  12.2 us
    pallas_call x8, Pallas kernels, call(): pl.pallas_call(body, out_shape=list(outs), in_specs=[pl.BlockSpec(memory_...  11.5 us
    ppermute x4, starting transfers between devices, swap(): return lax.ppermute(array, 'gx', [(0, 1), (1, 0)])  6 us
    ppermute x4, waiting for transfers between devices, swap(): return lax.ppermute(array, 'gx', [(0, 1), (1, 0)])  2.74 us
  transfers between devices with their start and end apart: 5, of which 3 were waited for; matrix products, arithmetic and copies ran while one was open for 1% of the time, Pallas kernels for 6%

profile of v4, /device:TPU:0, one launch (start us, length us, event | category | flops | bytes accessed | tf_op | source)
XLA Modules:
  0.0 52.5 jit_solution(415759060415707996)
XLA Ops:
  0.6 1.2 %pack.1 = (bf16[8,16,1024]{2,1,0:T(8,128)(2,1)S(1)}, bf16[8,16,1024]{2,1,0:T(8,128)(2,1)S(1)}, bf16[3,8,1024]{2,1,0:T(8,128)(2,1)S(1)}, bf16[3,24,1024]{2,1,0:T(8,128)(2,1)S(1)}) custom-call(bf16[8,16,1024]{2,1,0:T(8,128)(2,1)} %bitcast.15, bf16[8,16,1024]{2,1,0:T(8,128)(2,1)} %bitcast.16), custom_call_target="tpu_custom_call" | custom-call | bytes 524288 | tf_op jit(solution)/shard_map/pack/pallas_call | solution.py:321
  1.8 0.5 collective-permute-start
  2.3 1.0 %collective-permute-done.taken.side = bf16[3,24,1024]{2,1,0:T(8,128)(2,1)S(1)} collective-permute-done((bf16[3,24,1024]{2,1,0:T(8,128)(2,1)S(1)}, bf16[3,24,1024]{2,1,0:T(8,128)(2,1)S(1)}, u32[]{:S(2)}, u32[]{:S(2)}) %collective-permute-start) | collective-permute-done | bytes 147488 | tf_op jit(solution)/shard_map/ppermute | solution.py:20
  3.4 0.7 %collective-permute-start.1 = (bf16[3,16,1024]{2,1,0:T(8,128)(2,1)S(1)}, bf16[3,16,1024]{2,1,0:T(8,128)(2,1)S(1)}, u32[]{:S(2)}, u32[]{:S(2)}) collective-permute-start(bf16[3,16,1024]{2,1,0:T(8,128)(2,1)S(1)} %join_edges.1), channel_id=1, source_target_pairs={{16,4},{20,8},{24,12},{4,16},{8,20},{12,24},{17,5},{21,9},{25,13},... | collective-permute-start | bytes 294920 | tf_op jit(solution)/shard_map/ppermute | solution.py:352
  4.0 1.6 %prepare.1 = (bf16[2304,128]{1,0:T(8,128)(2,1)S(1)}, bf16[2304,128]{1,0:T(8,128)(2,1)S(1)}, bf16[128,2304]{1,0:T(8,128)(2,1)S(1)}, bf16[128,1024]{1,0:T(8,128)(2,1)S(1)}) custom-call(bf16[27,64,64]{2,1,0:T(8,128)(2,1)} %bitcast.13, bf16[27,64,64]{2,1,0:T(8,128)(2,1)} %bitcast.14, bf16[8,16,1024]{2,1,0:T(8,128)(2,1)S(1)} %get-tuple-element.24.cot), custom_call_target="tpu_custom_call" | custom-call | bytes 704512 | tf_op jit(solution)/shard_map/prepare/pallas_call | solution.py:321
  5.6 0.0 collective-permute-done.1.near_rows
  5.6 5.1 %collective-permute-start.2 = (bf16[3,16,1024]{2,1,0:T(8,128)(2,1)S(1)}, bf16[3,16,1024]{2,1,0:T(8,128)(2,1)S(1)}, u32[]{:S(2)}, u32[]{:S(2)}) collective-permute-start(bf16[3,16,1024]{2,1,0:T(8,128)(2,1)S(1)} %collective-permute-done.1.near_rows), channel_id=1, source_target_pairs={{0,16},{16,0},{1,17},{17,1},{2,18},{18,2},{3,19},{19,3},{4,20},{20... | collective-permute-start | bytes 294920 | tf_op jit(solution)/shard_map/ppermute | solution.py:20
  10.7 0.9 %collective-permute-done.2.far_rows = bf16[3,16,1024]{2,1,0:T(8,128)(2,1)S(1)} collective-permute-done((bf16[3,16,1024]{2,1,0:T(8,128)(2,1)S(1)}, bf16[3,16,1024]{2,1,0:T(8,128)(2,1)S(1)}, u32[]{:S(2)}, u32[]{:S(2)}) %collective-permute-start.2) | collective-permute-done | bytes 98336 | tf_op jit(solution)/shard_map/ppermute | solution.py:20
  11.6 5.8 %layers.1 = (bf16[3,10,16,1152]{3,2,1,0:T(8,128)(2,1)S(1)}, f32[896,128]{1,0:T(8,128)S(1)}, bf16[896,128]{1,0:T(8,128)(2,1)S(1)}) custom-call(bf16[8,16,1024]{2,1,0:T(8,128)(2,1)S(1)} %get-tuple-element.23.field, bf16[8,16,1024]{2,1,0:T(8,128)(2,1)S(1)} %get-tuple-element.24.cot, bf16[3,24,1024]{2,1,0:T(8,128)(2,1)S(1)} %collective-permute-done.taken.side, ...), custom_call_target="tpu_custom_call" | custom-call | flops 10000000000 | bytes 2310144 | tf_op jit(solution)/shard_map/layers/pallas_call | solution.py:321
  17.4 0.4 collective-permute-start.3
  17.9 1.4 %output_conv.1 = bf16[8,16,1024]{2,1,0:T(8,128)(2,1)S(1)} custom-call(bf16[3,10,16,1152]{3,2,1,0:T(8,128)(2,1)S(1)} %get-tuple-element.36.hd, bf16[2304,128]{1,0:T(8,128)(2,1)S(1)} %get-tuple-element.37.w2b), custom_call_target="tpu_custom_call" | custom-call | flops 2000000000 | bytes 1695744 | tf_op jit(solution)/shard_map/output_conv/pallas_call | solution.py:321
  19.3 0.0 collective-permute-done.3.other
  19.4 18.0 %all_to_all.10.terms = bf16[16,56,128]{2,1,0:T(8,128)(2,1)S(1)} all-to-all(bf16[16,56,128]{2,1,0:T(8,128)(2,1)S(1)} %bitcast.10), channel_id=1, replica_groups=mesh['gx'=2,'gy'=4,'grp'=4] {'gy','grp'}, dimensions={0} | all-to-all | bytes 458752 | tf_op jit(solution)/shard_map/all_to_all | solution.py:385
  37.4 12.2 %all_to_all.11 = bf16[16,56,128]{2,1,0:T(8,128)(2,1)S(1)} all-to-all(bf16[16,56,128]{2,1,0:T(8,128)(2,1)S(1)} %add_and_repeat.1), channel_id=1, replica_groups=mesh['gx'=2,'gy'=4,'grp'=4] {'gy','grp'}, dimensions={0} | all-to-all | bytes 458752 | tf_op jit(solution)/shard_map/all_to_all | solution.py:387
  49.6 0.0 collective-permute-start.4
  49.6 0.7 %copy.7 = bf16[1,8,16,1024]{3,2,1,0:T(8,128)(2,1)} copy(bf16[1,8,16,1024]{3,2,1,0:T(8,128)(2,1)S(1)} %bitcast.9) | data formatting | bytes 524288
  50.3 0.8 %collective-permute-done.4.other = bf16[896,128]{1,0:T(8,128)(2,1)S(1)} collective-permute-done((bf16[896,128]{1,0:T(8,128)(2,1)S(1)}, bf16[896,128]{1,0:T(8,128)(2,1)S(1)}, u32[]{:S(2)}, u32[]{:S(2)}) %collective-permute-start.4) | collective-permute-done | bytes 229408 | tf_op jit(solution)/shard_map/ppermute | solution.py:20
  51.1 1.4 %unpack.1 = (f32[27,64,64]{2,1,0:T(8,128)}, f32[27,64,64]{2,1,0:T(8,128)}) custom-call(bf16[896,128]{1,0:T(8,128)(2,1)S(1)} %bitcast.12, bf16[896,128]{1,0:T(8,128)(2,1)S(1)} %collective-permute-done.4.other), custom_call_target="tpu_custom_call" | custom-call | bytes 458752 | tf_op jit(solution)/shard_map/unpack/pallas_call | solution.py:321
  (3 shorter events, 0.1 us)
Async XLA Ops:
  1.8 1.5 %collective-permute-start = (bf16[3,24,1024]{2,1,0:T(8,128)(2,1)S(1)}, bf16[3,24,1024]{2,1,0:T(8,128)(2,1)S(1)}, u32[]{:S(2)}, u32[]{:S(2)}) collective-permute-start(bf16[3,24,1024]{2,1,0:T(8,128)(2,1)S(1)} %get-tuple-element.25), channel_id=1, source_target_pairs={{0,16},{16,0},{1,17},{17,1},{2,18},{18,2},{3,19},{19,3},{4,20},{20... | collective-permute-start | bytes 442376 | tf_op jit(solution)/shard_map/ppermute | solution.py:20
  3.4 2.3 %collective-permute-start.1 = (bf16[3,16,1024]{2,1,0:T(8,128)(2,1)S(1)}, bf16[3,16,1024]{2,1,0:T(8,128)(2,1)S(1)}, u32[]{:S(2)}, u32[]{:S(2)}) collective-permute-start(bf16[3,16,1024]{2,1,0:T(8,128)(2,1)S(1)} %join_edges.1), channel_id=1, source_target_pairs={{16,4},{20,8},{24,12},{4,16},{8,20},{12,24},{17,5},{21,9},{25,13},... | collective-permute-start | bytes 294920 | tf_op jit(solution)/shard_map/ppermute | solution.py:352
  5.6 6.0 %collective-permute-start.2 = (bf16[3,16,1024]{2,1,0:T(8,128)(2,1)S(1)}, bf16[3,16,1024]{2,1,0:T(8,128)(2,1)S(1)}, u32[]{:S(2)}, u32[]{:S(2)}) collective-permute-start(bf16[3,16,1024]{2,1,0:T(8,128)(2,1)S(1)} %collective-permute-done.1.near_rows), channel_id=1, source_target_pairs={{0,16},{16,0},{1,17},{17,1},{2,18},{18,2},{3,19},{19,3},{4,20},{20... | collective-permute-start | bytes 294920 | tf_op jit(solution)/shard_map/ppermute | solution.py:20
  17.4 1.9 %collective-permute-start.3 = (bf16[896,128]{1,0:T(8,128)(2,1)S(1)}, bf16[896,128]{1,0:T(8,128)(2,1)S(1)}, u32[]{:S(2)}, u32[]{:S(2)}) collective-permute-start(bf16[896,128]{1,0:T(8,128)(2,1)S(1)} %get-tuple-element.35), channel_id=1, source_target_pairs={{0,16},{16,0},{1,17},{17,1},{2,18},{18,2},{3,19},{19,3},{4,20},{20... | collective-permute-start | bytes 688136 | tf_op jit(solution)/shard_map/ppermute | solution.py:20
  49.6 1.5 %collective-permute-start.4 = (bf16[896,128]{1,0:T(8,128)(2,1)S(1)}, bf16[896,128]{1,0:T(8,128)(2,1)S(1)}, u32[]{:S(2)}, u32[]{:S(2)}) collective-permute-start(bf16[896,128]{1,0:T(8,128)(2,1)S(1)} %bitcast.11), channel_id=1, source_target_pairs={{0,16},{16,0},{1,17},{17,1},{2,18},{18,2},{3,19},{19,3},{4,20},{20... | collective-permute-start | bytes 688136 | tf_op jit(solution)/shard_map/ppermute | solution.py:20

commit v5 on v4

--- a/solution.py
+++ b/solution.py
@@ -12,7 +12,7 @@
 NZ = 16
 BF16 = jnp.bfloat16
 F32 = jnp.float32
-TAPS = [(dx, dy) for dx in range(3) for dy in range(3)]
+TAPS = [(dx, dy) for dy in range(3) for dx in range(3)]
 BLOCKS = 14
 
 
@@ -41,12 +41,6 @@
     upper = jnp.concatenate(back + [zero], axis=1)
     lower = jnp.concatenate([zero] + back, axis=1)
     return jnp.concatenate([upper, lower], axis=0)
-
-
-def shifted_rows(scratch, target, width):
-    rows = target.shape[2]
-    target[0, :, :, pl.ds(width, scratch.shape[2])] = scratch[:, 7:7 + rows, :].astype(BF16)
-    target[2, :, :, pl.ds(width, scratch.shape[2])] = scratch[:, 9:9 + rows, :].astype(BF16)
 
 
 def weight_gradient(rows_t, taps_of, total):
@@ -114,30 +108,89 @@
         whole[:, nx:2 * nx] = edge[...]
 
 
-def prepare(w1_hbm, w2_hbm, cot, w1b, w2b, wfb, cot_t, w1, w2, sems):
+def prepare(w1_hbm, w2_hbm, w1b, w2b, wfb, w1, w2, sems):
     copies = [
         pltpu.make_async_copy(source, target, sems.at[index])
         for index, (source, target) in enumerate(((w1_hbm, w1), (w2_hbm, w2)))
     ]
     for copy in copies:
         copy.start()
-    cells = cot.shape[0] * cot.shape[1]
-    lane = 2 * C
+    for copy in copies:
+        copy.wait()
+    for t, (dx, dy) in enumerate(TAPS):
+        rows = slice(t * 4 * C, (t + 1) * 4 * C)
+        first = 9 * dx + 3 * dy
+        w1b[rows, :] = band([w1[first + z] for z in range(3)])
+        w2b[rows, :] = band([w2[first + z] for z in range(3)])
+        wfb[:, rows] = band_flipped([w2[24 - first + z] for z in range(3)])
+
+
+def extend(gx_count, target, own, side):
+    gx = lax.axis_index("gx")
+    nx, ny, _ = own.shape
+    width = side.shape[0]
+    target[width:width + nx, 8:8 + ny, :] = own[...].astype(F32)
+    halo = side[:, 0:ny].astype(F32)
+    target[0:width, 8:8 + ny, :] = halo * (gx > 0).astype(F32)
+    target[width + nx:2 * width + nx, 8:8 + ny, :] = halo * (gx < gx_count - 1).astype(F32)
+
+
+def blank_edges(copies, width):
+    lane = 2 * C
+    zero = jnp.zeros(copies.shape[:-1] + (lane,), BF16)
+    copies[..., 0:lane] = zero
+    copies[..., lane + width:] = zero
+
+
+def fill_copies(scratch, copies):
+    depth, _, width = scratch.shape
+    ny = copies.shape[2]
+    lane = 2 * C
+    blank_edges(copies, width)
+    zero = jnp.zeros((depth, 1, width), F32)
+    scratch[:, 7:8, :] = zero
+    scratch[:, 8 + ny:9 + ny, :] = zero
+    for dy in range(3):
+        copies[dy, :, :, lane:lane + width] = scratch[:, 7 + dy:7 + dy + ny, :].astype(BF16)
+
+
+def interior_first(gx_count, field, cot, side, w1b, fs, middle, partial, cd, cot_t, fd, cs):
+    nx, ny, width = field.shape
+    lane = 2 * C
+    cells = nx * ny
+    depth = nx + 2
+    extend(gx_count, fs, field, side.at[0:2])
+    fill_copies(fs, fd)
+    middle[...] = fd[1]
+    for p in range(NZ // 2 + 1):
+        span = slice(lane * p, lane * (p + 2))
+        block = jnp.concatenate([fd[dy, dx:dx + depth, :, span].reshape(depth * ny, 2 * lane) for dx, dy in TAPS], axis=1)
+        partial[:, :, lane * p:lane * (p + 1)] = dot(block, w1b[...]).reshape(depth, ny, lane)
+    extend(gx_count, cs, cot, side.at[2:3])
+    fill_copies(cs, cd)
     for p in range(NZ // 2):
         cot_t[:, cells * p:cells * (p + 1)] = cot[:, :, lane * p:lane * (p + 1)].reshape(cells, lane).T
-    for copy in copies:
-        copy.wait()
-    for t in range(9):
-        w1b[t * 4 * C:(t + 1) * 4 * C, :] = band([w1[3 * t + z] for z in range(3)])
-        w2b[t * 4 * C:(t + 1) * 4 * C, :] = band([w2[3 * t + z] for z in range(3)])
-        wfb[:, t * 4 * C:(t + 1) * 4 * C] = band_flipped([w2[3 * (8 - t) + z] for z in range(3)])
-
-
-def layers(factor, gx_count, gy_count, field, cot, side, near_rows, far_rows, w1b, wfb, cot_t,
-           hd, keep, send, fd, cd, fs, cs, hs, es, ec, eh, pf):
-    nx, ny, width = field.shape
+
+
+def interior_grad(cd, wfb, partial):
+    nx, ny, _ = partial.shape
+    lane = 2 * C
+    for p in range(NZ // 2 + 1):
+        span = slice(lane * p, lane * (p + 2))
+        block = jnp.concatenate([cd[dy, dx:dx + nx, :, span].reshape(nx * ny, 2 * lane) for dx, dy in TAPS], axis=1)
+        partial[:, :, lane * p:lane * (p + 1)] = dot_nt(block, wfb[...]).reshape(nx, ny, lane)
+
+
+def layers(factor, gx_count, gy_count, fs, middle, pre_part, grad_part, near_rows, far_rows, w1b, wfb, cot_t,
+           hd, keep, send, fd, hs, es, ec, eh, eg, he, cr, pf, pg):
+    nx = middle.shape[0] - 4
+    ny = middle.shape[1]
+    width = fs.shape[2]
+    depth = nx + 2
     pairs = NZ // 2
     lane = 2 * C
+    wide = width + lane
+    cells = nx * ny
     gx = lax.axis_index("gx")
     gy = lax.axis_index("gy")
     low = (gx > 0).astype(F32)
@@ -145,23 +198,16 @@
     prev = (gy > 0).astype(F32)
     after = (gy < gy_count - 1).astype(F32)
 
-    fs[2:2 + nx, 8:8 + ny, :] = field[...].astype(F32)
-    fs[0:2, 8:8 + ny, :] = side[0:2, 0:ny].astype(F32) * low
-    fs[2 + nx:4 + nx, 8:8 + ny, :] = side[0:2, 0:ny].astype(F32) * high
-    cs[1:1 + nx, 8:8 + ny, :] = cot[...].astype(F32)
-    cs[0:1, 8:8 + ny, :] = side[2:3, 0:ny].astype(F32) * low
-    cs[1 + nx:2 + nx, 8:8 + ny, :] = side[2:3, 0:ny].astype(F32) * high
-
     es[...] = jnp.zeros(es.shape, F32)
     ec[...] = jnp.zeros(ec.shape, F32)
 
     def place(first, last, from_row, to_row):
-        span = slice(to_row, to_row + nx + 2)
+        span = slice(to_row, to_row + depth)
         for target, index, source in (
             (es, 0, first[0]), (es, 1, first[1]), (ec, 0, first[2]),
             (es, 4, last[0]), (es, 5, last[1]), (ec, 1, last[2]),
         ):
-            target[index, span, :] = source.astype(F32)[from_row:from_row + nx + 2]
+            target[index, span, :] = source.astype(F32)[from_row:from_row + depth]
 
     @pl.when(gx == 0)
     def _():
@@ -175,91 +221,89 @@
         es[2, 6 + x:7 + x, :] = fs[x, 8:9, :]
         es[3, 6 + x:7 + x, :] = fs[x, 7 + ny:8 + ny, :]
 
-    for x in range(nx + 4):
-        fs[x, 7:8, :] = es[1, 6 + x:7 + x, :]
-        fs[x, 8 + ny:9 + ny, :] = es[4, 6 + x:7 + x, :]
-    for x in range(nx + 2):
-        cs[x, 7:8, :] = ec[0, 7 + x:8 + x, :]
-        cs[x, 8 + ny:9 + ny, :] = ec[1, 7 + x:8 + x, :]
-
-    for copies in (fd, cd):
-        copies[:, :, :, 0:lane] = jnp.zeros(copies.shape[:3] + (lane,), BF16)
-        copies[:, :, :, lane + width:] = jnp.zeros(copies.shape[:3] + (lane,), BF16)
-    for scratch, copies in ((fs, fd), (cs, cd)):
-        shifted_rows(scratch, copies, lane)
-        copies[1, :, :, lane:lane + width] = scratch[:, 8:8 + ny, :].astype(BF16)
-
-    eh[:, :, :, 0:lane] = jnp.zeros((9, 2, 16, lane), BF16)
-    eh[:, :, :, lane + width:] = jnp.zeros((9, 2, 16, lane), BF16)
+    blank_edges(eh, width)
+    blank_edges(eg, width)
     for t, (dx, dy) in enumerate(TAPS):
         for end in range(2):
             eh[t, end, :, lane:lane + width] = es[3 * end + dy, 6 + dx:22 + dx, :].astype(BF16)
-
-    depth = nx + 2
-    main = depth * ny
-    x_of = lax.broadcasted_iota(jnp.int32, (depth, ny, lane), 0)
-    mask = jnp.where(x_of == 0, low, jnp.where(x_of == depth - 1, high, 1.0))
-    end_of = lax.broadcasted_iota(jnp.int32, (2, 16, lane), 0)
-    row_of = lax.broadcasted_iota(jnp.int32, (2, 16, lane), 1)
-    end_mask = jnp.where(row_of == 0, low, jnp.where(row_of == depth - 1, high, 1.0)) * jnp.where(end_of == 0, prev, after)
-    lane_of = lax.broadcasted_iota(jnp.int32, (1, 1, lane), 2)
+    for dx in range(3):
+        for end in range(2):
+            eg[dx, end, :, lane:lane + width] = ec[end, 7 + dx:23 + dx, :].astype(BF16)
+
+    def spans(pick):
+        return jnp.concatenate([pick(slice(lane * p, lane * (p + 2))) for p in range(pairs + 1)], axis=0)
+
+    def lanes(rows, count):
+        return [rows[count * p:count * (p + 1)] for p in range(pairs + 1)]
+
+    ends = lanes(dot(spans(lambda span: jnp.concatenate(
+        [eh[t, :, :, span].reshape(32, 2 * lane) for t in range(9)], axis=1)), w1b[...]), 32)
+    taps = (slice(0, 12 * C), slice(24 * C, 36 * C))
+    for end in range(2):
+        term = lanes(dot(spans(lambda span: jnp.concatenate(
+            [eh[3 + dx, end, :, span] for dx in range(3)], axis=1)), w1b[taps[end], :]), 16)
+        term_grad = lanes(dot_nt(spans(lambda span: jnp.concatenate(
+            [eg[dx, end, :, span] for dx in range(3)], axis=1)), wfb[:, taps[end]]), 16)
+        for p in range(pairs + 1):
+            cr[end, :, lane * p:lane * (p + 1)] = term[p]
+            cr[2 + end, :, lane * p:lane * (p + 1)] = term_grad[p]
+
+    lane_of = lax.broadcasted_iota(jnp.int32, (1, wide), 1)
+    inside = ((lane_of >= C) & (lane_of < wide - C)).astype(F32)
+    row_of = lax.broadcasted_iota(jnp.int32, (ny, wide), 0)
+    is_first = row_of == 0
+    is_last = row_of == ny - 1
+    end_row = lax.broadcasted_iota(jnp.int32, (16, lane), 0)
+    end_x = jnp.where(end_row == 0, low, jnp.where(end_row == depth - 1, high, 1.0))
     for p in range(pairs + 1):
-        span = slice(lane * p, lane * (p + 2))
         here = slice(lane * p, lane * (p + 1))
-        block = jnp.concatenate(
-            [
-                jnp.concatenate([fd[dy, dx:dx + depth, :, span].reshape(main, 2 * lane) for dx, dy in TAPS], axis=1),
-                jnp.concatenate([eh[t, :, :, span].reshape(32, 2 * lane) for t in range(9)], axis=1),
-            ],
-            axis=0,
-        )
-        pre = dot(block, w1b[...])
-        hidden = pre * jax.nn.sigmoid(pre)
-        hidden_main = hidden[:main].reshape(depth, ny, lane) * mask
-        hidden_ends = hidden[main:].reshape(2, 16, lane) * end_mask
-        if p == 0:
-            hidden_main = jnp.where(lane_of >= C, hidden_main, 0.0)
-            hidden_ends = jnp.where(lane_of >= C, hidden_ends, 0.0)
-        if p == pairs:
-            hidden_main = jnp.where(lane_of < C, hidden_main, 0.0)
-            hidden_ends = jnp.where(lane_of < C, hidden_ends, 0.0)
-        pf[p] = pre[ny:ny + nx * ny]
-        hs[:, 8:8 + ny, here] = hidden_main
-        hd[1, :, :, here] = hidden_main.astype(BF16)
-        for x in range(depth):
-            hs[x, 7:8, here] = hidden_ends[0, x:x + 1, :]
-            hs[x, 8 + ny:9 + ny, here] = hidden_ends[1, x:x + 1, :]
-    shifted_rows(hs, hd, 0)
-
-    cells = nx * ny
+        value = ends[p]
+        value = value * jax.nn.sigmoid(value)
+        he[0, :, here] = value[0:16] * end_x * prev * inside[:, here]
+        he[1, :, here] = value[16:32] * end_x * after * inside[:, here]
+    for x in range(depth):
+        pre = pre_part[x]
+        pre = pre + jnp.where(is_first, cr[0, x:x + 1, :], 0.0) + jnp.where(is_last, cr[1, x:x + 1, :], 0.0)
+        sigma = jax.nn.sigmoid(pre)
+        if 0 < x < depth - 1:
+            grad = grad_part[x - 1]
+            grad = grad + jnp.where(is_first, cr[2, x - 1:x, :], 0.0) + jnp.where(is_last, cr[3, x - 1:x, :], 0.0)
+            pg[x - 1] = (grad * sigma * (1.0 + pre * (1.0 - sigma)) * inside).astype(BF16)
+        hidden = pre * sigma * inside
+        if x == 0:
+            hidden = hidden * low
+        if x == depth - 1:
+            hidden = hidden * high
+        hs[x, 8:8 + ny, :] = hidden
+        hd[1, x] = hidden.astype(BF16)
+        hd[0, x] = jnp.where(is_first, he[0, x:x + 1, :], hs[x, 7:7 + ny, :]).astype(BF16)
+        hd[2, x] = jnp.where(is_last, he[1, x:x + 1, :], hs[x, 9:9 + ny, :]).astype(BF16)
 
     def hidden_span(dx, dy, p):
         return hd[dy, dx:dx + nx, :, lane * p:lane * (p + 2)].reshape(cells, 2 * lane)
-
-    def field_span(dx, dy, p):
-        return fd[dy, dx + 1:dx + 1 + nx, :, lane * p:lane * (p + 2)].reshape(cells, 2 * lane)
-
-    def cot_span(dx, dy, p):
-        return cd[dy, dx:dx + nx, :, lane * p:lane * (p + 2)].reshape(cells, 2 * lane)
 
     second = packed(weight_gradient(
         cot_t[...],
         lambda dx, dy: jnp.concatenate([hidden_span(dx, dy, p) for p in range(pairs)], axis=0),
         factor))
 
-    grads_t = []
-    for p in range(pairs + 1):
-        grad = dot_nt(jnp.concatenate([cot_span(dx, dy, p) for dx, dy in TAPS], axis=1), wfb[...])
-        pre = pf[p]
-        sigma = jax.nn.sigmoid(pre)
-        grad = grad * sigma * (1.0 + pre * (1.0 - sigma))
-        if p == 0:
-            grad = jnp.where(lane_of[0] >= C, grad, 0.0)
-        if p == pairs:
-            grad = jnp.where(lane_of[0] < C, grad, 0.0)
-        grads_t.append(grad.astype(BF16).T)
+    blank_edges(fd, width)
+    first_row = is_first[:, 0:width]
+    last_row = is_last[:, 0:width]
+    for x in range(depth):
+        fd[0, x, :, lane:lane + width] = jnp.where(first_row, es[1, 7 + x:8 + x, :], fs[x + 1, 7:7 + ny, :]).astype(BF16)
+        fd[1, x, :, lane:lane + width] = jnp.where(last_row, es[4, 7 + x:8 + x, :], fs[x + 1, 9:9 + ny, :]).astype(BF16)
+
+    def field_span(dx, dy, p):
+        span = slice(lane * p, lane * (p + 2))
+        if dy == 1:
+            return middle[dx + 1:dx + 1 + nx, :, span].reshape(cells, 2 * lane)
+        return fd[dy // 2, dx:dx + nx, :, span].reshape(cells, 2 * lane)
+
+    grad_t = jnp.concatenate(
+        [pg[:, :, lane * p:lane * (p + 1)].reshape(cells, lane).T for p in range(pairs + 1)], axis=1)
     first = packed(weight_gradient(
-        jnp.concatenate(grads_t, axis=1),
+        grad_t,
         lambda dx, dy: jnp.concatenate([field_span(dx, dy, p) for p in range(pairs + 1)], axis=0),
         factor))
 
@@ -300,15 +344,15 @@
     a = mine[...].astype(F32)
     b = other[...].astype(F32)
     for out, rows in ((first, jnp.where(gx == 0, a, b)), (second, jnp.where(gx == 0, b, a))):
-        for t in range(9):
+        for t, (dx, dy) in enumerate(TAPS):
             turned = rows[t * C:(t + 1) * C].T
-            out[3 * t] = turned[0:C]
-            out[3 * t + 1] = turned[C:2 * C]
+            out[9 * dx + 3 * dy] = turned[0:C]
+            out[9 * dx + 3 * dy + 1] = turned[C:2 * C]
         for pair in range(5):
             turned = rows[(9 + pair) * C:(10 + pair) * C].T
-            out[6 * pair + 2] = turned[0:C]
-            if pair < 4:
-                out[6 * pair + 5] = turned[C:2 * C]
+            for half in range(2 if pair < 4 else 1):
+                dx, dy = TAPS[2 * pair + half]
+                out[9 * dx + 3 * dy + 2] = turned[half * C:(half + 1) * C]
 
 
 def near(shape, dtype):
@@ -347,32 +391,48 @@
         [near((nx, ny, width), BF16), near((nx, ny, width), BF16), near((3, nx, width), BF16), near((3, ny + nx, width), BF16)],
         [pltpu.VMEM((6, nx, width), F32), pltpu.SemaphoreType.DMA((2,))])
     side = swap(given)
+    w1b, w2b, wfb = call(
+        prepare, "prepare",
+        [(first_weight.reshape(27, C, C), False), (second_weight.reshape(27, C, C), False)],
+        [near((9 * 4 * C, lane), BF16), near((9 * 4 * C, lane), BF16), near((lane, 9 * 4 * C), BF16)],
+        [pltpu.VMEM((27, C, C), BF16), pltpu.VMEM((27, C, C), BF16), pltpu.SemaphoreType.DMA((2,))])
+    side, w1b, w2b, wfb = lax.optimization_barrier((side, w1b, w2b, wfb))
     whole, = call(join_edges, "join_edges", [(edge, True), (side, True)], [near((3, 2 * nx, width), BF16)])
     ends = [(gy_count + j, j + 1) for j in range(gy_count - 1)]
     near_rows = lax.ppermute(whole, ("gx", "gy"), ends + [(b, a) for a, b in ends])
-    w1b, w2b, wfb, cot_t = call(
-        prepare, "prepare",
-        [(first_weight.reshape(27, C, C), False), (second_weight.reshape(27, C, C), False), (cot, True)],
-        [near((9 * 4 * C, lane), BF16), near((9 * 4 * C, lane), BF16), near((lane, 9 * 4 * C), BF16),
-         near((lane, cells * pairs), BF16)],
-        [pltpu.VMEM((27, C, C), BF16), pltpu.VMEM((27, C, C), BF16), pltpu.SemaphoreType.DMA((2,))])
-    near_rows, w1b, w2b, wfb, cot_t = lax.optimization_barrier((near_rows, w1b, w2b, wfb, cot_t))
+    fs, middle, pre_part, cd, cot_t = call(
+        functools.partial(interior_first, gx_count), "interior_first",
+        [(x, True) for x in (field, cot, side, w1b)],
+        [
+            near((nx + 4, ny + 16, width), F32),
+            near((nx + 4, ny, wide), BF16),
+            near((nx + 2, ny, width + lane), F32),
+            near((3, nx + 2, ny, wide), BF16),
+            near((lane, cells * pairs), BF16),
+        ],
+        [pltpu.VMEM((3, nx + 4, ny, wide), BF16), pltpu.VMEM((nx + 2, ny + 16, width), F32)],
+        flops=4 * 10 ** 9)
+    near_rows, fs, middle, pre_part, cd, cot_t = lax.optimization_barrier((near_rows, fs, middle, pre_part, cd, cot_t))
     far_rows = swap(near_rows)
+    grad_part, = call(
+        interior_grad, "interior_grad", [(cd, True), (wfb, True)], [near((nx, ny, width + lane), F32)], flops=3 * 10 ** 9)
+    far_rows, grad_part = lax.optimization_barrier((far_rows, grad_part))
 
     hd, keep, send = call(
         functools.partial(layers, factor, gx_count, gy_count), "layers",
-        [(x, True) for x in (field, cot, side, near_rows, far_rows, w1b, wfb, cot_t)],
+        [(x, True) for x in (fs, middle, pre_part, grad_part, near_rows, far_rows, w1b, wfb, cot_t)],
         [near((3, nx + 2, ny, width + lane), BF16), near((rows, lane), F32), near((rows, lane), BF16)],
         [
-            pltpu.VMEM((3, nx + 4, ny, wide), BF16),
-            pltpu.VMEM((3, nx + 2, ny, wide), BF16),
-            pltpu.VMEM((nx + 4, ny + 16, width), F32),
-            pltpu.VMEM((nx + 2, ny + 16, width), F32),
+            pltpu.VMEM((2, nx + 2, ny, wide), BF16),
             pltpu.VMEM((nx + 2, ny + 16, width + lane), F32),
             pltpu.VMEM((6, 24, width), F32),
-            pltpu.VMEM((2, 24, width), F32),
+            pltpu.VMEM((2, 32, width), F32),
             pltpu.VMEM((9, 2, 16, wide), BF16),
-            pltpu.VMEM((pairs + 1, cells, lane), F32),
+            pltpu.VMEM((3, 2, 16, wide), BF16),
+            pltpu.VMEM((2, 16, width + lane), F32),
+            pltpu.VMEM((4, 16, width + lane), F32),
+            pltpu.VMEM((nx, ny, width + lane), F32),
+            pltpu.VMEM((nx, ny, width + lane), BF16),
         ],
         limit=32, flops=10 ** 10)
 

time: 52.7 us -> 50.4 us (0.956)
  waiting for transfers between devices: 2.74 us -> 0.86 us
  starting transfers between devices: 6.66 us -> 5.19 us
  Pallas kernels: 11.5 us -> 12.6 us
    ppermute x4, waiting for transfers between devices: 2.74 us -> 0.86 us  [swap(): return lax.ppermute(array, 'gx', [(0, 1), (1, 0)])]
    ppermute x4, starting transfers between devices: 6 us -> 4.52 us  [swap(): return lax.ppermute(array, 'gx', [(0, 1), (1, 0)])]
    pallas_call x8 -> x10, Pallas kernels: 11.5 us -> 12.6 us  [call(): pl.pallas_call(body, out_shape=list(outs), in_specs=[pl.BlockSpec(memory_...]
  transfers between devices with their start and end apart: 5 -> 5, of which waited for: 3 -> 2; matrix products, arithmetic and copies ran while one was open for 1% -> 1% of each run, Pallas kernels for 6% -> 14%
where the time goes in v5:
time: 50.4 us; the launch traced here: 50.2 us
  blocking collectives  30.1 us (60%)
  Pallas kernels  12.6 us (25%)
  starting transfers between devices  5.19 us (10%)
  waiting for transfers between devices  0.86 us (2%)
  between operations  0.72 us (1%)
  local copies, waits for them, and re-layouts  0.7 us (1%)
    all_to_all x1, blocking collectives, shards(): lax.all_to_all(both.reshape(ranks, rows // ranks, lane), ('gy', 'grp'), 0...  17.9 us
    pallas_call x10, Pallas kernels, call(): pl.pallas_call(body, out_shape=list(outs), in_specs=[pl.BlockSpec(memory_...  12.6 us
    all_to_all x1, blocking collectives, shards(): mine = lax.all_to_all(spread, ('gy', 'grp'), 0, 0).reshape(rows, lane)  12.2 us
    ppermute x4, starting transfers between devices, swap(): return lax.ppermute(array, 'gx', [(0, 1), (1, 0)])  4.52 us
  transfers between devices with their start and end apart: 5, of which 2 were waited for; matrix products, arithmetic and copies ran while one was open for 1% of the time, Pallas kernels for 14%

profile of v5, /device:TPU:0, one launch (start us, length us, event | category | flops | bytes accessed | tf_op | source)
XLA Modules:
  0.0 50.2 jit_solution(2783586051116967581)
XLA Ops:
  0.6 1.2 %pack.1 = (bf16[8,16,1024]{2,1,0:T(8,128)(2,1)S(1)}, bf16[8,16,1024]{2,1,0:T(8,128)(2,1)S(1)}, bf16[3,8,1024]{2,1,0:T(8,128)(2,1)S(1)}, bf16[3,24,1024]{2,1,0:T(8,128)(2,1)S(1)}) custom-call(bf16[8,16,1024]{2,1,0:T(8,128)(2,1)} %bitcast.15, bf16[8,16,1024]{2,1,0:T(8,128)(2,1)} %bitcast.16), custom_call_target="tpu_custom_call" | custom-call | bytes 524288 | tf_op jit(solution)/shard_map/pack/pallas_call | solution.py:365
  1.8 0.5 %collective-permute-start = (bf16[3,24,1024]{2,1,0:T(8,128)(2,1)S(1)}, bf16[3,24,1024]{2,1,0:T(8,128)(2,1)S(1)}, u32[]{:S(2)}, u32[]{:S(2)}) collective-permute-start(bf16[3,24,1024]{2,1,0:T(8,128)(2,1)S(1)} %get-tuple-element.35), channel_id=1, source_target_pairs={{0,16},{16,0},{1,17},{17,1},{2,18},{18,2},{3,19},{19,3},{4,20},{20... | collective-permute-start | bytes 442376 | tf_op jit(solution)/shard_map/ppermute | solution.py:20
  2.3 1.6 %prepare.1 = (bf16[2304,128]{1,0:T(8,128)(2,1)S(1)}, bf16[2304,128]{1,0:T(8,128)(2,1)S(1)}, bf16[128,2304]{1,0:T(8,128)(2,1)S(1)}) custom-call(bf16[27,64,64]{2,1,0:T(8,128)(2,1)} %bitcast.13, bf16[27,64,64]{2,1,0:T(8,128)(2,1)} %bitcast.14), custom_call_target="tpu_custom_call" | custom-call | bytes 442368 | tf_op jit(solution)/shard_map/prepare/pallas_call | solution.py:365
  3.9 0.0 collective-permute-done.taken.side
  4.0 0.7 %collective-permute-start.1 = (bf16[3,16,1024]{2,1,0:T(8,128)(2,1)S(1)}, bf16[3,16,1024]{2,1,0:T(8,128)(2,1)S(1)}, u32[]{:S(2)}, u32[]{:S(2)}) collective-permute-start(bf16[3,16,1024]{2,1,0:T(8,128)(2,1)S(1)} %join_edges.1), channel_id=1, source_target_pairs={{16,4},{20,8},{24,12},{4,16},{8,20},{12,24},{17,5},{21,9},{25,13},... | collective-permute-start | bytes 294920 | tf_op jit(solution)/shard_map/ppermute | solution.py:402
  4.6 2.4 %interior_first.1 = (f32[12,32,1024]{2,1,0:T(8,128)S(1)}, bf16[12,16,1280]{2,1,0:T(8,128)(2,1)S(1)}, f32[10,16,1152]{2,1,0:T(8,128)S(1)}, bf16[3,10,16,1280]{3,2,1,0:T(8,128)(2,1)S(1)}, bf16[128,1024]{1,0:T(8,128)(2,1)S(1)}) custom-call(bf16[8,16,1024]{2,1,0:T(8,128)(2,1)S(1)} %get-tuple-element.40.field, bf16[8,16,1024]{2,1,0:T(8,128)(2,1)S(1)} %get-tuple-element.41.cot, ...), custom_call_target="tpu_custom_call" | custom-call | flops 4000000000 | bytes 1261568 | tf_op jit(solution)/shard_map/interior_first/pallas_call | solution.py:365
  7.0 0.0 collective-permute-done.1.near_rows
  7.1 3.9 %collective-permute-start.2 = (bf16[3,16,1024]{2,1,0:T(8,128)(2,1)S(1)}, bf16[3,16,1024]{2,1,0:T(8,128)(2,1)S(1)}, u32[]{:S(2)}, u32[]{:S(2)}) collective-permute-start(bf16[3,16,1024]{2,1,0:T(8,128)(2,1)S(1)} %collective-permute-done.1.near_rows), channel_id=1, source_target_pairs={{0,16},{16,0},{1,17},{17,1},{2,18},{18,2},{3,19},{19,3},{4,20},{20... | collective-permute-start | bytes 294920 | tf_op jit(solution)/shard_map/ppermute | solution.py:20
  11.0 1.5 %interior_grad.1.grad_part = f32[8,16,1152]{2,1,0:T(8,128)S(1)} custom-call(bf16[3,10,16,1280]{3,2,1,0:T(8,128)(2,1)S(1)} %get-tuple-element.52.cd, bf16[128,2304]{1,0:T(8,128)(2,1)S(1)} %get-tuple-element.53.wfb), custom_call_target="tpu_custom_call" | custom-call | flops 3000000000 | bytes 1818624 | tf_op jit(solution)/shard_map/interior_grad/pallas_call | solution.py:365
  12.5 0.0 collective-permute-done.2.far_rows
  12.5 3.0 %layers.1 = (bf16[3,10,16,1152]{3,2,1,0:T(8,128)(2,1)S(1)}, f32[896,128]{1,0:T(8,128)S(1)}, bf16[896,128]{1,0:T(8,128)(2,1)S(1)}) custom-call(f32[12,32,1024]{2,1,0:T(8,128)S(1)} %get-tuple-element.48.fs, bf16[12,16,1280]{2,1,0:T(8,128)(2,1)S(1)} %get-tuple-element.49.middle, f32[10,16,1152]{2,1,0:T(8,128)S(1)} %get-tuple-element.50.pre_part, ...), custom_call_target="tpu_custom_call" | custom-call | flops 10000000000 | bytes 5029888 | tf_op jit(solution)/shard_map/layers/pallas_call | solution.py:365
  15.5 0.1 collective-permute-start.3
  15.6 1.4 %output_conv.1 = bf16[8,16,1024]{2,1,0:T(8,128)(2,1)S(1)} custom-call(bf16[3,10,16,1152]{3,2,1,0:T(8,128)(2,1)S(1)} %get-tuple-element.58.hd, bf16[2304,128]{1,0:T(8,128)(2,1)S(1)} %get-tuple-element.59.w2b), custom_call_target="tpu_custom_call" | custom-call | flops 2000000000 | bytes 1695744 | tf_op jit(solution)/shard_map/output_conv/pallas_call | solution.py:365
  17.0 0.1 collective-permute-done.3.other
  17.1 17.9 %all_to_all.10.terms = bf16[16,56,128]{2,1,0:T(8,128)(2,1)S(1)} all-to-all(bf16[16,56,128]{2,1,0:T(8,128)(2,1)S(1)} %bitcast.10), channel_id=1, replica_groups=mesh['gx'=2,'gy'=4,'grp'=4] {'gy','grp'}, dimensions={0} | all-to-all | bytes 458752 | tf_op jit(solution)/shard_map/all_to_all | solution.py:445
  35.1 12.2 %all_to_all.11 = bf16[16,56,128]{2,1,0:T(8,128)(2,1)S(1)} all-to-all(bf16[16,56,128]{2,1,0:T(8,128)(2,1)S(1)} %add_and_repeat.1), channel_id=1, replica_groups=mesh['gx'=2,'gy'=4,'grp'=4] {'gy','grp'}, dimensions={0} | all-to-all | bytes 458752 | tf_op jit(solution)/shard_map/all_to_all | solution.py:447
  47.3 0.0 collective-permute-start.4
  47.3 0.7 %copy.7 = bf16[1,8,16,1024]{3,2,1,0:T(8,128)(2,1)} copy(bf16[1,8,16,1024]{3,2,1,0:T(8,128)(2,1)S(1)} %bitcast.9) | data formatting | bytes 524288
  48.0 0.8 %collective-permute-done.4.other = bf16[896,128]{1,0:T(8,128)(2,1)S(1)} collective-permute-done((bf16[896,128]{1,0:T(8,128)(2,1)S(1)}, bf16[896,128]{1,0:T(8,128)(2,1)S(1)}, u32[]{:S(2)}, u32[]{:S(2)}) %collective-permute-start.4) | collective-permute-done | bytes 229408 | tf_op jit(solution)/shard_map/ppermute | solution.py:20
  48.8 1.4 %unpack.1 = (f32[27,64,64]{2,1,0:T(8,128)}, f32[27,64,64]{2,1,0:T(8,128)}) custom-call(bf16[896,128]{1,0:T(8,128)(2,1)S(1)} %bitcast.12, bf16[896,128]{1,0:T(8,128)(2,1)S(1)} %collective-permute-done.4.other), custom_call_target="tpu_custom_call" | custom-call | bytes 458752 | tf_op jit(solution)/shard_map/unpack/pallas_call | solution.py:365
  (3 shorter events, 0.1 us)
Async XLA Ops:
  1.8 2.1 %collective-permute-start = (bf16[3,24,1024]{2,1,0:T(8,128)(2,1)S(1)}, bf16[3,24,1024]{2,1,0:T(8,128)(2,1)S(1)}, u32[]{:S(2)}, u32[]{:S(2)}) collective-permute-start(bf16[3,24,1024]{2,1,0:T(8,128)(2,1)S(1)} %get-tuple-element.35), channel_id=1, source_target_pairs={{0,16},{16,0},{1,17},{17,1},{2,18},{18,2},{3,19},{19,3},{4,20},{20... | collective-permute-start | bytes 442376 | tf_op jit(solution)/shard_map/ppermute | solution.py:20
  4.0 3.1 %collective-permute-start.1 = (bf16[3,16,1024]{2,1,0:T(8,128)(2,1)S(1)}, bf16[3,16,1024]{2,1,0:T(8,128)(2,1)S(1)}, u32[]{:S(2)}, u32[]{:S(2)}) collective-permute-start(bf16[3,16,1024]{2,1,0:T(8,128)(2,1)S(1)} %join_edges.1), channel_id=1, source_target_pairs={{16,4},{20,8},{24,12},{4,16},{8,20},{12,24},{17,5},{21,9},{25,13},... | collective-permute-start | bytes 294920 | tf_op jit(solution)/shard_map/ppermute | solution.py:402
  7.1 5.5 %collective-permute-start.2 = (bf16[3,16,1024]{2,1,0:T(8,128)(2,1)S(1)}, bf16[3,16,1024]{2,1,0:T(8,128)(2,1)S(1)}, u32[]{:S(2)}, u32[]{:S(2)}) collective-permute-start(bf16[3,16,1024]{2,1,0:T(8,128)(2,1)S(1)} %collective-permute-done.1.near_rows), channel_id=1, source_target_pairs={{0,16},{16,0},{1,17},{17,1},{2,18},{18,2},{3,19},{19,3},{4,20},{20... | collective-permute-start | bytes 294920 | tf_op jit(solution)/shard_map/ppermute | solution.py:20
  15.5 1.6 %collective-permute-start.3 = (bf16[896,128]{1,0:T(8,128)(2,1)S(1)}, bf16[896,128]{1,0:T(8,128)(2,1)S(1)}, u32[]{:S(2)}, u32[]{:S(2)}) collective-permute-start(bf16[896,128]{1,0:T(8,128)(2,1)S(1)} %get-tuple-element.57), channel_id=1, source_target_pairs={{0,16},{16,0},{1,17},{17,1},{2,18},{18,2},{3,19},{19,3},{4,20},{20... | collective-permute-start | bytes 688136 | tf_op jit(solution)/shard_map/ppermute | solution.py:20
  47.3 1.5 %collective-permute-start.4 = (bf16[896,128]{1,0:T(8,128)(2,1)S(1)}, bf16[896,128]{1,0:T(8,128)(2,1)S(1)}, u32[]{:S(2)}, u32[]{:S(2)}) collective-permute-start(bf16[896,128]{1,0:T(8,128)(2,1)S(1)} %bitcast.11), channel_id=1, source_target_pairs={{0,16},{16,0},{1,17},{17,1},{2,18},{18,2},{3,19},{19,3},{4,20},{20... | collective-permute-start | bytes 688136 | tf_op jit(solution)/shard_map/ppermute | solution.py:20

commit v6 on v5

--- a/solution.py
+++ b/solution.py
@@ -43,12 +43,29 @@
     return jnp.concatenate([upper, lower], axis=0)
 
 
-def weight_gradient(rows_t, taps_of, total):
+def weight_gradient(products, factor):
     result = []
-    for dx, dy in TAPS:
-        full = dot(rows_t, taps_of(dx, dy)) * total
-        result.append(full[0:C, 0:3 * C] + full[C:2 * C, C:4 * C])
+    for full in products:
+        for dx in range(3):
+            part = full[2 * C * dx:2 * C * (dx + 1)] * factor
+            result.append(part[0:C, 0:3 * C] + part[C:2 * C, C:4 * C])
     return result
+
+
+def turn_rows(source, x):
+    lane = 2 * C
+    return jnp.concatenate([source[x, :, lane * p:lane * (p + 1)] for p in range(NZ // 2)], axis=0).T
+
+
+def stack_shifts(target, source):
+    lane = 2 * C
+    nx = source.shape[0]
+    cells = source.shape[1] * NZ // 2
+    target[...] = jnp.zeros(target.shape, BF16)
+    for x in range(nx):
+        turned = turn_rows(source, x)
+        for dx in range(3):
+            target[lane * dx:lane * (dx + 1), cells * (x + dx):cells * (x + dx + 1)] = turned
 
 
 def packed(pieces):
@@ -108,7 +125,7 @@
         whole[:, nx:2 * nx] = edge[...]
 
 
-def prepare(w1_hbm, w2_hbm, w1b, w2b, wfb, w1, w2, sems):
+def load_weights(w1_hbm, w2_hbm, w1, w2, sems):
     copies = [
         pltpu.make_async_copy(source, target, sems.at[index])
         for index, (source, target) in enumerate(((w1_hbm, w1), (w2_hbm, w2)))
@@ -117,6 +134,9 @@
         copy.start()
     for copy in copies:
         copy.wait()
+
+
+def make_bands(w1, w2, w1b, w2b, wfb):
     for t, (dx, dy) in enumerate(TAPS):
         rows = slice(t * 4 * C, (t + 1) * 4 * C)
         first = 9 * dx + 3 * dy
@@ -154,11 +174,11 @@
         copies[dy, :, :, lane:lane + width] = scratch[:, 7 + dy:7 + dy + ny, :].astype(BF16)
 
 
-def interior_first(gx_count, field, cot, side, w1b, fs, middle, partial, cd, cot_t, fd, cs):
+def interior_first(gx_count, field, cot, side, w1, w2, fs, middle, partial, cd, cot_t, w1b, w2b, wfb, fd, cs):
     nx, ny, width = field.shape
     lane = 2 * C
-    cells = nx * ny
     depth = nx + 2
+    make_bands(w1, w2, w1b, w2b, wfb)
     extend(gx_count, fs, field, side.at[0:2])
     fill_copies(fs, fd)
     middle[...] = fd[1]
@@ -168,8 +188,7 @@
         partial[:, :, lane * p:lane * (p + 1)] = dot(block, w1b[...]).reshape(depth, ny, lane)
     extend(gx_count, cs, cot, side.at[2:3])
     fill_copies(cs, cd)
-    for p in range(NZ // 2):
-        cot_t[:, cells * p:cells * (p + 1)] = cot[:, :, lane * p:lane * (p + 1)].reshape(cells, lane).T
+    stack_shifts(cot_t, cot)
 
 
 def interior_grad(cd, wfb, partial):
@@ -182,7 +201,7 @@
 
 
 def layers(factor, gx_count, gy_count, fs, middle, pre_part, grad_part, near_rows, far_rows, w1b, wfb, cot_t,
-           hd, keep, send, fd, hs, es, ec, eh, eg, he, cr, pf, pg):
+           hd, keep, send, fd, hs, es, ec, eh, eg, he, cr, pg, pt):
     nx = middle.shape[0] - 4
     ny = middle.shape[1]
     width = fs.shape[2]
@@ -279,13 +298,12 @@
         hd[0, x] = jnp.where(is_first, he[0, x:x + 1, :], hs[x, 7:7 + ny, :]).astype(BF16)
         hd[2, x] = jnp.where(is_last, he[1, x:x + 1, :], hs[x, 9:9 + ny, :]).astype(BF16)
 
-    def hidden_span(dx, dy, p):
-        return hd[dy, dx:dx + nx, :, lane * p:lane * (p + 2)].reshape(cells, 2 * lane)
+    def by_rows(pick, count):
+        return jnp.concatenate(
+            [pick(x, slice(lane * p, lane * (p + 2))) for x in range(depth) for p in range(count)], axis=0)
 
     second = packed(weight_gradient(
-        cot_t[...],
-        lambda dx, dy: jnp.concatenate([hidden_span(dx, dy, p) for p in range(pairs)], axis=0),
-        factor))
+        [dot(cot_t[...], by_rows(lambda x, span: hd[dy, x, :, span], pairs)) for dy in range(3)], factor))
 
     blank_edges(fd, width)
     first_row = is_first[:, 0:width]
@@ -294,17 +312,27 @@
         fd[0, x, :, lane:lane + width] = jnp.where(first_row, es[1, 7 + x:8 + x, :], fs[x + 1, 7:7 + ny, :]).astype(BF16)
         fd[1, x, :, lane:lane + width] = jnp.where(last_row, es[4, 7 + x:8 + x, :], fs[x + 1, 9:9 + ny, :]).astype(BF16)
 
-    def field_span(dx, dy, p):
-        span = slice(lane * p, lane * (p + 2))
-        if dy == 1:
-            return middle[dx + 1:dx + 1 + nx, :, span].reshape(cells, 2 * lane)
-        return fd[dy // 2, dx:dx + nx, :, span].reshape(cells, 2 * lane)
-
-    grad_t = jnp.concatenate(
-        [pg[:, :, lane * p:lane * (p + 1)].reshape(cells, lane).T for p in range(pairs + 1)], axis=1)
+    def field_row(dy, x, span):
+        return middle[x + 1, :, span] if dy == 1 else fd[dy // 2, x, :, span]
+
+    stack_shifts(pt, pg)
+    last = pg[:, :, lane * pairs:].reshape(cells, lane)
+    extra = 2 * lane - cells
+    last_t = jnp.concatenate(
+        [
+            jnp.concatenate([jnp.zeros((ny * dx, lane), BF16)] * (dx > 0) + [last, jnp.zeros((extra - ny * dx, lane), BF16)], axis=0).T
+            for dx in range(3)
+        ],
+        axis=0,
+    )
+    span = slice(lane * pairs, lane * (pairs + 2))
+    pad = jnp.zeros((2 * lane - depth * ny, 2 * lane), BF16)
     first = packed(weight_gradient(
-        grad_t,
-        lambda dx, dy: jnp.concatenate([field_span(dx, dy, p) for p in range(pairs + 1)], axis=0),
+        [
+            dot(pt[...], by_rows(lambda x, span: field_row(dy, x, span), pairs))
+            + dot(last_t, jnp.concatenate([field_row(dy, x, span) for x in range(depth)] + [pad], axis=0))
+            for dy in range(3)
+        ],
         factor))
 
     for index in range(BLOCKS):
@@ -339,34 +367,43 @@
         out[index] = total
 
 
-def unpack(mine, other, first, second):
+def unpack(mine, other, first, second, held, sems):
     gx = lax.axis_index("gx")
-    a = mine[...].astype(F32)
-    b = other[...].astype(F32)
-    for out, rows in ((first, jnp.where(gx == 0, a, b)), (second, jnp.where(gx == 0, b, a))):
+    copies = []
+    for which, out in enumerate((first, second)):
+        def block(index):
+            rows = slice(index * C, (index + 1) * C)
+            a = mine[rows, :].astype(F32)
+            b = other[rows, :].astype(F32)
+            return (jnp.where(gx == 0, a, b) if which == 0 else jnp.where(gx == 0, b, a)).T
+
         for t, (dx, dy) in enumerate(TAPS):
-            turned = rows[t * C:(t + 1) * C].T
-            out[9 * dx + 3 * dy] = turned[0:C]
-            out[9 * dx + 3 * dy + 1] = turned[C:2 * C]
-        for pair in range(5):
-            turned = rows[(9 + pair) * C:(10 + pair) * C].T
-            for half in range(2 if pair < 4 else 1):
-                dx, dy = TAPS[2 * pair + half]
-                out[9 * dx + 3 * dy + 2] = turned[half * C:(half + 1) * C]
+            turned = block(t)
+            if t % 2 == 0:
+                rest = block(9 + t // 2)
+            place = 9 * dx + 3 * dy
+            held[which, place] = turned[0:C]
+            held[which, place + 1] = turned[C:2 * C]
+            held[which, place + 2] = rest[C * (t % 2):C * (t % 2 + 1)]
+            copy = pltpu.make_async_copy(held.at[which, place:place + 3], out.at[place:place + 3], sems.at[which, t])
+            copy.start()
+            copies.append(copy)
+    for copy in copies:
+        copy.wait()
 
 
 def near(shape, dtype):
     return pltpu.VMEM(shape, dtype)
 
 
-def call(body, name, inputs, outs, scratch=(), limit=16, flops=0):
+def call(body, name, inputs, outs, scratch=(), limit=16, flops=0, far=False):
     placed = [pltpu.with_memory_space_constraint(x, pltpu.VMEM if held else pltpu.HBM) for x, held in inputs]
     size = sum(x.size * x.dtype.itemsize for x, _ in inputs)
     return pl.pallas_call(
         body,
         out_shape=list(outs),
         in_specs=[pl.BlockSpec(memory_space=pltpu.VMEM if held else pl.ANY) for _, held in inputs],
-        out_specs=[pl.BlockSpec(memory_space=pltpu.VMEM)] * len(outs),
+        out_specs=[pl.BlockSpec(memory_space=pl.ANY if far else pltpu.VMEM)] * len(outs),
         scratch_shapes=list(scratch),
         compiler_params=pltpu.CompilerParams(vmem_limit_bytes=limit * 1024 * 1024),
         cost_estimate=pl.CostEstimate(flops=flops, bytes_accessed=size, transcendentals=0),
@@ -384,35 +421,36 @@
     lane = 2 * C
     wide = width + 2 * lane
     pairs = NZ // 2
-    cells = nx * ny
 
     field, cot, edge, given = call(
         pack, "pack", [(field_in[0], False), (cotangent[0], False)],
         [near((nx, ny, width), BF16), near((nx, ny, width), BF16), near((3, nx, width), BF16), near((3, ny + nx, width), BF16)],
         [pltpu.VMEM((6, nx, width), F32), pltpu.SemaphoreType.DMA((2,))])
     side = swap(given)
-    w1b, w2b, wfb = call(
-        prepare, "prepare",
+    w1, w2 = call(
+        load_weights, "load_weights",
         [(first_weight.reshape(27, C, C), False), (second_weight.reshape(27, C, C), False)],
-        [near((9 * 4 * C, lane), BF16), near((9 * 4 * C, lane), BF16), near((lane, 9 * 4 * C), BF16)],
-        [pltpu.VMEM((27, C, C), BF16), pltpu.VMEM((27, C, C), BF16), pltpu.SemaphoreType.DMA((2,))])
-    side, w1b, w2b, wfb = lax.optimization_barrier((side, w1b, w2b, wfb))
+        [near((27, C, C), BF16)] * 2, [pltpu.SemaphoreType.DMA((2,))])
+    side, w1, w2 = lax.optimization_barrier((side, w1, w2))
     whole, = call(join_edges, "join_edges", [(edge, True), (side, True)], [near((3, 2 * nx, width), BF16)])
     ends = [(gy_count + j, j + 1) for j in range(gy_count - 1)]
     near_rows = lax.ppermute(whole, ("gx", "gy"), ends + [(b, a) for a, b in ends])
-    fs, middle, pre_part, cd, cot_t = call(
+    fs, middle, pre_part, cd, cot_t, w1b, w2b, wfb = call(
         functools.partial(interior_first, gx_count), "interior_first",
-        [(x, True) for x in (field, cot, side, w1b)],
+        [(x, True) for x in (field, cot, side, w1, w2)],
         [
             near((nx + 4, ny + 16, width), F32),
             near((nx + 4, ny, wide), BF16),
             near((nx + 2, ny, width + lane), F32),
             near((3, nx + 2, ny, wide), BF16),
-            near((lane, cells * pairs), BF16),
+            near((3 * lane, (nx + 2) * ny * pairs), BF16),
+            near((9 * 4 * C, lane), BF16),
+            near((9 * 4 * C, lane), BF16),
+            near((lane, 9 * 4 * C), BF16),
         ],
         [pltpu.VMEM((3, nx + 4, ny, wide), BF16), pltpu.VMEM((nx + 2, ny + 16, width), F32)],
         flops=4 * 10 ** 9)
-    near_rows, fs, middle, pre_part, cd, cot_t = lax.optimization_barrier((near_rows, fs, middle, pre_part, cd, cot_t))
+    near_rows, pre_part, wfb = lax.optimization_barrier((near_rows, pre_part, wfb))
     far_rows = swap(near_rows)
     grad_part, = call(
         interior_grad, "interior_grad", [(cd, True), (wfb, True)], [near((nx, ny, width + lane), F32)], flops=3 * 10 ** 9)
@@ -431,8 +469,8 @@
             pltpu.VMEM((3, 2, 16, wide), BF16),
             pltpu.VMEM((2, 16, width + lane), F32),
             pltpu.VMEM((4, 16, width + lane), F32),
-            pltpu.VMEM((nx, ny, width + lane), F32),
             pltpu.VMEM((nx, ny, width + lane), BF16),
+            pltpu.VMEM((3 * lane, (nx + 2) * ny * pairs), BF16),
         ],
         limit=32, flops=10 ** 10)
 
@@ -447,7 +485,8 @@
     mine = lax.all_to_all(spread, ("gy", "grp"), 0, 0).reshape(rows, lane)
     other = swap(mine)
     first, second = call(
-        unpack, "unpack", [(mine, True), (other, True)], [jax.ShapeDtypeStruct((27, C, C), F32)] * 2)
+        unpack, "unpack", [(mine, True), (other, True)], [pltpu.HBM((27, C, C), F32)] * 2,
+        [pltpu.VMEM((2, 27, C, C), F32), pltpu.SemaphoreType.DMA((2, 9))], far=True)
     shape = (3, 3, 3, C, C)
     return out[None], first.reshape(shape), second.reshape(shape)
 

time: 50.4 us -> 50.6 us (level)
  transfers between devices with their start and end apart: 5 -> 5, of which waited for: 2 -> 2; matrix products, arithmetic and copies ran while one was open for 1% -> 1% of each run, Pallas kernels for 14% -> 13%
where the time goes in v6:
time: 50.6 us; the launch traced here: 50.4 us
  blocking collectives  30 us (59%)
  Pallas kernels  12.7 us (25%)
  starting transfers between devices  5.34 us (11%)
  waiting for transfers between devices  0.86 us (2%)
  between operations  0.73 us (1%)
  local copies, waits for them, and re-layouts  0.7 us (1%)
    all_to_all x1, blocking collectives, shards(): lax.all_to_all(both.reshape(ranks, rows // ranks, lane), ('gy', 'grp'), 0...  17.8 us
    pallas_call x10, Pallas kernels, call(): pl.pallas_call(body, out_shape=list(outs), in_specs=[pl.BlockSpec(memory_...  12.7 us
    all_to_all x1, blocking collectives, shards(): mine = lax.all_to_all(spread, ('gy', 'grp'), 0, 0).reshape(rows, lane)  12.2 us
    ppermute x4, starting transfers between devices, swap(): return lax.ppermute(array, 'gx', [(0, 1), (1, 0)])  4.67 us
  transfers between devices with their start and end apart: 5, of which 2 were waited for; matrix products, arithmetic and copies ran while one was open for 1% of the time, Pallas kernels for 13%

profile of v6, /device:TPU:0, one launch (start us, length us, event | category | flops | bytes accessed | tf_op | source)
XLA Modules:
  0.0 50.4 jit_solution(3670659098151907408)
XLA Ops:
  0.6 1.2 %pack.1 = (bf16[8,16,1024]{2,1,0:T(8,128)(2,1)S(1)}, bf16[8,16,1024]{2,1,0:T(8,128)(2,1)S(1)}, bf16[3,8,1024]{2,1,0:T(8,128)(2,1)S(1)}, bf16[3,24,1024]{2,1,0:T(8,128)(2,1)S(1)}) custom-call(bf16[8,16,1024]{2,1,0:T(8,128)(2,1)} %bitcast.15, bf16[8,16,1024]{2,1,0:T(8,128)(2,1)} %bitcast.16), custom_call_target="tpu_custom_call" | custom-call | bytes 524288 | tf_op jit(solution)/shard_map/pack/pallas_call | solution.py:402
  1.8 0.5 %collective-permute-start = (bf16[3,24,1024]{2,1,0:T(8,128)(2,1)S(1)}, bf16[3,24,1024]{2,1,0:T(8,128)(2,1)S(1)}, u32[]{:S(2)}, u32[]{:S(2)}) collective-permute-start(bf16[3,24,1024]{2,1,0:T(8,128)(2,1)S(1)} %get-tuple-element.34), channel_id=1, source_target_pairs={{0,16},{16,0},{1,17},{17,1},{2,18},{18,2},{3,19},{19,3},{4,20},{20... | collective-permute-start | bytes 442376 | tf_op jit(solution)/shard_map/ppermute | solution.py:20
  2.3 1.2 %load_weights.1 = (bf16[27,64,64]{2,1,0:T(8,128)(2,1)S(1)}, bf16[27,64,64]{2,1,0:T(8,128)(2,1)S(1)}) custom-call(bf16[27,64,64]{2,1,0:T(8,128)(2,1)} %bitcast.13, bf16[27,64,64]{2,1,0:T(8,128)(2,1)} %bitcast.14), custom_call_target="tpu_custom_call" | custom-call | bytes 442368 | tf_op jit(solution)/shard_map/load_weights/pallas_call | solution.py:402
  3.5 0.0 collective-permute-done.side.taken
  3.5 0.7 %collective-permute-start.1 = (bf16[3,16,1024]{2,1,0:T(8,128)(2,1)S(1)}, bf16[3,16,1024]{2,1,0:T(8,128)(2,1)S(1)}, u32[]{:S(2)}, u32[]{:S(2)}) collective-permute-start(bf16[3,16,1024]{2,1,0:T(8,128)(2,1)S(1)} %join_edges.1), channel_id=1, source_target_pairs={{16,4},{20,8},{24,12},{4,16},{8,20},{12,24},{17,5},{21,9},{25,13},... | collective-permute-start | bytes 294920 | tf_op jit(solution)/shard_map/ppermute | solution.py:437
  4.2 2.5 %interior_first.1 = (f32[12,32,1024]{2,1,0:T(8,128)S(1)}, bf16[12,16,1280]{2,1,0:T(8,128)(2,1)S(1)}, f32[10,16,1152]{2,1,0:T(8,128)S(1)}, bf16[3,10,16,1280]{3,2...) custom-call(bf16[8,16,1024]{2,1,0:T(8,128)(2,1)S(1)} %get-tuple-elem, ...), custom_call_target="tpu_custom_call" | custom-call | flops 4000000000 | bytes 1114112 | tf_op jit(solution)/shard_map/interior_first/pallas_call | solution.py:402
  6.7 0.0 collective-permute-done.1.near_rows
  6.7 4.1 %collective-permute-start.2 = (bf16[3,16,1024]{2,1,0:T(8,128)(2,1)S(1)}, bf16[3,16,1024]{2,1,0:T(8,128)(2,1)S(1)}, u32[]{:S(2)}, u32[]{:S(2)}) collective-permute-start(bf16[3,16,1024]{2,1,0:T(8,128)(2,1)S(1)} %collective-permute-done.1.near_rows), channel_id=1, source_target_pairs={{0,16},{16,0},{1,17},{17,1},{2,18},{18,2},{3,19},{19,3},{4,20},{20... | collective-permute-start | bytes 294920 | tf_op jit(solution)/shard_map/ppermute | solution.py:20
  10.8 1.5 %interior_grad.1.grad_part = f32[8,16,1152]{2,1,0:T(8,128)S(1)} custom-call(bf16[3,10,16,1280]{3,2,1,0:T(8,128)(2,1)S(1)} %get-tuple-element.47.cd, bf16[128,2304]{1,0:T(8,128)(2,1)S(1)} %get-tuple-element.48.wfb), custom_call_target="tpu_custom_call" | custom-call | flops 3000000000 | bytes 1818624 | tf_op jit(solution)/shard_map/interior_grad/pallas_call | solution.py:402
  12.4 0.0 collective-permute-done.2.far_rows
  12.4 3.4 %layers.1 = (bf16[3,10,16,1152]{3,2,1,0:T(8,128)(2,1)S(1)}, f32[896,128]{1,0:T(8,128)S(1)}, bf16[896,128]{1,0:T(8,128)(2,1)S(1)}) custom-call(f32[12,32,1024]{2,1,0:T(8,128)S(1)} %get-tuple-element.40.fs, bf16[12,16,1280]{2,1,0:T(8,128)(2,1)S(1)} %get-tuple-element.41.middle, f32[10,16,1152]{2,1,0:T(8,128)S(1)} %get-tuple-element.45.pre_part, ...), custom_call_target="tpu_custom_call" | custom-call | flops 10000000000 | bytes 5750784 | tf_op jit(solution)/shard_map/layers/pallas_call | solution.py:402
  15.8 0.1 collective-permute-start.3
  15.8 1.4 %output_conv.1 = bf16[8,16,1024]{2,1,0:T(8,128)(2,1)S(1)} custom-call(bf16[3,10,16,1152]{3,2,1,0:T(8,128)(2,1)S(1)} %get-tuple-element.54.hd, bf16[2304,128]{1,0:T(8,128)(2,1)S(1)} %get-tuple-element.55.w2b), custom_call_target="tpu_custom_call" | custom-call | flops 2000000000 | bytes 1695744 | tf_op jit(solution)/shard_map/output_conv/pallas_call | solution.py:402
  17.2 0.1 collective-permute-done.3.other
  17.4 17.8 %all_to_all.10.terms = bf16[16,56,128]{2,1,0:T(8,128)(2,1)S(1)} all-to-all(bf16[16,56,128]{2,1,0:T(8,128)(2,1)S(1)} %bitcast.10), channel_id=1, replica_groups=mesh['gx'=2,'gy'=4,'grp'=4] {'gy','grp'}, dimensions={0} | all-to-all | bytes 458752 | tf_op jit(solution)/shard_map/all_to_all | solution.py:483
  35.2 12.2 %all_to_all.11 = bf16[16,56,128]{2,1,0:T(8,128)(2,1)S(1)} all-to-all(bf16[16,56,128]{2,1,0:T(8,128)(2,1)S(1)} %add_and_repeat.1), channel_id=1, replica_groups=mesh['gx'=2,'gy'=4,'grp'=4] {'gy','grp'}, dimensions={0} | all-to-all | bytes 458752 | tf_op jit(solution)/shard_map/all_to_all | solution.py:485
  47.4 0.0 collective-permute-start.4
  47.4 0.7 %copy.7 = bf16[1,8,16,1024]{3,2,1,0:T(8,128)(2,1)} copy(bf16[1,8,16,1024]{3,2,1,0:T(8,128)(2,1)S(1)} %bitcast.9) | data formatting | bytes 524288
  48.1 0.8 %collective-permute-done.4.other = bf16[896,128]{1,0:T(8,128)(2,1)S(1)} collective-permute-done((bf16[896,128]{1,0:T(8,128)(2,1)S(1)}, bf16[896,128]{1,0:T(8,128)(2,1)S(1)}, u32[]{:S(2)}, u32[]{:S(2)}) %collective-permute-start.4) | collective-permute-done | bytes 229408 | tf_op jit(solution)/shard_map/ppermute | solution.py:20
  48.9 1.5 %unpack.1 = (f32[27,64,64]{2,1,0:T(8,128)}, f32[27,64,64]{2,1,0:T(8,128)}) custom-call(bf16[896,128]{1,0:T(8,128)(2,1)S(1)} %bitcast.12, bf16[896,128]{1,0:T(8,128)(2,1)S(1)} %collective-permute-done.4.other), custom_call_target="tpu_custom_call" | custom-call | bytes 458752 | tf_op jit(solution)/shard_map/unpack/pallas_call | solution.py:402
  (3 shorter events, 0.1 us)
Async XLA Ops:
  1.8 1.7 %collective-permute-start = (bf16[3,24,1024]{2,1,0:T(8,128)(2,1)S(1)}, bf16[3,24,1024]{2,1,0:T(8,128)(2,1)S(1)}, u32[]{:S(2)}, u32[]{:S(2)}) collective-permute-start(bf16[3,24,1024]{2,1,0:T(8,128)(2,1)S(1)} %get-tuple-element.34), channel_id=1, source_target_pairs={{0,16},{16,0},{1,17},{17,1},{2,18},{18,2},{3,19},{19,3},{4,20},{20... | collective-permute-start | bytes 442376 | tf_op jit(solution)/shard_map/ppermute | solution.py:20
  3.5 3.2 %collective-permute-start.1 = (bf16[3,16,1024]{2,1,0:T(8,128)(2,1)S(1)}, bf16[3,16,1024]{2,1,0:T(8,128)(2,1)S(1)}, u32[]{:S(2)}, u32[]{:S(2)}) collective-permute-start(bf16[3,16,1024]{2,1,0:T(8,128)(2,1)S(1)} %join_edges.1), channel_id=1, source_target_pairs={{16,4},{20,8},{24,12},{4,16},{8,20},{12,24},{17,5},{21,9},{25,13},... | collective-permute-start | bytes 294920 | tf_op jit(solution)/shard_map/ppermute | solution.py:437
  6.7 5.6 %collective-permute-start.2 = (bf16[3,16,1024]{2,1,0:T(8,128)(2,1)S(1)}, bf16[3,16,1024]{2,1,0:T(8,128)(2,1)S(1)}, u32[]{:S(2)}, u32[]{:S(2)}) collective-permute-start(bf16[3,16,1024]{2,1,0:T(8,128)(2,1)S(1)} %collective-permute-done.1.near_rows), channel_id=1, source_target_pairs={{0,16},{16,0},{1,17},{17,1},{2,18},{18,2},{3,19},{19,3},{4,20},{20... | collective-permute-start | bytes 294920 | tf_op jit(solution)/shard_map/ppermute | solution.py:20
  15.8 1.6 %collective-permute-start.3 = (bf16[896,128]{1,0:T(8,128)(2,1)S(1)}, bf16[896,128]{1,0:T(8,128)(2,1)S(1)}, u32[]{:S(2)}, u32[]{:S(2)}) collective-permute-start(bf16[896,128]{1,0:T(8,128)(2,1)S(1)} %get-tuple-element.53), channel_id=1, source_target_pairs={{0,16},{16,0},{1,17},{17,1},{2,18},{18,2},{3,19},{19,3},{4,20},{20... | collective-permute-start | bytes 688136 | tf_op jit(solution)/shard_map/ppermute | solution.py:20
  47.4 1.5 %collective-permute-start.4 = (bf16[896,128]{1,0:T(8,128)(2,1)S(1)}, bf16[896,128]{1,0:T(8,128)(2,1)S(1)}, u32[]{:S(2)}, u32[]{:S(2)}) collective-permute-start(bf16[896,128]{1,0:T(8,128)(2,1)S(1)} %bitcast.11), channel_id=1, source_target_pairs={{0,16},{16,0},{1,17},{17,1},{2,18},{18,2},{3,19},{19,3},{4,20},{20... | collective-permute-start | bytes 688136 | tf_op jit(solution)/shard_map/ppermute | solution.py:20

commit v7 on v5

--- a/solution.py
+++ b/solution.py
@@ -14,6 +14,7 @@
 F32 = jnp.float32
 TAPS = [(dx, dy) for dy in range(3) for dx in range(3)]
 BLOCKS = 14
+EARLY = 3
 
 
 def swap(array):
@@ -108,7 +109,7 @@
         whole[:, nx:2 * nx] = edge[...]
 
 
-def prepare(w1_hbm, w2_hbm, w1b, w2b, wfb, w1, w2, sems):
+def load_weights(w1_hbm, w2_hbm, w1, w2, sems):
     copies = [
         pltpu.make_async_copy(source, target, sems.at[index])
         for index, (source, target) in enumerate(((w1_hbm, w1), (w2_hbm, w2)))
@@ -117,6 +118,9 @@
         copy.start()
     for copy in copies:
         copy.wait()
+
+
+def make_bands(w1, w2, w1b, w2b, wfb):
     for t, (dx, dy) in enumerate(TAPS):
         rows = slice(t * 4 * C, (t + 1) * 4 * C)
         first = 9 * dx + 3 * dy
@@ -154,11 +158,11 @@
         copies[dy, :, :, lane:lane + width] = scratch[:, 7 + dy:7 + dy + ny, :].astype(BF16)
 
 
-def interior_first(gx_count, field, cot, side, w1b, fs, middle, partial, cd, cot_t, fd, cs):
+def interior_first(gx_count, field, cot, side, w1, w2, fs, middle, partial, cd, cot_t, w1b, w2b, wfb, grad_part, fd, cs):
     nx, ny, width = field.shape
     lane = 2 * C
-    cells = nx * ny
     depth = nx + 2
+    make_bands(w1, w2, w1b, w2b, wfb)
     extend(gx_count, fs, field, side.at[0:2])
     fill_copies(fs, fd)
     middle[...] = fd[1]
@@ -168,21 +172,24 @@
         partial[:, :, lane * p:lane * (p + 1)] = dot(block, w1b[...]).reshape(depth, ny, lane)
     extend(gx_count, cs, cot, side.at[2:3])
     fill_copies(cs, cd)
+    cells = nx * ny
     for p in range(NZ // 2):
         cot_t[:, cells * p:cells * (p + 1)] = cot[:, :, lane * p:lane * (p + 1)].reshape(cells, lane).T
-
-
-def interior_grad(cd, wfb, partial):
+    interior_grad(range(EARLY), cd, wfb, grad_part)
+
+
+def interior_grad(pairs, cd, wfb, partial):
     nx, ny, _ = partial.shape
     lane = 2 * C
-    for p in range(NZ // 2 + 1):
+    for p in pairs:
         span = slice(lane * p, lane * (p + 2))
         block = jnp.concatenate([cd[dy, dx:dx + nx, :, span].reshape(nx * ny, 2 * lane) for dx, dy in TAPS], axis=1)
-        partial[:, :, lane * p:lane * (p + 1)] = dot_nt(block, wfb[...]).reshape(nx, ny, lane)
-
-
-def layers(factor, gx_count, gy_count, fs, middle, pre_part, grad_part, near_rows, far_rows, w1b, wfb, cot_t,
-           hd, keep, send, fd, hs, es, ec, eh, eg, he, cr, pf, pg):
+        here = lane * (p - pairs[0])
+        partial[:, :, here:here + lane] = dot_nt(block, wfb[...]).reshape(nx, ny, lane)
+
+
+def layers(factor, gx_count, gy_count, fs, middle, pre_part, grad_early, grad_late, near_rows, far_rows, w1b, wfb, cot_t,
+           hd, keep, send, fd, hs, es, ec, eh, eg, he, cr, pg):
     nx = middle.shape[0] - 4
     ny = middle.shape[1]
     width = fs.shape[2]
@@ -266,7 +273,7 @@
         pre = pre + jnp.where(is_first, cr[0, x:x + 1, :], 0.0) + jnp.where(is_last, cr[1, x:x + 1, :], 0.0)
         sigma = jax.nn.sigmoid(pre)
         if 0 < x < depth - 1:
-            grad = grad_part[x - 1]
+            grad = jnp.concatenate([grad_early[x - 1], grad_late[x - 1]], axis=1)
             grad = grad + jnp.where(is_first, cr[2, x - 1:x, :], 0.0) + jnp.where(is_last, cr[3, x - 1:x, :], 0.0)
             pg[x - 1] = (grad * sigma * (1.0 + pre * (1.0 - sigma)) * inside).astype(BF16)
         hidden = pre * sigma * inside
@@ -384,43 +391,46 @@
     lane = 2 * C
     wide = width + 2 * lane
     pairs = NZ // 2
-    cells = nx * ny
 
     field, cot, edge, given = call(
         pack, "pack", [(field_in[0], False), (cotangent[0], False)],
         [near((nx, ny, width), BF16), near((nx, ny, width), BF16), near((3, nx, width), BF16), near((3, ny + nx, width), BF16)],
         [pltpu.VMEM((6, nx, width), F32), pltpu.SemaphoreType.DMA((2,))])
     side = swap(given)
-    w1b, w2b, wfb = call(
-        prepare, "prepare",
+    w1, w2 = call(
+        load_weights, "load_weights",
         [(first_weight.reshape(27, C, C), False), (second_weight.reshape(27, C, C), False)],
-        [near((9 * 4 * C, lane), BF16), near((9 * 4 * C, lane), BF16), near((lane, 9 * 4 * C), BF16)],
-        [pltpu.VMEM((27, C, C), BF16), pltpu.VMEM((27, C, C), BF16), pltpu.SemaphoreType.DMA((2,))])
-    side, w1b, w2b, wfb = lax.optimization_barrier((side, w1b, w2b, wfb))
+        [near((27, C, C), BF16)] * 2, [pltpu.SemaphoreType.DMA((2,))])
+    side, w1, w2 = lax.optimization_barrier((side, w1, w2))
     whole, = call(join_edges, "join_edges", [(edge, True), (side, True)], [near((3, 2 * nx, width), BF16)])
     ends = [(gy_count + j, j + 1) for j in range(gy_count - 1)]
     near_rows = lax.ppermute(whole, ("gx", "gy"), ends + [(b, a) for a, b in ends])
-    fs, middle, pre_part, cd, cot_t = call(
+    fs, middle, pre_part, cd, cot_t, w1b, w2b, wfb, grad_early = call(
         functools.partial(interior_first, gx_count), "interior_first",
-        [(x, True) for x in (field, cot, side, w1b)],
+        [(x, True) for x in (field, cot, side, w1, w2)],
         [
             near((nx + 4, ny + 16, width), F32),
             near((nx + 4, ny, wide), BF16),
             near((nx + 2, ny, width + lane), F32),
             near((3, nx + 2, ny, wide), BF16),
-            near((lane, cells * pairs), BF16),
+            near((lane, nx * ny * pairs), BF16),
+            near((9 * 4 * C, lane), BF16),
+            near((9 * 4 * C, lane), BF16),
+            near((lane, 9 * 4 * C), BF16),
+            near((nx, ny, EARLY * lane), F32),
         ],
         [pltpu.VMEM((3, nx + 4, ny, wide), BF16), pltpu.VMEM((nx + 2, ny + 16, width), F32)],
         flops=4 * 10 ** 9)
-    near_rows, fs, middle, pre_part, cd, cot_t = lax.optimization_barrier((near_rows, fs, middle, pre_part, cd, cot_t))
+    near_rows, pre_part, wfb = lax.optimization_barrier((near_rows, pre_part, wfb))
     far_rows = swap(near_rows)
-    grad_part, = call(
-        interior_grad, "interior_grad", [(cd, True), (wfb, True)], [near((nx, ny, width + lane), F32)], flops=3 * 10 ** 9)
-    far_rows, grad_part = lax.optimization_barrier((far_rows, grad_part))
+    grad_late, = call(
+        functools.partial(interior_grad, range(EARLY, pairs + 1)), "interior_grad", [(cd, True), (wfb, True)],
+        [near((nx, ny, (pairs + 1 - EARLY) * lane), F32)], flops=3 * 10 ** 9)
+    far_rows, grad_late = lax.optimization_barrier((far_rows, grad_late))
 
     hd, keep, send = call(
         functools.partial(layers, factor, gx_count, gy_count), "layers",
-        [(x, True) for x in (fs, middle, pre_part, grad_part, near_rows, far_rows, w1b, wfb, cot_t)],
+        [(x, True) for x in (fs, middle, pre_part, grad_early, grad_late, near_rows, far_rows, w1b, wfb, cot_t)],
         [near((3, nx + 2, ny, width + lane), BF16), near((rows, lane), F32), near((rows, lane), BF16)],
         [
             pltpu.VMEM((2, nx + 2, ny, wide), BF16),
@@ -431,7 +441,6 @@
             pltpu.VMEM((3, 2, 16, wide), BF16),
             pltpu.VMEM((2, 16, width + lane), F32),
             pltpu.VMEM((4, 16, width + lane), F32),
-            pltpu.VMEM((nx, ny, width + lane), F32),
             pltpu.VMEM((nx, ny, width + lane), BF16),
         ],
         limit=32, flops=10 ** 10)

time: 50.4 us -> 49.7 us (0.986)
    all_to_all x1, blocking collectives: 17.9 us -> 17.4 us  [shards(): lax.all_to_all(both.reshape(ranks, rows // ranks, lane), ('gy', 'grp'), 0...]
  transfers between devices with their start and end apart: 5 -> 5, of which waited for: 2 -> 1; matrix products, arithmetic and copies ran while one was open for 1% -> 1% of each run, Pallas kernels for 14% -> 13%
where the time goes in v7:
time: 49.7 us; the launch traced here: 49.5 us
  blocking collectives  29.6 us (60%)
  Pallas kernels  12.1 us (24%)
  starting transfers between devices  5.54 us (11%)
  waiting for transfers between devices  0.79 us (2%)
  between operations  0.73 us (1%)
  local copies, waits for them, and re-layouts  0.7 us (1%)
    all_to_all x1, blocking collectives, shards(): lax.all_to_all(both.reshape(ranks, rows // ranks, lane), ('gy', 'grp'), 0...  17.4 us
    all_to_all x1, blocking collectives, shards(): mine = lax.all_to_all(spread, ('gy', 'grp'), 0, 0).reshape(rows, lane)  12.2 us
    pallas_call x10, Pallas kernels, call(): pl.pallas_call(body, out_shape=list(outs), in_specs=[pl.BlockSpec(memory_...  12.1 us
    ppermute x4, starting transfers between devices, swap(): return lax.ppermute(array, 'gx', [(0, 1), (1, 0)])  4.88 us
  transfers between devices with their start and end apart: 5, of which 1 were waited for; matrix products, arithmetic and copies ran while one was open for 1% of the time, Pallas kernels for 13%

profile of v7, /device:TPU:0, one launch (start us, length us, event | category | flops | bytes accessed | tf_op | source)
XLA Modules:
  0.0 49.5 jit_solution(2517370914941582225)
XLA Ops:
  0.6 1.2 %pack.1 = (bf16[8,16,1024]{2,1,0:T(8,128)(2,1)S(1)}, bf16[8,16,1024]{2,1,0:T(8,128)(2,1)S(1)}, bf16[3,8,1024]{2,1,0:T(8,128)(2,1)S(1)}, bf16[3,24,1024]{2,1,0:T(8,128)(2,1)S(1)}) custom-call(bf16[8,16,1024]{2,1,0:T(8,128)(2,1)} %bitcast.15, bf16[8,16,1024]{2,1,0:T(8,128)(2,1)} %bitcast.16), custom_call_target="tpu_custom_call" | custom-call | bytes 524288 | tf_op jit(solution)/shard_map/pack/pallas_call | solution.py:372
  1.8 0.5 %collective-permute-start = (bf16[3,24,1024]{2,1,0:T(8,128)(2,1)S(1)}, bf16[3,24,1024]{2,1,0:T(8,128)(2,1)S(1)}, u32[]{:S(2)}, u32[]{:S(2)}) collective-permute-start(bf16[3,24,1024]{2,1,0:T(8,128)(2,1)S(1)} %get-tuple-element.35), channel_id=1, source_target_pairs={{0,16},{16,0},{1,17},{17,1},{2,18},{18,2},{3,19},{19,3},{4,20},{20... | collective-permute-start | bytes 442376 | tf_op jit(solution)/shard_map/ppermute | solution.py:21
  2.3 1.2 %load_weights.1 = (bf16[27,64,64]{2,1,0:T(8,128)(2,1)S(1)}, bf16[27,64,64]{2,1,0:T(8,128)(2,1)S(1)}) custom-call(bf16[27,64,64]{2,1,0:T(8,128)(2,1)} %bitcast.13, bf16[27,64,64]{2,1,0:T(8,128)(2,1)} %bitcast.14), custom_call_target="tpu_custom_call" | custom-call | bytes 442368 | tf_op jit(solution)/shard_map/load_weights/pallas_call | solution.py:372
  3.5 0.0 collective-permute-done.side.taken
  3.5 0.7 %collective-permute-start.1 = (bf16[3,16,1024]{2,1,0:T(8,128)(2,1)S(1)}, bf16[3,16,1024]{2,1,0:T(8,128)(2,1)S(1)}, u32[]{:S(2)}, u32[]{:S(2)}) collective-permute-start(bf16[3,16,1024]{2,1,0:T(8,128)(2,1)S(1)} %join_edges.1), channel_id=1, source_target_pairs={{16,4},{20,8},{24,12},{4,16},{8,20},{12,24},{17,5},{21,9},{25,13},... | collective-permute-start | bytes 294920 | tf_op jit(solution)/shard_map/ppermute | solution.py:407
  4.2 2.8 %interior_first.1 = (f32[12,32,1024]{2,1,0:T(8,128)S(1)}, bf16[12,16,1280]{2,1,0:T(8,128)(2,1)S(1)}, f32[10,16,1152]{2,1,0:T(8,128)S(1)}, bf16[3,10,16,1280]{3,2...) custom-call(bf16[8,16,1024]{2,1,0:T(8,128)(2,1)S(1)} %get-tuple-elem, ...), custom_call_target="tpu_custom_call" | custom-call | flops 4000000000 | bytes 1114112 | tf_op jit(solution)/shard_map/interior_first/pallas_call | solution.py:372
  7.0 0.0 collective-permute-done.1.near_rows
  7.0 4.1 %collective-permute-start.2 = (bf16[3,16,1024]{2,1,0:T(8,128)(2,1)S(1)}, bf16[3,16,1024]{2,1,0:T(8,128)(2,1)S(1)}, u32[]{:S(2)}, u32[]{:S(2)}) collective-permute-start(bf16[3,16,1024]{2,1,0:T(8,128)(2,1)S(1)} %collective-permute-done.1.near_rows), channel_id=1, source_target_pairs={{0,16},{16,0},{1,17},{17,1},{2,18},{18,2},{3,19},{19,3},{4,20},{20... | collective-permute-start | bytes 294920 | tf_op jit(solution)/shard_map/ppermute | solution.py:21
  11.1 1.1 %interior_grad.1.grad_late = f32[8,16,768]{2,1,0:T(8,128)S(1)} custom-call(bf16[3,10,16,1280]{3,2,1,0:T(8,128)(2,1)S(1)} %get-tuple-element.49.cd, bf16[128,2304]{1,0:T(8,128)(2,1)S(1)} %get-tuple-element.50.wfb), custom_call_target="tpu_custom_call" | custom-call | flops 3000000000 | bytes 1818624 | tf_op jit(solution)/shard_map/interior_grad/pallas_call | solution.py:372
  12.2 0.0 collective-permute-done.2.far_rows
  12.2 3.0 %layers.1 = (bf16[3,10,16,1152]{3,2,1,0:T(8,128)(2,1)S(1)}, f32[896,128]{1,0:T(8,128)S(1)}, bf16[896,128]{1,0:T(8,128)(2,1)S(1)}) custom-call(f32[12,32,1024]{2,1,0:T(8,128)S(1)} %get-tuple-element.41.fs, bf16[12,16,1280]{2,1,0:T(8,128)(2,1)S(1)} %get-tuple-element.42.middle, f32[10,16,1152]{2,1,0:T(8,128)S(1)} %get-tuple-element.46.pre_part, ...), custom_call_target="tpu_custom_call" | custom-call | flops 10000000000 | bytes 5029888 | tf_op jit(solution)/shard_map/layers/pallas_call | solution.py:372
  15.2 0.3 collective-permute-start.3
  15.5 1.4 %output_conv.1 = bf16[8,16,1024]{2,1,0:T(8,128)(2,1)S(1)} custom-call(bf16[3,10,16,1152]{3,2,1,0:T(8,128)(2,1)S(1)} %get-tuple-element.56.hd, bf16[2304,128]{1,0:T(8,128)(2,1)S(1)} %get-tuple-element.57.w2b), custom_call_target="tpu_custom_call" | custom-call | flops 2000000000 | bytes 1695744 | tf_op jit(solution)/shard_map/output_conv/pallas_call | solution.py:372
  16.9 0.0 collective-permute-done.3.other
  16.9 17.4 %all_to_all.10.terms = bf16[16,56,128]{2,1,0:T(8,128)(2,1)S(1)} all-to-all(bf16[16,56,128]{2,1,0:T(8,128)(2,1)S(1)} %bitcast.10), channel_id=1, replica_groups=mesh['gx'=2,'gy'=4,'grp'=4] {'gy','grp'}, dimensions={0} | all-to-all | bytes 458752 | tf_op jit(solution)/shard_map/all_to_all | solution.py:454
  34.4 12.2 %all_to_all.11 = bf16[16,56,128]{2,1,0:T(8,128)(2,1)S(1)} all-to-all(bf16[16,56,128]{2,1,0:T(8,128)(2,1)S(1)} %add_and_repeat.1), channel_id=1, replica_groups=mesh['gx'=2,'gy'=4,'grp'=4] {'gy','grp'}, dimensions={0} | all-to-all | bytes 458752 | tf_op jit(solution)/shard_map/all_to_all | solution.py:456
  46.6 0.0 collective-permute-start.4
  46.6 0.7 %copy.7 = bf16[1,8,16,1024]{3,2,1,0:T(8,128)(2,1)} copy(bf16[1,8,16,1024]{3,2,1,0:T(8,128)(2,1)S(1)} %bitcast.9) | data formatting | bytes 524288
  47.3 0.8 %collective-permute-done.4.other = bf16[896,128]{1,0:T(8,128)(2,1)S(1)} collective-permute-done((bf16[896,128]{1,0:T(8,128)(2,1)S(1)}, bf16[896,128]{1,0:T(8,128)(2,1)S(1)}, u32[]{:S(2)}, u32[]{:S(2)}) %collective-permute-start.4) | collective-permute-done | bytes 229408 | tf_op jit(solution)/shard_map/ppermute | solution.py:21
  48.1 1.4 %unpack.1 = (f32[27,64,64]{2,1,0:T(8,128)}, f32[27,64,64]{2,1,0:T(8,128)}) custom-call(bf16[896,128]{1,0:T(8,128)(2,1)S(1)} %bitcast.12, bf16[896,128]{1,0:T(8,128)(2,1)S(1)} %collective-permute-done.4.other), custom_call_target="tpu_custom_call" | custom-call | bytes 458752 | tf_op jit(solution)/shard_map/unpack/pallas_call | solution.py:372
  (3 shorter events, 0.1 us)
Async XLA Ops:
  1.8 1.7 %collective-permute-start = (bf16[3,24,1024]{2,1,0:T(8,128)(2,1)S(1)}, bf16[3,24,1024]{2,1,0:T(8,128)(2,1)S(1)}, u32[]{:S(2)}, u32[]{:S(2)}) collective-permute-start(bf16[3,24,1024]{2,1,0:T(8,128)(2,1)S(1)} %get-tuple-element.35), channel_id=1, source_target_pairs={{0,16},{16,0},{1,17},{17,1},{2,18},{18,2},{3,19},{19,3},{4,20},{20... | collective-permute-start | bytes 442376 | tf_op jit(solution)/shard_map/ppermute | solution.py:21
  3.5 3.5 %collective-permute-start.1 = (bf16[3,16,1024]{2,1,0:T(8,128)(2,1)S(1)}, bf16[3,16,1024]{2,1,0:T(8,128)(2,1)S(1)}, u32[]{:S(2)}, u32[]{:S(2)}) collective-permute-start(bf16[3,16,1024]{2,1,0:T(8,128)(2,1)S(1)} %join_edges.1), channel_id=1, source_target_pairs={{16,4},{20,8},{24,12},{4,16},{8,20},{12,24},{17,5},{21,9},{25,13},... | collective-permute-start | bytes 294920 | tf_op jit(solution)/shard_map/ppermute | solution.py:407
  7.0 5.2 %collective-permute-start.2 = (bf16[3,16,1024]{2,1,0:T(8,128)(2,1)S(1)}, bf16[3,16,1024]{2,1,0:T(8,128)(2,1)S(1)}, u32[]{:S(2)}, u32[]{:S(2)}) collective-permute-start(bf16[3,16,1024]{2,1,0:T(8,128)(2,1)S(1)} %collective-permute-done.1.near_rows), channel_id=1, source_target_pairs={{0,16},{16,0},{1,17},{17,1},{2,18},{18,2},{3,19},{19,3},{4,20},{20... | collective-permute-start | bytes 294920 | tf_op jit(solution)/shard_map/ppermute | solution.py:21
  15.2 1.7 %collective-permute-start.3 = (bf16[896,128]{1,0:T(8,128)(2,1)S(1)}, bf16[896,128]{1,0:T(8,128)(2,1)S(1)}, u32[]{:S(2)}, u32[]{:S(2)}) collective-permute-start(bf16[896,128]{1,0:T(8,128)(2,1)S(1)} %get-tuple-element.55), channel_id=1, source_target_pairs={{0,16},{16,0},{1,17},{17,1},{2,18},{18,2},{3,19},{19,3},{4,20},{20... | collective-permute-start | bytes 688136 | tf_op jit(solution)/shard_map/ppermute | solution.py:21
  46.6 1.5 %collective-permute-start.4 = (bf16[896,128]{1,0:T(8,128)(2,1)S(1)}, bf16[896,128]{1,0:T(8,128)(2,1)S(1)}, u32[]{:S(2)}, u32[]{:S(2)}) collective-permute-start(bf16[896,128]{1,0:T(8,128)(2,1)S(1)} %bitcast.11), channel_id=1, source_target_pairs={{0,16},{16,0},{1,17},{17,1},{2,18},{18,2},{3,19},{19,3},{4,20},{20... | collective-permute-start | bytes 688136 | tf_op jit(solution)/shard_map/ppermute | solution.py:21

commit v8 on v7

--- a/solution.py
+++ b/solution.py
@@ -189,7 +189,7 @@
 
 
 def layers(factor, gx_count, gy_count, fs, middle, pre_part, grad_early, grad_late, near_rows, far_rows, w1b, wfb, cot_t,
-           hd, keep, send, fd, hs, es, ec, eh, eg, he, cr, pg):
+           hd, pg, fd, send, hs, es, ec, eh, eg, he, cr):
     nx = middle.shape[0] - 4
     ny = middle.shape[1]
     width = fs.shape[2]
@@ -286,14 +286,6 @@
         hd[0, x] = jnp.where(is_first, he[0, x:x + 1, :], hs[x, 7:7 + ny, :]).astype(BF16)
         hd[2, x] = jnp.where(is_last, he[1, x:x + 1, :], hs[x, 9:9 + ny, :]).astype(BF16)
 
-    def hidden_span(dx, dy, p):
-        return hd[dy, dx:dx + nx, :, lane * p:lane * (p + 2)].reshape(cells, 2 * lane)
-
-    second = packed(weight_gradient(
-        cot_t[...],
-        lambda dx, dy: jnp.concatenate([hidden_span(dx, dy, p) for p in range(pairs)], axis=0),
-        factor))
-
     blank_edges(fd, width)
     first_row = is_first[:, 0:width]
     last_row = is_last[:, 0:width]
@@ -301,6 +293,34 @@
         fd[0, x, :, lane:lane + width] = jnp.where(first_row, es[1, 7 + x:8 + x, :], fs[x + 1, 7:7 + ny, :]).astype(BF16)
         fd[1, x, :, lane:lane + width] = jnp.where(last_row, es[4, 7 + x:8 + x, :], fs[x + 1, 9:9 + ny, :]).astype(BF16)
 
+    @pl.when(gx == 0)
+    def _():
+        store_blocks(send, second_gradient(factor, hd, cot_t))
+
+    @pl.when(gx != 0)
+    def _():
+        store_blocks(send, first_gradient(factor, middle, fd, pg))
+
+
+def second_gradient(factor, hd, cot_t):
+    nx, ny = hd.shape[1] - 2, hd.shape[2]
+    lane = 2 * C
+
+    def hidden_span(dx, dy, p):
+        return hd[dy, dx:dx + nx, :, lane * p:lane * (p + 2)].reshape(nx * ny, 2 * lane)
+
+    return packed(weight_gradient(
+        cot_t[...],
+        lambda dx, dy: jnp.concatenate([hidden_span(dx, dy, p) for p in range(NZ // 2)], axis=0),
+        factor))
+
+
+def first_gradient(factor, middle, fd, pg):
+    nx, ny, _ = pg.shape
+    cells = nx * ny
+    pairs = NZ // 2
+    lane = 2 * C
+
     def field_span(dx, dy, p):
         span = slice(lane * p, lane * (p + 2))
         if dy == 1:
@@ -309,28 +329,57 @@
 
     grad_t = jnp.concatenate(
         [pg[:, :, lane * p:lane * (p + 1)].reshape(cells, lane).T for p in range(pairs + 1)], axis=1)
-    first = packed(weight_gradient(
+    return packed(weight_gradient(
         grad_t,
         lambda dx, dy: jnp.concatenate([field_span(dx, dy, p) for p in range(pairs + 1)], axis=0),
         factor))
 
-    for index in range(BLOCKS):
-        rows = slice(index * C, (index + 1) * C)
-        keep[rows, :] = jnp.where(gx == 0, first[index], second[index])
-        send[rows, :] = jnp.where(gx == 0, second[index], first[index]).astype(BF16)
-    if keep.shape[0] > BLOCKS * C:
-        rest = (keep.shape[0] - BLOCKS * C, lane)
-        keep[BLOCKS * C:, :] = jnp.zeros(rest, F32)
-        send[BLOCKS * C:, :] = jnp.zeros(rest, BF16)
-
-
-def output_conv(hd, w2b, out):
+
+def store_blocks(target, blocks):
+    for index, block in enumerate(blocks):
+        target[index * C:(index + 1) * C, :] = block.astype(target.dtype)
+    if target.shape[0] > BLOCKS * C:
+        target[BLOCKS * C:, :] = jnp.zeros((target.shape[0] - BLOCKS * C, 2 * C), target.dtype)
+
+
+def keep_sums(factor, hd, pg, fd, middle, cot_t, w2b, keep, out):
+    gx = lax.axis_index("gx")
+
+    @pl.when(gx == 0)
+    def _():
+        store_blocks(keep, first_gradient(factor, middle, fd, pg))
+
+    @pl.when(gx != 0)
+    def _():
+        store_blocks(keep, second_gradient(factor, hd, cot_t))
+
+    conv_pairs(range(0, NZ // 4), hd, w2b, out)
+
+
+def conv_pairs(pairs, hd, w2b, out):
     nx, ny, _ = out.shape
     lane = 2 * C
-    for p in range(NZ // 2):
+    for p in pairs:
         block = jnp.concatenate(
             [hd[dy, dx:dx + nx, :, lane * p:lane * (p + 2)].reshape(nx * ny, 2 * lane) for dx, dy in TAPS], axis=1)
-        out[:, :, lane * p:lane * (p + 1)] = dot(block, w2b[...]).astype(BF16).reshape(nx, ny, lane)
+        here = lane * (p - pairs[0])
+        out[:, :, here:here + lane] = dot(block, w2b[...]).astype(BF16).reshape(nx, ny, lane)
+
+
+def finish_conv(hd, w2b, half, out, rest, sems):
+    done = half.shape[2]
+    step = done // 2
+    copies = [pltpu.make_async_copy(half, out.at[:, :, 0:done], sems.at[0])]
+    copies[0].start()
+    for part in range(2):
+        piece = rest.at[part]
+        first = NZ // 4 + part * NZ // 8
+        conv_pairs(range(first, first + NZ // 8), hd, w2b, piece)
+        start = done + part * step
+        copies.append(pltpu.make_async_copy(piece, out.at[:, :, start:start + step], sems.at[1 + part]))
+        copies[-1].start()
+    for copy in copies:
+        copy.wait()
 
 
 def add_pair(keep, other, out):
@@ -366,14 +415,14 @@
     return pltpu.VMEM(shape, dtype)
 
 
-def call(body, name, inputs, outs, scratch=(), limit=16, flops=0):
+def call(body, name, inputs, outs, scratch=(), limit=16, flops=0, far=False):
     placed = [pltpu.with_memory_space_constraint(x, pltpu.VMEM if held else pltpu.HBM) for x, held in inputs]
     size = sum(x.size * x.dtype.itemsize for x, _ in inputs)
     return pl.pallas_call(
         body,
         out_shape=list(outs),
         in_specs=[pl.BlockSpec(memory_space=pltpu.VMEM if held else pl.ANY) for _, held in inputs],
-        out_specs=[pl.BlockSpec(memory_space=pltpu.VMEM)] * len(outs),
+        out_specs=[pl.BlockSpec(memory_space=pl.ANY if far else pltpu.VMEM)] * len(outs),
         scratch_shapes=list(scratch),
         compiler_params=pltpu.CompilerParams(vmem_limit_bytes=limit * 1024 * 1024),
         cost_estimate=pl.CostEstimate(flops=flops, bytes_accessed=size, transcendentals=0),
@@ -428,12 +477,16 @@
         [near((nx, ny, (pairs + 1 - EARLY) * lane), F32)], flops=3 * 10 ** 9)
     far_rows, grad_late = lax.optimization_barrier((far_rows, grad_late))
 
-    hd, keep, send = call(
+    hd, pg, fd, send = call(
         functools.partial(layers, factor, gx_count, gy_count), "layers",
         [(x, True) for x in (fs, middle, pre_part, grad_early, grad_late, near_rows, far_rows, w1b, wfb, cot_t)],
-        [near((3, nx + 2, ny, width + lane), BF16), near((rows, lane), F32), near((rows, lane), BF16)],
         [
-            pltpu.VMEM((2, nx + 2, ny, wide), BF16),
+            near((3, nx + 2, ny, width + lane), BF16),
+            near((nx, ny, width + lane), BF16),
+            near((2, nx + 2, ny, wide), BF16),
+            near((rows, lane), BF16),
+        ],
+        [
             pltpu.VMEM((nx + 2, ny + 16, width + lane), F32),
             pltpu.VMEM((6, 24, width), F32),
             pltpu.VMEM((2, 32, width), F32),
@@ -441,20 +494,26 @@
             pltpu.VMEM((3, 2, 16, wide), BF16),
             pltpu.VMEM((2, 16, width + lane), F32),
             pltpu.VMEM((4, 16, width + lane), F32),
-            pltpu.VMEM((nx, ny, width + lane), BF16),
         ],
         limit=32, flops=10 ** 10)
 
     other = swap(send)
-    out, = call(
-        output_conv, "output_conv", [(hd, True), (w2b, True)],
-        [near((nx, ny, width), BF16)], flops=2 * 10 ** 9)
-    other, out = lax.optimization_barrier((other, out))
+    keep, half = call(
+        functools.partial(keep_sums, factor), "keep_sums",
+        [(x, True) for x in (hd, pg, fd, middle, cot_t, w2b)],
+        [near((rows, lane), F32), near((nx, ny, width // 2), BF16)], flops=5 * 10 ** 9)
+    other, keep, half = lax.optimization_barrier((other, keep, half))
     both, = call(add_pair, "add_pair", [(keep, True), (other, True)], [near((rows, lane), BF16)])
     terms = lax.all_to_all(both.reshape(ranks, rows // ranks, lane), ("gy", "grp"), 0, 0)
     spread, = call(add_and_repeat, "add_and_repeat", [(terms, True)], [near(terms.shape, BF16)])
     mine = lax.all_to_all(spread, ("gy", "grp"), 0, 0).reshape(rows, lane)
+    mine, hd, w2b, half = lax.optimization_barrier((mine, hd, w2b, half))
     other = swap(mine)
+    out, = call(
+        finish_conv, "finish_conv", [(hd, True), (w2b, True), (half, True)],
+        [pltpu.HBM((nx, ny, width), BF16)],
+        [pltpu.VMEM((2, nx, ny, width // 4), BF16), pltpu.SemaphoreType.DMA((3,))], flops=2 * 10 ** 9, far=True)
+    other, out = lax.optimization_barrier((other, out))
     first, second = call(
         unpack, "unpack", [(mine, True), (other, True)], [jax.ShapeDtypeStruct((27, C, C), F32)] * 2)
     shape = (3, 3, 3, C, C)

time: 49.7 us -> 49.3 us (level)
  Pallas kernels: 12.1 us -> 13.5 us
  waiting for transfers between devices: 0.79 us -> 0.05 us
  local copies, waits for them, and re-layouts: 0.7 us -> 0 us
  blocking collectives: 29.6 us -> 29.1 us
    pallas_call x10 -> x11, Pallas kernels: 12.1 us -> 13.5 us  [call(): pl.pallas_call(body, out_shape=list(outs), in_specs=[pl.BlockSpec(memory_...]
    ppermute x4, waiting for transfers between devices: 0.79 us -> 0.05 us  [swap(): return lax.ppermute(array, 'gx', [(0, 1), (1, 0)])]
    unnamed x1 -> x0, local copies, waits for them, and re-layouts: 0.7 us -> none
  transfers between devices with their start and end apart: 5 -> 5, of which waited for: 1 -> 0; matrix products, arithmetic and copies ran while one was open for 1% -> 0% of each run, Pallas kernels for 13% -> 17%
where the time goes in v8:
time: 49.3 us; the launch traced here: 49.1 us
  blocking collectives  29.1 us (59%)
  Pallas kernels  13.5 us (27%)
  starting transfers between devices  5.71 us (12%)
  between operations  0.74 us (2%)
    all_to_all x1, blocking collectives, shards(): lax.all_to_all(both.reshape(ranks, rows // ranks, lane), ('gy', 'grp'), 0...  17.1 us
    pallas_call x11, Pallas kernels, call(): pl.pallas_call(body, out_shape=list(outs), in_specs=[pl.BlockSpec(memory_...  13.5 us
    all_to_all x1, blocking collectives, shards(): mine = lax.all_to_all(spread, ('gy', 'grp'), 0, 0).reshape(rows, lane)  12 us
    ppermute x4, starting transfers between devices, swap(): return lax.ppermute(array, 'gx', [(0, 1), (1, 0)])  5.04 us
  transfers between devices with their start and end apart: 5, of which 0 were waited for; matrix products, arithmetic and copies ran while one was open for 0% of the time, Pallas kernels for 17%

profile of v8, /device:TPU:0, one launch (start us, length us, event | category | flops | bytes accessed | tf_op | source)
XLA Modules:
  0.0 49.1 jit_solution(10677613377954121698)
XLA Ops:
  0.6 1.2 %pack.1 = (bf16[8,16,1024]{2,1,0:T(8,128)(2,1)S(1)}, bf16[8,16,1024]{2,1,0:T(8,128)(2,1)S(1)}, bf16[3,8,1024]{2,1,0:T(8,128)(2,1)S(1)}, bf16[3,24,1024]{2,1,0:T(8,128)(2,1)S(1)}) custom-call(bf16[8,16,1024]{2,1,0:T(8,128)(2,1)} %bitcast.14, bf16[8,16,1024]{2,1,0:T(8,128)(2,1)} %bitcast.15), custom_call_target="tpu_custom_call" | custom-call | bytes 524288 | tf_op jit(solution)/shard_map/pack/pallas_call | solution.py:421
  1.8 0.5 %collective-permute-start = (bf16[3,24,1024]{2,1,0:T(8,128)(2,1)S(1)}, bf16[3,24,1024]{2,1,0:T(8,128)(2,1)S(1)}, u32[]{:S(2)}, u32[]{:S(2)}) collective-permute-start(bf16[3,24,1024]{2,1,0:T(8,128)(2,1)S(1)} %get-tuple-element.45), channel_id=1, source_target_pairs={{0,16},{16,0},{1,17},{17,1},{2,18},{18,2},{3,19},{19,3},{4,20},{20... | collective-permute-start | bytes 442376 | tf_op jit(solution)/shard_map/ppermute | solution.py:21
  2.3 1.2 %load_weights.1 = (bf16[27,64,64]{2,1,0:T(8,128)(2,1)S(1)}, bf16[27,64,64]{2,1,0:T(8,128)(2,1)S(1)}) custom-call(bf16[27,64,64]{2,1,0:T(8,128)(2,1)} %bitcast.12, bf16[27,64,64]{2,1,0:T(8,128)(2,1)} %bitcast.13), custom_call_target="tpu_custom_call" | custom-call | bytes 442368 | tf_op jit(solution)/shard_map/load_weights/pallas_call | solution.py:421
  3.5 0.0 collective-permute-done.side.taken
  3.5 0.7 %collective-permute-start.1 = (bf16[3,16,1024]{2,1,0:T(8,128)(2,1)S(1)}, bf16[3,16,1024]{2,1,0:T(8,128)(2,1)S(1)}, u32[]{:S(2)}, u32[]{:S(2)}) collective-permute-start(bf16[3,16,1024]{2,1,0:T(8,128)(2,1)S(1)} %join_edges.1), channel_id=1, source_target_pairs={{16,4},{20,8},{24,12},{4,16},{8,20},{12,24},{17,5},{21,9},{25,13},... | collective-permute-start | bytes 294920 | tf_op jit(solution)/shard_map/ppermute | solution.py:456
  4.2 2.8 %interior_first.1 = (f32[12,32,1024]{2,1,0:T(8,128)S(1)}, bf16[12,16,1280]{2,1,0:T(8,128)(2,1)S(1)}, f32[10,16,1152]{2,1,0:T(8,128)S(1)}, bf16[3,10,16,1280]{3,2...) custom-call(bf16[8,16,1024]{2,1,0:T(8,128)(2,1)S(1)} %get-tuple-elem, ...), custom_call_target="tpu_custom_call" | custom-call | flops 4000000000 | bytes 1114112 | tf_op jit(solution)/shard_map/interior_first/pallas_call | solution.py:421
  7.0 0.0 collective-permute-done.1.near_rows
  7.0 4.1 %collective-permute-start.2 = (bf16[3,16,1024]{2,1,0:T(8,128)(2,1)S(1)}, bf16[3,16,1024]{2,1,0:T(8,128)(2,1)S(1)}, u32[]{:S(2)}, u32[]{:S(2)}) collective-permute-start(bf16[3,16,1024]{2,1,0:T(8,128)(2,1)S(1)} %collective-permute-done.1.near_rows), channel_id=1, source_target_pairs={{0,16},{16,0},{1,17},{17,1},{2,18},{18,2},{3,19},{19,3},{4,20},{20... | collective-permute-start | bytes 294920 | tf_op jit(solution)/shard_map/ppermute | solution.py:21
  11.1 1.1 %interior_grad.1.grad_late = f32[8,16,768]{2,1,0:T(8,128)S(1)} custom-call(bf16[3,10,16,1280]{3,2,1,0:T(8,128)(2,1)S(1)} %get-tuple-element.59.cd, bf16[128,2304]{1,0:T(8,128)(2,1)S(1)} %get-tuple-element.60.wfb), custom_call_target="tpu_custom_call" | custom-call | flops 3000000000 | bytes 1818624 | tf_op jit(solution)/shard_map/interior_grad/pallas_call | solution.py:421
  12.2 0.0 collective-permute-done.2.far_rows
  12.2 2.5 %layers.1 = (bf16[3,10,16,1152]{3,2,1,0:T(8,128)(2,1)S(1)}, bf16[8,16,1152]{2,1,0:T(8,128)(2,1)S(1)}, bf16[2,10,16,1280]{3,2,1,0:T(8,128)(2,1)S(1)}, bf16[896,128]{1,0:T(8,128)(2,1)S(1)}) custom-call(f32[12,32,1024]{2,1,0:T(8,128)S(1)} %get-tuple-element.51.fs, bf16[12,16,1280]{2,1,0:T(8,128)(2,1)S(1)} %get-tuple-element.52.middle, ...), custom_call_target="tpu_custom_call" | custom-call | flops 10000000000 | bytes 5029888 | tf_op jit(solution)/shard_map/layers/pallas_call | solution.py:421
  14.7 0.4 collective-permute-start.3
  15.1 1.9 %keep_sums.1 = (f32[896,128]{1,0:T(8,128)S(1)}, bf16[8,16,512]{2,1,0:T(8,128)(2,1)S(1)}) custom-call(bf16[3,10,16,1152]{3,2,1,0:T(8,128)(2,1)S(1)} %get-tuple-element.76.hd, bf16[8,16,1152]{2,1,0:T(8,128)(2,1)S(1)} %get-tuple-element.67.pg, bf16[2,10,16,1280]{3,2,1,0:T(8,128)(2,1)S(1)} %get-tuple-element.68.fd, ...), custom_call_target="tpu_custom_call" | custom-call | flops 5000000000 | bytes 3563520 | tf_op jit(solution)/shard_map/keep_sums/pallas_call | solution.py:421
  17.0 0.0 collective-permute-done.3.other
  17.1 17.1 %all_to_all.10.terms = bf16[16,56,128]{2,1,0:T(8,128)(2,1)S(1)} all-to-all(bf16[16,56,128]{2,1,0:T(8,128)(2,1)S(1)} %bitcast.9), channel_id=1, replica_groups=mesh['gx'=2,'gy'=4,'grp'=4] {'gy','grp'}, dimensions={0} | all-to-all | bytes 458752 | tf_op jit(solution)/shard_map/all_to_all | solution.py:507
  34.2 12.0 %all_to_all.11 = bf16[16,56,128]{2,1,0:T(8,128)(2,1)S(1)} all-to-all(bf16[16,56,128]{2,1,0:T(8,128)(2,1)S(1)} %add_and_repeat.1), channel_id=1, replica_groups=mesh['gx'=2,'gy'=4,'grp'=4] {'gy','grp'}, dimensions={0} | all-to-all | bytes 458752 | tf_op jit(solution)/shard_map/all_to_all | solution.py:509
  46.2 0.0 collective-permute-start.4
  46.2 1.4 %finish_conv.1 = bf16[8,16,1024]{2,1,0:T(8,128)(2,1)} custom-call(bf16[3,10,16,1152]{3,2,1,0:T(8,128)(2,1)S(1)} %get-tuple-element.76.hd, bf16[2304,128]{1,0:T(8,128)(2,1)S(1)} %get-tuple-element.77.w2b, bf16[8,16,512]{2,1,0:T(8,128)(2,1)S(1)} %get-tuple-element.78.half), custom_call_target="tpu_custom_call" | custom-call | flops 2000000000 | bytes 1826816 | tf_op jit(solution)/shard_map/finish_conv/pallas_call | solution.py:421
  47.6 0.0 collective-permute-done.4.other
  47.7 1.4 %unpack.1 = (f32[27,64,64]{2,1,0:T(8,128)}, f32[27,64,64]{2,1,0:T(8,128)}) custom-call(bf16[896,128]{1,0:T(8,128)(2,1)S(1)} %bitcast.11, bf16[896,128]{1,0:T(8,128)(2,1)S(1)} %collective-permute-done.4.other), custom_call_target="tpu_custom_call" | custom-call | bytes 458752 | tf_op jit(solution)/shard_map/unpack/pallas_call | solution.py:421
  (3 shorter events, 0.1 us)
Async XLA Ops:
  1.8 1.7 %collective-permute-start = (bf16[3,24,1024]{2,1,0:T(8,128)(2,1)S(1)}, bf16[3,24,1024]{2,1,0:T(8,128)(2,1)S(1)}, u32[]{:S(2)}, u32[]{:S(2)}) collective-permute-start(bf16[3,24,1024]{2,1,0:T(8,128)(2,1)S(1)} %get-tuple-element.45), channel_id=1, source_target_pairs={{0,16},{16,0},{1,17},{17,1},{2,18},{18,2},{3,19},{19,3},{4,20},{20... | collective-permute-start | bytes 442376 | tf_op jit(solution)/shard_map/ppermute | solution.py:21
  3.5 3.5 %collective-permute-start.1 = (bf16[3,16,1024]{2,1,0:T(8,128)(2,1)S(1)}, bf16[3,16,1024]{2,1,0:T(8,128)(2,1)S(1)}, u32[]{:S(2)}, u32[]{:S(2)}) collective-permute-start(bf16[3,16,1024]{2,1,0:T(8,128)(2,1)S(1)} %join_edges.1), channel_id=1, source_target_pairs={{16,4},{20,8},{24,12},{4,16},{8,20},{12,24},{17,5},{21,9},{25,13},... | collective-permute-start | bytes 294920 | tf_op jit(solution)/shard_map/ppermute | solution.py:456
  7.0 5.2 %collective-permute-start.2 = (bf16[3,16,1024]{2,1,0:T(8,128)(2,1)S(1)}, bf16[3,16,1024]{2,1,0:T(8,128)(2,1)S(1)}, u32[]{:S(2)}, u32[]{:S(2)}) collective-permute-start(bf16[3,16,1024]{2,1,0:T(8,128)(2,1)S(1)} %collective-permute-done.1.near_rows), channel_id=1, source_target_pairs={{0,16},{16,0},{1,17},{17,1},{2,18},{18,2},{3,19},{19,3},{4,20},{20... | collective-permute-start | bytes 294920 | tf_op jit(solution)/shard_map/ppermute | solution.py:21
  14.7 2.3 %collective-permute-start.3 = (bf16[896,128]{1,0:T(8,128)(2,1)S(1)}, bf16[896,128]{1,0:T(8,128)(2,1)S(1)}, u32[]{:S(2)}, u32[]{:S(2)}) collective-permute-start(bf16[896,128]{1,0:T(8,128)(2,1)S(1)} %get-tuple-element.65), channel_id=1, source_target_pairs={{0,16},{16,0},{1,17},{17,1},{2,18},{18,2},{3,19},{19,3},{4,20},{20... | collective-permute-start | bytes 688136 | tf_op jit(solution)/shard_map/ppermute | solution.py:21
  46.2 1.5 %collective-permute-start.4 = (bf16[896,128]{1,0:T(8,128)(2,1)S(1)}, bf16[896,128]{1,0:T(8,128)(2,1)S(1)}, u32[]{:S(2)}, u32[]{:S(2)}) collective-permute-start(bf16[896,128]{1,0:T(8,128)(2,1)S(1)} %bitcast.10), channel_id=1, source_target_pairs={{0,16},{16,0},{1,17},{17,1},{2,18},{18,2},{3,19},{19,3},{4,20},{20... | collective-permute-start | bytes 688136 | tf_op jit(solution)/shard_map/ppermute | solution.py:21

commit v9 on v0

v9 whole, which is shorter than its diff:
```python
import functools
import math

import jax
import jax.numpy as jnp
from jax import lax
from jax.experimental import pallas as pl
from jax.experimental.pallas import tpu as pltpu
from jax.sharding import PartitionSpec as P

C = 64
NZ = 16
BF16 = jnp.bfloat16
F32 = jnp.float32
TAPS = [(dx, dy) for dy in range(3) for dx in range(3)]
BLOCKS = 14


def swap(array):
    return lax.ppermute(array, "gx", [(0, 1), (1, 0)])


def dot(a, b):
    return jnp.dot(a, b, preferred_element_type=F32)


def dot_nt(a, b):
    return lax.dot_general(a, b, (((1,), (1,)), ((), ())), preferred_element_type=F32)


def band(taps):
    zero = jnp.zeros((C, C), BF16)
    left = jnp.concatenate(list(taps) + [zero], axis=0)
    right = jnp.concatenate([zero] + list(taps), axis=0)
    return jnp.concatenate([left, right], axis=1)


def band_flipped(taps):
    zero = jnp.zeros((C, C), BF16)
    back = list(taps)[::-1]
    upper = jnp.concatenate(back + [zero], axis=1)
    lower = jnp.concatenate([zero] + back, axis=1)
    return jnp.concatenate([upper, lower], axis=0)


def packed(pieces):
    blocks = [piece[:, 0:2 * C] for piece in pieces]
    for pair in range(0, 9, 2):
        second = pieces[pair + 1][:, 2 * C:3 * C] if pair + 1 < 9 else jnp.zeros((C, C), F32)
        blocks.append(jnp.concatenate([pieces[pair][:, 2 * C:3 * C], second], axis=1))
    return blocks


def pack_edges(field_hbm, cot_hbm, field, cot, edge, given, rows, sems):
    copies = [
        pltpu.make_async_copy(source, target, sems.at[index])
        for index, (source, target) in enumerate(((field_hbm, field), (cot_hbm, cot)))
    ]
    for copy in copies:
        copy.start()
    for copy in copies:
        copy.wait()
    nx, ny, _ = field.shape
    gx = lax.axis_index("gx")
    for x in range(nx):
        fields = field[x].astype(F32)
        cots = cot[x].astype(F32)
        for index, row in enumerate((fields[0:1], fields[1:2], cots[0:1], fields[ny - 2:ny - 1], fields[ny - 1:ny], cots[ny - 1:ny])):
            rows[index, x:x + 1, :] = row
    head = rows[0:3].astype(BF16)
    tail = rows[3:6].astype(BF16)
    edge[...] = jnp.where(gx == 0, head, tail)
    given[...] = jnp.where(gx == 0, tail, head)


def join_edges(edge, taken, whole):
    nx = edge.shape[1]
    gx = lax.axis_index("gx")

    @pl.when(gx == 0)
    def _():
        whole[:, 0:nx] = edge[...]
        whole[:, nx:2 * nx] = taken[...]

    @pl.when(gx != 0)
    def _():
        whole[:, 0:nx] = taken[...]
        whole[:, nx:2 * nx] = edge[...]


def put_rows(scratch, start, rows):
    lane = 2 * C
    for tile in range(scratch.shape[0]):
        scratch[tile, start:start + rows.shape[0], :] = rows[:, lane * tile:lane * (tile + 1)]


def take_rows(scratch, start, count, stride):
    return jnp.concatenate(
        [scratch[tile, pl.ds(start, count, stride=stride), :] for tile in range(scratch.shape[0])], axis=1).astype(BF16)


def turn_rows(source, scratch):
    nx, ny, _ = source.shape
    for x in range(nx):
        put_rows(scratch, x * ny, source[x].astype(F32))
    return [take_rows(scratch, y, nx, ny) for y in range(ny)]


def pack_halves(field, cot, w1_hbm, w2_hbm, own, bulk, w1, w2, turned_f, turned_c, scratch, sems):
    copies = [
        pltpu.make_async_copy(source, target, sems.at[index])
        for index, (source, target) in enumerate(((w1_hbm, w1), (w2_hbm, w2)))
    ]
    for copy in copies:
        copy.start()
    ny = field.shape[1]
    half = ny // 2
    for source, target in ((field, turned_f), (cot, turned_c)):
        for y, rows in enumerate(turn_rows(source, scratch)):
            target[y] = rows
    low_f, high_f = turned_f.at[0:half + 2], turned_f.at[half - 2:ny]
    low_c, high_c = turned_c.at[0:half + 1], turned_c.at[half - 1:ny]
    gx = lax.axis_index("gx")

    def place(mine_f, mine_c, given_f, given_c):
        own[0:half + 2] = mine_f[...]
        own[half + 2:] = mine_c[...]
        bulk[0:half + 2] = given_f[...]
        bulk[half + 2:] = given_c[...]

    @pl.when(gx == 0)
    def _():
        place(low_f, low_c, high_f, high_c)

    @pl.when(gx != 0)
    def _():
        place(high_f, high_c, low_f, low_c)

    for copy in copies:
        copy.wait()


def make_bands(w1, w2, w1b, w2b, wfb):
    for t, (dx, dy) in enumerate(TAPS):
        rows = slice(t * 4 * C, (t + 1) * 4 * C)
        first = 9 * dx + 3 * dy
        w1b[rows, :] = band([w1[first + z] for z in range(3)])
        w2b[rows, :] = band([w2[first + z] for z in range(3)])
        wfb[:, rows] = band_flipped([w2[24 - first + z] for z in range(3)])


def blank_edges(copies):
    lane = 2 * C
    zero = jnp.zeros(copies.shape[:-1] + (lane,), BF16)
    copies[..., 0:lane] = zero
    copies[..., copies.shape[-1] - lane:] = zero


def blank_rows(scratch):
    zero = jnp.zeros((scratch.shape[0], 1, scratch.shape[2]), F32)
    scratch[:, 7:8, :] = zero
    scratch[:, scratch.shape[1] - 8:scratch.shape[1] - 7, :] = zero


def shift_rows(scratch, copies, start, first_lane):
    count, rows, width = scratch.shape
    for dx in range(3):
        copies[dx, pl.ds(start, count), :, first_lane:first_lane + width] = scratch[:, 7 + dx:rows - 9 + dx, :].astype(BF16)


def inside_lanes(p):
    lane_of = lax.broadcasted_iota(jnp.int32, (1, 2 * C), 1)
    if p == 0:
        return (lane_of >= C).astype(F32)
    if p == NZ // 2:
        return (lane_of < C).astype(F32)
    return 1.0


def windows(copies, first, count, p):
    lane = 2 * C
    rows = copies.shape[2]
    return jnp.concatenate(
        [
            copies[dx, pl.ds(first + dy, count), :, lane * p:lane * (p + 2)].reshape(count * rows, 2 * lane)
            for dx, dy in TAPS
        ],
        axis=1,
    )


def pre_gradient(grad, pre, p):
    sigma = jax.nn.sigmoid(pre)
    return grad * sigma * (1.0 + pre * (1.0 - sigma)) * inside_lanes(p)


def interior(own, got, w1, w2, fd, cd, hd, pg, acc1, acc2, w1b, w2b, wfb, fs, cs, hs, pre):
    gx = lax.axis_index("gx")
    nx = own.shape[1]
    across = 2 * nx
    count = pg.shape[0]
    cells = count * across
    lane = 2 * C
    pairs = NZ // 2
    make_bands(w1, w2, w1b, w2b, wfb)

    def place(left, right):
        for scratch, start, size in ((fs, 0, count + 2), (cs, count + 2, count + 1)):
            scratch[:, 8:8 + nx, :] = left[start:start + size].astype(F32)
            scratch[:, 8 + nx:8 + across, :] = right[start:start + size].astype(F32)

    @pl.when(gx == 0)
    def _():
        place(own, got)

    @pl.when(gx != 0)
    def _():
        place(got, own)

    for scratch in (fs, cs, hs):
        blank_rows(scratch)
    blank_edges(fd)
    blank_edges(cd)
    shift_rows(fs, fd, 2 - 2 * gx, lane)
    shift_rows(cs, cd, 1 - gx, lane)
    for p in range(pairs + 1):
        here = slice(lane * p, lane * (p + 1))
        value = dot(windows(fd, 2 - 2 * gx, count, p), w1b[...])
        pre[:, :, here] = value.reshape(count, across, lane)
        hidden = value * jax.nn.sigmoid(value) * inside_lanes(p)
        hs[:, 8:8 + across, here] = hidden.reshape(count, across, lane)
    hd[:, pl.ds(8 * gx, 2)] = jnp.zeros((3, 2) + hd.shape[2:], BF16)
    shift_rows(hs, hd, 2 - 2 * gx, 0)
    for p in range(pairs + 1):
        here = slice(lane * p, lane * (p + 1))
        grad = dot_nt(windows(cd, 1 - gx, count - 1, p), wfb[...])
        grad = pre_gradient(grad, pre[pl.ds(gx, count - 1), :, here].reshape((count - 1) * across, lane), p)
        pg[pl.ds(1 - gx, count - 1), :, here] = grad.astype(BF16).reshape(count - 1, across, lane)
    pg[pl.ds((count - 1) * gx, 1)] = jnp.zeros((1,) + pg.shape[1:], BF16)

    cot_t = jnp.concatenate(
        [cd[1, 1:1 + count, :, lane * (p + 1):lane * (p + 2)].reshape(cells, lane).T for p in range(pairs)], axis=1)
    grad_t = jnp.concatenate(
        [pg[:, :, lane * p:lane * (p + 1)].reshape(cells, lane).T for p in range(pairs + 1)], axis=1)
    for t, (dx, dy) in enumerate(TAPS):
        acc2[t] = dot(cot_t, jnp.concatenate(
            [hd[dx, dy:dy + count, :, lane * p:lane * (p + 2)].reshape(cells, 2 * lane) for p in range(pairs)], axis=0))
        acc1[t] = dot(grad_t, jnp.concatenate(
            [fd[dx, 1 + dy:1 + dy + count, :, lane * p:lane * (p + 2)].reshape(cells, 2 * lane) for p in range(pairs + 1)], axis=0))


def folded(total, factor):
    total = total * factor
    return total[0:C, 0:3 * C] + total[C:2 * C, C:4 * C]


def second_sums(factor, side, hd, cd, acc2):
    lane = 2 * C
    pairs = NZ // 2
    last = hd.shape[1] - 3
    late = ((0, 1), (0,), ()) if side == 0 else ((), (last,), (last - 1, last))
    pieces = []
    for t, (dx, dy) in enumerate(TAPS):
        total = acc2[t]
        if late[dy]:
            cots = jnp.concatenate(
                [cd[1, 1 + y, :, lane * (p + 1):lane * (p + 2)] for y in late[dy] for p in range(pairs)], axis=0)
            rows = jnp.concatenate(
                [hd[dx, y + dy, :, lane * p:lane * (p + 2)] for y in late[dy] for p in range(pairs)], axis=0)
            total = total + dot(cots.T, rows)
        pieces.append(folded(total, factor))
    return packed(pieces)


def first_sums(factor, side, fd, pg, acc1):
    lane = 2 * C
    pairs = NZ // 2
    count, across, _ = pg.shape
    y = 0 if side == 0 else count - 1
    extra = 2 * lane - (pairs + 1) * across
    grad_t = jnp.concatenate(
        [pg[y, :, lane * p:lane * (p + 1)] for p in range(pairs + 1)] + [jnp.zeros((extra, lane), BF16)], axis=0).T
    pad = jnp.zeros((extra, 2 * lane), BF16)
    return packed([
        folded(acc1[t] + dot(grad_t, jnp.concatenate(
            [fd[dx, y + dy + 1, :, lane * p:lane * (p + 2)] for p in range(pairs + 1)] + [pad], axis=0)), factor)
        for t, (dx, dy) in enumerate(TAPS)
    ])


def store_blocks(target, blocks):
    for index, block in enumerate(blocks):
        target[index * C:(index + 1) * C, :] = block.astype(target.dtype)
    if target.shape[0] > BLOCKS * C:
        target[BLOCKS * C:, :] = jnp.zeros((target.shape[0] - BLOCKS * C, 2 * C), target.dtype)


def late_rows(factor, gy_count, fd_in, cd_in, hd_in, pg_in, rows, acc1, acc2, w1b, wfb, fd, cd, hd, pg, send, rs, hs):
    gx = lax.axis_index("gx")
    gy = lax.axis_index("gy")
    count, across, _ = pg.shape
    lane = 2 * C
    pairs = NZ // 2
    rs[:, 8:8 + across, :] = rows[...].astype(F32)
    blank_rows(rs)
    blank_rows(hs)
    shift_rows(rs.at[0:2], fd, (count + 2) * gx, lane)
    shift_rows(rs.at[2:3], cd, (count + 1) * gx, lane)
    value = dot(jnp.concatenate([windows(fd, count * gx, 2, p) for p in range(pairs + 1)], axis=0), w1b[...])
    grad = dot_nt(jnp.concatenate([windows(cd, (count - 1) * gx, 1, p) for p in range(pairs + 1)], axis=0), wfb[...])
    before = jnp.where((gx == 0) & (gy == 0), 0.0, 1.0)
    beyond = jnp.where((gx != 0) & (gy == gy_count - 1), 0.0, 1.0)
    for p in range(pairs + 1):
        here = slice(lane * p, lane * (p + 1))
        early = value[2 * across * p:2 * across * p + across]
        later = value[2 * across * p + across:2 * across * (p + 1)]
        hs[0, 8:8 + across, here] = early * jax.nn.sigmoid(early) * inside_lanes(p) * before
        hs[1, 8:8 + across, here] = later * jax.nn.sigmoid(later) * inside_lanes(p) * beyond
        mine = pre_gradient(grad[across * p:across * (p + 1)], jnp.where(gx == 0, later, early), p)
        pg[pl.ds((count - 1) * gx, 1), :, here] = mine.astype(BF16)[None]
    shift_rows(hs, hd, count * gx, 0)

    @pl.when(gx == 0)
    def _():
        store_blocks(send, second_sums(factor, 0, hd, cd, acc2))

    @pl.when(gx != 0)
    def _():
        store_blocks(send, first_sums(factor, 1, fd, pg, acc1))


def keep_sums(factor, fd, cd, hd, pg, acc1, acc2, w2b, keep, mine, given):
    gx = lax.axis_index("gx")
    count, across, _ = pg.shape
    lane = 2 * C
    half = across // 2

    @pl.when(gx == 0)
    def _():
        store_blocks(keep, first_sums(factor, 0, fd, pg, acc1))

    @pl.when(gx != 0)
    def _():
        store_blocks(keep, second_sums(factor, 1, hd, cd, acc2))

    for p in range(NZ // 2):
        here = slice(lane * p, lane * (p + 1))
        value = dot(windows(hd, 0, count, p), w2b[...]).reshape(count, across, lane)
        left, right = value[:, 0:half], value[:, half:across]
        mine[:, :, here] = jnp.where(gx == 0, left, right).astype(BF16)
        given[:, :, here] = jnp.where(gx == 0, right, left).astype(BF16)


def finish_output(mine, other, out, turned, scratch, sems):
    count, nx, width = mine.shape
    gx = lax.axis_index("gx")
    for y in range(count):
        a = mine[y].astype(F32)
        b = other[y].astype(F32)
        put_rows(scratch, y * nx, jnp.where(gx == 0, a, b))
        put_rows(scratch, (count + y) * nx, jnp.where(gx == 0, b, a))
    copies = []
    for x in range(nx):
        turned[x] = take_rows(scratch, x, 2 * count, nx)
        if x % 2:
            copies.append(pltpu.make_async_copy(turned.at[x - 1:x + 1], out.at[x - 1:x + 1], sems.at[x // 2]))
            copies[-1].start()
    for copy in copies:
        copy.wait()


def add_pair(keep, other, out):
    out[...] = (keep[...] + other[...].astype(F32)).astype(BF16)


def add_and_repeat(terms, out):
    total = terms[0].astype(F32)
    for index in range(1, terms.shape[0]):
        total = total + terms[index].astype(F32)
    total = total.astype(BF16)
    for index in range(out.shape[0]):
        out[index] = total


def unpack(mine, other, first, second):
    gx = lax.axis_index("gx")
    a = mine[...].astype(F32)
    b = other[...].astype(F32)
    for out, rows in ((first, jnp.where(gx == 0, a, b)), (second, jnp.where(gx == 0, b, a))):
        for t, (dx, dy) in enumerate(TAPS):
            turned = rows[t * C:(t + 1) * C].T
            out[9 * dx + 3 * dy] = turned[0:C]
            out[9 * dx + 3 * dy + 1] = turned[C:2 * C]
        for pair in range(5):
            turned = rows[(9 + pair) * C:(10 + pair) * C].T
            for half in range(2 if pair < 4 else 1):
                dx, dy = TAPS[2 * pair + half]
                out[9 * dx + 3 * dy + 2] = turned[half * C:(half + 1) * C]


def near(shape, dtype):
    return pltpu.VMEM(shape, dtype)


def call(body, name, inputs, outs, scratch=(), limit=16, flops=0, far=False, aliases=None):
    placed = [pltpu.with_memory_space_constraint(x, pltpu.VMEM if held else pltpu.HBM) for x, held in inputs]
    size = sum(x.size * x.dtype.itemsize for x, _ in inputs)
    return pl.pallas_call(
        body,
        out_shape=list(outs),
        in_specs=[pl.BlockSpec(memory_space=pltpu.VMEM if held else pl.ANY) for _, held in inputs],
        out_specs=[pl.BlockSpec(memory_space=pl.ANY if far else pltpu.VMEM)] * len(outs),
        scratch_shapes=list(scratch),
        input_output_aliases=aliases or {},
        compiler_params=pltpu.CompilerParams(vmem_limit_bytes=limit * 1024 * 1024),
        cost_estimate=pl.CostEstimate(flops=flops, bytes_accessed=size, transcendentals=0),
        name=name,
    )(*placed)


def shards(field_in, first_weight, second_weight, cotangent):
    nx, ny, width = field_in.shape[1:]
    gx_count, gy_count, grp_count = (lax.axis_size(axis) for axis in ("gx", "gy", "grp"))
    total = field_in.shape[0] * nx * ny * NZ * gx_count * gy_count * grp_count
    factor = 1.0 / math.sqrt(total)
    ranks = gy_count * grp_count
    rows = -(-BLOCKS * C // (8 * ranks)) * 8 * ranks
    lane = 2 * C
    wide = width + 2 * lane
    count = ny // 2
    across = 2 * nx
    size = 2 * count + 3

    field, cot, edge, given = call(
        pack_edges, "pack_edges", [(field_in[0], False), (cotangent[0], False)],
        [near((nx, ny, width), BF16), near((nx, ny, width), BF16), near((3, nx, width), BF16), near((3, nx, width), BF16)],
        [pltpu.VMEM((6, nx, width), F32), pltpu.SemaphoreType.DMA((2,))])
    taken = swap(given)
    own, bulk, w1, w2 = call(
        pack_halves, "pack_halves",
        [(field, True), (cot, True), (first_weight.reshape(27, C, C), False), (second_weight.reshape(27, C, C), False)],
        [near((size, nx, width), BF16), near((size, nx, width), BF16), near((27, C, C), BF16), near((27, C, C), BF16)],
        [
            pltpu.VMEM((ny, nx, width), BF16),
            pltpu.VMEM((ny, nx, width), BF16),
            pltpu.VMEM((width // lane, nx * ny, lane), F32),
            pltpu.SemaphoreType.DMA((2,)),
        ])
    bulk, taken, w1, w2 = lax.optimization_barrier((bulk, taken, w1, w2))
    got = swap(bulk)
    whole, = call(join_edges, "join_edges", [(edge, True), (taken, True)], [near((3, across, width), BF16)])
    ends = [(gy_count + j, j + 1) for j in range(gy_count - 1)]
    late = lax.ppermute(whole, ("gx", "gy"), ends + [(b, a) for a, b in ends])
    held = [
        near((3, count + 4, across, wide), BF16),
        near((3, count + 2, across, wide), BF16),
        near((3, count + 2, across, width + lane), BF16),
        near((count, across, width + lane), BF16),
    ]
    fd, cd, hd, pg, acc1, acc2, w1b, w2b, wfb = call(
        interior, "interior",
        [(x, True) for x in (own, got, w1, w2)],
        held + [
            near((9, lane, 2 * lane), F32),
            near((9, lane, 2 * lane), F32),
            near((9 * 4 * C, lane), BF16),
            near((9 * 4 * C, lane), BF16),
            near((lane, 9 * 4 * C), BF16),
        ],
        [
            pltpu.VMEM((count + 2, across + 16, width), F32),
            pltpu.VMEM((count + 1, across + 16, width), F32),
            pltpu.VMEM((count, across + 16, width + lane), F32),
            pltpu.VMEM((count, across, width + lane), F32),
        ],
        limit=32, flops=4 * 10 ** 9)
    fd, cd, hd, pg, send = call(
        functools.partial(late_rows, factor, gy_count), "late_rows",
        [(x, True) for x in (fd, cd, hd, pg, late, acc1, acc2, w1b, wfb)],
        held + [near((rows, lane), BF16)],
        [pltpu.VMEM((3, across + 16, width), F32), pltpu.VMEM((2, across + 16, width + lane), F32)],
        limit=32, flops=10 ** 9, aliases={0: 0, 1: 1, 2: 2, 3: 3})

    other = swap(send)
    keep, mine, given = call(
        functools.partial(keep_sums, factor), "keep_sums",
        [(x, True) for x in (fd, cd, hd, pg, acc1, acc2, w2b)],
        [near((rows, lane), F32), near((count, nx, width), BF16), near((count, nx, width), BF16)], flops=4 * 10 ** 9)
    other, keep = lax.optimization_barrier((other, keep))
    both, = call(add_pair, "add_pair", [(keep, True), (other, True)], [near((rows, lane), BF16)])
    given_out = swap(given)
    terms = lax.all_to_all(both.reshape(ranks, rows // ranks, lane), ("gy", "grp"), 0, 0)
    spread, = call(add_and_repeat, "add_and_repeat", [(terms, True)], [near(terms.shape, BF16)])
    sums = lax.all_to_all(spread, ("gy", "grp"), 0, 0).reshape(rows, lane)
    sums, mine, given_out = lax.optimization_barrier((sums, mine, given_out))
    other = swap(sums)
    out, = call(
        finish_output, "finish_output", [(mine, True), (given_out, True)],
        [pltpu.HBM((nx, ny, width), BF16)],
        [pltpu.VMEM((nx, ny, width), BF16), pltpu.VMEM((width // lane, nx * ny, lane), F32), pltpu.SemaphoreType.DMA((nx // 2,))], far=True)
    other, out = lax.optimization_barrier((other, out))
    first, second = call(
        unpack, "unpack", [(sums, True), (other, True)], [jax.ShapeDtypeStruct((27, C, C), F32)] * 2)
    shape = (3, 3, 3, C, C)
    return out[None], first.reshape(shape), second.reshape(shape)


def solution(mesh):
    return jax.shard_map(
        shards,
        mesh=mesh,
        in_specs=(P("grp", "gx", "gy", None), P(), P(), P("grp", "gx", "gy", None)),
        out_specs=(P("grp", "gx", "gy", None), P(), P()),
        check_vma=False,
    )
```

time: 271 us -> 49.8 us (0.18); the launches traced: 267 us -> 49.5 us
  waiting for transfers between devices: 128 us -> 10.2 us
  matrix products: 49.5 us -> 0 us
  local copies, waits for them, and re-layouts: 39.1 us -> 0 us
  starting transfers between devices: 31.7 us -> 8.46 us
  blocking collectives: 0 us -> 15.7 us
  Pallas kernels: 0 us -> 14.4 us
  between operations: 14.8 us -> 0.73 us
  other arithmetic: 4.27 us -> 0 us
    psum x1 -> x0, waiting for transfers between devices: 128 us -> none  [reduce_grad(): return lax.psum(local, ('gx', 'gy', 'grp'))]
    transpose x2 -> x0, matrix products: 41.1 us -> none  [kernel_local(): return jnp.transpose(result, (1, 2, 3, 0, 4))]
    ppermute x12 -> x6, starting transfers between devices: 31.6 us -> 4.93 us  [the longest x5 4.27 us: swap(): return lax.ppermute(array, 'gx', [(0, 1), (1, 0)])]
    reshape x15 -> x0, local copies, waits for them, and re-layouts: 18.9 us -> none  [the longest x13 16.8 us: as_cells(): return field.reshape(field.shape[0], field.shape[1], field.shape[2], NZ, C)]
    all_to_all x0 -> x1, blocking collectives: none -> 15.7 us  [shards(): lax.all_to_all(both.reshape(ranks, rows // ranks, lane), ('gy', 'grp'), 0...]
    pallas_call x0 -> x10, Pallas kernels: none -> 14.4 us  [call(): pl.pallas_call(body, out_shape=list(outs), in_specs=[pl.BlockSpec(memory_...]
    unnamed x50 -> x0, local copies, waits for them, and re-layouts: 9.48 us -> none
    conv_general_dilated x2 -> x0, matrix products: 8.46 us -> none  [conv_local(): lax.conv_general_dilated(padded, weight, (1, 1, 1), ((0, 0), (0, 0), (1,...]
  transfers between devices with their start and end apart: 13 -> 7, of which waited for: 1 -> 4; matrix products, arithmetic and copies ran while one was open for 24% -> 0% of each run, Pallas kernels for 0% -> 20%
where the time goes in v9:
time: 49.8 us; the launch traced here: 49.5 us
  blocking collectives  15.7 us (32%)
  Pallas kernels  14.4 us (29%)
  waiting for transfers between devices  10.2 us (20%)
  starting transfers between devices  8.46 us (17%)
  between operations  0.73 us (1%)
    all_to_all x1, blocking collectives, shards(): lax.all_to_all(both.reshape(ranks, rows // ranks, lane), ('gy', 'grp'), 0...  15.7 us
    pallas_call x10, Pallas kernels, call(): pl.pallas_call(body, out_shape=list(outs), in_specs=[pl.BlockSpec(memory_...  14.4 us
    all_to_all x1, waiting for transfers between devices, shards(): sums = lax.all_to_all(spread, ('gy', 'grp'), 0, 0).reshape(rows, lane)  7.38 us
    ppermute x5, starting transfers between devices, swap(): return lax.ppermute(array, 'gx', [(0, 1), (1, 0)])  4.27 us
    all_to_all x1, starting transfers between devices, shards(): sums = lax.all_to_all(spread, ('gy', 'grp'), 0, 0).reshape(rows, lane)  3.53 us
    ppermute x5, waiting for transfers between devices, swap(): return lax.ppermute(array, 'gx', [(0, 1), (1, 0)])  2.86 us
  transfers between devices with their start and end apart: 7, of which 4 were waited for; matrix products, arithmetic and copies ran while one was open for 0% of the time, Pallas kernels for 20%

profile of v9, /device:TPU:0, one launch (start us, length us, event | category | flops | bytes accessed | tf_op | source)
XLA Modules:
  0.0 49.5 jit_solution(7522019063461457527)
XLA Ops:
  0.6 1.2 %pack_edges.1 = (bf16[8,16,1024]{2,1,0:T(8,128)(2,1)S(1)}, bf16[8,16,1024]{2,1,0:T(8,128)(2,1)S(1)}, bf16[3,8,1024]{2,1,0:T(8,128)(2,1)S(1)}, bf16[3,8,1024]{2,1,0:T(8,128)(2,1)S(1)}) custom-call(bf16[8,16,1024]{2,1,0:T(8,128)(2,1)} %bitcast.14, bf16[8,16,1024]{2,1,0:T(8,128)(2,1)} %bitcast.15), custom_call_target="tpu_custom_call" | custom-call | bytes 524288 | tf_op jit(solution)/shard_map/pack_edges/pallas_call | solution.py:408
  1.8 0.5 %collective-permute-start = (bf16[3,8,1024]{2,1,0:T(8,128)(2,1)S(1)}, bf16[3,8,1024]{2,1,0:T(8,128)(2,1)S(1)}, u32[]{:S(2)}, u32[]{:S(2)}) collective-permute-start(bf16[3,8,1024]{2,1,0:T(8,128)(2,1)S(1)} %get-tuple-element.45), channel_id=1, source_target_pairs={{0,16},{16,0},{1,17},{17,1},{2,18},{18,2},{3,19},{19,3},{4,20},{20... | collective-permute-start | bytes 147464 | tf_op jit(solution)/shard_map/ppermute | solution.py:20
  2.3 1.2 %pack_halves.1 = (bf16[19,8,1024]{2,1,0:T(8,128)(2,1)S(1)}, bf16[19,8,1024]{2,1,0:T(8,128)(2,1)S(1)}, bf16[27,64,64]{2,1,0:T(8,128)(2,1)S(1)}, bf16[27,64,64]{2,1,0:T(8,128)(2,1)S(1)}) custom-call(bf16[8,16,1024]{2,1,0:T(8,128)(2,1)S(1)} %get-tuple-element.41.field, bf16[8,16,1024]{2,1,0:T(8,128)(2,1)S(1)} %get-tuple-element.42.cot, ...), custom_call_target="tpu_custom_call" | custom-call | bytes 966656 | tf_op jit(solution)/shard_map/pack_halves/pallas_call | solution.py:408
  3.5 0.0 collective-permute-done.taken
  3.5 0.1 collective-permute-start.1
  3.6 0.7 %collective-permute-start.2 = (bf16[3,16,1024]{2,1,0:T(8,128)(2,1)S(1)}, bf16[3,16,1024]{2,1,0:T(8,128)(2,1)S(1)}, u32[]{:S(2)}, u32[]{:S(2)}) collective-permute-start(bf16[3,16,1024]{2,1,0:T(8,128)(2,1)S(1)} %join_edges.1), channel_id=1, source_target_pairs={{16,4},{20,8},{24,12},{4,16},{8,20},{12,24},{17,5},{21,9},{25,13},... | collective-permute-start | bytes 294920 | tf_op jit(solution)/shard_map/ppermute | solution.py:453
  4.3 0.9 %collective-permute-done.1.got = bf16[19,8,1024]{2,1,0:T(8,128)(2,1)S(1)} collective-permute-done((bf16[19,8,1024]{2,1,0:T(8,128)(2,1)S(1)}, bf16[19,8,1024]{2,1,0:T(8,128)(2,1)S(1)}, u32[]{:S(2)}, u32[]{:S(2)}) %collective-permute-start.1) | collective-permute-done | bytes 311328 | tf_op jit(solution)/shard_map/ppermute | solution.py:20
  5.2 5.8 %interior.1 = (bf16[3,12,16,1280]{3,2,1,0:T(8,128)(2,1)S(1)}, bf16[3,10,16,1280]{3,2,1,0:T(8,128)(2,1)S(1)}, bf16[3,10,16,1152]{3,2,1,0:T(8,128)(2,1)S(1)}, bf16...) custom-call(bf16[19,8,1024]{2,1,0:T(8,128)(2,1)S(1)} %get-tuple-elem, ...), custom_call_target="tpu_custom_call" | custom-call | flops 4000000000 | bytes 1064960 | tf_op jit(solution)/shard_map/interior/pallas_call | solution.py:408
  11.0 0.0 collective-permute-done.2.rows
  11.0 1.3 %late_rows.1 = (bf16[3,12,16,1280]{3,2,1,0:T(8,128)(2,1)S(1)}, bf16[3,10,16,1280]{3,2,1,0:T(8,128)(2,1)S(1)}, bf16[3,10,16,1152]{3,2,1,0:T(8,128)(2,1)S(1)}, bf1...) custom-call(bf16[3,12,16,1280]{3,2,1,0:T(8,128)(2,1)S(1)} %get-tuple, ...), custom_call_target="tpu_custom_call", output_to_operand_aliasing={{0}: (0, {}), {1}: (1, {}), {2}: (2, {}), {3}: (3, {})} | custom-call | flops 1000000000 | bytes 7741440 | tf_op jit(solution)/shard_map/late_rows/pallas_call | solution.py:408
  12.3 3.6 %collective-permute-start.3 = (bf16[896,128]{1,0:T(8,128)(2,1)S(1)}, bf16[896,128]{1,0:T(8,128)(2,1)S(1)}, u32[]{:S(2)}, u32[]{:S(2)}) collective-permute-start(bf16[896,128]{1,0:T(8,128)(2,1)S(1)} %get-tuple-element.61), channel_id=1, source_target_pairs={{0,16},{16,0},{1,17},{17,1},{2,18},{18,2},{3,19},{19,3},{4,20},{20... | collective-permute-start | bytes 688136 | tf_op jit(solution)/shard_map/ppermute | solution.py:20
  15.8 1.9 %keep_sums.1 = (f32[896,128]{1,0:T(8,128)S(1)}, bf16[8,8,1024]{2,1,0:T(8,128)(2,1)S(1)}, bf16[8,8,1024]{2,1,0:T(8,128)(2,1)S(1)}) custom-call(bf16[3,12,16,1280]{3,2,1,0:T(8,128)(2,1)S(1)} %get-tuple-element.62.fd, bf16[3,10,16,1280]{3,2,1,0:T(8,128)(2,1)S(1)} %get-tuple-element.63.cd, bf16[3,10,16,1152]{3,2,1,0:T(8,128)(2,1)S(1)} %get-tuple-element.64.hd, ...), custom_call_target="tpu_custom_call" | custom-call | flops 4000000000 | bytes 7053312 | tf_op jit(solution)/shard_map/keep_sums/pallas_call | solution.py:408
  17.8 0.0 collective-permute-done.3.other
  17.8 0.1 add_pair.1
  17.8 15.7 %all_to_all.10.terms = bf16[16,56,128]{2,1,0:T(8,128)(2,1)S(1)} all-to-all(bf16[16,56,128]{2,1,0:T(8,128)(2,1)S(1)} %bitcast.9), channel_id=1, replica_groups=mesh['gx'=2,'gy'=4,'grp'=4] {'gy','grp'}, dimensions={0} | all-to-all | bytes 458752 | tf_op jit(solution)/shard_map/all_to_all | solution.py:492
  33.6 0.7 %add_and_repeat.1 = bf16[16,56,128]{2,1,0:T(8,128)(2,1)} custom-call(bf16[16,56,128]{2,1,0:T(8,128)(2,1)S(1)} %all_to_all.10.terms), custom_call_target="tpu_custom_call" | custom-call | bytes 229376 | tf_op jit(solution)/shard_map/add_and_repeat/pallas_call | solution.py:408
  34.3 3.5 %all-to-all-start.1 = ((bf16[16,56,128]{2,1,0:T(8,128)(2,1)}), bf16[16,56,128]{2,1,0:T(8,128)(2,1)S(1)}, u32[]{:S(2)}, u32[]{:S(2)}) async-start(bf16[16,56,128]{2,1,0:T(8,128)(2,1)} %add_and_repeat.1), calls=%async_computation.1 | async-start | bytes 458752 | tf_op jit(solution)/shard_map/all_to_all | solution.py:494
  37.8 0.1 collective-permute-start.4
  37.9 1.3 %collective-permute-done.4.other = bf16[8,8,1024]{2,1,0:T(8,128)(2,1)S(1)} collective-permute-done((bf16[8,8,1024]{2,1,0:T(8,128)(2,1)S(1)}, bf16[8,8,1024]{2,1,0:T(8,128)(2,1)S(1)}, u32[]{:S(2)}, u32[]{:S(2)}) %collective-permute-start.4) | collective-permute-done | bytes 131104 | tf_op jit(solution)/shard_map/ppermute | solution.py:20
  39.3 7.4 %all-to-all-done.1 = bf16[16,56,128]{2,1,0:T(8,128)(2,1)S(1)} async-done(((bf16[16,56,128]{2,1,0:T(8,128)(2,1)}), bf16[16,56,128]{2,1,0:T(8,128)(2,1)S(1)}, u32[]{:S(2)}, u32[]{:S(2)}) %all-to-all-start.1) | async-done | bytes 229408 | tf_op jit(solution)/shard_map/all_to_all | solution.py:494
  46.6 0.0 collective-permute-start.5
  46.6 0.8 %finish_output.1 = bf16[8,16,1024]{2,1,0:T(8,128)(2,1)} custom-call(bf16[8,8,1024]{2,1,0:T(8,128)(2,1)S(1)} %get-tuple-element.73.mine, bf16[8,8,1024]{2,1,0:T(8,128)(2,1)S(1)} %collective-permute-done.4.other), custom_call_target="tpu_custom_call" | custom-call | bytes 262144 | tf_op jit(solution)/shard_map/finish_output/pallas_call | solution.py:408
  47.5 0.6 %collective-permute-done.5.other = bf16[896,128]{1,0:T(8,128)(2,1)S(1)} collective-permute-done((bf16[896,128]{1,0:T(8,128)(2,1)S(1)}, bf16[896,128]{1,0:T(8,128)(2,1)S(1)}, u32[]{:S(2)}, u32[]{:S(2)}) %collective-permute-start.5) | collective-permute-done | bytes 229408 | tf_op jit(solution)/shard_map/ppermute | solution.py:20
  48.1 1.4 %unpack.1 = (f32[27,64,64]{2,1,0:T(8,128)}, f32[27,64,64]{2,1,0:T(8,128)}) custom-call(bf16[896,128]{1,0:T(8,128)(2,1)S(1)} %bitcast.11, bf16[896,128]{1,0:T(8,128)(2,1)S(1)} %collective-permute-done.5.other), custom_call_target="tpu_custom_call" | custom-call | bytes 458752 | tf_op jit(solution)/shard_map/unpack/pallas_call | solution.py:408
  (1 shorter events, 0.0 us)
Async XLA Ops:
  1.8 1.7 %collective-permute-start = (bf16[3,8,1024]{2,1,0:T(8,128)(2,1)S(1)}, bf16[3,8,1024]{2,1,0:T(8,128)(2,1)S(1)}, u32[]{:S(2)}, u32[]{:S(2)}) collective-permute-start(bf16[3,8,1024]{2,1,0:T(8,128)(2,1)S(1)} %get-tuple-element.45), channel_id=1, source_target_pairs={{0,16},{16,0},{1,17},{17,1},{2,18},{18,2},{3,19},{19,3},{4,20},{20... | collective-permute-start | bytes 147464 | tf_op jit(solution)/shard_map/ppermute | solution.py:20
  3.5 1.7 %collective-permute-start.1 = (bf16[19,8,1024]{2,1,0:T(8,128)(2,1)S(1)}, bf16[19,8,1024]{2,1,0:T(8,128)(2,1)S(1)}, u32[]{:S(2)}, u32[]{:S(2)}) collective-permute-start(bf16[19,8,1024]{2,1,0:T(8,128)(2,1)S(1)} %get-tuple-element.48), channel_id=1, source_target_pairs={{0,16},{16,0},{1,17},{17,1},{2,18},{18,2},{3,19},{19,3},{4,20},{20... | collective-permute-start | bytes 933896 | tf_op jit(solution)/shard_map/ppermute | solution.py:20
  3.6 7.3 %collective-permute-start.2 = (bf16[3,16,1024]{2,1,0:T(8,128)(2,1)S(1)}, bf16[3,16,1024]{2,1,0:T(8,128)(2,1)S(1)}, u32[]{:S(2)}, u32[]{:S(2)}) collective-permute-start(bf16[3,16,1024]{2,1,0:T(8,128)(2,1)S(1)} %join_edges.1), channel_id=1, source_target_pairs={{16,4},{20,8},{24,12},{4,16},{8,20},{12,24},{17,5},{21,9},{25,13},... | collective-permute-start | bytes 294920 | tf_op jit(solution)/shard_map/ppermute | solution.py:453
  12.3 5.5 %collective-permute-start.3 = (bf16[896,128]{1,0:T(8,128)(2,1)S(1)}, bf16[896,128]{1,0:T(8,128)(2,1)S(1)}, u32[]{:S(2)}, u32[]{:S(2)}) collective-permute-start(bf16[896,128]{1,0:T(8,128)(2,1)S(1)} %get-tuple-element.61), channel_id=1, source_target_pairs={{0,16},{16,0},{1,17},{17,1},{2,18},{18,2},{3,19},{19,3},{4,20},{20... | collective-permute-start | bytes 688136 | tf_op jit(solution)/shard_map/ppermute | solution.py:20
  34.3 12.3 %all-to-all-start.1 = ((bf16[16,56,128]{2,1,0:T(8,128)(2,1)}), bf16[16,56,128]{2,1,0:T(8,128)(2,1)S(1)}, u32[]{:S(2)}, u32[]{:S(2)}) async-start(bf16[16,56,128]{2,1,0:T(8,128)(2,1)} %add_and_repeat.1), calls=%async_computation.1 | async-start | bytes 458752 | tf_op jit(solution)/shard_map/all_to_all | solution.py:494
  37.8 1.4 %collective-permute-start.4 = (bf16[8,8,1024]{2,1,0:T(8,128)(2,1)S(1)}, bf16[8,8,1024]{2,1,0:T(8,128)(2,1)S(1)}, u32[]{:S(2)}, u32[]{:S(2)}) collective-permute-start(bf16[8,8,1024]{2,1,0:T(8,128)(2,1)S(1)} %get-tuple-element.71), channel_id=1, source_target_pairs={{0,16},{16,0},{1,17},{17,1},{2,18},{18,2},{3,19},{19,3},{4,20},{20... | collective-permute-start | bytes 393224 | tf_op jit(solution)/shard_map/ppermute | solution.py:20
  46.6 1.5 %collective-permute-start.5 = (bf16[896,128]{1,0:T(8,128)(2,1)S(1)}, bf16[896,128]{1,0:T(8,128)(2,1)S(1)}, u32[]{:S(2)}, u32[]{:S(2)}) collective-permute-start(bf16[896,128]{1,0:T(8,128)(2,1)S(1)} %bitcast.10), channel_id=1, source_target_pairs={{0,16},{16,0},{1,17},{17,1},{2,18},{18,2},{3,19},{19,3},{4,20},{20... | collective-permute-start | bytes 688136 | tf_op jit(solution)/shard_map/ppermute | solution.py:20

commit v10 on v9

--- a/solution.py
+++ b/solution.py
@@ -51,14 +51,14 @@
     return blocks
 
 
-def pack_edges(field_hbm, cot_hbm, field, cot, edge, given, rows, sems):
+def pack_edges(field_hbm, cot_hbm, w1_hbm, w2_hbm, field, cot, edge, given, w1, w2, rows, sems):
     copies = [
         pltpu.make_async_copy(source, target, sems.at[index])
-        for index, (source, target) in enumerate(((field_hbm, field), (cot_hbm, cot)))
+        for index, (source, target) in enumerate(((field_hbm, field), (cot_hbm, cot), (w1_hbm, w1), (w2_hbm, w2)))
     ]
     for copy in copies:
         copy.start()
-    for copy in copies:
+    for copy in copies[:2]:
         copy.wait()
     nx, ny, _ = field.shape
     gx = lax.axis_index("gx")
@@ -71,6 +71,8 @@
     tail = rows[3:6].astype(BF16)
     edge[...] = jnp.where(gx == 0, head, tail)
     given[...] = jnp.where(gx == 0, tail, head)
+    for copy in copies[2:]:
+        copy.wait()
 
 
 def join_edges(edge, taken, whole):
@@ -106,13 +108,7 @@
     return [take_rows(scratch, y, nx, ny) for y in range(ny)]
 
 
-def pack_halves(field, cot, w1_hbm, w2_hbm, own, bulk, w1, w2, turned_f, turned_c, scratch, sems):
-    copies = [
-        pltpu.make_async_copy(source, target, sems.at[index])
-        for index, (source, target) in enumerate(((w1_hbm, w1), (w2_hbm, w2)))
-    ]
-    for copy in copies:
-        copy.start()
+def pack_halves(field, cot, w1, w2, own, bulk, w1b, w2b, wfb, turned_f, turned_c, scratch):
     ny = field.shape[1]
     half = ny // 2
     for source, target in ((field, turned_f), (cot, turned_c)):
@@ -136,8 +132,7 @@
     def _():
         place(high_f, high_c, low_f, low_c)
 
-    for copy in copies:
-        copy.wait()
+    make_bands(w1, w2, w1b, w2b, wfb)
 
 
 def make_bands(w1, w2, w1b, w2b, wfb):
@@ -194,7 +189,7 @@
     return grad * sigma * (1.0 + pre * (1.0 - sigma)) * inside_lanes(p)
 
 
-def interior(own, got, w1, w2, fd, cd, hd, pg, acc1, acc2, w1b, w2b, wfb, fs, cs, hs, pre):
+def interior(own, got, w1b, wfb, fd, cd, hd, pg, acc, fs, cs, hs, pre):
     gx = lax.axis_index("gx")
     nx = own.shape[1]
     across = 2 * nx
@@ -202,7 +197,6 @@
     cells = count * across
     lane = 2 * C
     pairs = NZ // 2
-    make_bands(w1, w2, w1b, w2b, wfb)
 
     def place(left, right):
         for scratch, start, size in ((fs, 0, count + 2), (cs, count + 2, count + 1)):
@@ -238,15 +232,43 @@
         pg[pl.ds(1 - gx, count - 1), :, here] = grad.astype(BF16).reshape(count - 1, across, lane)
     pg[pl.ds((count - 1) * gx, 1)] = jnp.zeros((1,) + pg.shape[1:], BF16)
 
+    @pl.when(gx == 0)
+    def _():
+        for t, total in enumerate(second_products(hd, cd)):
+            acc[t] = total
+
+    @pl.when(gx != 0)
+    def _():
+        for t, total in enumerate(first_products(fd, pg)):
+            acc[t] = total
+
+
+def second_products(hd, cd):
+    lane = 2 * C
+    pairs = NZ // 2
+    count, across = hd.shape[1] - 2, hd.shape[2]
+    cells = count * across
     cot_t = jnp.concatenate(
         [cd[1, 1:1 + count, :, lane * (p + 1):lane * (p + 2)].reshape(cells, lane).T for p in range(pairs)], axis=1)
+    return [
+        dot(cot_t, jnp.concatenate(
+            [hd[dx, dy:dy + count, :, lane * p:lane * (p + 2)].reshape(cells, 2 * lane) for p in range(pairs)], axis=0))
+        for dx, dy in TAPS
+    ]
+
+
+def first_products(fd, pg):
+    lane = 2 * C
+    pairs = NZ // 2
+    count, across, _ = pg.shape
+    cells = count * across
     grad_t = jnp.concatenate(
         [pg[:, :, lane * p:lane * (p + 1)].reshape(cells, lane).T for p in range(pairs + 1)], axis=1)
-    for t, (dx, dy) in enumerate(TAPS):
-        acc2[t] = dot(cot_t, jnp.concatenate(
-            [hd[dx, dy:dy + count, :, lane * p:lane * (p + 2)].reshape(cells, 2 * lane) for p in range(pairs)], axis=0))
-        acc1[t] = dot(grad_t, jnp.concatenate(
+    return [
+        dot(grad_t, jnp.concatenate(
             [fd[dx, 1 + dy:1 + dy + count, :, lane * p:lane * (p + 2)].reshape(cells, 2 * lane) for p in range(pairs + 1)], axis=0))
+        for dx, dy in TAPS
+    ]
 
 
 def folded(total, factor):
@@ -254,38 +276,41 @@
     return total[0:C, 0:3 * C] + total[C:2 * C, C:4 * C]
 
 
-def second_sums(factor, side, hd, cd, acc2):
+def second_late(hd, cd):
     lane = 2 * C
     pairs = NZ // 2
-    last = hd.shape[1] - 3
-    late = ((0, 1), (0,), ()) if side == 0 else ((), (last,), (last - 1, last))
-    pieces = []
-    for t, (dx, dy) in enumerate(TAPS):
-        total = acc2[t]
+    late = ((0, 1), (0,), ())
+    products = []
+    for dx, dy in TAPS:
         if late[dy]:
             cots = jnp.concatenate(
                 [cd[1, 1 + y, :, lane * (p + 1):lane * (p + 2)] for y in late[dy] for p in range(pairs)], axis=0)
             rows = jnp.concatenate(
                 [hd[dx, y + dy, :, lane * p:lane * (p + 2)] for y in late[dy] for p in range(pairs)], axis=0)
-            total = total + dot(cots.T, rows)
-        pieces.append(folded(total, factor))
-    return packed(pieces)
-
-
-def first_sums(factor, side, fd, pg, acc1):
+            products.append(dot(cots.T, rows))
+        else:
+            products.append(0.0)
+    return products
+
+
+def first_late(fd, pg):
     lane = 2 * C
     pairs = NZ // 2
     count, across, _ = pg.shape
-    y = 0 if side == 0 else count - 1
+    y = count - 1
     extra = 2 * lane - (pairs + 1) * across
     grad_t = jnp.concatenate(
         [pg[y, :, lane * p:lane * (p + 1)] for p in range(pairs + 1)] + [jnp.zeros((extra, lane), BF16)], axis=0).T
     pad = jnp.zeros((extra, 2 * lane), BF16)
-    return packed([
-        folded(acc1[t] + dot(grad_t, jnp.concatenate(
-            [fd[dx, y + dy + 1, :, lane * p:lane * (p + 2)] for p in range(pairs + 1)] + [pad], axis=0)), factor)
-        for t, (dx, dy) in enumerate(TAPS)
-    ])
+    return [
+        dot(grad_t, jnp.concatenate(
+            [fd[dx, y + dy + 1, :, lane * p:lane * (p + 2)] for p in range(pairs + 1)] + [pad], axis=0))
+        for dx, dy in TAPS
+    ]
+
+
+def sums_of(factor, products):
+    return packed([folded(product, factor) for product in products])
 
 
 def store_blocks(target, blocks):
@@ -295,7 +320,7 @@
         target[BLOCKS * C:, :] = jnp.zeros((target.shape[0] - BLOCKS * C, 2 * C), target.dtype)
 
 
-def late_rows(factor, gy_count, fd_in, cd_in, hd_in, pg_in, rows, acc1, acc2, w1b, wfb, fd, cd, hd, pg, send, rs, hs):
+def late_rows(factor, gy_count, fd_in, cd_in, hd_in, pg_in, rows, acc, w1b, wfb, fd, cd, hd, pg, send, rs, hs):
     gx = lax.axis_index("gx")
     gy = lax.axis_index("gy")
     count, across, _ = pg.shape
@@ -322,31 +347,33 @@
 
     @pl.when(gx == 0)
     def _():
-        store_blocks(send, second_sums(factor, 0, hd, cd, acc2))
+        store_blocks(send, sums_of(factor, [acc[t] + late for t, late in enumerate(second_late(hd, cd))]))
 
     @pl.when(gx != 0)
     def _():
-        store_blocks(send, first_sums(factor, 1, fd, pg, acc1))
-
-
-def keep_sums(factor, fd, cd, hd, pg, acc1, acc2, w2b, keep, mine, given):
-    gx = lax.axis_index("gx")
-    count, across, _ = pg.shape
-    lane = 2 * C
-    half = across // 2
+        store_blocks(send, sums_of(factor, [acc[t] + late for t, late in enumerate(first_late(fd, pg))]))
+
+
+def keep_sums(factor, fd, cd, hd, pg, keep):
+    gx = lax.axis_index("gx")
 
     @pl.when(gx == 0)
     def _():
-        store_blocks(keep, first_sums(factor, 0, fd, pg, acc1))
+        store_blocks(keep, sums_of(factor, first_products(fd, pg)))
 
     @pl.when(gx != 0)
     def _():
-        store_blocks(keep, second_sums(factor, 1, hd, cd, acc2))
-
+        store_blocks(keep, sums_of(factor, second_products(hd, cd)))
+
+
+def output_conv(hd, w2b, mine, given):
+    gx = lax.axis_index("gx")
+    count, half, _ = mine.shape
+    lane = 2 * C
     for p in range(NZ // 2):
         here = slice(lane * p, lane * (p + 1))
-        value = dot(windows(hd, 0, count, p), w2b[...]).reshape(count, across, lane)
-        left, right = value[:, 0:half], value[:, half:across]
+        value = dot(windows(hd, 0, count, p), w2b[...]).reshape(count, 2 * half, lane)
+        left, right = value[:, 0:half], value[:, half:]
         mine[:, :, here] = jnp.where(gx == 0, left, right).astype(BF16)
         given[:, :, here] = jnp.where(gx == 0, right, left).astype(BF16)
 
@@ -382,20 +409,35 @@
         out[index] = total
 
 
-def unpack(mine, other, first, second):
-    gx = lax.axis_index("gx")
-    a = mine[...].astype(F32)
-    b = other[...].astype(F32)
-    for out, rows in ((first, jnp.where(gx == 0, a, b)), (second, jnp.where(gx == 0, b, a))):
-        for t, (dx, dy) in enumerate(TAPS):
-            turned = rows[t * C:(t + 1) * C].T
-            out[9 * dx + 3 * dy] = turned[0:C]
-            out[9 * dx + 3 * dy + 1] = turned[C:2 * C]
-        for pair in range(5):
-            turned = rows[(9 + pair) * C:(10 + pair) * C].T
-            for half in range(2 if pair < 4 else 1):
-                dx, dy = TAPS[2 * pair + half]
-                out[9 * dx + 3 * dy + 2] = turned[half * C:(half + 1) * C]
+def unpack(rows, held):
+    for t, (dx, dy) in enumerate(TAPS):
+        turned = rows[t * C:(t + 1) * C, :].astype(F32).T
+        held[9 * dx + 3 * dy] = turned[0:C]
+        held[9 * dx + 3 * dy + 1] = turned[C:2 * C]
+    for pair in range(5):
+        turned = rows[(9 + pair) * C:(10 + pair) * C, :].astype(F32).T
+        for half in range(2 if pair < 4 else 1):
+            dx, dy = TAPS[2 * pair + half]
+            held[9 * dx + 3 * dy + 2] = turned[half * C:(half + 1) * C]
+
+
+def write_either(is_first, held, first, second, sem):
+    for chosen, target in ((is_first, first), (jnp.logical_not(is_first), second)):
+        @pl.when(chosen)
+        def _():
+            copy = pltpu.make_async_copy(held, target, sem.at[0])
+            copy.start()
+            copy.wait()
+
+
+def unpack_own(rows, first, second, held, sem):
+    unpack(rows, held)
+    write_either(lax.axis_index("gx") == 0, held, first, second, sem)
+
+
+def unpack_other(rows, first_in, second_in, first, second, held, sem):
+    unpack(rows, held)
+    write_either(lax.axis_index("gx") != 0, held, first, second, sem)
 
 
 def near(shape, dtype):
@@ -431,22 +473,34 @@
     across = 2 * nx
     size = 2 * count + 3
 
-    field, cot, edge, given = call(
-        pack_edges, "pack_edges", [(field_in[0], False), (cotangent[0], False)],
-        [near((nx, ny, width), BF16), near((nx, ny, width), BF16), near((3, nx, width), BF16), near((3, nx, width), BF16)],
-        [pltpu.VMEM((6, nx, width), F32), pltpu.SemaphoreType.DMA((2,))])
+    field, cot, edge, given, w1, w2 = call(
+        pack_edges, "pack_edges",
+        [(x, False) for x in (field_in[0], cotangent[0], first_weight.reshape(27, C, C), second_weight.reshape(27, C, C))],
+        [
+            near((nx, ny, width), BF16),
+            near((nx, ny, width), BF16),
+            near((3, nx, width), BF16),
+            near((3, nx, width), BF16),
+            near((27, C, C), BF16),
+            near((27, C, C), BF16),
+        ],
+        [pltpu.VMEM((6, nx, width), F32), pltpu.SemaphoreType.DMA((4,))])
     taken = swap(given)
-    own, bulk, w1, w2 = call(
-        pack_halves, "pack_halves",
-        [(field, True), (cot, True), (first_weight.reshape(27, C, C), False), (second_weight.reshape(27, C, C), False)],
-        [near((size, nx, width), BF16), near((size, nx, width), BF16), near((27, C, C), BF16), near((27, C, C), BF16)],
+    own, bulk, w1b, w2b, wfb = call(
+        pack_halves, "pack_halves", [(x, True) for x in (field, cot, w1, w2)],
+        [
+            near((size, nx, width), BF16),
+            near((size, nx, width), BF16),
+            near((9 * 4 * C, lane), BF16),
+            near((9 * 4 * C, lane), BF16),
+            near((lane, 9 * 4 * C), BF16),
+        ],
         [
             pltpu.VMEM((ny, nx, width), BF16),
             pltpu.VMEM((ny, nx, width), BF16),
             pltpu.VMEM((width // lane, nx * ny, lane), F32),
-            pltpu.SemaphoreType.DMA((2,)),
-        ])
-    bulk, taken, w1, w2 = lax.optimization_barrier((bulk, taken, w1, w2))
+        ], flops=10 ** 9)
+    bulk, taken, wfb = lax.optimization_barrier((bulk, taken, wfb))
     got = swap(bulk)
     whole, = call(join_edges, "join_edges", [(edge, True), (taken, True)], [near((3, across, width), BF16)])
     ends = [(gy_count + j, j + 1) for j in range(gy_count - 1)]
@@ -457,16 +511,10 @@
         near((3, count + 2, across, width + lane), BF16),
         near((count, across, width + lane), BF16),
     ]
-    fd, cd, hd, pg, acc1, acc2, w1b, w2b, wfb = call(
+    fd, cd, hd, pg, acc = call(
         interior, "interior",
-        [(x, True) for x in (own, got, w1, w2)],
-        held + [
-            near((9, lane, 2 * lane), F32),
-            near((9, lane, 2 * lane), F32),
-            near((9 * 4 * C, lane), BF16),
-            near((9 * 4 * C, lane), BF16),
-            near((lane, 9 * 4 * C), BF16),
-        ],
+        [(x, True) for x in (own, got, w1b, wfb)],
+        held + [near((9, lane, 2 * lane), F32)],
         [
             pltpu.VMEM((count + 2, across + 16, width), F32),
             pltpu.VMEM((count + 1, across + 16, width), F32),
@@ -476,31 +524,38 @@
         limit=32, flops=4 * 10 ** 9)
     fd, cd, hd, pg, send = call(
         functools.partial(late_rows, factor, gy_count), "late_rows",
-        [(x, True) for x in (fd, cd, hd, pg, late, acc1, acc2, w1b, wfb)],
+        [(x, True) for x in (fd, cd, hd, pg, late, acc, w1b, wfb)],
         held + [near((rows, lane), BF16)],
         [pltpu.VMEM((3, across + 16, width), F32), pltpu.VMEM((2, across + 16, width + lane), F32)],
         limit=32, flops=10 ** 9, aliases={0: 0, 1: 1, 2: 2, 3: 3})
 
     other = swap(send)
-    keep, mine, given = call(
+    keep, = call(
         functools.partial(keep_sums, factor), "keep_sums",
-        [(x, True) for x in (fd, cd, hd, pg, acc1, acc2, w2b)],
-        [near((rows, lane), F32), near((count, nx, width), BF16), near((count, nx, width), BF16)], flops=4 * 10 ** 9)
+        [(x, True) for x in (fd, cd, hd, pg)], [near((rows, lane), F32)], flops=2 * 10 ** 9)
     other, keep = lax.optimization_barrier((other, keep))
     both, = call(add_pair, "add_pair", [(keep, True), (other, True)], [near((rows, lane), BF16)])
-    given_out = swap(given)
     terms = lax.all_to_all(both.reshape(ranks, rows // ranks, lane), ("gy", "grp"), 0, 0)
     spread, = call(add_and_repeat, "add_and_repeat", [(terms, True)], [near(terms.shape, BF16)])
+    spread, hd, w2b = lax.optimization_barrier((spread, hd, w2b))
     sums = lax.all_to_all(spread, ("gy", "grp"), 0, 0).reshape(rows, lane)
-    sums, mine, given_out = lax.optimization_barrier((sums, mine, given_out))
-    other = swap(sums)
+    mine, given = call(
+        output_conv, "output_conv", [(hd, True), (w2b, True)],
+        [near((count, nx, width), BF16), near((count, nx, width), BF16)], flops=2 * 10 ** 9)
+    given = swap(given)
     out, = call(
-        finish_output, "finish_output", [(mine, True), (given_out, True)],
+        finish_output, "finish_output", [(mine, True), (given, True)],
         [pltpu.HBM((nx, ny, width), BF16)],
         [pltpu.VMEM((nx, ny, width), BF16), pltpu.VMEM((width // lane, nx * ny, lane), F32), pltpu.SemaphoreType.DMA((nx // 2,))], far=True)
-    other, out = lax.optimization_barrier((other, out))
+    sums, out = lax.optimization_barrier((sums, out))
+    other = swap(sums)
+    outs = [pltpu.HBM((27, C, C), F32)] * 2
+    scratch = [pltpu.VMEM((27, C, C), F32), pltpu.SemaphoreType.DMA((1,))]
+    first, second = call(unpack_own, "unpack_own", [(sums, True)], outs, scratch, far=True)
+    other, first, second = lax.optimization_barrier((other, first, second))
     first, second = call(
-        unpack, "unpack", [(sums, True), (other, True)], [jax.ShapeDtypeStruct((27, C, C), F32)] * 2)
+        unpack_other, "unpack_other", [(other, True), (first, False), (second, False)], outs, scratch, far=True,
+        aliases={1: 0, 2: 1})
     shape = (3, 3, 3, C, C)
     return out[None], first.reshape(shape), second.reshape(shape)
 

time: 49.8 us -> 47.8 us (0.960)
  waiting for transfers between devices: 10.2 us -> 7.52 us
    all_to_all x1, waiting for transfers between devices: 7.38 us -> 5.18 us  [shards(): sums = lax.all_to_all(spread, ('gy', 'grp'), 0, 0).reshape(rows, lane)]
    ppermute x5, waiting for transfers between devices: 2.86 us -> 2.34 us  [swap(): return lax.ppermute(array, 'gx', [(0, 1), (1, 0)])]
    pallas_call x10 -> x12, Pallas kernels: 14.4 us -> 14.3 us  [call(): pl.pallas_call(body, out_shape=list(outs), in_specs=[pl.BlockSpec(memory_...]
  transfers between devices with their start and end apart: 7 -> 7, of which waited for: 4 -> 4; matrix products, arithmetic and copies ran while one was open for 0% -> 0% of each run, Pallas kernels for 20% -> 21%
where the time goes in v10:
time: 47.8 us; the launch traced here: 47.5 us
  blocking collectives  16.1 us (34%)
  Pallas kernels  14.3 us (30%)
  starting transfers between devices  8.86 us (19%)
  waiting for transfers between devices  7.52 us (16%)
  between operations  0.74 us (2%)
    all_to_all x1, blocking collectives, shards(): lax.all_to_all(both.reshape(ranks, rows // ranks, lane), ('gy', 'grp'), 0...  16.1 us
    pallas_call x12, Pallas kernels, call(): pl.pallas_call(body, out_shape=list(outs), in_specs=[pl.BlockSpec(memory_...  14.3 us
    all_to_all x1, waiting for transfers between devices, shards(): sums = lax.all_to_all(spread, ('gy', 'grp'), 0, 0).reshape(rows, lane)  5.18 us
    ppermute x5, starting transfers between devices, swap(): return lax.ppermute(array, 'gx', [(0, 1), (1, 0)])  4.67 us
    all_to_all x1, starting transfers between devices, shards(): sums = lax.all_to_all(spread, ('gy', 'grp'), 0, 0).reshape(rows, lane)  3.53 us
    ppermute x5, waiting for transfers between devices, swap(): return lax.ppermute(array, 'gx', [(0, 1), (1, 0)])  2.34 us
  transfers between devices with their start and end apart: 7, of which 4 were waited for; matrix products, arithmetic and copies ran while one was open for 0% of the time, Pallas kernels for 21%

profile of v10, /device:TPU:0, one launch (start us, length us, event | category | flops | bytes accessed | tf_op | source)
XLA Modules:
  0.0 47.5 jit_solution(1791156581708072999)
XLA Ops:
  0.6 1.3 %pack_edges.1 = (bf16[8,16,1024]{2,1,0:T(8,128)(2,1)S(1)}, bf16[8,16,1024]{2,1,0:T(8,128)(2,1)S(1)}, bf16[3,8,1024]{2,1,0:T(8,128)(2,1)S(1)}, bf16[3,8,1024]{2,1...) custom-call(bf16[8,16,1024]{2,1,0:T(8,128)(2,1)} %bitcast.17, ...), custom_call_target="tpu_custom_call" | custom-call | bytes 966656 | tf_op jit(solution)/shard_map/pack_edges/pallas_call | solution.py:450
  2.0 0.5 %collective-permute-start = (bf16[3,8,1024]{2,1,0:T(8,128)(2,1)S(1)}, bf16[3,8,1024]{2,1,0:T(8,128)(2,1)S(1)}, u32[]{:S(2)}, u32[]{:S(2)}) collective-permute-start(bf16[3,8,1024]{2,1,0:T(8,128)(2,1)S(1)} %get-tuple-element.49), channel_id=1, source_target_pairs={{0,16},{16,0},{1,17},{17,1},{2,18},{18,2},{3,19},{19,3},{4,20},{20... | collective-permute-start | bytes 147464 | tf_op jit(solution)/shard_map/ppermute | solution.py:20
  2.5 0.8 %pack_halves.1 = (bf16[19,8,1024]{2,1,0:T(8,128)(2,1)S(1)}, bf16[19,8,1024]{2,1,0:T(8,128)(2,1)S(1)}, bf16[2304,128]{1,0:T(8,128)(2,1)S(1)}, bf16[2304,128]{1,0:T(8,128)(2,1)S(1)}, bf16[128,2304]{1,0:T(8,128)(2,1)S(1)}) custom-call(bf16[8,16,1024]{2,1,0:T(8,128)(2,1)S(1)} %get-tuple-element.43.field, bf16[8,16,1024]{2,1,0:T(8,128)(2,1)S(1)} %get-tuple-element.44.cot, ...), custom_call_target="tpu_custom_call" | custom-call | flops 1000000000 | bytes 966656 | tf_op jit(solution)/shard_map/pack_halves/pallas_call | solution.py:450
  3.3 0.0 collective-permute-done.taken
  3.4 0.3 collective-permute-start.1
  3.7 0.7 %collective-permute-start.2 = (bf16[3,16,1024]{2,1,0:T(8,128)(2,1)S(1)}, bf16[3,16,1024]{2,1,0:T(8,128)(2,1)S(1)}, u32[]{:S(2)}, u32[]{:S(2)}) collective-permute-start(bf16[3,16,1024]{2,1,0:T(8,128)(2,1)S(1)} %join_edges.1), channel_id=1, source_target_pairs={{16,4},{20,8},{24,12},{4,16},{8,20},{12,24},{17,5},{21,9},{25,13},... | collective-permute-start | bytes 294920 | tf_op jit(solution)/shard_map/ppermute | solution.py:507
  4.4 0.6 %collective-permute-done.1.got = bf16[19,8,1024]{2,1,0:T(8,128)(2,1)S(1)} collective-permute-done((bf16[19,8,1024]{2,1,0:T(8,128)(2,1)S(1)}, bf16[19,8,1024]{2,1,0:T(8,128)(2,1)S(1)}, u32[]{:S(2)}, u32[]{:S(2)}) %collective-permute-start.1) | collective-permute-done | bytes 311328 | tf_op jit(solution)/shard_map/ppermute | solution.py:20
  5.0 4.4 %interior.1 = (bf16[3,12,16,1280]{3,2,1,0:T(8,128)(2,1)S(1)}, bf16[3,10,16,1280]{3,2,1,0:T(8,128)(2,1)S(1)}, bf16[3,10,16,1152]{3,2,1,0:T(8,128)(2,1)S(1)}, bf16...) custom-call(bf16[19,8,1024]{2,1,0:T(8,128)(2,1)S(1)} %get-tuple-element.47.own, ...), custom_call_target="tpu_custom_call" | custom-call | flops 4000000000 | bytes 1802240 | tf_op jit(solution)/shard_map/interior/pallas_call | solution.py:450
  9.4 0.0 collective-permute-done.2.rows
  9.5 1.3 %late_rows.1 = (bf16[3,12,16,1280]{3,2,1,0:T(8,128)(2,1)S(1)}, bf16[3,10,16,1280]{3,2,1,0:T(8,128)(2,1)S(1)}, bf16[3,10,16,1152]{3,2,1,0:T(8,128)(2,1)S(1)}, bf1...) custom-call(bf16[3,12,16,1280]{3,2,1,0:T(8,128)(2,1)S(1)} %get-tuple, ...), custom_call_target="tpu_custom_call", output_to_operand_aliasing={{0}: (0, {}), {1}: (1, {}), {2}: (2, {}), {3}: (3, {})} | custom-call | flops 1000000000 | bytes 6561792 | tf_op jit(solution)/shard_map/late_rows/pallas_call | solution.py:450
  10.7 3.7 %collective-permute-start.3 = (bf16[896,128]{1,0:T(8,128)(2,1)S(1)}, bf16[896,128]{1,0:T(8,128)(2,1)S(1)}, u32[]{:S(2)}, u32[]{:S(2)}) collective-permute-start(bf16[896,128]{1,0:T(8,128)(2,1)S(1)} %get-tuple-element.61), channel_id=1, source_target_pairs={{0,16},{16,0},{1,17},{17,1},{2,18},{18,2},{3,19},{19,3},{4,20},{20... | collective-permute-start | bytes 688136 | tf_op jit(solution)/shard_map/ppermute | solution.py:20
  14.5 1.1 %keep_sums.1.keep = f32[896,128]{1,0:T(8,128)S(1)} custom-call(bf16[3,12,16,1280]{3,2,1,0:T(8,128)(2,1)S(1)} %get-tuple-element.62.fd, bf16[3,10,16,1280]{3,2,1,0:T(8,128)(2,1)S(1)} %get-tuple-element.63.cd, bf16[3,10,16,1152]{3,2,1,0:T(8,128)(2,1)S(1)} %get-tuple-element.70.hd, bf16[8,16,1152]{2,1,0:T(8,128)(2,1)S(1)} %get-tuple-element.65.pg), custom_call_target="tpu_custom_call" | custom-call | flops 2000000000 | bytes 4104192 | tf_op jit(solution)/shard_map/keep_sums/pallas_call | solution.py:450
  15.6 0.0 collective-permute-done.3.other
  15.6 16.1 %all_to_all.10.terms = bf16[16,56,128]{2,1,0:T(8,128)(2,1)S(1)} all-to-all(bf16[16,56,128]{2,1,0:T(8,128)(2,1)S(1)} %bitcast.9), channel_id=1, replica_groups=mesh['gx'=2,'gy'=4,'grp'=4] {'gy','grp'}, dimensions={0} | all-to-all | bytes 458752 | tf_op jit(solution)/shard_map/all_to_all | solution.py:538
  31.8 0.7 %add_and_repeat.1 = bf16[16,56,128]{2,1,0:T(8,128)(2,1)} custom-call(bf16[16,56,128]{2,1,0:T(8,128)(2,1)S(1)} %all_to_all.10.terms), custom_call_target="tpu_custom_call" | custom-call | bytes 229376 | tf_op jit(solution)/shard_map/add_and_repeat/pallas_call | solution.py:450
  32.5 3.5 %all-to-all-start.1 = ((bf16[16,56,128]{2,1,0:T(8,128)(2,1)}), bf16[16,56,128]{2,1,0:T(8,128)(2,1)S(1)}, u32[]{:S(2)}, u32[]{:S(2)}) async-start(bf16[16,56,128]{2,1,0:T(8,128)(2,1)} %add_and_repeat.1), calls=%async_computation.1 | async-start | bytes 458752 | tf_op jit(solution)/shard_map/all_to_all | solution.py:541
  36.0 1.4 %output_conv.1 = (bf16[8,8,1024]{2,1,0:T(8,128)(2,1)S(1)}, bf16[8,8,1024]{2,1,0:T(8,128)(2,1)S(1)}) custom-call(bf16[3,10,16,1152]{3,2,1,0:T(8,128)(2,1)S(1)} %get-tuple-element.70.hd, bf16[2304,128]{1,0:T(8,128)(2,1)S(1)} %get-tuple-element.71.w2b), custom_call_target="tpu_custom_call" | custom-call | flops 2000000000 | bytes 1695744 | tf_op jit(solution)/shard_map/output_conv/pallas_call | solution.py:450
  37.5 0.1 collective-permute-start.4
  37.5 1.3 %collective-permute-done.4.other = bf16[8,8,1024]{2,1,0:T(8,128)(2,1)S(1)} collective-permute-done((bf16[8,8,1024]{2,1,0:T(8,128)(2,1)S(1)}, bf16[8,8,1024]{2,1,0:T(8,128)(2,1)S(1)}, u32[]{:S(2)}, u32[]{:S(2)}) %collective-permute-start.4) | collective-permute-done | bytes 131104 | tf_op jit(solution)/shard_map/ppermute | solution.py:20
  38.9 0.8 %finish_output.1 = bf16[8,16,1024]{2,1,0:T(8,128)(2,1)} custom-call(bf16[8,8,1024]{2,1,0:T(8,128)(2,1)S(1)} %get-tuple-element.72.mine, bf16[8,8,1024]{2,1,0:T(8,128)(2,1)S(1)} %collective-permute-done.4.other), custom_call_target="tpu_custom_call" | custom-call | bytes 262144 | tf_op jit(solution)/shard_map/finish_output/pallas_call | solution.py:450
  39.7 5.2 %all-to-all-done.1 = bf16[16,56,128]{2,1,0:T(8,128)(2,1)S(1)} async-done(((bf16[16,56,128]{2,1,0:T(8,128)(2,1)}), bf16[16,56,128]{2,1,0:T(8,128)(2,1)S(1)}, u32[]{:S(2)}, u32[]{:S(2)}) %all-to-all-start.1) | async-done | bytes 229408 | tf_op jit(solution)/shard_map/all_to_all | solution.py:541
  44.9 1.1 %unpack_own.1 = (f32[27,64,64]{2,1,0:T(8,128)}, f32[27,64,64]{2,1,0:T(8,128)}) custom-call(bf16[896,128]{1,0:T(8,128)(2,1)S(1)} %bitcast.11), custom_call_target="tpu_custom_call" | custom-call | bytes 229376 | tf_op jit(solution)/shard_map/unpack_own/pallas_call | solution.py:450
  46.0 0.3 collective-permute-done.5.rows
  46.4 1.1 %unpack_other.1 = (f32[27,64,64]{2,1,0:T(8,128)}, f32[27,64,64]{2,1,0:T(8,128)}) custom-call(bf16[896,128]{1,0:T(8,128)(2,1)S(1)} %collective-permute-done.5.rows, f32[27,64,64]{2,1,0:T(8,128)} %get-tuple-element.79.first_in, f32[27,64,64]{2,1,0:T(8,128)} %get-tuple-element.80.second_in), custom_call_target="tpu_custom_call", output_to_operand_aliasing={{0}: (1, {}), {1}: (2, {})} | custom-call | bytes 1114112 | tf_op jit(solution)/shard_map/unpack_other/pallas_call | solution.py:450
  (3 shorter events, 0.1 us)
Async XLA Ops:
  2.0 1.4 %collective-permute-start = (bf16[3,8,1024]{2,1,0:T(8,128)(2,1)S(1)}, bf16[3,8,1024]{2,1,0:T(8,128)(2,1)S(1)}, u32[]{:S(2)}, u32[]{:S(2)}) collective-permute-start(bf16[3,8,1024]{2,1,0:T(8,128)(2,1)S(1)} %get-tuple-element.49), channel_id=1, source_target_pairs={{0,16},{16,0},{1,17},{17,1},{2,18},{18,2},{3,19},{19,3},{4,20},{20... | collective-permute-start | bytes 147464 | tf_op jit(solution)/shard_map/ppermute | solution.py:20
  3.4 1.6 %collective-permute-start.1 = (bf16[19,8,1024]{2,1,0:T(8,128)(2,1)S(1)}, bf16[19,8,1024]{2,1,0:T(8,128)(2,1)S(1)}, u32[]{:S(2)}, u32[]{:S(2)}) collective-permute-start(bf16[19,8,1024]{2,1,0:T(8,128)(2,1)S(1)} %get-tuple-element.51), channel_id=1, source_target_pairs={{0,16},{16,0},{1,17},{17,1},{2,18},{18,2},{3,19},{19,3},{4,20},{20... | collective-permute-start | bytes 933896 | tf_op jit(solution)/shard_map/ppermute | solution.py:20
  3.7 5.7 %collective-permute-start.2 = (bf16[3,16,1024]{2,1,0:T(8,128)(2,1)S(1)}, bf16[3,16,1024]{2,1,0:T(8,128)(2,1)S(1)}, u32[]{:S(2)}, u32[]{:S(2)}) collective-permute-start(bf16[3,16,1024]{2,1,0:T(8,128)(2,1)S(1)} %join_edges.1), channel_id=1, source_target_pairs={{16,4},{20,8},{24,12},{4,16},{8,20},{12,24},{17,5},{21,9},{25,13},... | collective-permute-start | bytes 294920 | tf_op jit(solution)/shard_map/ppermute | solution.py:507
  10.7 4.8 %collective-permute-start.3 = (bf16[896,128]{1,0:T(8,128)(2,1)S(1)}, bf16[896,128]{1,0:T(8,128)(2,1)S(1)}, u32[]{:S(2)}, u32[]{:S(2)}) collective-permute-start(bf16[896,128]{1,0:T(8,128)(2,1)S(1)} %get-tuple-element.61), channel_id=1, source_target_pairs={{0,16},{16,0},{1,17},{17,1},{2,18},{18,2},{3,19},{19,3},{4,20},{20... | collective-permute-start | bytes 688136 | tf_op jit(solution)/shard_map/ppermute | solution.py:20
  32.5 12.4 %all-to-all-start.1 = ((bf16[16,56,128]{2,1,0:T(8,128)(2,1)}), bf16[16,56,128]{2,1,0:T(8,128)(2,1)S(1)}, u32[]{:S(2)}, u32[]{:S(2)}) async-start(bf16[16,56,128]{2,1,0:T(8,128)(2,1)} %add_and_repeat.1), calls=%async_computation.1 | async-start | bytes 458752 | tf_op jit(solution)/shard_map/all_to_all | solution.py:541
  37.5 1.4 %collective-permute-start.4 = (bf16[8,8,1024]{2,1,0:T(8,128)(2,1)S(1)}, bf16[8,8,1024]{2,1,0:T(8,128)(2,1)S(1)}, u32[]{:S(2)}, u32[]{:S(2)}) collective-permute-start(bf16[8,8,1024]{2,1,0:T(8,128)(2,1)S(1)} %get-tuple-element.73), channel_id=1, source_target_pairs={{0,16},{16,0},{1,17},{17,1},{2,18},{18,2},{3,19},{19,3},{4,20},{20... | collective-permute-start | bytes 393224 | tf_op jit(solution)/shard_map/ppermute | solution.py:20
  44.9 1.5 %collective-permute-start.5 = (bf16[896,128]{1,0:T(8,128)(2,1)S(1)}, bf16[896,128]{1,0:T(8,128)(2,1)S(1)}, u32[]{:S(2)}, u32[]{:S(2)}) collective-permute-start(bf16[896,128]{1,0:T(8,128)(2,1)S(1)} %bitcast.10), channel_id=1, source_target_pairs={{0,16},{16,0},{1,17},{17,1},{2,18},{18,2},{3,19},{19,3},{4,20},{20... | collective-permute-start | bytes 688136 | tf_op jit(solution)/shard_map/ppermute | solution.py:20

commit v11 on v10

--- a/solution.py
+++ b/solution.py
@@ -101,46 +101,38 @@
         [scratch[tile, pl.ds(start, count, stride=stride), :] for tile in range(scratch.shape[0])], axis=1).astype(BF16)
 
 
-def turn_rows(source, scratch):
-    nx, ny, _ = source.shape
-    for x in range(nx):
-        put_rows(scratch, x * ny, source[x].astype(F32))
-    return [take_rows(scratch, y, nx, ny) for y in range(ny)]
-
-
-def pack_halves(field, cot, w1, w2, own, bulk, w1b, w2b, wfb, turned_f, turned_c, scratch):
-    ny = field.shape[1]
+def pack_halves(field, cot, w1, w2, own, bulk, w1b, wfb, turned_f, turned_c):
+    nx, ny, _ = field.shape
     half = ny // 2
     for source, target in ((field, turned_f), (cot, turned_c)):
-        for y, rows in enumerate(turn_rows(source, scratch)):
-            target[y] = rows
-    low_f, high_f = turned_f.at[0:half + 2], turned_f.at[half - 2:ny]
-    low_c, high_c = turned_c.at[0:half + 1], turned_c.at[half - 1:ny]
-    gx = lax.axis_index("gx")
-
-    def place(mine_f, mine_c, given_f, given_c):
-        own[0:half + 2] = mine_f[...]
-        own[half + 2:] = mine_c[...]
-        bulk[0:half + 2] = given_f[...]
-        bulk[half + 2:] = given_c[...]
+        for x in range(nx):
+            put_rows(target, x * ny, source[x].astype(F32))
+    gx = lax.axis_index("gx")
+
+    def place(target, first_f, first_c):
+        for y in range(half + 2):
+            target[y] = take_rows(turned_f, first_f + y, nx, ny)
+        for y in range(half + 1):
+            target[half + 2 + y] = take_rows(turned_c, first_c + y, nx, ny)
 
     @pl.when(gx == 0)
     def _():
-        place(low_f, low_c, high_f, high_c)
+        place(own, 0, 0)
+        place(bulk, half - 2, half - 1)
 
     @pl.when(gx != 0)
     def _():
-        place(high_f, high_c, low_f, low_c)
-
-    make_bands(w1, w2, w1b, w2b, wfb)
-
-
-def make_bands(w1, w2, w1b, w2b, wfb):
+        place(own, half - 2, half - 1)
+        place(bulk, 0, 0)
+
+    make_bands(w1, w2, w1b, wfb)
+
+
+def make_bands(w1, w2, w1b, wfb):
     for t, (dx, dy) in enumerate(TAPS):
         rows = slice(t * 4 * C, (t + 1) * 4 * C)
         first = 9 * dx + 3 * dy
         w1b[rows, :] = band([w1[first + z] for z in range(3)])
-        w2b[rows, :] = band([w2[first + z] for z in range(3)])
         wfb[:, rows] = band_flipped([w2[24 - first + z] for z in range(3)])
 
 
@@ -157,9 +149,9 @@
     scratch[:, scratch.shape[1] - 8:scratch.shape[1] - 7, :] = zero
 
 
-def shift_rows(scratch, copies, start, first_lane):
+def shift_rows(scratch, copies, start, first_lane, taps=(0, 1, 2)):
     count, rows, width = scratch.shape
-    for dx in range(3):
+    for dx in taps:
         copies[dx, pl.ds(start, count), :, first_lane:first_lane + width] = scratch[:, 7 + dx:rows - 9 + dx, :].astype(BF16)
 
 
@@ -191,7 +183,7 @@
 
 def interior(own, got, w1b, wfb, fd, cd, hd, pg, acc, fs, cs, hs, pre):
     gx = lax.axis_index("gx")
-    nx = own.shape[1]
+    nx, width = own.shape[1:]
     across = 2 * nx
     count = pg.shape[0]
     cells = count * across
@@ -199,9 +191,11 @@
     pairs = NZ // 2
 
     def place(left, right):
-        for scratch, start, size in ((fs, 0, count + 2), (cs, count + 2, count + 1)):
-            scratch[:, 8:8 + nx, :] = left[start:start + size].astype(F32)
-            scratch[:, 8 + nx:8 + across, :] = right[start:start + size].astype(F32)
+        for scratch, copies, offset, start, size in ((fs, fd, 2 - 2 * gx, 0, count + 2), (cs, cd, 1 - gx, count + 2, count + 1)):
+            for source, row in ((left, 0), (right, nx)):
+                rows = source[start:start + size]
+                scratch[:, 8 + row:8 + row + nx, :] = rows.astype(F32)
+                copies[1, pl.ds(offset, size), row:row + nx, lane:lane + width] = rows
 
     @pl.when(gx == 0)
     def _():
@@ -215,16 +209,18 @@
         blank_rows(scratch)
     blank_edges(fd)
     blank_edges(cd)
-    shift_rows(fs, fd, 2 - 2 * gx, lane)
-    shift_rows(cs, cd, 1 - gx, lane)
+    shift_rows(fs, fd, 2 - 2 * gx, lane, (0, 2))
+    shift_rows(cs, cd, 1 - gx, lane, (0, 2))
     for p in range(pairs + 1):
         here = slice(lane * p, lane * (p + 1))
         value = dot(windows(fd, 2 - 2 * gx, count, p), w1b[...])
         pre[:, :, here] = value.reshape(count, across, lane)
         hidden = value * jax.nn.sigmoid(value) * inside_lanes(p)
-        hs[:, 8:8 + across, here] = hidden.reshape(count, across, lane)
-    hd[:, pl.ds(8 * gx, 2)] = jnp.zeros((3, 2) + hd.shape[2:], BF16)
-    shift_rows(hs, hd, 2 - 2 * gx, 0)
+        hidden = hidden.reshape(count, across, lane)
+        hs[:, 8:8 + across, here] = hidden
+        hd[1, pl.ds(2 - 2 * gx, count), :, here] = hidden.astype(BF16)
+    hd[:, pl.ds(count * gx, 2)] = jnp.zeros((3, 2) + hd.shape[2:], BF16)
+    shift_rows(hs, hd, 2 - 2 * gx, 0, (0, 2))
     for p in range(pairs + 1):
         here = slice(lane * p, lane * (p + 1))
         grad = dot_nt(windows(cd, 1 - gx, count - 1, p), wfb[...])
@@ -271,8 +267,7 @@
     ]
 
 
-def folded(total, factor):
-    total = total * factor
+def folded(total):
     return total[0:C, 0:3 * C] + total[C:2 * C, C:4 * C]
 
 
@@ -309,8 +304,8 @@
     ]
 
 
-def sums_of(factor, products):
-    return packed([folded(product, factor) for product in products])
+def sums_of(products):
+    return packed([folded(product) for product in products])
 
 
 def store_blocks(target, blocks):
@@ -320,7 +315,7 @@
         target[BLOCKS * C:, :] = jnp.zeros((target.shape[0] - BLOCKS * C, 2 * C), target.dtype)
 
 
-def late_rows(factor, gy_count, fd_in, cd_in, hd_in, pg_in, rows, acc, w1b, wfb, fd, cd, hd, pg, send, rs, hs):
+def late_rows(gy_count, fd_in, cd_in, hd_in, pg_in, rows, acc, w1b, wfb, fd, cd, hd, pg, send, rs, hs):
     gx = lax.axis_index("gx")
     gy = lax.axis_index("gy")
     count, across, _ = pg.shape
@@ -347,26 +342,28 @@
 
     @pl.when(gx == 0)
     def _():
-        store_blocks(send, sums_of(factor, [acc[t] + late for t, late in enumerate(second_late(hd, cd))]))
+        store_blocks(send, sums_of([acc[t] + late for t, late in enumerate(second_late(hd, cd))]))
 
     @pl.when(gx != 0)
     def _():
-        store_blocks(send, sums_of(factor, [acc[t] + late for t, late in enumerate(first_late(fd, pg))]))
-
-
-def keep_sums(factor, fd, cd, hd, pg, keep):
+        store_blocks(send, sums_of([acc[t] + late for t, late in enumerate(first_late(fd, pg))]))
+
+
+def keep_sums(fd, cd, hd, pg, keep):
     gx = lax.axis_index("gx")
 
     @pl.when(gx == 0)
     def _():
-        store_blocks(keep, sums_of(factor, first_products(fd, pg)))
+        store_blocks(keep, sums_of(first_products(fd, pg)))
 
     @pl.when(gx != 0)
     def _():
-        store_blocks(keep, sums_of(factor, second_products(hd, cd)))
-
-
-def output_conv(hd, w2b, mine, given):
+        store_blocks(keep, sums_of(second_products(hd, cd)))
+
+
+def output_conv(hd, w2, mine, given, w2b):
+    for t, (dx, dy) in enumerate(TAPS):
+        w2b[t * 4 * C:(t + 1) * 4 * C, :] = band([w2[9 * dx + 3 * dy + z] for z in range(3)])
     gx = lax.axis_index("gx")
     count, half, _ = mine.shape
     lane = 2 * C
@@ -400,22 +397,25 @@
     out[...] = (keep[...] + other[...].astype(F32)).astype(BF16)
 
 
-def add_and_repeat(terms, out):
+def add_and_repeat(terms, out, held, sems):
     total = terms[0].astype(F32)
     for index in range(1, terms.shape[0]):
         total = total + terms[index].astype(F32)
-    total = total.astype(BF16)
-    for index in range(out.shape[0]):
-        out[index] = total
-
-
-def unpack(rows, held):
+    held[...] = total.astype(BF16)
+    copies = [pltpu.make_async_copy(held, out.at[index], sems.at[index]) for index in range(terms.shape[0])]
+    for copy in copies:
+        copy.start()
+    for copy in copies:
+        copy.wait()
+
+
+def unpack(factor, rows, held):
     for t, (dx, dy) in enumerate(TAPS):
-        turned = rows[t * C:(t + 1) * C, :].astype(F32).T
+        turned = rows[t * C:(t + 1) * C, :].astype(F32).T * factor
         held[9 * dx + 3 * dy] = turned[0:C]
         held[9 * dx + 3 * dy + 1] = turned[C:2 * C]
     for pair in range(5):
-        turned = rows[(9 + pair) * C:(10 + pair) * C, :].astype(F32).T
+        turned = rows[(9 + pair) * C:(10 + pair) * C, :].astype(F32).T * factor
         for half in range(2 if pair < 4 else 1):
             dx, dy = TAPS[2 * pair + half]
             held[9 * dx + 3 * dy + 2] = turned[half * C:(half + 1) * C]
@@ -430,13 +430,13 @@
             copy.wait()
 
 
-def unpack_own(rows, first, second, held, sem):
-    unpack(rows, held)
+def unpack_own(factor, rows, first, second, held, sem):
+    unpack(factor, rows, held)
     write_either(lax.axis_index("gx") == 0, held, first, second, sem)
 
 
-def unpack_other(rows, first_in, second_in, first, second, held, sem):
-    unpack(rows, held)
+def unpack_other(factor, rows, first_in, second_in, first, second, held, sem):
+    unpack(factor, rows, held)
     write_either(lax.axis_index("gx") != 0, held, first, second, sem)
 
 
@@ -486,20 +486,15 @@
         ],
         [pltpu.VMEM((6, nx, width), F32), pltpu.SemaphoreType.DMA((4,))])
     taken = swap(given)
-    own, bulk, w1b, w2b, wfb = call(
+    own, bulk, w1b, wfb = call(
         pack_halves, "pack_halves", [(x, True) for x in (field, cot, w1, w2)],
         [
             near((size, nx, width), BF16),
             near((size, nx, width), BF16),
             near((9 * 4 * C, lane), BF16),
-            near((9 * 4 * C, lane), BF16),
             near((lane, 9 * 4 * C), BF16),
         ],
-        [
-            pltpu.VMEM((ny, nx, width), BF16),
-            pltpu.VMEM((ny, nx, width), BF16),
-            pltpu.VMEM((width // lane, nx * ny, lane), F32),
-        ], flops=10 ** 9)
+        [pltpu.VMEM((width // lane, nx * ny, lane), F32)] * 2, flops=10 ** 9)
     bulk, taken, wfb = lax.optimization_barrier((bulk, taken, wfb))
     got = swap(bulk)
     whole, = call(join_edges, "join_edges", [(edge, True), (taken, True)], [near((3, across, width), BF16)])
@@ -523,7 +518,7 @@
         ],
         limit=32, flops=4 * 10 ** 9)
     fd, cd, hd, pg, send = call(
-        functools.partial(late_rows, factor, gy_count), "late_rows",
+        functools.partial(late_rows, gy_count), "late_rows",
         [(x, True) for x in (fd, cd, hd, pg, late, acc, w1b, wfb)],
         held + [near((rows, lane), BF16)],
         [pltpu.VMEM((3, across + 16, width), F32), pltpu.VMEM((2, across + 16, width + lane), F32)],
@@ -531,17 +526,20 @@
 
     other = swap(send)
     keep, = call(
-        functools.partial(keep_sums, factor), "keep_sums",
+        keep_sums, "keep_sums",
         [(x, True) for x in (fd, cd, hd, pg)], [near((rows, lane), F32)], flops=2 * 10 ** 9)
     other, keep = lax.optimization_barrier((other, keep))
     both, = call(add_pair, "add_pair", [(keep, True), (other, True)], [near((rows, lane), BF16)])
     terms = lax.all_to_all(both.reshape(ranks, rows // ranks, lane), ("gy", "grp"), 0, 0)
-    spread, = call(add_and_repeat, "add_and_repeat", [(terms, True)], [near(terms.shape, BF16)])
-    spread, hd, w2b = lax.optimization_barrier((spread, hd, w2b))
+    spread, = call(
+        add_and_repeat, "add_and_repeat", [(terms, True)], [pltpu.HBM(terms.shape, BF16)],
+        [pltpu.VMEM(terms.shape[1:], BF16), pltpu.SemaphoreType.DMA((ranks,))], far=True)
+    spread, hd, w2 = lax.optimization_barrier((spread, hd, w2))
     sums = lax.all_to_all(spread, ("gy", "grp"), 0, 0).reshape(rows, lane)
     mine, given = call(
-        output_conv, "output_conv", [(hd, True), (w2b, True)],
-        [near((count, nx, width), BF16), near((count, nx, width), BF16)], flops=2 * 10 ** 9)
+        output_conv, "output_conv", [(hd, True), (w2, True)],
+        [near((count, nx, width), BF16), near((count, nx, width), BF16)],
+        [pltpu.VMEM((9 * 4 * C, lane), BF16)], flops=2 * 10 ** 9)
     given = swap(given)
     out, = call(
         finish_output, "finish_output", [(mine, True), (given, True)],
@@ -551,10 +549,10 @@
     other = swap(sums)
     outs = [pltpu.HBM((27, C, C), F32)] * 2
     scratch = [pltpu.VMEM((27, C, C), F32), pltpu.SemaphoreType.DMA((1,))]
-    first, second = call(unpack_own, "unpack_own", [(sums, True)], outs, scratch, far=True)
+    first, second = call(functools.partial(unpack_own, factor), "unpack_own", [(sums, True)], outs, scratch, far=True)
     other, first, second = lax.optimization_barrier((other, first, second))
     first, second = call(
-        unpack_other, "unpack_other", [(other, True), (first, False), (second, False)], outs, scratch, far=True,
+        functools.partial(unpack_other, factor), "unpack_other", [(other, True), (first, False), (second, False)], outs, scratch, far=True,
         aliases={1: 0, 2: 1})
     shape = (3, 3, 3, C, C)
     return out[None], first.reshape(shape), second.reshape(shape)

time: 47.8 us -> 47.9 us (level)
  transfers between devices with their start and end apart: 7 -> 7, of which waited for: 4 -> 5; matrix products, arithmetic and copies ran while one was open for 0% -> 0% of each run, Pallas kernels for 21% -> 20%
where the time goes in v11:
time: 47.9 us; the launch traced here: 47.6 us
  blocking collectives  16.1 us (34%)
  Pallas kernels  14.3 us (30%)
  starting transfers between devices  8.86 us (18%)
  waiting for transfers between devices  7.52 us (16%)
  between operations  0.75 us (2%)
    all_to_all x1, blocking collectives, shards(): lax.all_to_all(both.reshape(ranks, rows // ranks, lane), ('gy', 'grp'), 0...  16.1 us
    pallas_call x12, Pallas kernels, call(): pl.pallas_call(body, out_shape=list(outs), in_specs=[pl.BlockSpec(memory_...  14.3 us
    all_to_all x1, waiting for transfers between devices, shards(): sums = lax.all_to_all(spread, ('gy', 'grp'), 0, 0).reshape(rows, lane)  5.1 us
    ppermute x5, starting transfers between devices, swap(): return lax.ppermute(array, 'gx', [(0, 1), (1, 0)])  4.66 us
    all_to_all x1, starting transfers between devices, shards(): sums = lax.all_to_all(spread, ('gy', 'grp'), 0, 0).reshape(rows, lane)  3.54 us
    ppermute x5, waiting for transfers between devices, swap(): return lax.ppermute(array, 'gx', [(0, 1), (1, 0)])  2.42 us
  transfers between devices with their start and end apart: 7, of which 5 were waited for; matrix products, arithmetic and copies ran while one was open for 0% of the time, Pallas kernels for 20%

profile of v11, /device:TPU:0, one launch (start us, length us, event | category | flops | bytes accessed | tf_op | source)
XLA Modules:
  0.0 47.6 jit_solution(11002545680012869747)
XLA Ops:
  0.6 1.3 %pack_edges.1 = (bf16[8,16,1024]{2,1,0:T(8,128)(2,1)S(1)}, bf16[8,16,1024]{2,1,0:T(8,128)(2,1)S(1)}, bf16[3,8,1024]{2,1,0:T(8,128)(2,1)S(1)}, bf16[3,8,1024]{2,1...) custom-call(bf16[8,16,1024]{2,1,0:T(8,128)(2,1)} %bitcast.17, ...), custom_call_target="tpu_custom_call" | custom-call | bytes 966656 | tf_op jit(solution)/shard_map/pack_edges/pallas_call | solution.py:450
  2.0 0.5 %collective-permute-start = (bf16[3,8,1024]{2,1,0:T(8,128)(2,1)S(1)}, bf16[3,8,1024]{2,1,0:T(8,128)(2,1)S(1)}, u32[]{:S(2)}, u32[]{:S(2)}) collective-permute-start(bf16[3,8,1024]{2,1,0:T(8,128)(2,1)S(1)} %get-tuple-element.48), channel_id=1, source_target_pairs={{0,16},{16,0},{1,17},{17,1},{2,18},{18,2},{3,19},{19,3},{4,20},{20... | collective-permute-start | bytes 147464 | tf_op jit(solution)/shard_map/ppermute | solution.py:20
  2.5 0.7 %pack_halves.1 = (bf16[19,8,1024]{2,1,0:T(8,128)(2,1)S(1)}, bf16[19,8,1024]{2,1,0:T(8,128)(2,1)S(1)}, bf16[2304,128]{1,0:T(8,128)(2,1)S(1)}, bf16[128,2304]{1,0:T(8,128)(2,1)S(1)}) custom-call(bf16[8,16,1024]{2,1,0:T(8,128)(2,1)S(1)} %get-tuple-element.42.field, bf16[8,16,1024]{2,1,0:T(8,128)(2,1)S(1)} %get-tuple-element.43.cot, ...), custom_call_target="tpu_custom_call" | custom-call | flops 1000000000 | bytes 966656 | tf_op jit(solution)/shard_map/pack_halves/pallas_call | solution.py:450
  3.2 0.2 collective-permute-done.taken
  3.4 0.3 collective-permute-start.1
  3.7 0.7 %collective-permute-start.2 = (bf16[3,16,1024]{2,1,0:T(8,128)(2,1)S(1)}, bf16[3,16,1024]{2,1,0:T(8,128)(2,1)S(1)}, u32[]{:S(2)}, u32[]{:S(2)}) collective-permute-start(bf16[3,16,1024]{2,1,0:T(8,128)(2,1)S(1)} %join_edges.1), channel_id=1, source_target_pairs={{16,4},{20,8},{24,12},{4,16},{8,20},{12,24},{17,5},{21,9},{25,13},... | collective-permute-start | bytes 294920 | tf_op jit(solution)/shard_map/ppermute | solution.py:502
  4.4 0.6 %collective-permute-done.1.got = bf16[19,8,1024]{2,1,0:T(8,128)(2,1)S(1)} collective-permute-done((bf16[19,8,1024]{2,1,0:T(8,128)(2,1)S(1)}, bf16[19,8,1024]{2,1,0:T(8,128)(2,1)S(1)}, u32[]{:S(2)}, u32[]{:S(2)}) %collective-permute-start.1) | collective-permute-done | bytes 311328 | tf_op jit(solution)/shard_map/ppermute | solution.py:20
  5.0 4.4 %interior.1 = (bf16[3,12,16,1280]{3,2,1,0:T(8,128)(2,1)S(1)}, bf16[3,10,16,1280]{3,2,1,0:T(8,128)(2,1)S(1)}, bf16[3,10,16,1152]{3,2,1,0:T(8,128)(2,1)S(1)}, bf16...) custom-call(bf16[19,8,1024]{2,1,0:T(8,128)(2,1)S(1)} %get-tuple-element.46.own, ...), custom_call_target="tpu_custom_call" | custom-call | flops 4000000000 | bytes 1802240 | tf_op jit(solution)/shard_map/interior/pallas_call | solution.py:450
  9.4 0.0 collective-permute-done.2.rows
  9.4 1.3 %late_rows.1 = (bf16[3,12,16,1280]{3,2,1,0:T(8,128)(2,1)S(1)}, bf16[3,10,16,1280]{3,2,1,0:T(8,128)(2,1)S(1)}, bf16[3,10,16,1152]{3,2,1,0:T(8,128)(2,1)S(1)}, bf1...) custom-call(bf16[3,12,16,1280]{3,2,1,0:T(8,128)(2,1)S(1)} %get-tuple, ...), custom_call_target="tpu_custom_call", output_to_operand_aliasing={{0}: (0, {}), {1}: (1, {}), {2}: (2, {}), {3}: (3, {})} | custom-call | flops 1000000000 | bytes 6561792 | tf_op jit(solution)/shard_map/late_rows/pallas_call | solution.py:450
  10.7 3.7 %collective-permute-start.3 = (bf16[896,128]{1,0:T(8,128)(2,1)S(1)}, bf16[896,128]{1,0:T(8,128)(2,1)S(1)}, u32[]{:S(2)}, u32[]{:S(2)}) collective-permute-start(bf16[896,128]{1,0:T(8,128)(2,1)S(1)} %get-tuple-element.60), channel_id=1, source_target_pairs={{0,16},{16,0},{1,17},{17,1},{2,18},{18,2},{3,19},{19,3},{4,20},{20... | collective-permute-start | bytes 688136 | tf_op jit(solution)/shard_map/ppermute | solution.py:20
  14.4 1.1 %keep_sums.1.keep = f32[896,128]{1,0:T(8,128)S(1)} custom-call(bf16[3,12,16,1280]{3,2,1,0:T(8,128)(2,1)S(1)} %get-tuple-element.61.fd, bf16[3,10,16,1280]{3,2,1,0:T(8,128)(2,1)S(1)} %get-tuple-element.62.cd, bf16[3,10,16,1152]{3,2,1,0:T(8,128)(2,1)S(1)} %get-tuple-element.68.hd, bf16[8,16,1152]{2,1,0:T(8,128)(2,1)S(1)} %get-tuple-element.64.pg), custom_call_target="tpu_custom_call" | custom-call | flops 2000000000 | bytes 4104192 | tf_op jit(solution)/shard_map/keep_sums/pallas_call | solution.py:450
  15.5 0.0 collective-permute-done.3.other
  15.6 16.1 %all_to_all.10.terms = bf16[16,56,128]{2,1,0:T(8,128)(2,1)S(1)} all-to-all(bf16[16,56,128]{2,1,0:T(8,128)(2,1)S(1)} %bitcast.9), channel_id=1, replica_groups=mesh['gx'=2,'gy'=4,'grp'=4] {'gy','grp'}, dimensions={0} | all-to-all | bytes 458752 | tf_op jit(solution)/shard_map/all_to_all | solution.py:533
  31.7 0.8 %add_and_repeat.1 = bf16[16,56,128]{2,1,0:T(8,128)(2,1)} custom-call(bf16[16,56,128]{2,1,0:T(8,128)(2,1)S(1)} %all_to_all.10.terms), custom_call_target="tpu_custom_call" | custom-call | bytes 229376 | tf_op jit(solution)/shard_map/add_and_repeat/pallas_call | solution.py:450
  32.5 3.5 %all-to-all-start.1 = ((bf16[16,56,128]{2,1,0:T(8,128)(2,1)}), bf16[16,56,128]{2,1,0:T(8,128)(2,1)S(1)}, u32[]{:S(2)}, u32[]{:S(2)}) async-start(bf16[16,56,128]{2,1,0:T(8,128)(2,1)} %add_and_repeat.1), calls=%async_computation.1 | async-start | bytes 458752 | tf_op jit(solution)/shard_map/all_to_all | solution.py:538
  36.1 1.5 %output_conv.1 = (bf16[8,8,1024]{2,1,0:T(8,128)(2,1)S(1)}, bf16[8,8,1024]{2,1,0:T(8,128)(2,1)S(1)}) custom-call(bf16[3,10,16,1152]{3,2,1,0:T(8,128)(2,1)S(1)} %get-tuple-element.68.hd, bf16[27,64,64]{2,1,0:T(8,128)(2,1)S(1)} %get-tuple-element.69.w2), custom_call_target="tpu_custom_call" | custom-call | flops 2000000000 | bytes 1327104 | tf_op jit(solution)/shard_map/output_conv/pallas_call | solution.py:450
  37.6 0.1 collective-permute-start.4
  37.7 1.3 %collective-permute-done.4.other = bf16[8,8,1024]{2,1,0:T(8,128)(2,1)S(1)} collective-permute-done((bf16[8,8,1024]{2,1,0:T(8,128)(2,1)S(1)}, bf16[8,8,1024]{2,1,0:T(8,128)(2,1)S(1)}, u32[]{:S(2)}, u32[]{:S(2)}) %collective-permute-start.4) | collective-permute-done | bytes 131104 | tf_op jit(solution)/shard_map/ppermute | solution.py:20
  39.0 0.8 %finish_output.1 = bf16[8,16,1024]{2,1,0:T(8,128)(2,1)} custom-call(bf16[8,8,1024]{2,1,0:T(8,128)(2,1)S(1)} %get-tuple-element.70.mine, bf16[8,8,1024]{2,1,0:T(8,128)(2,1)S(1)} %collective-permute-done.4.other), custom_call_target="tpu_custom_call" | custom-call | bytes 262144 | tf_op jit(solution)/shard_map/finish_output/pallas_call | solution.py:450
  39.9 5.1 %all-to-all-done.1 = bf16[16,56,128]{2,1,0:T(8,128)(2,1)S(1)} async-done(((bf16[16,56,128]{2,1,0:T(8,128)(2,1)}), bf16[16,56,128]{2,1,0:T(8,128)(2,1)S(1)}, u32[]{:S(2)}, u32[]{:S(2)}) %all-to-all-start.1) | async-done | bytes 229408 | tf_op jit(solution)/shard_map/all_to_all | solution.py:538
  45.0 1.1 %unpack_own.1 = (f32[27,64,64]{2,1,0:T(8,128)}, f32[27,64,64]{2,1,0:T(8,128)}) custom-call(bf16[896,128]{1,0:T(8,128)(2,1)S(1)} %bitcast.11), custom_call_target="tpu_custom_call" | custom-call | bytes 229376 | tf_op jit(solution)/shard_map/unpack_own/pallas_call | solution.py:450
  46.1 0.3 collective-permute-done.5.rows
  46.4 1.1 %unpack_other.1 = (f32[27,64,64]{2,1,0:T(8,128)}, f32[27,64,64]{2,1,0:T(8,128)}) custom-call(bf16[896,128]{1,0:T(8,128)(2,1)S(1)} %collective-permute-done.5.rows, f32[27,64,64]{2,1,0:T(8,128)} %get-tuple-element.77.first_in, f32[27,64,64]{2,1,0:T(8,128)} %get-tuple-element.78.second_in), custom_call_target="tpu_custom_call", output_to_operand_aliasing={{0}: (1, {}), {1}: (2, {})} | custom-call | bytes 1114112 | tf_op jit(solution)/shard_map/unpack_other/pallas_call | solution.py:450
  (3 shorter events, 0.1 us)
Async XLA Ops:
  2.0 1.4 %collective-permute-start = (bf16[3,8,1024]{2,1,0:T(8,128)(2,1)S(1)}, bf16[3,8,1024]{2,1,0:T(8,128)(2,1)S(1)}, u32[]{:S(2)}, u32[]{:S(2)}) collective-permute-start(bf16[3,8,1024]{2,1,0:T(8,128)(2,1)S(1)} %get-tuple-element.48), channel_id=1, source_target_pairs={{0,16},{16,0},{1,17},{17,1},{2,18},{18,2},{3,19},{19,3},{4,20},{20... | collective-permute-start | bytes 147464 | tf_op jit(solution)/shard_map/ppermute | solution.py:20
  3.4 1.6 %collective-permute-start.1 = (bf16[19,8,1024]{2,1,0:T(8,128)(2,1)S(1)}, bf16[19,8,1024]{2,1,0:T(8,128)(2,1)S(1)}, u32[]{:S(2)}, u32[]{:S(2)}) collective-permute-start(bf16[19,8,1024]{2,1,0:T(8,128)(2,1)S(1)} %get-tuple-element.50), channel_id=1, source_target_pairs={{0,16},{16,0},{1,17},{17,1},{2,18},{18,2},{3,19},{19,3},{4,20},{20... | collective-permute-start | bytes 933896 | tf_op jit(solution)/shard_map/ppermute | solution.py:20
  3.7 5.6 %collective-permute-start.2 = (bf16[3,16,1024]{2,1,0:T(8,128)(2,1)S(1)}, bf16[3,16,1024]{2,1,0:T(8,128)(2,1)S(1)}, u32[]{:S(2)}, u32[]{:S(2)}) collective-permute-start(bf16[3,16,1024]{2,1,0:T(8,128)(2,1)S(1)} %join_edges.1), channel_id=1, source_target_pairs={{16,4},{20,8},{24,12},{4,16},{8,20},{12,24},{17,5},{21,9},{25,13},... | collective-permute-start | bytes 294920 | tf_op jit(solution)/shard_map/ppermute | solution.py:502
  10.7 4.8 %collective-permute-start.3 = (bf16[896,128]{1,0:T(8,128)(2,1)S(1)}, bf16[896,128]{1,0:T(8,128)(2,1)S(1)}, u32[]{:S(2)}, u32[]{:S(2)}) collective-permute-start(bf16[896,128]{1,0:T(8,128)(2,1)S(1)} %get-tuple-element.60), channel_id=1, source_target_pairs={{0,16},{16,0},{1,17},{17,1},{2,18},{18,2},{3,19},{19,3},{4,20},{20... | collective-permute-start | bytes 688136 | tf_op jit(solution)/shard_map/ppermute | solution.py:20
  32.5 12.4 %all-to-all-start.1 = ((bf16[16,56,128]{2,1,0:T(8,128)(2,1)}), bf16[16,56,128]{2,1,0:T(8,128)(2,1)S(1)}, u32[]{:S(2)}, u32[]{:S(2)}) async-start(bf16[16,56,128]{2,1,0:T(8,128)(2,1)} %add_and_repeat.1), calls=%async_computation.1 | async-start | bytes 458752 | tf_op jit(solution)/shard_map/all_to_all | solution.py:538
  37.6 1.4 %collective-permute-start.4 = (bf16[8,8,1024]{2,1,0:T(8,128)(2,1)S(1)}, bf16[8,8,1024]{2,1,0:T(8,128)(2,1)S(1)}, u32[]{:S(2)}, u32[]{:S(2)}) collective-permute-start(bf16[8,8,1024]{2,1,0:T(8,128)(2,1)S(1)} %get-tuple-element.71), channel_id=1, source_target_pairs={{0,16},{16,0},{1,17},{17,1},{2,18},{18,2},{3,19},{19,3},{4,20},{20... | collective-permute-start | bytes 393224 | tf_op jit(solution)/shard_map/ppermute | solution.py:20
  45.0 1.5 %collective-permute-start.5 = (bf16[896,128]{1,0:T(8,128)(2,1)S(1)}, bf16[896,128]{1,0:T(8,128)(2,1)S(1)}, u32[]{:S(2)}, u32[]{:S(2)}) collective-permute-start(bf16[896,128]{1,0:T(8,128)(2,1)S(1)} %bitcast.10), channel_id=1, source_target_pairs={{0,16},{16,0},{1,17},{17,1},{2,18},{18,2},{3,19},{19,3},{4,20},{20... | collective-permute-start | bytes 688136 | tf_op jit(solution)/shard_map/ppermute | solution.py:20

commit v12 on v11

--- a/solution.py
+++ b/solution.py
@@ -181,7 +181,7 @@
     return grad * sigma * (1.0 + pre * (1.0 - sigma)) * inside_lanes(p)
 
 
-def interior(own, got, w1b, wfb, fd, cd, hd, pg, acc, fs, cs, hs, pre):
+def interior(own, got, w1b, wfb, fd, cd, hd, pg, hs, acc, fs, cs, pre):
     gx = lax.axis_index("gx")
     nx, width = own.shape[1:]
     across = 2 * nx
@@ -211,25 +211,29 @@
     blank_edges(cd)
     shift_rows(fs, fd, 2 - 2 * gx, lane, (0, 2))
     shift_rows(cs, cd, 1 - gx, lane, (0, 2))
-    for p in range(pairs + 1):
-        here = slice(lane * p, lane * (p + 1))
-        value = dot(windows(fd, 2 - 2 * gx, count, p), w1b[...])
-        pre[:, :, here] = value.reshape(count, across, lane)
-        hidden = value * jax.nn.sigmoid(value) * inside_lanes(p)
-        hidden = hidden.reshape(count, across, lane)
-        hs[:, 8:8 + across, here] = hidden
-        hd[1, pl.ds(2 - 2 * gx, count), :, here] = hidden.astype(BF16)
-    hd[:, pl.ds(count * gx, 2)] = jnp.zeros((3, 2) + hd.shape[2:], BF16)
-    shift_rows(hs, hd, 2 - 2 * gx, 0, (0, 2))
-    for p in range(pairs + 1):
-        here = slice(lane * p, lane * (p + 1))
-        grad = dot_nt(windows(cd, 1 - gx, count - 1, p), wfb[...])
-        grad = pre_gradient(grad, pre[pl.ds(gx, count - 1), :, here].reshape((count - 1) * across, lane), p)
-        pg[pl.ds(1 - gx, count - 1), :, here] = grad.astype(BF16).reshape(count - 1, across, lane)
+    for group in range(0, pairs + 1, 3):
+        value = dot(jnp.concatenate([windows(fd, 2 - 2 * gx, count, p) for p in range(group, group + 3)], axis=0), w1b[...])
+        for p in range(group, group + 3):
+            here = slice(lane * p, lane * (p + 1))
+            part = value[cells * (p - group):cells * (p - group + 1)]
+            pre[:, :, here] = part.reshape(count, across, lane)
+            hidden = (part * jax.nn.sigmoid(part) * inside_lanes(p)).reshape(count, across, lane)
+            hs[pl.ds(2 - 2 * gx, count), 8:8 + across, here] = hidden
+            hd[1, pl.ds(2 - 2 * gx, count), :, here] = hidden.astype(BF16)
+    cells = cells - across
+    for group in range(0, pairs + 1, 3):
+        value = dot_nt(jnp.concatenate([windows(cd, 1 - gx, count - 1, p) for p in range(group, group + 3)], axis=0), wfb[...])
+        for p in range(group, group + 3):
+            here = slice(lane * p, lane * (p + 1))
+            part = value[cells * (p - group):cells * (p - group + 1)]
+            grad = pre_gradient(part, pre[pl.ds(gx, count - 1), :, here].reshape(cells, lane), p)
+            pg[pl.ds(1 - gx, count - 1), :, here] = grad.astype(BF16).reshape(count - 1, across, lane)
     pg[pl.ds((count - 1) * gx, 1)] = jnp.zeros((1,) + pg.shape[1:], BF16)
 
     @pl.when(gx == 0)
     def _():
+        hd[:, 0:2] = jnp.zeros((3, 2) + hd.shape[2:], BF16)
+        shift_rows(hs.at[2:2 + count], hd, 2, 0, (0, 2))
         for t, total in enumerate(second_products(hd, cd)):
             acc[t] = total
 
@@ -315,7 +319,7 @@
         target[BLOCKS * C:, :] = jnp.zeros((target.shape[0] - BLOCKS * C, 2 * C), target.dtype)
 
 
-def late_rows(gy_count, fd_in, cd_in, hd_in, pg_in, rows, acc, w1b, wfb, fd, cd, hd, pg, send, rs, hs):
+def late_rows(gy_count, fd_in, cd_in, hd_in, pg_in, hs_in, rows, acc, w1b, wfb, fd, cd, hd, pg, hs, send, rs):
     gx = lax.axis_index("gx")
     gy = lax.axis_index("gy")
     count, across, _ = pg.shape
@@ -323,7 +327,6 @@
     pairs = NZ // 2
     rs[:, 8:8 + across, :] = rows[...].astype(F32)
     blank_rows(rs)
-    blank_rows(hs)
     shift_rows(rs.at[0:2], fd, (count + 2) * gx, lane)
     shift_rows(rs.at[2:3], cd, (count + 1) * gx, lane)
     value = dot(jnp.concatenate([windows(fd, count * gx, 2, p) for p in range(pairs + 1)], axis=0), w1b[...])
@@ -334,14 +337,18 @@
         here = slice(lane * p, lane * (p + 1))
         early = value[2 * across * p:2 * across * p + across]
         later = value[2 * across * p + across:2 * across * (p + 1)]
-        hs[0, 8:8 + across, here] = early * jax.nn.sigmoid(early) * inside_lanes(p) * before
-        hs[1, 8:8 + across, here] = later * jax.nn.sigmoid(later) * inside_lanes(p) * beyond
+        both = jnp.stack([
+            early * jax.nn.sigmoid(early) * inside_lanes(p) * before,
+            later * jax.nn.sigmoid(later) * inside_lanes(p) * beyond,
+        ])
+        hs[pl.ds(count * gx, 2), 8:8 + across, here] = both
+        hd[1, pl.ds(count * gx, 2), :, here] = both.astype(BF16)
         mine = pre_gradient(grad[across * p:across * (p + 1)], jnp.where(gx == 0, later, early), p)
         pg[pl.ds((count - 1) * gx, 1), :, here] = mine.astype(BF16)[None]
-    shift_rows(hs, hd, count * gx, 0)
 
     @pl.when(gx == 0)
     def _():
+        shift_rows(hs.at[0:2], hd, 0, 0, (0, 2))
         store_blocks(send, sums_of([acc[t] + late for t, late in enumerate(second_late(hd, cd))]))
 
     @pl.when(gx != 0)
@@ -349,7 +356,7 @@
         store_blocks(send, sums_of([acc[t] + late for t, late in enumerate(first_late(fd, pg))]))
 
 
-def keep_sums(fd, cd, hd, pg, keep):
+def keep_sums(fd, cd, hd_in, pg, hs, hd, keep):
     gx = lax.axis_index("gx")
 
     @pl.when(gx == 0)
@@ -358,6 +365,7 @@
 
     @pl.when(gx != 0)
     def _():
+        shift_rows(hs, hd, 0, 0, (0, 2))
         store_blocks(keep, sums_of(second_products(hd, cd)))
 
 
@@ -397,16 +405,13 @@
     out[...] = (keep[...] + other[...].astype(F32)).astype(BF16)
 
 
-def add_and_repeat(terms, out, held, sems):
+def add_and_repeat(terms, out):
     total = terms[0].astype(F32)
     for index in range(1, terms.shape[0]):
         total = total + terms[index].astype(F32)
-    held[...] = total.astype(BF16)
-    copies = [pltpu.make_async_copy(held, out.at[index], sems.at[index]) for index in range(terms.shape[0])]
-    for copy in copies:
-        copy.start()
-    for copy in copies:
-        copy.wait()
+    total = total.astype(BF16)
+    for index in range(out.shape[0]):
+        out[index] = total
 
 
 def unpack(factor, rows, held):
@@ -505,35 +510,33 @@
         near((3, count + 2, across, wide), BF16),
         near((3, count + 2, across, width + lane), BF16),
         near((count, across, width + lane), BF16),
+        near((count + 2, across + 16, width + lane), F32),
     ]
-    fd, cd, hd, pg, acc = call(
+    fd, cd, hd, pg, hs, acc = call(
         interior, "interior",
         [(x, True) for x in (own, got, w1b, wfb)],
         held + [near((9, lane, 2 * lane), F32)],
         [
             pltpu.VMEM((count + 2, across + 16, width), F32),
             pltpu.VMEM((count + 1, across + 16, width), F32),
-            pltpu.VMEM((count, across + 16, width + lane), F32),
             pltpu.VMEM((count, across, width + lane), F32),
         ],
         limit=32, flops=4 * 10 ** 9)
-    fd, cd, hd, pg, send = call(
+    fd, cd, hd, pg, hs, send = call(
         functools.partial(late_rows, gy_count), "late_rows",
-        [(x, True) for x in (fd, cd, hd, pg, late, acc, w1b, wfb)],
+        [(x, True) for x in (fd, cd, hd, pg, hs, late, acc, w1b, wfb)],
         held + [near((rows, lane), BF16)],
-        [pltpu.VMEM((3, across + 16, width), F32), pltpu.VMEM((2, across + 16, width + lane), F32)],
-        limit=32, flops=10 ** 9, aliases={0: 0, 1: 1, 2: 2, 3: 3})
+        [pltpu.VMEM((3, across + 16, width), F32)],
+        limit=32, flops=10 ** 9, aliases={0: 0, 1: 1, 2: 2, 3: 3, 4: 4})
 
     other = swap(send)
-    keep, = call(
+    hd, keep = call(
         keep_sums, "keep_sums",
-        [(x, True) for x in (fd, cd, hd, pg)], [near((rows, lane), F32)], flops=2 * 10 ** 9)
+        [(x, True) for x in (fd, cd, hd, pg, hs)], [held[2], near((rows, lane), F32)], flops=2 * 10 ** 9, aliases={2: 0})
     other, keep = lax.optimization_barrier((other, keep))
     both, = call(add_pair, "add_pair", [(keep, True), (other, True)], [near((rows, lane), BF16)])
     terms = lax.all_to_all(both.reshape(ranks, rows // ranks, lane), ("gy", "grp"), 0, 0)
-    spread, = call(
-        add_and_repeat, "add_and_repeat", [(terms, True)], [pltpu.HBM(terms.shape, BF16)],
-        [pltpu.VMEM(terms.shape[1:], BF16), pltpu.SemaphoreType.DMA((ranks,))], far=True)
+    spread, = call(add_and_repeat, "add_and_repeat", [(terms, True)], [near(terms.shape, BF16)])
     spread, hd, w2 = lax.optimization_barrier((spread, hd, w2))
     sums = lax.all_to_all(spread, ("gy", "grp"), 0, 0).reshape(rows, lane)
     mine, given = call(

time: 47.9 us -> 47.3 us (0.987)
  Pallas kernels: 14.3 us -> 13.8 us
    pallas_call x12, Pallas kernels: 14.3 us -> 13.8 us  [call(): pl.pallas_call(body, out_shape=list(outs), in_specs=[pl.BlockSpec(memory_...]
where the time goes in v12:
time: 47.3 us; the launch traced here: 47 us
  blocking collectives  16.2 us (34%)
  Pallas kernels  13.8 us (29%)
  starting transfers between devices  8.75 us (18%)
  waiting for transfers between devices  7.5 us (16%)
  between operations  0.74 us (2%)
    all_to_all x1, blocking collectives, shards(): lax.all_to_all(both.reshape(ranks, rows // ranks, lane), ('gy', 'grp'), 0...  16.2 us
    pallas_call x12, Pallas kernels, call(): pl.pallas_call(body, out_shape=list(outs), in_specs=[pl.BlockSpec(memory_...  13.8 us
    all_to_all x1, waiting for transfers between devices, shards(): sums = lax.all_to_all(spread, ('gy', 'grp'), 0, 0).reshape(rows, lane)  5.08 us
    ppermute x5, starting transfers between devices, swap(): return lax.ppermute(array, 'gx', [(0, 1), (1, 0)])  4.56 us
    all_to_all x1, starting transfers between devices, shards(): sums = lax.all_to_all(spread, ('gy', 'grp'), 0, 0).reshape(rows, lane)  3.53 us
    ppermute x5, waiting for transfers between devices, swap(): return lax.ppermute(array, 'gx', [(0, 1), (1, 0)])  2.42 us
  transfers between devices with their start and end apart: 7, of which 5 were waited for; matrix products, arithmetic and copies ran while one was open for 0% of the time, Pallas kernels for 20%

profile of v12, /device:TPU:0, one launch (start us, length us, event | category | flops | bytes accessed | tf_op | source)
XLA Modules:
  0.0 47.0 jit_solution(10923496678994850181)
XLA Ops:
  0.6 1.3 %pack_edges.1 = (bf16[8,16,1024]{2,1,0:T(8,128)(2,1)S(1)}, bf16[8,16,1024]{2,1,0:T(8,128)(2,1)S(1)}, bf16[3,8,1024]{2,1,0:T(8,128)(2,1)S(1)}, bf16[3,8,1024]{2,1...) custom-call(bf16[8,16,1024]{2,1,0:T(8,128)(2,1)} %bitcast.17, ...), custom_call_target="tpu_custom_call" | custom-call | bytes 966656 | tf_op jit(solution)/shard_map/pack_edges/pallas_call | solution.py:455
  2.0 0.5 %collective-permute-start = (bf16[3,8,1024]{2,1,0:T(8,128)(2,1)S(1)}, bf16[3,8,1024]{2,1,0:T(8,128)(2,1)S(1)}, u32[]{:S(2)}, u32[]{:S(2)}) collective-permute-start(bf16[3,8,1024]{2,1,0:T(8,128)(2,1)S(1)} %get-tuple-element.52), channel_id=1, source_target_pairs={{0,16},{16,0},{1,17},{17,1},{2,18},{18,2},{3,19},{19,3},{4,20},{20... | collective-permute-start | bytes 147464 | tf_op jit(solution)/shard_map/ppermute | solution.py:20
  2.5 0.7 %pack_halves.1 = (bf16[19,8,1024]{2,1,0:T(8,128)(2,1)S(1)}, bf16[19,8,1024]{2,1,0:T(8,128)(2,1)S(1)}, bf16[2304,128]{1,0:T(8,128)(2,1)S(1)}, bf16[128,2304]{1,0:T(8,128)(2,1)S(1)}) custom-call(bf16[8,16,1024]{2,1,0:T(8,128)(2,1)S(1)} %get-tuple-element.46.field, bf16[8,16,1024]{2,1,0:T(8,128)(2,1)S(1)} %get-tuple-element.47.cot, ...), custom_call_target="tpu_custom_call" | custom-call | flops 1000000000 | bytes 966656 | tf_op jit(solution)/shard_map/pack_halves/pallas_call | solution.py:455
  3.2 0.2 collective-permute-done.taken
  3.4 0.3 collective-permute-start.1
  3.7 0.7 %collective-permute-start.2 = (bf16[3,16,1024]{2,1,0:T(8,128)(2,1)S(1)}, bf16[3,16,1024]{2,1,0:T(8,128)(2,1)S(1)}, u32[]{:S(2)}, u32[]{:S(2)}) collective-permute-start(bf16[3,16,1024]{2,1,0:T(8,128)(2,1)S(1)} %join_edges.1), channel_id=1, source_target_pairs={{16,4},{20,8},{24,12},{4,16},{8,20},{12,24},{17,5},{21,9},{25,13},... | collective-permute-start | bytes 294920 | tf_op jit(solution)/shard_map/ppermute | solution.py:507
  4.4 0.6 %collective-permute-done.1.got = bf16[19,8,1024]{2,1,0:T(8,128)(2,1)S(1)} collective-permute-done((bf16[19,8,1024]{2,1,0:T(8,128)(2,1)S(1)}, bf16[19,8,1024]{2,1,0:T(8,128)(2,1)S(1)}, u32[]{:S(2)}, u32[]{:S(2)}) %collective-permute-start.1) | collective-permute-done | bytes 311328 | tf_op jit(solution)/shard_map/ppermute | solution.py:20
  5.0 4.0 %interior.1 = (bf16[3,12,16,1280]{3,2,1,0:T(8,128)(2,1)S(1)}, bf16[3,10,16,1280]{3,2,1,0:T(8,128)(2,1)S(1)}, bf16[3,10,16,1152]{3,2,1,0:T(8,128)(2,1)S(1)}, bf16...) custom-call(bf16[19,8,1024]{2,1,0:T(8,128)(2,1)S(1)} %get-tuple-element.50.own, ...), custom_call_target="tpu_custom_call" | custom-call | flops 4000000000 | bytes 1802240 | tf_op jit(solution)/shard_map/interior/pallas_call | solution.py:455
  9.0 1.3 %late_rows.1 = (bf16[3,12,16,1280]{3,2,1,0:T(8,128)(2,1)S(1)}, bf16[3,10,16,1280]{3,2,1,0:T(8,128)(2,1)S(1)}, bf16[3,10,16,1152]{3,2,1,0:T(8,128)(2,1)S(1)}, bf1...) custom-call(bf16[3,12,16,1280]{3,2,1,0:T(8,128)(2,1)S(1)} %get-tuple, ...), custom_call_target="tpu_custom_call", output_to_operand_aliasing={{0}: (0, {}), {1}: (1, {}), {2}: (2, {}), {3}: (3, {}), {4}... | custom-call | flops 1000000000 | bytes 8036352 | tf_op jit(solution)/shard_map/late_rows/pallas_call | solution.py:455
  10.3 3.6 %collective-permute-start.3 = (bf16[896,128]{1,0:T(8,128)(2,1)S(1)}, bf16[896,128]{1,0:T(8,128)(2,1)S(1)}, u32[]{:S(2)}, u32[]{:S(2)}) collective-permute-start(bf16[896,128]{1,0:T(8,128)(2,1)S(1)} %get-tuple-element.65), channel_id=1, source_target_pairs={{0,16},{16,0},{1,17},{17,1},{2,18},{18,2},{3,19},{19,3},{4,20},{20... | collective-permute-start | bytes 688136 | tf_op jit(solution)/shard_map/ppermute | solution.py:20
  13.9 1.1 %keep_sums.1 = (bf16[3,10,16,1152]{3,2,1,0:T(8,128)(2,1)S(1)}, f32[896,128]{1,0:T(8,128)S(1)}) custom-call(bf16[3,12,16,1280]{3,2,1,0:T(8,128)(2,1)S(1)} %get-tuple-element.66.fd, bf16[3,10,16,1280]{3,2,1,0:T(8,128)(2,1)S(1)} %get-tuple-element.67.cd, bf16[3,10,16,1152]{3,2,1,0:T(8,128)(2,1)S(1)} %get-tuple-element.68.hd_in, ...), custom_call_target="tpu_custom_call", output_to_operand_aliasing={{0}: (2, {})} | custom-call | flops 2000000000 | bytes 5578752 | tf_op jit(solution)/shard_map/keep_sums/pallas_call | solution.py:455
  15.0 0.0 collective-permute-done.3.other
  15.1 16.2 %all_to_all.10.terms = bf16[16,56,128]{2,1,0:T(8,128)(2,1)S(1)} all-to-all(bf16[16,56,128]{2,1,0:T(8,128)(2,1)S(1)} %bitcast.9), channel_id=1, replica_groups=mesh['gx'=2,'gy'=4,'grp'=4] {'gy','grp'}, dimensions={0} | all-to-all | bytes 458752 | tf_op jit(solution)/shard_map/all_to_all | solution.py:538
  31.3 0.7 %add_and_repeat.1 = bf16[16,56,128]{2,1,0:T(8,128)(2,1)} custom-call(bf16[16,56,128]{2,1,0:T(8,128)(2,1)S(1)} %all_to_all.10.terms), custom_call_target="tpu_custom_call" | custom-call | bytes 229376 | tf_op jit(solution)/shard_map/add_and_repeat/pallas_call | solution.py:455
  32.0 3.5 %all-to-all-start.1 = ((bf16[16,56,128]{2,1,0:T(8,128)(2,1)}), bf16[16,56,128]{2,1,0:T(8,128)(2,1)S(1)}, u32[]{:S(2)}, u32[]{:S(2)}) async-start(bf16[16,56,128]{2,1,0:T(8,128)(2,1)} %add_and_repeat.1), calls=%async_computation.1 | async-start | bytes 458752 | tf_op jit(solution)/shard_map/all_to_all | solution.py:541
  35.6 1.5 %output_conv.1 = (bf16[8,8,1024]{2,1,0:T(8,128)(2,1)S(1)}, bf16[8,8,1024]{2,1,0:T(8,128)(2,1)S(1)}) custom-call(bf16[3,10,16,1152]{3,2,1,0:T(8,128)(2,1)S(1)} %get-tuple-element.76.hd, bf16[27,64,64]{2,1,0:T(8,128)(2,1)S(1)} %get-tuple-element.77.w2), custom_call_target="tpu_custom_call" | custom-call | flops 2000000000 | bytes 1327104 | tf_op jit(solution)/shard_map/output_conv/pallas_call | solution.py:455
  37.1 0.1 collective-permute-start.4
  37.1 1.3 %collective-permute-done.4.other = bf16[8,8,1024]{2,1,0:T(8,128)(2,1)S(1)} collective-permute-done((bf16[8,8,1024]{2,1,0:T(8,128)(2,1)S(1)}, bf16[8,8,1024]{2,1,0:T(8,128)(2,1)S(1)}, u32[]{:S(2)}, u32[]{:S(2)}) %collective-permute-start.4) | collective-permute-done | bytes 131104 | tf_op jit(solution)/shard_map/ppermute | solution.py:20
  38.5 0.8 %finish_output.1 = bf16[8,16,1024]{2,1,0:T(8,128)(2,1)} custom-call(bf16[8,8,1024]{2,1,0:T(8,128)(2,1)S(1)} %get-tuple-element.78.mine, bf16[8,8,1024]{2,1,0:T(8,128)(2,1)S(1)} %collective-permute-done.4.other), custom_call_target="tpu_custom_call" | custom-call | bytes 262144 | tf_op jit(solution)/shard_map/finish_output/pallas_call | solution.py:455
  39.3 5.1 %all-to-all-done.1 = bf16[16,56,128]{2,1,0:T(8,128)(2,1)S(1)} async-done(((bf16[16,56,128]{2,1,0:T(8,128)(2,1)}), bf16[16,56,128]{2,1,0:T(8,128)(2,1)S(1)}, u32[]{:S(2)}, u32[]{:S(2)}) %all-to-all-start.1) | async-done | bytes 229408 | tf_op jit(solution)/shard_map/all_to_all | solution.py:541
  44.4 0.0 collective-permute-start.5
  44.4 1.1 %unpack_own.1 = (f32[27,64,64]{2,1,0:T(8,128)}, f32[27,64,64]{2,1,0:T(8,128)}) custom-call(bf16[896,128]{1,0:T(8,128)(2,1)S(1)} %bitcast.11), custom_call_target="tpu_custom_call" | custom-call | bytes 229376 | tf_op jit(solution)/shard_map/unpack_own/pallas_call | solution.py:455
  45.5 0.3 collective-permute-done.5.rows
  45.9 1.1 %unpack_other.1 = (f32[27,64,64]{2,1,0:T(8,128)}, f32[27,64,64]{2,1,0:T(8,128)}) custom-call(bf16[896,128]{1,0:T(8,128)(2,1)S(1)} %collective-permute-done.5.rows, f32[27,64,64]{2,1,0:T(8,128)} %get-tuple-element.85.first_in, f32[27,64,64]{2,1,0:T(8,128)} %get-tuple-element.86.second_in), custom_call_target="tpu_custom_call", output_to_operand_aliasing={{0}: (1, {}), {1}: (2, {})} | custom-call | bytes 1114112 | tf_op jit(solution)/shard_map/unpack_other/pallas_call | solution.py:455
  (3 shorter events, 0.1 us)
Async XLA Ops:
  2.0 1.4 %collective-permute-start = (bf16[3,8,1024]{2,1,0:T(8,128)(2,1)S(1)}, bf16[3,8,1024]{2,1,0:T(8,128)(2,1)S(1)}, u32[]{:S(2)}, u32[]{:S(2)}) collective-permute-start(bf16[3,8,1024]{2,1,0:T(8,128)(2,1)S(1)} %get-tuple-element.52), channel_id=1, source_target_pairs={{0,16},{16,0},{1,17},{17,1},{2,18},{18,2},{3,19},{19,3},{4,20},{20... | collective-permute-start | bytes 147464 | tf_op jit(solution)/shard_map/ppermute | solution.py:20
  3.4 1.6 %collective-permute-start.1 = (bf16[19,8,1024]{2,1,0:T(8,128)(2,1)S(1)}, bf16[19,8,1024]{2,1,0:T(8,128)(2,1)S(1)}, u32[]{:S(2)}, u32[]{:S(2)}) collective-permute-start(bf16[19,8,1024]{2,1,0:T(8,128)(2,1)S(1)} %get-tuple-element.54), channel_id=1, source_target_pairs={{0,16},{16,0},{1,17},{17,1},{2,18},{18,2},{3,19},{19,3},{4,20},{20... | collective-permute-start | bytes 933896 | tf_op jit(solution)/shard_map/ppermute | solution.py:20
  3.7 5.3 %collective-permute-start.2 = (bf16[3,16,1024]{2,1,0:T(8,128)(2,1)S(1)}, bf16[3,16,1024]{2,1,0:T(8,128)(2,1)S(1)}, u32[]{:S(2)}, u32[]{:S(2)}) collective-permute-start(bf16[3,16,1024]{2,1,0:T(8,128)(2,1)S(1)} %join_edges.1), channel_id=1, source_target_pairs={{16,4},{20,8},{24,12},{4,16},{8,20},{12,24},{17,5},{21,9},{25,13},... | collective-permute-start | bytes 294920 | tf_op jit(solution)/shard_map/ppermute | solution.py:507
  10.3 4.7 %collective-permute-start.3 = (bf16[896,128]{1,0:T(8,128)(2,1)S(1)}, bf16[896,128]{1,0:T(8,128)(2,1)S(1)}, u32[]{:S(2)}, u32[]{:S(2)}) collective-permute-start(bf16[896,128]{1,0:T(8,128)(2,1)S(1)} %get-tuple-element.65), channel_id=1, source_target_pairs={{0,16},{16,0},{1,17},{17,1},{2,18},{18,2},{3,19},{19,3},{4,20},{20... | collective-permute-start | bytes 688136 | tf_op jit(solution)/shard_map/ppermute | solution.py:20
  32.0 12.4 %all-to-all-start.1 = ((bf16[16,56,128]{2,1,0:T(8,128)(2,1)}), bf16[16,56,128]{2,1,0:T(8,128)(2,1)S(1)}, u32[]{:S(2)}, u32[]{:S(2)}) async-start(bf16[16,56,128]{2,1,0:T(8,128)(2,1)} %add_and_repeat.1), calls=%async_computation.1 | async-start | bytes 458752 | tf_op jit(solution)/shard_map/all_to_all | solution.py:541
  37.1 1.4 %collective-permute-start.4 = (bf16[8,8,1024]{2,1,0:T(8,128)(2,1)S(1)}, bf16[8,8,1024]{2,1,0:T(8,128)(2,1)S(1)}, u32[]{:S(2)}, u32[]{:S(2)}) collective-permute-start(bf16[8,8,1024]{2,1,0:T(8,128)(2,1)S(1)} %get-tuple-element.79), channel_id=1, source_target_pairs={{0,16},{16,0},{1,17},{17,1},{2,18},{18,2},{3,19},{19,3},{4,20},{20... | collective-permute-start | bytes 393224 | tf_op jit(solution)/shard_map/ppermute | solution.py:20
  44.4 1.5 %collective-permute-start.5 = (bf16[896,128]{1,0:T(8,128)(2,1)S(1)}, bf16[896,128]{1,0:T(8,128)(2,1)S(1)}, u32[]{:S(2)}, u32[]{:S(2)}) collective-permute-start(bf16[896,128]{1,0:T(8,128)(2,1)S(1)} %bitcast.10), channel_id=1, source_target_pairs={{0,16},{16,0},{1,17},{17,1},{2,18},{18,2},{3,19},{19,3},{4,20},{20... | collective-permute-start | bytes 688136 | tf_op jit(solution)/shard_map/ppermute | solution.py:20

commit v13 on v12

--- a/solution.py
+++ b/solution.py
@@ -319,7 +319,15 @@
         target[BLOCKS * C:, :] = jnp.zeros((target.shape[0] - BLOCKS * C, 2 * C), target.dtype)
 
 
-def late_rows(gy_count, fd_in, cd_in, hd_in, pg_in, hs_in, rows, acc, w1b, wfb, fd, cd, hd, pg, hs, send, rs):
+def hidden_of(value, p):
+    return value * jax.nn.sigmoid(value) * inside_lanes(p)
+
+
+def stacked(copies, first, count, pairs):
+    return jnp.concatenate([windows(copies, first, count, p) for p in range(pairs + 1)], axis=0)
+
+
+def late_rows(gy_count, fd_in, cd_in, hd_in, pg_in, hs_in, rows, acc, w1b, wfb, fd, cd, hd, pg, hs, send, pre_late, rs):
     gx = lax.axis_index("gx")
     gy = lax.axis_index("gy")
     count, across, _ = pg.shape
@@ -327,44 +335,64 @@
     pairs = NZ // 2
     rs[:, 8:8 + across, :] = rows[...].astype(F32)
     blank_rows(rs)
-    shift_rows(rs.at[0:2], fd, (count + 2) * gx, lane)
-    shift_rows(rs.at[2:3], cd, (count + 1) * gx, lane)
-    value = dot(jnp.concatenate([windows(fd, count * gx, 2, p) for p in range(pairs + 1)], axis=0), w1b[...])
-    grad = dot_nt(jnp.concatenate([windows(cd, (count - 1) * gx, 1, p) for p in range(pairs + 1)], axis=0), wfb[...])
-    before = jnp.where((gx == 0) & (gy == 0), 0.0, 1.0)
-    beyond = jnp.where((gx != 0) & (gy == gy_count - 1), 0.0, 1.0)
-    for p in range(pairs + 1):
-        here = slice(lane * p, lane * (p + 1))
-        early = value[2 * across * p:2 * across * p + across]
-        later = value[2 * across * p + across:2 * across * (p + 1)]
-        both = jnp.stack([
-            early * jax.nn.sigmoid(early) * inside_lanes(p) * before,
-            later * jax.nn.sigmoid(later) * inside_lanes(p) * beyond,
-        ])
-        hs[pl.ds(count * gx, 2), 8:8 + across, here] = both
-        hd[1, pl.ds(count * gx, 2), :, here] = both.astype(BF16)
-        mine = pre_gradient(grad[across * p:across * (p + 1)], jnp.where(gx == 0, later, early), p)
-        pg[pl.ds((count - 1) * gx, 1), :, here] = mine.astype(BF16)[None]
 
     @pl.when(gx == 0)
     def _():
+        shift_rows(rs.at[0:2], fd, 0, lane)
+        shift_rows(rs.at[2:3], cd, 0, lane)
+        value = dot(stacked(fd, 0, 2, pairs), w1b[...])
+        before = jnp.where(gy == 0, 0.0, 1.0)
+        for p in range(pairs + 1):
+            here = slice(lane * p, lane * (p + 1))
+            early = value[2 * across * p:2 * across * p + across]
+            later = value[2 * across * p + across:2 * across * (p + 1)]
+            pre_late[:, here] = later
+            both = jnp.stack([hidden_of(early, p) * before, hidden_of(later, p)])
+            hs[0:2, 8:8 + across, here] = both
+            hd[1, 0:2, :, here] = both.astype(BF16)
         shift_rows(hs.at[0:2], hd, 0, 0, (0, 2))
         store_blocks(send, sums_of([acc[t] + late for t, late in enumerate(second_late(hd, cd))]))
 
     @pl.when(gx != 0)
     def _():
+        shift_rows(rs.at[0:2], fd, count + 2, lane)
+        shift_rows(rs.at[2:3], cd, count + 1, lane)
+        value = dot(stacked(fd, count, 1, pairs), w1b[...])
+        grad = dot_nt(stacked(cd, count - 1, 1, pairs), wfb[...])
+        for p in range(pairs + 1):
+            here = slice(lane * p, lane * (p + 1))
+            part = slice(across * p, across * (p + 1))
+            pre_late[:, here] = value[part]
+            pg[count - 1, :, here] = pre_gradient(grad[part], value[part], p).astype(BF16)
         store_blocks(send, sums_of([acc[t] + late for t, late in enumerate(first_late(fd, pg))]))
 
 
-def keep_sums(fd, cd, hd_in, pg, hs, hd, keep):
-    gx = lax.axis_index("gx")
+def keep_sums(gy_count, fd, cd, hd_in, pg_in, hs_in, pre_late, w1b, wfb, hd, pg, hs, keep):
+    gx = lax.axis_index("gx")
+    gy = lax.axis_index("gy")
+    count, across, _ = pg.shape
+    lane = 2 * C
+    pairs = NZ // 2
 
     @pl.when(gx == 0)
     def _():
+        grad = dot_nt(stacked(cd, 0, 1, pairs), wfb[...])
+        for p in range(pairs + 1):
+            here = slice(lane * p, lane * (p + 1))
+            part = slice(across * p, across * (p + 1))
+            pg[0, :, here] = pre_gradient(grad[part], pre_late[:, here], p).astype(BF16)
         store_blocks(keep, sums_of(first_products(fd, pg)))
 
     @pl.when(gx != 0)
     def _():
+        value = dot(stacked(fd, count + 1, 1, pairs), w1b[...])
+        beyond = jnp.where(gy == gy_count - 1, 0.0, 1.0)
+        for p in range(pairs + 1):
+            here = slice(lane * p, lane * (p + 1))
+            part = slice(across * p, across * (p + 1))
+            both = jnp.stack([hidden_of(pre_late[:, here], p), hidden_of(value[part], p) * beyond])
+            hs[count:count + 2, 8:8 + across, here] = both
+            hd[1, count:count + 2, :, here] = both.astype(BF16)
         shift_rows(hs, hd, 0, 0, (0, 2))
         store_blocks(keep, sums_of(second_products(hd, cd)))
 
@@ -414,35 +442,36 @@
         out[index] = total
 
 
-def unpack(factor, rows, held):
-    for t, (dx, dy) in enumerate(TAPS):
-        turned = rows[t * C:(t + 1) * C, :].astype(F32).T * factor
-        held[9 * dx + 3 * dy] = turned[0:C]
-        held[9 * dx + 3 * dy + 1] = turned[C:2 * C]
-    for pair in range(5):
-        turned = rows[(9 + pair) * C:(10 + pair) * C, :].astype(F32).T * factor
-        for half in range(2 if pair < 4 else 1):
-            dx, dy = TAPS[2 * pair + half]
-            held[9 * dx + 3 * dy + 2] = turned[half * C:(half + 1) * C]
-
-
-def write_either(is_first, held, first, second, sem):
-    for chosen, target in ((is_first, first), (jnp.logical_not(is_first), second)):
-        @pl.when(chosen)
-        def _():
-            copy = pltpu.make_async_copy(held, target, sem.at[0])
-            copy.start()
-            copy.wait()
-
-
-def unpack_own(factor, rows, first, second, held, sem):
-    unpack(factor, rows, held)
-    write_either(lax.axis_index("gx") == 0, held, first, second, sem)
-
-
-def unpack_other(factor, rows, first_in, second_in, first, second, held, sem):
-    unpack(factor, rows, held)
-    write_either(lax.axis_index("gx") != 0, held, first, second, sem)
+def unpack(factor, is_first, rows, first, second, held, sems):
+    def each(act):
+        for chosen, target in ((is_first, first), (jnp.logical_not(is_first), second)):
+            @pl.when(chosen)
+            def _():
+                act(target)
+
+    def copy_of(dx, target):
+        piece = slice(9 * dx, 9 * dx + 9)
+        return pltpu.make_async_copy(held.at[piece], target.at[piece], sems.at[dx])
+
+    for dx in range(3):
+        for dy in range(3):
+            t = 3 * dy + dx
+            place = 9 * dx + 3 * dy
+            turned = rows[t * C:(t + 1) * C, :].astype(F32).T * factor
+            held[place] = turned[0:C]
+            held[place + 1] = turned[C:2 * C]
+            turned = rows[(9 + t // 2) * C:(10 + t // 2) * C, :].astype(F32).T * factor
+            held[place + 2] = turned[t % 2 * C:(t % 2 + 1) * C]
+        each(lambda target: copy_of(dx, target).start())
+    each(lambda target: [copy_of(dx, target).wait() for dx in range(3)])
+
+
+def unpack_own(factor, rows, first, second, held, sems):
+    unpack(factor, lax.axis_index("gx") == 0, rows, first, second, held, sems)
+
+
+def unpack_other(factor, rows, first_in, second_in, first, second, held, sems):
+    unpack(factor, lax.axis_index("gx") != 0, rows, first, second, held, sems)
 
 
 def near(shape, dtype):
@@ -522,17 +551,18 @@
             pltpu.VMEM((count, across, width + lane), F32),
         ],
         limit=32, flops=4 * 10 ** 9)
-    fd, cd, hd, pg, hs, send = call(
+    fd, cd, hd, pg, hs, send, pre_late = call(
         functools.partial(late_rows, gy_count), "late_rows",
         [(x, True) for x in (fd, cd, hd, pg, hs, late, acc, w1b, wfb)],
-        held + [near((rows, lane), BF16)],
+        held + [near((rows, lane), BF16), near((across, width + lane), F32)],
         [pltpu.VMEM((3, across + 16, width), F32)],
         limit=32, flops=10 ** 9, aliases={0: 0, 1: 1, 2: 2, 3: 3, 4: 4})
 
     other = swap(send)
-    hd, keep = call(
-        keep_sums, "keep_sums",
-        [(x, True) for x in (fd, cd, hd, pg, hs)], [held[2], near((rows, lane), F32)], flops=2 * 10 ** 9, aliases={2: 0})
+    hd, _, _, keep = call(
+        functools.partial(keep_sums, gy_count), "keep_sums",
+        [(x, True) for x in (fd, cd, hd, pg, hs, pre_late, w1b, wfb)], held[2:] + [near((rows, lane), F32)],
+        flops=2 * 10 ** 9, aliases={2: 0, 3: 1, 4: 2})
     other, keep = lax.optimization_barrier((other, keep))
     both, = call(add_pair, "add_pair", [(keep, True), (other, True)], [near((rows, lane), BF16)])
     terms = lax.all_to_all(both.reshape(ranks, rows // ranks, lane), ("gy", "grp"), 0, 0)
@@ -551,7 +581,7 @@
     sums, out = lax.optimization_barrier((sums, out))
     other = swap(sums)
     outs = [pltpu.HBM((27, C, C), F32)] * 2
-    scratch = [pltpu.VMEM((27, C, C), F32), pltpu.SemaphoreType.DMA((1,))]
+    scratch = [pltpu.VMEM((27, C, C), F32), pltpu.SemaphoreType.DMA((3,))]
     first, second = call(functools.partial(unpack_own, factor), "unpack_own", [(sums, True)], outs, scratch, far=True)
     other, first, second = lax.optimization_barrier((other, first, second))
     first, second = call(

time: 47.3 us -> 46.9 us (level)
  blocking collectives: 16.2 us -> 15.6 us
  Pallas kernels: 13.8 us -> 14.3 us
    all_to_all x1, blocking collectives: 16.2 us -> 15.6 us  [shards(): lax.all_to_all(both.reshape(ranks, rows // ranks, lane), ('gy', 'grp'), 0...]
  transfers between devices with their start and end apart: 7 -> 7, of which waited for: 5 -> 5; matrix products, arithmetic and copies ran while one was open for 0% -> 0% of each run, Pallas kernels for 20% -> 21%
where the time goes in v13:
time: 46.9 us; the launch traced here: 46.7 us
  blocking collectives  15.6 us (33%)
  Pallas kernels  14.3 us (30%)
  starting transfers between devices  8.85 us (19%)
  waiting for transfers between devices  7.23 us (15%)
  between operations  0.74 us (2%)
    all_to_all x1, blocking collectives, shards(): lax.all_to_all(both.reshape(ranks, rows // ranks, lane), ('gy', 'grp'), 0...  15.6 us
    pallas_call x12, Pallas kernels, call(): pl.pallas_call(body, out_shape=list(outs), in_specs=[pl.BlockSpec(memory_...  14.3 us
    all_to_all x1, waiting for transfers between devices, shards(): sums = lax.all_to_all(spread, ('gy', 'grp'), 0, 0).reshape(rows, lane)  4.76 us
    ppermute x5, starting transfers between devices, swap(): return lax.ppermute(array, 'gx', [(0, 1), (1, 0)])  4.66 us
    all_to_all x1, starting transfers between devices, shards(): sums = lax.all_to_all(spread, ('gy', 'grp'), 0, 0).reshape(rows, lane)  3.53 us
    ppermute x5, waiting for transfers between devices, swap(): return lax.ppermute(array, 'gx', [(0, 1), (1, 0)])  2.47 us
  transfers between devices with their start and end apart: 7, of which 5 were waited for; matrix products, arithmetic and copies ran while one was open for 0% of the time, Pallas kernels for 21%

profile of v13, /device:TPU:0, one launch (start us, length us, event | category | flops | bytes accessed | tf_op | source)
XLA Modules:
  0.0 46.7 jit_solution(9411117182902266594)
XLA Ops:
  0.6 1.3 %pack_edges.1 = (bf16[8,16,1024]{2,1,0:T(8,128)(2,1)S(1)}, bf16[8,16,1024]{2,1,0:T(8,128)(2,1)S(1)}, bf16[3,8,1024]{2,1,0:T(8,128)(2,1)S(1)}, bf16[3,8,1024]{2,1...) custom-call(bf16[8,16,1024]{2,1,0:T(8,128)(2,1)} %bitcast.17, ...), custom_call_target="tpu_custom_call" | custom-call | bytes 966656 | tf_op jit(solution)/shard_map/pack_edges/pallas_call | solution.py:484
  2.0 0.5 %collective-permute-start = (bf16[3,8,1024]{2,1,0:T(8,128)(2,1)S(1)}, bf16[3,8,1024]{2,1,0:T(8,128)(2,1)S(1)}, u32[]{:S(2)}, u32[]{:S(2)}) collective-permute-start(bf16[3,8,1024]{2,1,0:T(8,128)(2,1)S(1)} %get-tuple-element.53), channel_id=1, source_target_pairs={{0,16},{16,0},{1,17},{17,1},{2,18},{18,2},{3,19},{19,3},{4,20},{20... | collective-permute-start | bytes 147464 | tf_op jit(solution)/shard_map/ppermute | solution.py:20
  2.5 0.7 %pack_halves.1 = (bf16[19,8,1024]{2,1,0:T(8,128)(2,1)S(1)}, bf16[19,8,1024]{2,1,0:T(8,128)(2,1)S(1)}, bf16[2304,128]{1,0:T(8,128)(2,1)S(1)}, bf16[128,2304]{1,0:T(8,128)(2,1)S(1)}) custom-call(bf16[8,16,1024]{2,1,0:T(8,128)(2,1)S(1)} %get-tuple-element.47.field, bf16[8,16,1024]{2,1,0:T(8,128)(2,1)S(1)} %get-tuple-element.48.cot, ...), custom_call_target="tpu_custom_call" | custom-call | flops 1000000000 | bytes 966656 | tf_op jit(solution)/shard_map/pack_halves/pallas_call | solution.py:484
  3.2 0.2 collective-permute-done.taken
  3.4 0.3 collective-permute-start.1
  3.7 0.7 %collective-permute-start.2 = (bf16[3,16,1024]{2,1,0:T(8,128)(2,1)S(1)}, bf16[3,16,1024]{2,1,0:T(8,128)(2,1)S(1)}, u32[]{:S(2)}, u32[]{:S(2)}) collective-permute-start(bf16[3,16,1024]{2,1,0:T(8,128)(2,1)S(1)} %join_edges.1), channel_id=1, source_target_pairs={{16,4},{20,8},{24,12},{4,16},{8,20},{12,24},{17,5},{21,9},{25,13},... | collective-permute-start | bytes 294920 | tf_op jit(solution)/shard_map/ppermute | solution.py:536
  4.4 0.6 %collective-permute-done.1.got = bf16[19,8,1024]{2,1,0:T(8,128)(2,1)S(1)} collective-permute-done((bf16[19,8,1024]{2,1,0:T(8,128)(2,1)S(1)}, bf16[19,8,1024]{2,1,0:T(8,128)(2,1)S(1)}, u32[]{:S(2)}, u32[]{:S(2)}) %collective-permute-start.1) | collective-permute-done | bytes 311328 | tf_op jit(solution)/shard_map/ppermute | solution.py:20
  5.0 4.0 %interior.1 = (bf16[3,12,16,1280]{3,2,1,0:T(8,128)(2,1)S(1)}, bf16[3,10,16,1280]{3,2,1,0:T(8,128)(2,1)S(1)}, bf16[3,10,16,1152]{3,2,1,0:T(8,128)(2,1)S(1)}, bf16...) custom-call(bf16[19,8,1024]{2,1,0:T(8,128)(2,1)S(1)} %get-tuple-element.51.own, ...), custom_call_target="tpu_custom_call" | custom-call | flops 4000000000 | bytes 1802240 | tf_op jit(solution)/shard_map/interior/pallas_call | solution.py:484
  9.0 0.0 collective-permute-done.2.rows
  9.0 1.2 %late_rows.1 = (bf16[3,12,16,1280]{3,2,1,0:T(8,128)(2,1)S(1)}, bf16[3,10,16,1280]{3,2,1,0:T(8,128)(2,1)S(1)}, bf16[3,10,16,1152]{3,2,1,0:T(8,128)(2,1)S(1)}, bf1...) custom-call(bf16[3,12,16,1280]{3,2,1,0:T(8,128)(2,1)S(1)} %get-tuple, ...), custom_call_target="tpu_custom_call", output_to_operand_aliasing={{0}: (0, {}), {1}: (1, {}), {2}: (2, {}), {3}: (3, {}), {4}... | custom-call | flops 1000000000 | bytes 8036352 | tf_op jit(solution)/shard_map/late_rows/pallas_call | solution.py:484
  10.2 3.7 %collective-permute-start.3 = (bf16[896,128]{1,0:T(8,128)(2,1)S(1)}, bf16[896,128]{1,0:T(8,128)(2,1)S(1)}, u32[]{:S(2)}, u32[]{:S(2)}) collective-permute-start(bf16[896,128]{1,0:T(8,128)(2,1)S(1)} %get-tuple-element.66), channel_id=1, source_target_pairs={{0,16},{16,0},{1,17},{17,1},{2,18},{18,2},{3,19},{19,3},{4,20},{20... | collective-permute-start | bytes 688136 | tf_op jit(solution)/shard_map/ppermute | solution.py:20
  13.9 1.7 %keep_sums.1 = (bf16[3,10,16,1152]{3,2,1,0:T(8,128)(2,1)S(1)}, bf16[8,16,1152]{2,1,0:T(8,128)(2,1)S(1)}, f32[10,32,1152]{2,1,0:T(8,128)S(1)}, f32[896,128]{1,0:T(8,128)S(1)}) custom-call(bf16[3,12,16,1280]{3,2,1,0:T(8,128)(2,1)S(1)} %get-tuple-element.67.fd, ...), custom_call_target="tpu_custom_call", output_to_operand_aliasing={{0}: (2, {}), {1}: (3, {}), {2}: (4, {})} | custom-call | flops 2000000000 | bytes 6832128 | tf_op jit(solution)/shard_map/keep_sums/pallas_call | solution.py:484
  15.7 0.1 add_pair.1
  15.7 15.6 %all_to_all.10.terms = bf16[16,56,128]{2,1,0:T(8,128)(2,1)S(1)} all-to-all(bf16[16,56,128]{2,1,0:T(8,128)(2,1)S(1)} %bitcast.9), channel_id=1, replica_groups=mesh['gx'=2,'gy'=4,'grp'=4] {'gy','grp'}, dimensions={0} | all-to-all | bytes 458752 | tf_op jit(solution)/shard_map/all_to_all | solution.py:568
  31.3 0.7 %add_and_repeat.1 = bf16[16,56,128]{2,1,0:T(8,128)(2,1)} custom-call(bf16[16,56,128]{2,1,0:T(8,128)(2,1)S(1)} %all_to_all.10.terms), custom_call_target="tpu_custom_call" | custom-call | bytes 229376 | tf_op jit(solution)/shard_map/add_and_repeat/pallas_call | solution.py:484
  32.0 3.5 %all-to-all-start.1 = ((bf16[16,56,128]{2,1,0:T(8,128)(2,1)}), bf16[16,56,128]{2,1,0:T(8,128)(2,1)S(1)}, u32[]{:S(2)}, u32[]{:S(2)}) async-start(bf16[16,56,128]{2,1,0:T(8,128)(2,1)} %add_and_repeat.1), calls=%async_computation.1 | async-start | bytes 458752 | tf_op jit(solution)/shard_map/all_to_all | solution.py:571
  35.6 1.5 %output_conv.1 = (bf16[8,8,1024]{2,1,0:T(8,128)(2,1)S(1)}, bf16[8,8,1024]{2,1,0:T(8,128)(2,1)S(1)}) custom-call(bf16[3,10,16,1152]{3,2,1,0:T(8,128)(2,1)S(1)} %get-tuple-element.78.hd, bf16[27,64,64]{2,1,0:T(8,128)(2,1)S(1)} %get-tuple-element.79.w2), custom_call_target="tpu_custom_call" | custom-call | flops 2000000000 | bytes 1327104 | tf_op jit(solution)/shard_map/output_conv/pallas_call | solution.py:484
  37.1 0.1 collective-permute-start.4
  37.2 1.3 %collective-permute-done.4.other = bf16[8,8,1024]{2,1,0:T(8,128)(2,1)S(1)} collective-permute-done((bf16[8,8,1024]{2,1,0:T(8,128)(2,1)S(1)}, bf16[8,8,1024]{2,1,0:T(8,128)(2,1)S(1)}, u32[]{:S(2)}, u32[]{:S(2)}) %collective-permute-start.4) | collective-permute-done | bytes 131104 | tf_op jit(solution)/shard_map/ppermute | solution.py:20
  38.5 0.8 %finish_output.1 = bf16[8,16,1024]{2,1,0:T(8,128)(2,1)} custom-call(bf16[8,8,1024]{2,1,0:T(8,128)(2,1)S(1)} %get-tuple-element.80.mine, bf16[8,8,1024]{2,1,0:T(8,128)(2,1)S(1)} %collective-permute-done.4.other), custom_call_target="tpu_custom_call" | custom-call | bytes 262144 | tf_op jit(solution)/shard_map/finish_output/pallas_call | solution.py:484
  39.3 4.8 %all-to-all-done.1 = bf16[16,56,128]{2,1,0:T(8,128)(2,1)S(1)} async-done(((bf16[16,56,128]{2,1,0:T(8,128)(2,1)}), bf16[16,56,128]{2,1,0:T(8,128)(2,1)S(1)}, u32[]{:S(2)}, u32[]{:S(2)}) %all-to-all-start.1) | async-done | bytes 229408 | tf_op jit(solution)/shard_map/all_to_all | solution.py:571
  44.1 1.1 %unpack_own.1 = (f32[27,64,64]{2,1,0:T(8,128)}, f32[27,64,64]{2,1,0:T(8,128)}) custom-call(bf16[896,128]{1,0:T(8,128)(2,1)S(1)} %bitcast.11), custom_call_target="tpu_custom_call" | custom-call | bytes 229376 | tf_op jit(solution)/shard_map/unpack_own/pallas_call | solution.py:484
  45.2 0.4 collective-permute-done.5.rows
  45.6 1.1 %unpack_other.1 = (f32[27,64,64]{2,1,0:T(8,128)}, f32[27,64,64]{2,1,0:T(8,128)}) custom-call(bf16[896,128]{1,0:T(8,128)(2,1)S(1)} %collective-permute-done.5.rows, f32[27,64,64]{2,1,0:T(8,128)} %get-tuple-element.87.first_in, f32[27,64,64]{2,1,0:T(8,128)} %get-tuple-element.88.second_in), custom_call_target="tpu_custom_call", output_to_operand_aliasing={{0}: (1, {}), {1}: (2, {})} | custom-call | bytes 1114112 | tf_op jit(solution)/shard_map/unpack_other/pallas_call | solution.py:484
  (3 shorter events, 0.0 us)
Async XLA Ops:
  2.0 1.4 %collective-permute-start = (bf16[3,8,1024]{2,1,0:T(8,128)(2,1)S(1)}, bf16[3,8,1024]{2,1,0:T(8,128)(2,1)S(1)}, u32[]{:S(2)}, u32[]{:S(2)}) collective-permute-start(bf16[3,8,1024]{2,1,0:T(8,128)(2,1)S(1)} %get-tuple-element.53), channel_id=1, source_target_pairs={{0,16},{16,0},{1,17},{17,1},{2,18},{18,2},{3,19},{19,3},{4,20},{20... | collective-permute-start | bytes 147464 | tf_op jit(solution)/shard_map/ppermute | solution.py:20
  3.4 1.6 %collective-permute-start.1 = (bf16[19,8,1024]{2,1,0:T(8,128)(2,1)S(1)}, bf16[19,8,1024]{2,1,0:T(8,128)(2,1)S(1)}, u32[]{:S(2)}, u32[]{:S(2)}) collective-permute-start(bf16[19,8,1024]{2,1,0:T(8,128)(2,1)S(1)} %get-tuple-element.55), channel_id=1, source_target_pairs={{0,16},{16,0},{1,17},{17,1},{2,18},{18,2},{3,19},{19,3},{4,20},{20... | collective-permute-start | bytes 933896 | tf_op jit(solution)/shard_map/ppermute | solution.py:20
  3.7 5.3 %collective-permute-start.2 = (bf16[3,16,1024]{2,1,0:T(8,128)(2,1)S(1)}, bf16[3,16,1024]{2,1,0:T(8,128)(2,1)S(1)}, u32[]{:S(2)}, u32[]{:S(2)}) collective-permute-start(bf16[3,16,1024]{2,1,0:T(8,128)(2,1)S(1)} %join_edges.1), channel_id=1, source_target_pairs={{16,4},{20,8},{24,12},{4,16},{8,20},{12,24},{17,5},{21,9},{25,13},... | collective-permute-start | bytes 294920 | tf_op jit(solution)/shard_map/ppermute | solution.py:536
  10.2 5.4 %collective-permute-start.3 = (bf16[896,128]{1,0:T(8,128)(2,1)S(1)}, bf16[896,128]{1,0:T(8,128)(2,1)S(1)}, u32[]{:S(2)}, u32[]{:S(2)}) collective-permute-start(bf16[896,128]{1,0:T(8,128)(2,1)S(1)} %get-tuple-element.66), channel_id=1, source_target_pairs={{0,16},{16,0},{1,17},{17,1},{2,18},{18,2},{3,19},{19,3},{4,20},{20... | collective-permute-start | bytes 688136 | tf_op jit(solution)/shard_map/ppermute | solution.py:20
  32.0 12.1 %all-to-all-start.1 = ((bf16[16,56,128]{2,1,0:T(8,128)(2,1)}), bf16[16,56,128]{2,1,0:T(8,128)(2,1)S(1)}, u32[]{:S(2)}, u32[]{:S(2)}) async-start(bf16[16,56,128]{2,1,0:T(8,128)(2,1)} %add_and_repeat.1), calls=%async_computation.1 | async-start | bytes 458752 | tf_op jit(solution)/shard_map/all_to_all | solution.py:571
  37.1 1.4 %collective-permute-start.4 = (bf16[8,8,1024]{2,1,0:T(8,128)(2,1)S(1)}, bf16[8,8,1024]{2,1,0:T(8,128)(2,1)S(1)}, u32[]{:S(2)}, u32[]{:S(2)}) collective-permute-start(bf16[8,8,1024]{2,1,0:T(8,128)(2,1)S(1)} %get-tuple-element.81), channel_id=1, source_target_pairs={{0,16},{16,0},{1,17},{17,1},{2,18},{18,2},{3,19},{19,3},{4,20},{20... | collective-permute-start | bytes 393224 | tf_op jit(solution)/shard_map/ppermute | solution.py:20
  44.1 1.5 %collective-permute-start.5 = (bf16[896,128]{1,0:T(8,128)(2,1)S(1)}, bf16[896,128]{1,0:T(8,128)(2,1)S(1)}, u32[]{:S(2)}, u32[]{:S(2)}) collective-permute-start(bf16[896,128]{1,0:T(8,128)(2,1)S(1)} %bitcast.10), channel_id=1, source_target_pairs={{0,16},{16,0},{1,17},{17,1},{2,18},{18,2},{3,19},{19,3},{4,20},{20... | collective-permute-start | bytes 688136 | tf_op jit(solution)/shard_map/ppermute | solution.py:20

commit v14 on v13

--- a/solution.py
+++ b/solution.py
@@ -341,12 +341,14 @@
         shift_rows(rs.at[0:2], fd, 0, lane)
         shift_rows(rs.at[2:3], cd, 0, lane)
         value = dot(stacked(fd, 0, 2, pairs), w1b[...])
+        grad = dot_nt(stacked(cd, 0, 1, pairs), wfb[...])
         before = jnp.where(gy == 0, 0.0, 1.0)
         for p in range(pairs + 1):
             here = slice(lane * p, lane * (p + 1))
             early = value[2 * across * p:2 * across * p + across]
             later = value[2 * across * p + across:2 * across * (p + 1)]
-            pre_late[:, here] = later
+            mine = pre_gradient(grad[across * p:across * (p + 1)], later, p)
+            pg[0, :, here] = mine.astype(BF16)
             both = jnp.stack([hidden_of(early, p) * before, hidden_of(later, p)])
             hs[0:2, 8:8 + across, here] = both
             hd[1, 0:2, :, here] = both.astype(BF16)
@@ -367,7 +369,7 @@
         store_blocks(send, sums_of([acc[t] + late for t, late in enumerate(first_late(fd, pg))]))
 
 
-def keep_sums(gy_count, fd, cd, hd_in, pg_in, hs_in, pre_late, w1b, wfb, hd, pg, hs, keep):
+def keep_sums(gy_count, fd, cd, hd_in, pg, hs_in, pre_late, w1b, hd, hs, keep):
     gx = lax.axis_index("gx")
     gy = lax.axis_index("gy")
     count, across, _ = pg.shape
@@ -376,11 +378,6 @@
 
     @pl.when(gx == 0)
     def _():
-        grad = dot_nt(stacked(cd, 0, 1, pairs), wfb[...])
-        for p in range(pairs + 1):
-            here = slice(lane * p, lane * (p + 1))
-            part = slice(across * p, across * (p + 1))
-            pg[0, :, here] = pre_gradient(grad[part], pre_late[:, here], p).astype(BF16)
         store_blocks(keep, sums_of(first_products(fd, pg)))
 
     @pl.when(gx != 0)
@@ -559,16 +556,16 @@
         limit=32, flops=10 ** 9, aliases={0: 0, 1: 1, 2: 2, 3: 3, 4: 4})
 
     other = swap(send)
-    hd, _, _, keep = call(
+    hd, _, keep = call(
         functools.partial(keep_sums, gy_count), "keep_sums",
-        [(x, True) for x in (fd, cd, hd, pg, hs, pre_late, w1b, wfb)], held[2:] + [near((rows, lane), F32)],
-        flops=2 * 10 ** 9, aliases={2: 0, 3: 1, 4: 2})
+        [(x, True) for x in (fd, cd, hd, pg, hs, pre_late, w1b)], [held[2], held[4], near((rows, lane), F32)],
+        flops=2 * 10 ** 9, aliases={2: 0, 4: 1})
     other, keep = lax.optimization_barrier((other, keep))
     both, = call(add_pair, "add_pair", [(keep, True), (other, True)], [near((rows, lane), BF16)])
-    terms = lax.all_to_all(both.reshape(ranks, rows // ranks, lane), ("gy", "grp"), 0, 0)
+    terms = lax.all_to_all(both.reshape(ranks, rows // ranks, lane), ("grp", "gy"), 0, 0)
     spread, = call(add_and_repeat, "add_and_repeat", [(terms, True)], [near(terms.shape, BF16)])
     spread, hd, w2 = lax.optimization_barrier((spread, hd, w2))
-    sums = lax.all_to_all(spread, ("gy", "grp"), 0, 0).reshape(rows, lane)
+    sums = lax.all_to_all(spread, ("grp", "gy"), 0, 0).reshape(rows, lane)
     mine, given = call(
         output_conv, "output_conv", [(hd, True), (w2, True)],
         [near((count, nx, width), BF16), near((count, nx, width), BF16)],

time: 46.9 us -> 46.7 us (level)
  Pallas kernels: 14.3 us -> 13.8 us
  transfers between devices with their start and end apart: 7 -> 7, of which waited for: 5 -> 5; matrix products, arithmetic and copies ran while one was open for 0% -> 0% of each run, Pallas kernels for 21% -> 20%
where the time goes in v14:
time: 46.7 us; the launch traced here: 46.5 us
  blocking collectives  15.7 us (34%)
  Pallas kernels  13.8 us (30%)
  starting transfers between devices  8.68 us (19%)
  waiting for transfers between devices  7.53 us (16%)
  between operations  0.74 us (2%)
    all_to_all x1, blocking collectives, shards(): lax.all_to_all(both.reshape(ranks, rows // ranks, lane), ('grp', 'gy'), 0...  15.7 us
    pallas_call x12, Pallas kernels, call(): pl.pallas_call(body, out_shape=list(outs), in_specs=[pl.BlockSpec(memory_...  13.8 us
    all_to_all x1, waiting for transfers between devices, shards(): sums = lax.all_to_all(spread, ('grp', 'gy'), 0, 0).reshape(rows, lane)  5.06 us
    ppermute x5, starting transfers between devices, swap(): return lax.ppermute(array, 'gx', [(0, 1), (1, 0)])  4.49 us
    all_to_all x1, starting transfers between devices, shards(): sums = lax.all_to_all(spread, ('grp', 'gy'), 0, 0).reshape(rows, lane)  3.53 us
    ppermute x5, waiting for transfers between devices, swap(): return lax.ppermute(array, 'gx', [(0, 1), (1, 0)])  2.47 us
  transfers between devices with their start and end apart: 7, of which 5 were waited for; matrix products, arithmetic and copies ran while one was open for 0% of the time, Pallas kernels for 20%

profile of v14, /device:TPU:0, one launch (start us, length us, event | category | flops | bytes accessed | tf_op | source)
XLA Modules:
  0.0 46.5 jit_solution(11321033118284677348)
XLA Ops:
  0.6 1.3 %pack_edges.1 = (bf16[8,16,1024]{2,1,0:T(8,128)(2,1)S(1)}, bf16[8,16,1024]{2,1,0:T(8,128)(2,1)S(1)}, bf16[3,8,1024]{2,1,0:T(8,128)(2,1)S(1)}, bf16[3,8,1024]{2,1...) custom-call(bf16[8,16,1024]{2,1,0:T(8,128)(2,1)} %bitcast.17, ...), custom_call_target="tpu_custom_call" | custom-call | bytes 966656 | tf_op jit(solution)/shard_map/pack_edges/pallas_call | solution.py:481
  2.0 0.5 %collective-permute-start = (bf16[3,8,1024]{2,1,0:T(8,128)(2,1)S(1)}, bf16[3,8,1024]{2,1,0:T(8,128)(2,1)S(1)}, u32[]{:S(2)}, u32[]{:S(2)}) collective-permute-start(bf16[3,8,1024]{2,1,0:T(8,128)(2,1)S(1)} %get-tuple-element.53), channel_id=1, source_target_pairs={{0,16},{16,0},{1,17},{17,1},{2,18},{18,2},{3,19},{19,3},{4,20},{20... | collective-permute-start | bytes 147464 | tf_op jit(solution)/shard_map/ppermute | solution.py:20
  2.5 0.7 %pack_halves.1 = (bf16[19,8,1024]{2,1,0:T(8,128)(2,1)S(1)}, bf16[19,8,1024]{2,1,0:T(8,128)(2,1)S(1)}, bf16[2304,128]{1,0:T(8,128)(2,1)S(1)}, bf16[128,2304]{1,0:T(8,128)(2,1)S(1)}) custom-call(bf16[8,16,1024]{2,1,0:T(8,128)(2,1)S(1)} %get-tuple-element.47.field, bf16[8,16,1024]{2,1,0:T(8,128)(2,1)S(1)} %get-tuple-element.48.cot, ...), custom_call_target="tpu_custom_call" | custom-call | flops 1000000000 | bytes 966656 | tf_op jit(solution)/shard_map/pack_halves/pallas_call | solution.py:481
  3.2 0.2 collective-permute-done.taken
  3.4 0.3 collective-permute-start.1
  3.7 0.7 %collective-permute-start.2 = (bf16[3,16,1024]{2,1,0:T(8,128)(2,1)S(1)}, bf16[3,16,1024]{2,1,0:T(8,128)(2,1)S(1)}, u32[]{:S(2)}, u32[]{:S(2)}) collective-permute-start(bf16[3,16,1024]{2,1,0:T(8,128)(2,1)S(1)} %join_edges.1), channel_id=1, source_target_pairs={{16,4},{20,8},{24,12},{4,16},{8,20},{12,24},{17,5},{21,9},{25,13},... | collective-permute-start | bytes 294920 | tf_op jit(solution)/shard_map/ppermute | solution.py:533
  4.4 0.6 %collective-permute-done.1.got = bf16[19,8,1024]{2,1,0:T(8,128)(2,1)S(1)} collective-permute-done((bf16[19,8,1024]{2,1,0:T(8,128)(2,1)S(1)}, bf16[19,8,1024]{2,1,0:T(8,128)(2,1)S(1)}, u32[]{:S(2)}, u32[]{:S(2)}) %collective-permute-start.1) | collective-permute-done | bytes 311328 | tf_op jit(solution)/shard_map/ppermute | solution.py:20
  5.0 4.0 %interior.1 = (bf16[3,12,16,1280]{3,2,1,0:T(8,128)(2,1)S(1)}, bf16[3,10,16,1280]{3,2,1,0:T(8,128)(2,1)S(1)}, bf16[3,10,16,1152]{3,2,1,0:T(8,128)(2,1)S(1)}, bf16...) custom-call(bf16[19,8,1024]{2,1,0:T(8,128)(2,1)S(1)} %get-tuple-element.51.own, ...), custom_call_target="tpu_custom_call" | custom-call | flops 4000000000 | bytes 1802240 | tf_op jit(solution)/shard_map/interior/pallas_call | solution.py:481
  9.0 0.0 collective-permute-done.2.rows
  9.0 1.4 %late_rows.1 = (bf16[3,12,16,1280]{3,2,1,0:T(8,128)(2,1)S(1)}, bf16[3,10,16,1280]{3,2,1,0:T(8,128)(2,1)S(1)}, bf16[3,10,16,1152]{3,2,1,0:T(8,128)(2,1)S(1)}, bf1...) custom-call(bf16[3,12,16,1280]{3,2,1,0:T(8,128)(2,1)S(1)} %get-tuple, ...), custom_call_target="tpu_custom_call", output_to_operand_aliasing={{0}: (0, {}), {1}: (1, {}), {2}: (2, {}), {3}: (3, {}), {4}... | custom-call | flops 1000000000 | bytes 8036352 | tf_op jit(solution)/shard_map/late_rows/pallas_call | solution.py:481
  10.4 3.5 %collective-permute-start.3 = (bf16[896,128]{1,0:T(8,128)(2,1)S(1)}, bf16[896,128]{1,0:T(8,128)(2,1)S(1)}, u32[]{:S(2)}, u32[]{:S(2)}) collective-permute-start(bf16[896,128]{1,0:T(8,128)(2,1)S(1)} %get-tuple-element.66), channel_id=1, source_target_pairs={{0,16},{16,0},{1,17},{17,1},{2,18},{18,2},{3,19},{19,3},{4,20},{20... | collective-permute-start | bytes 688136 | tf_op jit(solution)/shard_map/ppermute | solution.py:20
  13.9 1.1 %keep_sums.1 = (bf16[3,10,16,1152]{3,2,1,0:T(8,128)(2,1)S(1)}, f32[10,32,1152]{2,1,0:T(8,128)S(1)}, f32[896,128]{1,0:T(8,128)S(1)}) custom-call(bf16[3,12,16,1280]{3,2,1,0:T(8,128)(2,1)S(1)} %get-tuple-element.67.fd, bf16[3,10,16,1280]{3,2,1,0:T(8,128)(2,1)S(1)} %get-tuple-element.68.cd, ...), custom_call_target="tpu_custom_call", output_to_operand_aliasing={{0}: (2, {}), {1}: (4, {})} | custom-call | flops 2000000000 | bytes 6242304 | tf_op jit(solution)/shard_map/keep_sums/pallas_call | solution.py:481
  15.1 0.1 add_pair.1
  15.1 15.7 %all_to_all.10.terms = bf16[16,56,128]{2,1,0:T(8,128)(2,1)S(1)} all-to-all(bf16[16,56,128]{2,1,0:T(8,128)(2,1)S(1)} %bitcast.9), channel_id=1, replica_groups=mesh['gx'=2,'gy'=4,'grp'=4] {'grp','gy'}, dimensions={0} | all-to-all | bytes 458752 | tf_op jit(solution)/shard_map/all_to_all | solution.py:565
  30.8 0.7 %add_and_repeat.1 = bf16[16,56,128]{2,1,0:T(8,128)(2,1)} custom-call(bf16[16,56,128]{2,1,0:T(8,128)(2,1)S(1)} %all_to_all.10.terms), custom_call_target="tpu_custom_call" | custom-call | bytes 229376 | tf_op jit(solution)/shard_map/add_and_repeat/pallas_call | solution.py:481
  31.6 3.5 %all-to-all-start.1 = ((bf16[16,56,128]{2,1,0:T(8,128)(2,1)}), bf16[16,56,128]{2,1,0:T(8,128)(2,1)S(1)}, u32[]{:S(2)}, u32[]{:S(2)}) async-start(bf16[16,56,128]{2,1,0:T(8,128)(2,1)} %add_and_repeat.1), calls=%async_computation.1 | async-start | bytes 458752 | tf_op jit(solution)/shard_map/all_to_all | solution.py:568
  35.1 1.5 %output_conv.1 = (bf16[8,8,1024]{2,1,0:T(8,128)(2,1)S(1)}, bf16[8,8,1024]{2,1,0:T(8,128)(2,1)S(1)}) custom-call(bf16[3,10,16,1152]{3,2,1,0:T(8,128)(2,1)S(1)} %get-tuple-element.78.hd, bf16[27,64,64]{2,1,0:T(8,128)(2,1)S(1)} %get-tuple-element.79.w2), custom_call_target="tpu_custom_call" | custom-call | flops 2000000000 | bytes 1327104 | tf_op jit(solution)/shard_map/output_conv/pallas_call | solution.py:481
  36.6 0.1 collective-permute-start.4
  36.7 1.3 %collective-permute-done.4.other = bf16[8,8,1024]{2,1,0:T(8,128)(2,1)S(1)} collective-permute-done((bf16[8,8,1024]{2,1,0:T(8,128)(2,1)S(1)}, bf16[8,8,1024]{2,1,0:T(8,128)(2,1)S(1)}, u32[]{:S(2)}, u32[]{:S(2)}) %collective-permute-start.4) | collective-permute-done | bytes 131104 | tf_op jit(solution)/shard_map/ppermute | solution.py:20
  38.0 0.8 %finish_output.1 = bf16[8,16,1024]{2,1,0:T(8,128)(2,1)} custom-call(bf16[8,8,1024]{2,1,0:T(8,128)(2,1)S(1)} %get-tuple-element.80.mine, bf16[8,8,1024]{2,1,0:T(8,128)(2,1)S(1)} %collective-permute-done.4.other), custom_call_target="tpu_custom_call" | custom-call | bytes 262144 | tf_op jit(solution)/shard_map/finish_output/pallas_call | solution.py:481
  38.8 5.1 %all-to-all-done.1 = bf16[16,56,128]{2,1,0:T(8,128)(2,1)S(1)} async-done(((bf16[16,56,128]{2,1,0:T(8,128)(2,1)}), bf16[16,56,128]{2,1,0:T(8,128)(2,1)S(1)}, u32[]{:S(2)}, u32[]{:S(2)}) %all-to-all-start.1) | async-done | bytes 229408 | tf_op jit(solution)/shard_map/all_to_all | solution.py:568
  43.9 1.1 %unpack_own.1 = (f32[27,64,64]{2,1,0:T(8,128)}, f32[27,64,64]{2,1,0:T(8,128)}) custom-call(bf16[896,128]{1,0:T(8,128)(2,1)S(1)} %bitcast.11), custom_call_target="tpu_custom_call" | custom-call | bytes 229376 | tf_op jit(solution)/shard_map/unpack_own/pallas_call | solution.py:481
  45.0 0.4 collective-permute-done.5.rows
  45.4 1.1 %unpack_other.1 = (f32[27,64,64]{2,1,0:T(8,128)}, f32[27,64,64]{2,1,0:T(8,128)}) custom-call(bf16[896,128]{1,0:T(8,128)(2,1)S(1)} %collective-permute-done.5.rows, f32[27,64,64]{2,1,0:T(8,128)} %get-tuple-element.87.first_in, f32[27,64,64]{2,1,0:T(8,128)} %get-tuple-element.88.second_in), custom_call_target="tpu_custom_call", output_to_operand_aliasing={{0}: (1, {}), {1}: (2, {})} | custom-call | bytes 1114112 | tf_op jit(solution)/shard_map/unpack_other/pallas_call | solution.py:481
  (3 shorter events, 0.0 us)
Async XLA Ops:
  2.0 1.4 %collective-permute-start = (bf16[3,8,1024]{2,1,0:T(8,128)(2,1)S(1)}, bf16[3,8,1024]{2,1,0:T(8,128)(2,1)S(1)}, u32[]{:S(2)}, u32[]{:S(2)}) collective-permute-start(bf16[3,8,1024]{2,1,0:T(8,128)(2,1)S(1)} %get-tuple-element.53), channel_id=1, source_target_pairs={{0,16},{16,0},{1,17},{17,1},{2,18},{18,2},{3,19},{19,3},{4,20},{20... | collective-permute-start | bytes 147464 | tf_op jit(solution)/shard_map/ppermute | solution.py:20
  3.4 1.6 %collective-permute-start.1 = (bf16[19,8,1024]{2,1,0:T(8,128)(2,1)S(1)}, bf16[19,8,1024]{2,1,0:T(8,128)(2,1)S(1)}, u32[]{:S(2)}, u32[]{:S(2)}) collective-permute-start(bf16[19,8,1024]{2,1,0:T(8,128)(2,1)S(1)} %get-tuple-element.55), channel_id=1, source_target_pairs={{0,16},{16,0},{1,17},{17,1},{2,18},{18,2},{3,19},{19,3},{4,20},{20... | collective-permute-start | bytes 933896 | tf_op jit(solution)/shard_map/ppermute | solution.py:20
  3.7 5.3 %collective-permute-start.2 = (bf16[3,16,1024]{2,1,0:T(8,128)(2,1)S(1)}, bf16[3,16,1024]{2,1,0:T(8,128)(2,1)S(1)}, u32[]{:S(2)}, u32[]{:S(2)}) collective-permute-start(bf16[3,16,1024]{2,1,0:T(8,128)(2,1)S(1)} %join_edges.1), channel_id=1, source_target_pairs={{16,4},{20,8},{24,12},{4,16},{8,20},{12,24},{17,5},{21,9},{25,13},... | collective-permute-start | bytes 294920 | tf_op jit(solution)/shard_map/ppermute | solution.py:533
  10.4 4.7 %collective-permute-start.3 = (bf16[896,128]{1,0:T(8,128)(2,1)S(1)}, bf16[896,128]{1,0:T(8,128)(2,1)S(1)}, u32[]{:S(2)}, u32[]{:S(2)}) collective-permute-start(bf16[896,128]{1,0:T(8,128)(2,1)S(1)} %get-tuple-element.66), channel_id=1, source_target_pairs={{0,16},{16,0},{1,17},{17,1},{2,18},{18,2},{3,19},{19,3},{4,20},{20... | collective-permute-start | bytes 688136 | tf_op jit(solution)/shard_map/ppermute | solution.py:20
  31.6 12.3 %all-to-all-start.1 = ((bf16[16,56,128]{2,1,0:T(8,128)(2,1)}), bf16[16,56,128]{2,1,0:T(8,128)(2,1)S(1)}, u32[]{:S(2)}, u32[]{:S(2)}) async-start(bf16[16,56,128]{2,1,0:T(8,128)(2,1)} %add_and_repeat.1), calls=%async_computation.1 | async-start | bytes 458752 | tf_op jit(solution)/shard_map/all_to_all | solution.py:568
  36.6 1.4 %collective-permute-start.4 = (bf16[8,8,1024]{2,1,0:T(8,128)(2,1)S(1)}, bf16[8,8,1024]{2,1,0:T(8,128)(2,1)S(1)}, u32[]{:S(2)}, u32[]{:S(2)}) collective-permute-start(bf16[8,8,1024]{2,1,0:T(8,128)(2,1)S(1)} %get-tuple-element.81), channel_id=1, source_target_pairs={{0,16},{16,0},{1,17},{17,1},{2,18},{18,2},{3,19},{19,3},{4,20},{20... | collective-permute-start | bytes 393224 | tf_op jit(solution)/shard_map/ppermute | solution.py:20
  43.9 1.5 %collective-permute-start.5 = (bf16[896,128]{1,0:T(8,128)(2,1)S(1)}, bf16[896,128]{1,0:T(8,128)(2,1)S(1)}, u32[]{:S(2)}, u32[]{:S(2)}) collective-permute-start(bf16[896,128]{1,0:T(8,128)(2,1)S(1)} %bitcast.10), channel_id=1, source_target_pairs={{0,16},{16,0},{1,17},{17,1},{2,18},{18,2},{3,19},{19,3},{4,20},{20... | collective-permute-start | bytes 688136 | tf_op jit(solution)/shard_map/ppermute | solution.py:20

commit v15 on v14

--- a/solution.py
+++ b/solution.py
@@ -430,13 +430,11 @@
     out[...] = (keep[...] + other[...].astype(F32)).astype(BF16)
 
 
-def add_and_repeat(terms, out):
+def add_terms(terms, out):
     total = terms[0].astype(F32)
     for index in range(1, terms.shape[0]):
         total = total + terms[index].astype(F32)
-    total = total.astype(BF16)
-    for index in range(out.shape[0]):
-        out[index] = total
+    out[...] = total.astype(BF16)
 
 
 def unpack(factor, is_first, rows, first, second, held, sems):
@@ -454,10 +452,10 @@
         for dy in range(3):
             t = 3 * dy + dx
             place = 9 * dx + 3 * dy
-            turned = rows[t * C:(t + 1) * C, :].astype(F32).T * factor
+            turned = rows[t * C:(t + 1) * C, :].T.astype(F32) * factor
             held[place] = turned[0:C]
             held[place + 1] = turned[C:2 * C]
-            turned = rows[(9 + t // 2) * C:(10 + t // 2) * C, :].astype(F32).T * factor
+            turned = rows[(9 + t // 2) * C:(10 + t // 2) * C, :].T.astype(F32) * factor
             held[place + 2] = turned[t % 2 * C:(t % 2 + 1) * C]
         each(lambda target: copy_of(dx, target).start())
     each(lambda target: [copy_of(dx, target).wait() for dx in range(3)])
@@ -563,8 +561,9 @@
     other, keep = lax.optimization_barrier((other, keep))
     both, = call(add_pair, "add_pair", [(keep, True), (other, True)], [near((rows, lane), BF16)])
     terms = lax.all_to_all(both.reshape(ranks, rows // ranks, lane), ("grp", "gy"), 0, 0)
-    spread, = call(add_and_repeat, "add_and_repeat", [(terms, True)], [near(terms.shape, BF16)])
-    spread, hd, w2 = lax.optimization_barrier((spread, hd, w2))
+    part, = call(add_terms, "add_terms", [(terms, True)], [near(terms.shape[1:], BF16)])
+    part, hd, w2 = lax.optimization_barrier((part, hd, w2))
+    spread = jnp.broadcast_to(part[None], terms.shape)
     sums = lax.all_to_all(spread, ("grp", "gy"), 0, 0).reshape(rows, lane)
     mine, given = call(
         output_conv, "output_conv", [(hd, True), (w2, True)],

time: 46.7 us -> 46.7 us (level)
  local copies, waits for them, and re-layouts: 0 us -> 0.72 us
  Pallas kernels: 13.8 us -> 13.1 us
    pallas_call x12, Pallas kernels: 13.8 us -> 13.1 us  [call(): pl.pallas_call(body, out_shape=list(outs), in_specs=[pl.BlockSpec(memory_...]
    broadcast_in_dim x0 -> x1, local copies, waits for them, and re-layouts: none -> 0.72 us  [shards(): spread = jnp.broadcast_to(part[None], terms.shape)]
where the time goes in v15:
time: 46.7 us; the launch traced here: 46.5 us
  blocking collectives  15.7 us (34%)
  Pallas kernels  13.1 us (28%)
  starting transfers between devices  8.68 us (19%)
  waiting for transfers between devices  7.56 us (16%)
  between operations  0.74 us (2%)
  local copies, waits for them, and re-layouts  0.72 us (2%)
    all_to_all x1, blocking collectives, shards(): lax.all_to_all(both.reshape(ranks, rows // ranks, lane), ('grp', 'gy'), 0...  15.7 us
    pallas_call x12, Pallas kernels, call(): pl.pallas_call(body, out_shape=list(outs), in_specs=[pl.BlockSpec(memory_...  13.1 us
    all_to_all x1, waiting for transfers between devices, shards(): sums = lax.all_to_all(spread, ('grp', 'gy'), 0, 0).reshape(rows, lane)  5.06 us
    ppermute x5, starting transfers between devices, swap(): return lax.ppermute(array, 'gx', [(0, 1), (1, 0)])  4.49 us
    all_to_all x1, starting transfers between devices, shards(): sums = lax.all_to_all(spread, ('grp', 'gy'), 0, 0).reshape(rows, lane)  3.53 us
    ppermute x5, waiting for transfers between devices, swap(): return lax.ppermute(array, 'gx', [(0, 1), (1, 0)])  2.51 us
  transfers between devices with their start and end apart: 7, of which 5 were waited for; matrix products, arithmetic and copies ran while one was open for 0% of the time, Pallas kernels for 20%

profile of v15, /device:TPU:0, one launch (start us, length us, event | category | flops | bytes accessed | tf_op | source)
XLA Modules:
  0.0 46.5 jit_solution(18108120327346808257)
XLA Ops:
  0.6 1.3 %pack_edges.1 = (bf16[8,16,1024]{2,1,0:T(8,128)(2,1)S(1)}, bf16[8,16,1024]{2,1,0:T(8,128)(2,1)S(1)}, bf16[3,8,1024]{2,1,0:T(8,128)(2,1)S(1)}, bf16[3,8,1024]{2,1...) custom-call(bf16[8,16,1024]{2,1,0:T(8,128)(2,1)} %bitcast.17, ...), custom_call_target="tpu_custom_call" | custom-call | bytes 966656 | tf_op jit(solution)/shard_map/pack_edges/pallas_call | solution.py:479
  2.0 0.5 %collective-permute-start = (bf16[3,8,1024]{2,1,0:T(8,128)(2,1)S(1)}, bf16[3,8,1024]{2,1,0:T(8,128)(2,1)S(1)}, u32[]{:S(2)}, u32[]{:S(2)}) collective-permute-start(bf16[3,8,1024]{2,1,0:T(8,128)(2,1)S(1)} %get-tuple-element.53), channel_id=1, source_target_pairs={{0,16},{16,0},{1,17},{17,1},{2,18},{18,2},{3,19},{19,3},{4,20},{20... | collective-permute-start | bytes 147464 | tf_op jit(solution)/shard_map/ppermute | solution.py:20
  2.5 0.7 %pack_halves.1 = (bf16[19,8,1024]{2,1,0:T(8,128)(2,1)S(1)}, bf16[19,8,1024]{2,1,0:T(8,128)(2,1)S(1)}, bf16[2304,128]{1,0:T(8,128)(2,1)S(1)}, bf16[128,2304]{1,0:T(8,128)(2,1)S(1)}) custom-call(bf16[8,16,1024]{2,1,0:T(8,128)(2,1)S(1)} %get-tuple-element.47.field, bf16[8,16,1024]{2,1,0:T(8,128)(2,1)S(1)} %get-tuple-element.48.cot, ...), custom_call_target="tpu_custom_call" | custom-call | flops 1000000000 | bytes 966656 | tf_op jit(solution)/shard_map/pack_halves/pallas_call | solution.py:479
  3.2 0.2 collective-permute-done.taken
  3.4 0.3 collective-permute-start.1
  3.7 0.7 %collective-permute-start.2 = (bf16[3,16,1024]{2,1,0:T(8,128)(2,1)S(1)}, bf16[3,16,1024]{2,1,0:T(8,128)(2,1)S(1)}, u32[]{:S(2)}, u32[]{:S(2)}) collective-permute-start(bf16[3,16,1024]{2,1,0:T(8,128)(2,1)S(1)} %join_edges.1), channel_id=1, source_target_pairs={{16,4},{20,8},{24,12},{4,16},{8,20},{12,24},{17,5},{21,9},{25,13},... | collective-permute-start | bytes 294920 | tf_op jit(solution)/shard_map/ppermute | solution.py:531
  4.4 0.6 %collective-permute-done.1.got = bf16[19,8,1024]{2,1,0:T(8,128)(2,1)S(1)} collective-permute-done((bf16[19,8,1024]{2,1,0:T(8,128)(2,1)S(1)}, bf16[19,8,1024]{2,1,0:T(8,128)(2,1)S(1)}, u32[]{:S(2)}, u32[]{:S(2)}) %collective-permute-start.1) | collective-permute-done | bytes 311328 | tf_op jit(solution)/shard_map/ppermute | solution.py:20
  5.0 4.0 %interior.1 = (bf16[3,12,16,1280]{3,2,1,0:T(8,128)(2,1)S(1)}, bf16[3,10,16,1280]{3,2,1,0:T(8,128)(2,1)S(1)}, bf16[3,10,16,1152]{3,2,1,0:T(8,128)(2,1)S(1)}, bf16...) custom-call(bf16[19,8,1024]{2,1,0:T(8,128)(2,1)S(1)} %get-tuple-element.51.own, ...), custom_call_target="tpu_custom_call" | custom-call | flops 4000000000 | bytes 1802240 | tf_op jit(solution)/shard_map/interior/pallas_call | solution.py:479
  9.0 1.4 %late_rows.1 = (bf16[3,12,16,1280]{3,2,1,0:T(8,128)(2,1)S(1)}, bf16[3,10,16,1280]{3,2,1,0:T(8,128)(2,1)S(1)}, bf16[3,10,16,1152]{3,2,1,0:T(8,128)(2,1)S(1)}, bf1...) custom-call(bf16[3,12,16,1280]{3,2,1,0:T(8,128)(2,1)S(1)} %get-tuple, ...), custom_call_target="tpu_custom_call", output_to_operand_aliasing={{0}: (0, {}), {1}: (1, {}), {2}: (2, {}), {3}: (3, {}), {4}... | custom-call | flops 1000000000 | bytes 8036352 | tf_op jit(solution)/shard_map/late_rows/pallas_call | solution.py:479
  10.4 3.5 %collective-permute-start.3 = (bf16[896,128]{1,0:T(8,128)(2,1)S(1)}, bf16[896,128]{1,0:T(8,128)(2,1)S(1)}, u32[]{:S(2)}, u32[]{:S(2)}) collective-permute-start(bf16[896,128]{1,0:T(8,128)(2,1)S(1)} %get-tuple-element.66), channel_id=1, source_target_pairs={{0,16},{16,0},{1,17},{17,1},{2,18},{18,2},{3,19},{19,3},{4,20},{20... | collective-permute-start | bytes 688136 | tf_op jit(solution)/shard_map/ppermute | solution.py:20
  13.9 1.1 %keep_sums.1 = (bf16[3,10,16,1152]{3,2,1,0:T(8,128)(2,1)S(1)}, f32[10,32,1152]{2,1,0:T(8,128)S(1)}, f32[896,128]{1,0:T(8,128)S(1)}) custom-call(bf16[3,12,16,1280]{3,2,1,0:T(8,128)(2,1)S(1)} %get-tuple-element.67.fd, bf16[3,10,16,1280]{3,2,1,0:T(8,128)(2,1)S(1)} %get-tuple-element.68.cd, ...), custom_call_target="tpu_custom_call", output_to_operand_aliasing={{0}: (2, {}), {1}: (4, {})} | custom-call | flops 2000000000 | bytes 6242304 | tf_op jit(solution)/shard_map/keep_sums/pallas_call | solution.py:479
  15.1 0.1 add_pair.1
  15.1 15.7 %all_to_all.10.terms = bf16[16,56,128]{2,1,0:T(8,128)(2,1)S(1)} all-to-all(bf16[16,56,128]{2,1,0:T(8,128)(2,1)S(1)} %bitcast.9), channel_id=1, replica_groups=mesh['gx'=2,'gy'=4,'grp'=4] {'grp','gy'}, dimensions={0} | all-to-all | bytes 458752 | tf_op jit(solution)/shard_map/all_to_all | solution.py:563
  30.9 0.7 %broadcast_in_dim.4 = bf16[16,56,128]{2,1,0:T(8,128)(2,1)} broadcast(bf16[56,128]{1,0:T(8,128)(2,1)S(1)} %add_terms.1), dimensions={1,2} | broadcast | bytes 243712 | tf_op jit(solution)/shard_map/broadcast_in_dim | solution.py:566
  31.6 3.5 %all-to-all-start.1 = ((bf16[16,56,128]{2,1,0:T(8,128)(2,1)}), bf16[16,56,128]{2,1,0:T(8,128)(2,1)S(1)}, u32[]{:S(2)}, u32[]{:S(2)}) async-start(bf16[16,56,128]{2,1,0:T(8,128)(2,1)} %broadcast_in_dim.4), calls=%async_computation.1 | async-start | bytes 458752 | tf_op jit(solution)/shard_map/all_to_all | solution.py:567
  35.1 1.5 %output_conv.1 = (bf16[8,8,1024]{2,1,0:T(8,128)(2,1)S(1)}, bf16[8,8,1024]{2,1,0:T(8,128)(2,1)S(1)}) custom-call(bf16[3,10,16,1152]{3,2,1,0:T(8,128)(2,1)S(1)} %get-tuple-element.78.hd, bf16[27,64,64]{2,1,0:T(8,128)(2,1)S(1)} %get-tuple-element.79.w2), custom_call_target="tpu_custom_call" | custom-call | flops 2000000000 | bytes 1327104 | tf_op jit(solution)/shard_map/output_conv/pallas_call | solution.py:479
  36.6 0.1 collective-permute-start.4
  36.7 1.3 %collective-permute-done.4.other = bf16[8,8,1024]{2,1,0:T(8,128)(2,1)S(1)} collective-permute-done((bf16[8,8,1024]{2,1,0:T(8,128)(2,1)S(1)}, bf16[8,8,1024]{2,1,0:T(8,128)(2,1)S(1)}, u32[]{:S(2)}, u32[]{:S(2)}) %collective-permute-start.4) | collective-permute-done | bytes 131104 | tf_op jit(solution)/shard_map/ppermute | solution.py:20
  38.0 0.8 %finish_output.1 = bf16[8,16,1024]{2,1,0:T(8,128)(2,1)} custom-call(bf16[8,8,1024]{2,1,0:T(8,128)(2,1)S(1)} %get-tuple-element.80.mine, bf16[8,8,1024]{2,1,0:T(8,128)(2,1)S(1)} %collective-permute-done.4.other), custom_call_target="tpu_custom_call" | custom-call | bytes 262144 | tf_op jit(solution)/shard_map/finish_output/pallas_call | solution.py:479
  38.9 5.1 %all-to-all-done.1 = bf16[16,56,128]{2,1,0:T(8,128)(2,1)S(1)} async-done(((bf16[16,56,128]{2,1,0:T(8,128)(2,1)}), bf16[16,56,128]{2,1,0:T(8,128)(2,1)S(1)}, u32[]{:S(2)}, u32[]{:S(2)}) %all-to-all-start.1) | async-done | bytes 229408 | tf_op jit(solution)/shard_map/all_to_all | solution.py:567
  43.9 0.0 collective-permute-start.5
  43.9 1.0 %unpack_own.1 = (f32[27,64,64]{2,1,0:T(8,128)}, f32[27,64,64]{2,1,0:T(8,128)}) custom-call(bf16[896,128]{1,0:T(8,128)(2,1)S(1)} %bitcast.11), custom_call_target="tpu_custom_call" | custom-call | bytes 229376 | tf_op jit(solution)/shard_map/unpack_own/pallas_call | solution.py:479
  45.0 0.4 collective-permute-done.5.rows
  45.4 1.0 %unpack_other.1 = (f32[27,64,64]{2,1,0:T(8,128)}, f32[27,64,64]{2,1,0:T(8,128)}) custom-call(bf16[896,128]{1,0:T(8,128)(2,1)S(1)} %collective-permute-done.5.rows, f32[27,64,64]{2,1,0:T(8,128)} %get-tuple-element.87.first_in, f32[27,64,64]{2,1,0:T(8,128)} %get-tuple-element.88.second_in), custom_call_target="tpu_custom_call", output_to_operand_aliasing={{0}: (1, {}), {1}: (2, {})} | custom-call | bytes 1114112 | tf_op jit(solution)/shard_map/unpack_other/pallas_call | solution.py:479
  (4 shorter events, 0.1 us)
Async XLA Ops:
  2.0 1.4 %collective-permute-start = (bf16[3,8,1024]{2,1,0:T(8,128)(2,1)S(1)}, bf16[3,8,1024]{2,1,0:T(8,128)(2,1)S(1)}, u32[]{:S(2)}, u32[]{:S(2)}) collective-permute-start(bf16[3,8,1024]{2,1,0:T(8,128)(2,1)S(1)} %get-tuple-element.53), channel_id=1, source_target_pairs={{0,16},{16,0},{1,17},{17,1},{2,18},{18,2},{3,19},{19,3},{4,20},{20... | collective-permute-start | bytes 147464 | tf_op jit(solution)/shard_map/ppermute | solution.py:20
  3.4 1.6 %collective-permute-start.1 = (bf16[19,8,1024]{2,1,0:T(8,128)(2,1)S(1)}, bf16[19,8,1024]{2,1,0:T(8,128)(2,1)S(1)}, u32[]{:S(2)}, u32[]{:S(2)}) collective-permute-start(bf16[19,8,1024]{2,1,0:T(8,128)(2,1)S(1)} %get-tuple-element.55), channel_id=1, source_target_pairs={{0,16},{16,0},{1,17},{17,1},{2,18},{18,2},{3,19},{19,3},{4,20},{20... | collective-permute-start | bytes 933896 | tf_op jit(solution)/shard_map/ppermute | solution.py:20
  3.7 5.3 %collective-permute-start.2 = (bf16[3,16,1024]{2,1,0:T(8,128)(2,1)S(1)}, bf16[3,16,1024]{2,1,0:T(8,128)(2,1)S(1)}, u32[]{:S(2)}, u32[]{:S(2)}) collective-permute-start(bf16[3,16,1024]{2,1,0:T(8,128)(2,1)S(1)} %join_edges.1), channel_id=1, source_target_pairs={{16,4},{20,8},{24,12},{4,16},{8,20},{12,24},{17,5},{21,9},{25,13},... | collective-permute-start | bytes 294920 | tf_op jit(solution)/shard_map/ppermute | solution.py:531
  10.4 4.7 %collective-permute-start.3 = (bf16[896,128]{1,0:T(8,128)(2,1)S(1)}, bf16[896,128]{1,0:T(8,128)(2,1)S(1)}, u32[]{:S(2)}, u32[]{:S(2)}) collective-permute-start(bf16[896,128]{1,0:T(8,128)(2,1)S(1)} %get-tuple-element.66), channel_id=1, source_target_pairs={{0,16},{16,0},{1,17},{17,1},{2,18},{18,2},{3,19},{19,3},{4,20},{20... | collective-permute-start | bytes 688136 | tf_op jit(solution)/shard_map/ppermute | solution.py:20
  31.6 12.3 %all-to-all-start.1 = ((bf16[16,56,128]{2,1,0:T(8,128)(2,1)}), bf16[16,56,128]{2,1,0:T(8,128)(2,1)S(1)}, u32[]{:S(2)}, u32[]{:S(2)}) async-start(bf16[16,56,128]{2,1,0:T(8,128)(2,1)} %broadcast_in_dim.4), calls=%async_computation.1 | async-start | bytes 458752 | tf_op jit(solution)/shard_map/all_to_all | solution.py:567
  36.6 1.4 %collective-permute-start.4 = (bf16[8,8,1024]{2,1,0:T(8,128)(2,1)S(1)}, bf16[8,8,1024]{2,1,0:T(8,128)(2,1)S(1)}, u32[]{:S(2)}, u32[]{:S(2)}) collective-permute-start(bf16[8,8,1024]{2,1,0:T(8,128)(2,1)S(1)} %get-tuple-element.81), channel_id=1, source_target_pairs={{0,16},{16,0},{1,17},{17,1},{2,18},{18,2},{3,19},{19,3},{4,20},{20... | collective-permute-start | bytes 393224 | tf_op jit(solution)/shard_map/ppermute | solution.py:20
  43.9 1.5 %collective-permute-start.5 = (bf16[896,128]{1,0:T(8,128)(2,1)S(1)}, bf16[896,128]{1,0:T(8,128)(2,1)S(1)}, u32[]{:S(2)}, u32[]{:S(2)}) collective-permute-start(bf16[896,128]{1,0:T(8,128)(2,1)S(1)} %bitcast.10), channel_id=1, source_target_pairs={{0,16},{16,0},{1,17},{17,1},{2,18},{18,2},{3,19},{19,3},{4,20},{20... | collective-permute-start | bytes 688136 | tf_op jit(solution)/shard_map/ppermute | solution.py:20

commit v16 on v15

--- a/solution.py
+++ b/solution.py
@@ -239,6 +239,7 @@
 
     @pl.when(gx != 0)
     def _():
+        fd[:, count + 2:count + 4] = jnp.zeros((3, 2) + fd.shape[2:], BF16)
         for t, total in enumerate(first_products(fd, pg)):
             acc[t] = total
 
@@ -560,11 +561,11 @@
         flops=2 * 10 ** 9, aliases={2: 0, 4: 1})
     other, keep = lax.optimization_barrier((other, keep))
     both, = call(add_pair, "add_pair", [(keep, True), (other, True)], [near((rows, lane), BF16)])
-    terms = lax.all_to_all(both.reshape(ranks, rows // ranks, lane), ("grp", "gy"), 0, 0)
+    terms = lax.all_to_all(both.reshape(ranks, rows // ranks, lane), ("gy", "grp"), 0, 0)
     part, = call(add_terms, "add_terms", [(terms, True)], [near(terms.shape[1:], BF16)])
     part, hd, w2 = lax.optimization_barrier((part, hd, w2))
     spread = jnp.broadcast_to(part[None], terms.shape)
-    sums = lax.all_to_all(spread, ("grp", "gy"), 0, 0).reshape(rows, lane)
+    sums = lax.all_to_all(spread, ("gy", "grp"), 0, 0).reshape(rows, lane)
     mine, given = call(
         output_conv, "output_conv", [(hd, True), (w2, True)],
         [near((count, nx, width), BF16), near((count, nx, width), BF16)],

time: 46.7 us -> 47.4 us (1.015)
  blocking collectives: 15.7 us -> 16.3 us
    all_to_all x1, blocking collectives: 15.7 us -> 16.3 us  [shards(): lax.all_to_all(both.reshape(ranks, rows // ranks, lane), ('gy', 'grp'), 0...]
where the time goes in v16:
time: 47.4 us; the launch traced here: 47.1 us
  blocking collectives  16.3 us (34%)
  Pallas kernels  13.1 us (28%)
  starting transfers between devices  8.68 us (18%)
  waiting for transfers between devices  7.59 us (16%)
  between operations  0.74 us (2%)
  local copies, waits for them, and re-layouts  0.72 us (2%)
    all_to_all x1, blocking collectives, shards(): lax.all_to_all(both.reshape(ranks, rows // ranks, lane), ('gy', 'grp'), 0...  16.3 us
    pallas_call x12, Pallas kernels, call(): pl.pallas_call(body, out_shape=list(outs), in_specs=[pl.BlockSpec(memory_...  13.1 us
    all_to_all x1, waiting for transfers between devices, shards(): sums = lax.all_to_all(spread, ('gy', 'grp'), 0, 0).reshape(rows, lane)  5.08 us
    ppermute x5, starting transfers between devices, swap(): return lax.ppermute(array, 'gx', [(0, 1), (1, 0)])  4.49 us
    all_to_all x1, starting transfers between devices, shards(): sums = lax.all_to_all(spread, ('gy', 'grp'), 0, 0).reshape(rows, lane)  3.53 us
    ppermute x5, waiting for transfers between devices, swap(): return lax.ppermute(array, 'gx', [(0, 1), (1, 0)])  2.51 us
  transfers between devices with their start and end apart: 7, of which 5 were waited for; matrix products, arithmetic and copies ran while one was open for 0% of the time, Pallas kernels for 20%

profile of v16, /device:TPU:0, one launch (start us, length us, event | category | flops | bytes accessed | tf_op | source)
XLA Modules:
  0.0 47.1 jit_solution(14166608646065186031)
XLA Ops:
  0.6 1.3 %pack_edges.1 = (bf16[8,16,1024]{2,1,0:T(8,128)(2,1)S(1)}, bf16[8,16,1024]{2,1,0:T(8,128)(2,1)S(1)}, bf16[3,8,1024]{2,1,0:T(8,128)(2,1)S(1)}, bf16[3,8,1024]{2,1...) custom-call(bf16[8,16,1024]{2,1,0:T(8,128)(2,1)} %bitcast.17, ...), custom_call_target="tpu_custom_call" | custom-call | bytes 966656 | tf_op jit(solution)/shard_map/pack_edges/pallas_call | solution.py:480
  2.0 0.5 %collective-permute-start = (bf16[3,8,1024]{2,1,0:T(8,128)(2,1)S(1)}, bf16[3,8,1024]{2,1,0:T(8,128)(2,1)S(1)}, u32[]{:S(2)}, u32[]{:S(2)}) collective-permute-start(bf16[3,8,1024]{2,1,0:T(8,128)(2,1)S(1)} %get-tuple-element.53), channel_id=1, source_target_pairs={{0,16},{16,0},{1,17},{17,1},{2,18},{18,2},{3,19},{19,3},{4,20},{20... | collective-permute-start | bytes 147464 | tf_op jit(solution)/shard_map/ppermute | solution.py:20
  2.5 0.7 %pack_halves.1 = (bf16[19,8,1024]{2,1,0:T(8,128)(2,1)S(1)}, bf16[19,8,1024]{2,1,0:T(8,128)(2,1)S(1)}, bf16[2304,128]{1,0:T(8,128)(2,1)S(1)}, bf16[128,2304]{1,0:T(8,128)(2,1)S(1)}) custom-call(bf16[8,16,1024]{2,1,0:T(8,128)(2,1)S(1)} %get-tuple-element.47.field, bf16[8,16,1024]{2,1,0:T(8,128)(2,1)S(1)} %get-tuple-element.48.cot, ...), custom_call_target="tpu_custom_call" | custom-call | flops 1000000000 | bytes 966656 | tf_op jit(solution)/shard_map/pack_halves/pallas_call | solution.py:480
  3.2 0.2 collective-permute-done.taken
  3.4 0.3 collective-permute-start.1
  3.7 0.7 %collective-permute-start.2 = (bf16[3,16,1024]{2,1,0:T(8,128)(2,1)S(1)}, bf16[3,16,1024]{2,1,0:T(8,128)(2,1)S(1)}, u32[]{:S(2)}, u32[]{:S(2)}) collective-permute-start(bf16[3,16,1024]{2,1,0:T(8,128)(2,1)S(1)} %join_edges.1), channel_id=1, source_target_pairs={{16,4},{20,8},{24,12},{4,16},{8,20},{12,24},{17,5},{21,9},{25,13},... | collective-permute-start | bytes 294920 | tf_op jit(solution)/shard_map/ppermute | solution.py:532
  4.4 0.6 %collective-permute-done.1.got = bf16[19,8,1024]{2,1,0:T(8,128)(2,1)S(1)} collective-permute-done((bf16[19,8,1024]{2,1,0:T(8,128)(2,1)S(1)}, bf16[19,8,1024]{2,1,0:T(8,128)(2,1)S(1)}, u32[]{:S(2)}, u32[]{:S(2)}) %collective-permute-start.1) | collective-permute-done | bytes 311328 | tf_op jit(solution)/shard_map/ppermute | solution.py:20
  5.0 4.0 %interior.1 = (bf16[3,12,16,1280]{3,2,1,0:T(8,128)(2,1)S(1)}, bf16[3,10,16,1280]{3,2,1,0:T(8,128)(2,1)S(1)}, bf16[3,10,16,1152]{3,2,1,0:T(8,128)(2,1)S(1)}, bf16...) custom-call(bf16[19,8,1024]{2,1,0:T(8,128)(2,1)S(1)} %get-tuple-element.51.own, ...), custom_call_target="tpu_custom_call" | custom-call | flops 4000000000 | bytes 1802240 | tf_op jit(solution)/shard_map/interior/pallas_call | solution.py:480
  9.0 1.4 %late_rows.1 = (bf16[3,12,16,1280]{3,2,1,0:T(8,128)(2,1)S(1)}, bf16[3,10,16,1280]{3,2,1,0:T(8,128)(2,1)S(1)}, bf16[3,10,16,1152]{3,2,1,0:T(8,128)(2,1)S(1)}, bf1...) custom-call(bf16[3,12,16,1280]{3,2,1,0:T(8,128)(2,1)S(1)} %get-tuple, ...), custom_call_target="tpu_custom_call", output_to_operand_aliasing={{0}: (0, {}), {1}: (1, {}), {2}: (2, {}), {3}: (3, {}), {4}... | custom-call | flops 1000000000 | bytes 8036352 | tf_op jit(solution)/shard_map/late_rows/pallas_call | solution.py:480
  10.4 3.5 %collective-permute-start.3 = (bf16[896,128]{1,0:T(8,128)(2,1)S(1)}, bf16[896,128]{1,0:T(8,128)(2,1)S(1)}, u32[]{:S(2)}, u32[]{:S(2)}) collective-permute-start(bf16[896,128]{1,0:T(8,128)(2,1)S(1)} %get-tuple-element.66), channel_id=1, source_target_pairs={{0,16},{16,0},{1,17},{17,1},{2,18},{18,2},{3,19},{19,3},{4,20},{20... | collective-permute-start | bytes 688136 | tf_op jit(solution)/shard_map/ppermute | solution.py:20
  13.9 1.1 %keep_sums.1 = (bf16[3,10,16,1152]{3,2,1,0:T(8,128)(2,1)S(1)}, f32[10,32,1152]{2,1,0:T(8,128)S(1)}, f32[896,128]{1,0:T(8,128)S(1)}) custom-call(bf16[3,12,16,1280]{3,2,1,0:T(8,128)(2,1)S(1)} %get-tuple-element.67.fd, bf16[3,10,16,1280]{3,2,1,0:T(8,128)(2,1)S(1)} %get-tuple-element.68.cd, ...), custom_call_target="tpu_custom_call", output_to_operand_aliasing={{0}: (2, {}), {1}: (4, {})} | custom-call | flops 2000000000 | bytes 6242304 | tf_op jit(solution)/shard_map/keep_sums/pallas_call | solution.py:480
  15.1 0.1 add_pair.1
  15.1 16.3 %all_to_all.10.terms = bf16[16,56,128]{2,1,0:T(8,128)(2,1)S(1)} all-to-all(bf16[16,56,128]{2,1,0:T(8,128)(2,1)S(1)} %bitcast.9), channel_id=1, replica_groups=mesh['gx'=2,'gy'=4,'grp'=4] {'gy','grp'}, dimensions={0} | all-to-all | bytes 458752 | tf_op jit(solution)/shard_map/all_to_all | solution.py:564
  31.5 0.7 %broadcast_in_dim.4 = bf16[16,56,128]{2,1,0:T(8,128)(2,1)} broadcast(bf16[56,128]{1,0:T(8,128)(2,1)S(1)} %add_terms.1), dimensions={1,2} | broadcast | bytes 243712 | tf_op jit(solution)/shard_map/broadcast_in_dim | solution.py:567
  32.2 3.5 %all-to-all-start.1 = ((bf16[16,56,128]{2,1,0:T(8,128)(2,1)}), bf16[16,56,128]{2,1,0:T(8,128)(2,1)S(1)}, u32[]{:S(2)}, u32[]{:S(2)}) async-start(bf16[16,56,128]{2,1,0:T(8,128)(2,1)} %broadcast_in_dim.4), calls=%async_computation.1 | async-start | bytes 458752 | tf_op jit(solution)/shard_map/all_to_all | solution.py:568
  35.7 1.5 %output_conv.1 = (bf16[8,8,1024]{2,1,0:T(8,128)(2,1)S(1)}, bf16[8,8,1024]{2,1,0:T(8,128)(2,1)S(1)}) custom-call(bf16[3,10,16,1152]{3,2,1,0:T(8,128)(2,1)S(1)} %get-tuple-element.78.hd, bf16[27,64,64]{2,1,0:T(8,128)(2,1)S(1)} %get-tuple-element.79.w2), custom_call_target="tpu_custom_call" | custom-call | flops 2000000000 | bytes 1327104 | tf_op jit(solution)/shard_map/output_conv/pallas_call | solution.py:480
  37.2 0.1 collective-permute-start.4
  37.3 1.3 %collective-permute-done.4.other = bf16[8,8,1024]{2,1,0:T(8,128)(2,1)S(1)} collective-permute-done((bf16[8,8,1024]{2,1,0:T(8,128)(2,1)S(1)}, bf16[8,8,1024]{2,1,0:T(8,128)(2,1)S(1)}, u32[]{:S(2)}, u32[]{:S(2)}) %collective-permute-start.4) | collective-permute-done | bytes 131104 | tf_op jit(solution)/shard_map/ppermute | solution.py:20
  38.7 0.8 %finish_output.1 = bf16[8,16,1024]{2,1,0:T(8,128)(2,1)} custom-call(bf16[8,8,1024]{2,1,0:T(8,128)(2,1)S(1)} %get-tuple-element.80.mine, bf16[8,8,1024]{2,1,0:T(8,128)(2,1)S(1)} %collective-permute-done.4.other), custom_call_target="tpu_custom_call" | custom-call | bytes 262144 | tf_op jit(solution)/shard_map/finish_output/pallas_call | solution.py:480
  39.5 5.1 %all-to-all-done.1 = bf16[16,56,128]{2,1,0:T(8,128)(2,1)S(1)} async-done(((bf16[16,56,128]{2,1,0:T(8,128)(2,1)}), bf16[16,56,128]{2,1,0:T(8,128)(2,1)S(1)}, u32[]{:S(2)}, u32[]{:S(2)}) %all-to-all-start.1) | async-done | bytes 229408 | tf_op jit(solution)/shard_map/all_to_all | solution.py:568
  44.6 0.0 collective-permute-start.5
  44.6 1.0 %unpack_own.1 = (f32[27,64,64]{2,1,0:T(8,128)}, f32[27,64,64]{2,1,0:T(8,128)}) custom-call(bf16[896,128]{1,0:T(8,128)(2,1)S(1)} %bitcast.11), custom_call_target="tpu_custom_call" | custom-call | bytes 229376 | tf_op jit(solution)/shard_map/unpack_own/pallas_call | solution.py:480
  45.6 0.4 collective-permute-done.5.rows
  46.1 1.0 %unpack_other.1 = (f32[27,64,64]{2,1,0:T(8,128)}, f32[27,64,64]{2,1,0:T(8,128)}) custom-call(bf16[896,128]{1,0:T(8,128)(2,1)S(1)} %collective-permute-done.5.rows, f32[27,64,64]{2,1,0:T(8,128)} %get-tuple-element.87.first_in, f32[27,64,64]{2,1,0:T(8,128)} %get-tuple-element.88.second_in), custom_call_target="tpu_custom_call", output_to_operand_aliasing={{0}: (1, {}), {1}: (2, {})} | custom-call | bytes 1114112 | tf_op jit(solution)/shard_map/unpack_other/pallas_call | solution.py:480
  (4 shorter events, 0.1 us)
Async XLA Ops:
  2.0 1.4 %collective-permute-start = (bf16[3,8,1024]{2,1,0:T(8,128)(2,1)S(1)}, bf16[3,8,1024]{2,1,0:T(8,128)(2,1)S(1)}, u32[]{:S(2)}, u32[]{:S(2)}) collective-permute-start(bf16[3,8,1024]{2,1,0:T(8,128)(2,1)S(1)} %get-tuple-element.53), channel_id=1, source_target_pairs={{0,16},{16,0},{1,17},{17,1},{2,18},{18,2},{3,19},{19,3},{4,20},{20... | collective-permute-start | bytes 147464 | tf_op jit(solution)/shard_map/ppermute | solution.py:20
  3.4 1.6 %collective-permute-start.1 = (bf16[19,8,1024]{2,1,0:T(8,128)(2,1)S(1)}, bf16[19,8,1024]{2,1,0:T(8,128)(2,1)S(1)}, u32[]{:S(2)}, u32[]{:S(2)}) collective-permute-start(bf16[19,8,1024]{2,1,0:T(8,128)(2,1)S(1)} %get-tuple-element.55), channel_id=1, source_target_pairs={{0,16},{16,0},{1,17},{17,1},{2,18},{18,2},{3,19},{19,3},{4,20},{20... | collective-permute-start | bytes 933896 | tf_op jit(solution)/shard_map/ppermute | solution.py:20
  3.7 5.3 %collective-permute-start.2 = (bf16[3,16,1024]{2,1,0:T(8,128)(2,1)S(1)}, bf16[3,16,1024]{2,1,0:T(8,128)(2,1)S(1)}, u32[]{:S(2)}, u32[]{:S(2)}) collective-permute-start(bf16[3,16,1024]{2,1,0:T(8,128)(2,1)S(1)} %join_edges.1), channel_id=1, source_target_pairs={{16,4},{20,8},{24,12},{4,16},{8,20},{12,24},{17,5},{21,9},{25,13},... | collective-permute-start | bytes 294920 | tf_op jit(solution)/shard_map/ppermute | solution.py:532
  10.4 4.7 %collective-permute-start.3 = (bf16[896,128]{1,0:T(8,128)(2,1)S(1)}, bf16[896,128]{1,0:T(8,128)(2,1)S(1)}, u32[]{:S(2)}, u32[]{:S(2)}) collective-permute-start(bf16[896,128]{1,0:T(8,128)(2,1)S(1)} %get-tuple-element.66), channel_id=1, source_target_pairs={{0,16},{16,0},{1,17},{17,1},{2,18},{18,2},{3,19},{19,3},{4,20},{20... | collective-permute-start | bytes 688136 | tf_op jit(solution)/shard_map/ppermute | solution.py:20
  32.2 12.4 %all-to-all-start.1 = ((bf16[16,56,128]{2,1,0:T(8,128)(2,1)}), bf16[16,56,128]{2,1,0:T(8,128)(2,1)S(1)}, u32[]{:S(2)}, u32[]{:S(2)}) async-start(bf16[16,56,128]{2,1,0:T(8,128)(2,1)} %broadcast_in_dim.4), calls=%async_computation.1 | async-start | bytes 458752 | tf_op jit(solution)/shard_map/all_to_all | solution.py:568
  37.2 1.4 %collective-permute-start.4 = (bf16[8,8,1024]{2,1,0:T(8,128)(2,1)S(1)}, bf16[8,8,1024]{2,1,0:T(8,128)(2,1)S(1)}, u32[]{:S(2)}, u32[]{:S(2)}) collective-permute-start(bf16[8,8,1024]{2,1,0:T(8,128)(2,1)S(1)} %get-tuple-element.81), channel_id=1, source_target_pairs={{0,16},{16,0},{1,17},{17,1},{2,18},{18,2},{3,19},{19,3},{4,20},{20... | collective-permute-start | bytes 393224 | tf_op jit(solution)/shard_map/ppermute | solution.py:20
  44.6 1.5 %collective-permute-start.5 = (bf16[896,128]{1,0:T(8,128)(2,1)S(1)}, bf16[896,128]{1,0:T(8,128)(2,1)S(1)}, u32[]{:S(2)}, u32[]{:S(2)}) collective-permute-start(bf16[896,128]{1,0:T(8,128)(2,1)S(1)} %bitcast.10), channel_id=1, source_target_pairs={{0,16},{16,0},{1,17},{17,1},{2,18},{18,2},{3,19},{19,3},{4,20},{20... | collective-permute-start | bytes 688136 | tf_op jit(solution)/shard_map/ppermute | solution.py:20

commit v17 on v15

--- a/solution.py
+++ b/solution.py
@@ -239,6 +239,7 @@
 
     @pl.when(gx != 0)
     def _():
+        fd[:, count + 2:count + 4] = jnp.zeros((3, 2) + fd.shape[2:], BF16)
         for t, total in enumerate(first_products(fd, pg)):
             acc[t] = total
 

time: 46.7 us -> 46.7 us (level)
  no operation moved by 1% of the time
where the time goes in v17:
time: 46.7 us; the launch traced here: 46.5 us
  blocking collectives  15.7 us (34%)
  Pallas kernels  13.1 us (28%)
  starting transfers between devices  8.68 us (19%)
  waiting for transfers between devices  7.56 us (16%)
  between operations  0.74 us (2%)
  local copies, waits for them, and re-layouts  0.72 us (2%)
    all_to_all x1, blocking collectives, shards(): lax.all_to_all(both.reshape(ranks, rows // ranks, lane), ('grp', 'gy'), 0...  15.7 us
    pallas_call x12, Pallas kernels, call(): pl.pallas_call(body, out_shape=list(outs), in_specs=[pl.BlockSpec(memory_...  13.1 us
    all_to_all x1, waiting for transfers between devices, shards(): sums = lax.all_to_all(spread, ('grp', 'gy'), 0, 0).reshape(rows, lane)  5.06 us
    ppermute x5, starting transfers between devices, swap(): return lax.ppermute(array, 'gx', [(0, 1), (1, 0)])  4.49 us
    all_to_all x1, starting transfers between devices, shards(): sums = lax.all_to_all(spread, ('grp', 'gy'), 0, 0).reshape(rows, lane)  3.53 us
    ppermute x5, waiting for transfers between devices, swap(): return lax.ppermute(array, 'gx', [(0, 1), (1, 0)])  2.51 us
  transfers between devices with their start and end apart: 7, of which 5 were waited for; matrix products, arithmetic and copies ran while one was open for 0% of the time, Pallas kernels for 20%

profile of v17, /device:TPU:0, one launch (start us, length us, event | category | flops | bytes accessed | tf_op | source)
XLA Modules:
  0.0 46.5 jit_solution(11572168598918072997)
XLA Ops:
  0.6 1.3 %pack_edges.1 = (bf16[8,16,1024]{2,1,0:T(8,128)(2,1)S(1)}, bf16[8,16,1024]{2,1,0:T(8,128)(2,1)S(1)}, bf16[3,8,1024]{2,1,0:T(8,128)(2,1)S(1)}, bf16[3,8,1024]{2,1...) custom-call(bf16[8,16,1024]{2,1,0:T(8,128)(2,1)} %bitcast.17, ...), custom_call_target="tpu_custom_call" | custom-call | bytes 966656 | tf_op jit(solution)/shard_map/pack_edges/pallas_call | solution.py:480
  2.0 0.5 %collective-permute-start = (bf16[3,8,1024]{2,1,0:T(8,128)(2,1)S(1)}, bf16[3,8,1024]{2,1,0:T(8,128)(2,1)S(1)}, u32[]{:S(2)}, u32[]{:S(2)}) collective-permute-start(bf16[3,8,1024]{2,1,0:T(8,128)(2,1)S(1)} %get-tuple-element.53), channel_id=1, source_target_pairs={{0,16},{16,0},{1,17},{17,1},{2,18},{18,2},{3,19},{19,3},{4,20},{20... | collective-permute-start | bytes 147464 | tf_op jit(solution)/shard_map/ppermute | solution.py:20
  2.5 0.7 %pack_halves.1 = (bf16[19,8,1024]{2,1,0:T(8,128)(2,1)S(1)}, bf16[19,8,1024]{2,1,0:T(8,128)(2,1)S(1)}, bf16[2304,128]{1,0:T(8,128)(2,1)S(1)}, bf16[128,2304]{1,0:T(8,128)(2,1)S(1)}) custom-call(bf16[8,16,1024]{2,1,0:T(8,128)(2,1)S(1)} %get-tuple-element.47.field, bf16[8,16,1024]{2,1,0:T(8,128)(2,1)S(1)} %get-tuple-element.48.cot, ...), custom_call_target="tpu_custom_call" | custom-call | flops 1000000000 | bytes 966656 | tf_op jit(solution)/shard_map/pack_halves/pallas_call | solution.py:480
  3.2 0.2 collective-permute-done.taken
  3.4 0.3 collective-permute-start.1
  3.7 0.7 %collective-permute-start.2 = (bf16[3,16,1024]{2,1,0:T(8,128)(2,1)S(1)}, bf16[3,16,1024]{2,1,0:T(8,128)(2,1)S(1)}, u32[]{:S(2)}, u32[]{:S(2)}) collective-permute-start(bf16[3,16,1024]{2,1,0:T(8,128)(2,1)S(1)} %join_edges.1), channel_id=1, source_target_pairs={{16,4},{20,8},{24,12},{4,16},{8,20},{12,24},{17,5},{21,9},{25,13},... | collective-permute-start | bytes 294920 | tf_op jit(solution)/shard_map/ppermute | solution.py:532
  4.4 0.6 %collective-permute-done.1.got = bf16[19,8,1024]{2,1,0:T(8,128)(2,1)S(1)} collective-permute-done((bf16[19,8,1024]{2,1,0:T(8,128)(2,1)S(1)}, bf16[19,8,1024]{2,1,0:T(8,128)(2,1)S(1)}, u32[]{:S(2)}, u32[]{:S(2)}) %collective-permute-start.1) | collective-permute-done | bytes 311328 | tf_op jit(solution)/shard_map/ppermute | solution.py:20
  5.0 4.0 %interior.1 = (bf16[3,12,16,1280]{3,2,1,0:T(8,128)(2,1)S(1)}, bf16[3,10,16,1280]{3,2,1,0:T(8,128)(2,1)S(1)}, bf16[3,10,16,1152]{3,2,1,0:T(8,128)(2,1)S(1)}, bf16...) custom-call(bf16[19,8,1024]{2,1,0:T(8,128)(2,1)S(1)} %get-tuple-element.51.own, ...), custom_call_target="tpu_custom_call" | custom-call | flops 4000000000 | bytes 1802240 | tf_op jit(solution)/shard_map/interior/pallas_call | solution.py:480
  9.0 1.4 %late_rows.1 = (bf16[3,12,16,1280]{3,2,1,0:T(8,128)(2,1)S(1)}, bf16[3,10,16,1280]{3,2,1,0:T(8,128)(2,1)S(1)}, bf16[3,10,16,1152]{3,2,1,0:T(8,128)(2,1)S(1)}, bf1...) custom-call(bf16[3,12,16,1280]{3,2,1,0:T(8,128)(2,1)S(1)} %get-tuple, ...), custom_call_target="tpu_custom_call", output_to_operand_aliasing={{0}: (0, {}), {1}: (1, {}), {2}: (2, {}), {3}: (3, {}), {4}... | custom-call | flops 1000000000 | bytes 8036352 | tf_op jit(solution)/shard_map/late_rows/pallas_call | solution.py:480
  10.4 3.5 %collective-permute-start.3 = (bf16[896,128]{1,0:T(8,128)(2,1)S(1)}, bf16[896,128]{1,0:T(8,128)(2,1)S(1)}, u32[]{:S(2)}, u32[]{:S(2)}) collective-permute-start(bf16[896,128]{1,0:T(8,128)(2,1)S(1)} %get-tuple-element.66), channel_id=1, source_target_pairs={{0,16},{16,0},{1,17},{17,1},{2,18},{18,2},{3,19},{19,3},{4,20},{20... | collective-permute-start | bytes 688136 | tf_op jit(solution)/shard_map/ppermute | solution.py:20
  13.9 1.1 %keep_sums.1 = (bf16[3,10,16,1152]{3,2,1,0:T(8,128)(2,1)S(1)}, f32[10,32,1152]{2,1,0:T(8,128)S(1)}, f32[896,128]{1,0:T(8,128)S(1)}) custom-call(bf16[3,12,16,1280]{3,2,1,0:T(8,128)(2,1)S(1)} %get-tuple-element.67.fd, bf16[3,10,16,1280]{3,2,1,0:T(8,128)(2,1)S(1)} %get-tuple-element.68.cd, ...), custom_call_target="tpu_custom_call", output_to_operand_aliasing={{0}: (2, {}), {1}: (4, {})} | custom-call | flops 2000000000 | bytes 6242304 | tf_op jit(solution)/shard_map/keep_sums/pallas_call | solution.py:480
  15.1 0.1 add_pair.1
  15.1 15.7 %all_to_all.10.terms = bf16[16,56,128]{2,1,0:T(8,128)(2,1)S(1)} all-to-all(bf16[16,56,128]{2,1,0:T(8,128)(2,1)S(1)} %bitcast.9), channel_id=1, replica_groups=mesh['gx'=2,'gy'=4,'grp'=4] {'grp','gy'}, dimensions={0} | all-to-all | bytes 458752 | tf_op jit(solution)/shard_map/all_to_all | solution.py:564
  30.9 0.7 %broadcast_in_dim.4 = bf16[16,56,128]{2,1,0:T(8,128)(2,1)} broadcast(bf16[56,128]{1,0:T(8,128)(2,1)S(1)} %add_terms.1), dimensions={1,2} | broadcast | bytes 243712 | tf_op jit(solution)/shard_map/broadcast_in_dim | solution.py:567
  31.6 3.5 %all-to-all-start.1 = ((bf16[16,56,128]{2,1,0:T(8,128)(2,1)}), bf16[16,56,128]{2,1,0:T(8,128)(2,1)S(1)}, u32[]{:S(2)}, u32[]{:S(2)}) async-start(bf16[16,56,128]{2,1,0:T(8,128)(2,1)} %broadcast_in_dim.4), calls=%async_computation.1 | async-start | bytes 458752 | tf_op jit(solution)/shard_map/all_to_all | solution.py:568
  35.1 1.5 %output_conv.1 = (bf16[8,8,1024]{2,1,0:T(8,128)(2,1)S(1)}, bf16[8,8,1024]{2,1,0:T(8,128)(2,1)S(1)}) custom-call(bf16[3,10,16,1152]{3,2,1,0:T(8,128)(2,1)S(1)} %get-tuple-element.78.hd, bf16[27,64,64]{2,1,0:T(8,128)(2,1)S(1)} %get-tuple-element.79.w2), custom_call_target="tpu_custom_call" | custom-call | flops 2000000000 | bytes 1327104 | tf_op jit(solution)/shard_map/output_conv/pallas_call | solution.py:480
  36.6 0.1 collective-permute-start.4
  36.7 1.3 %collective-permute-done.4.other = bf16[8,8,1024]{2,1,0:T(8,128)(2,1)S(1)} collective-permute-done((bf16[8,8,1024]{2,1,0:T(8,128)(2,1)S(1)}, bf16[8,8,1024]{2,1,0:T(8,128)(2,1)S(1)}, u32[]{:S(2)}, u32[]{:S(2)}) %collective-permute-start.4) | collective-permute-done | bytes 131104 | tf_op jit(solution)/shard_map/ppermute | solution.py:20
  38.0 0.8 %finish_output.1 = bf16[8,16,1024]{2,1,0:T(8,128)(2,1)} custom-call(bf16[8,8,1024]{2,1,0:T(8,128)(2,1)S(1)} %get-tuple-element.80.mine, bf16[8,8,1024]{2,1,0:T(8,128)(2,1)S(1)} %collective-permute-done.4.other), custom_call_target="tpu_custom_call" | custom-call | bytes 262144 | tf_op jit(solution)/shard_map/finish_output/pallas_call | solution.py:480
  38.9 5.1 %all-to-all-done.1 = bf16[16,56,128]{2,1,0:T(8,128)(2,1)S(1)} async-done(((bf16[16,56,128]{2,1,0:T(8,128)(2,1)}), bf16[16,56,128]{2,1,0:T(8,128)(2,1)S(1)}, u32[]{:S(2)}, u32[]{:S(2)}) %all-to-all-start.1) | async-done | bytes 229408 | tf_op jit(solution)/shard_map/all_to_all | solution.py:568
  43.9 0.0 collective-permute-start.5
  43.9 1.0 %unpack_own.1 = (f32[27,64,64]{2,1,0:T(8,128)}, f32[27,64,64]{2,1,0:T(8,128)}) custom-call(bf16[896,128]{1,0:T(8,128)(2,1)S(1)} %bitcast.11), custom_call_target="tpu_custom_call" | custom-call | bytes 229376 | tf_op jit(solution)/shard_map/unpack_own/pallas_call | solution.py:480
  45.0 0.4 collective-permute-done.5.rows
  45.4 1.0 %unpack_other.1 = (f32[27,64,64]{2,1,0:T(8,128)}, f32[27,64,64]{2,1,0:T(8,128)}) custom-call(bf16[896,128]{1,0:T(8,128)(2,1)S(1)} %collective-permute-done.5.rows, f32[27,64,64]{2,1,0:T(8,128)} %get-tuple-element.87.first_in, f32[27,64,64]{2,1,0:T(8,128)} %get-tuple-element.88.second_in), custom_call_target="tpu_custom_call", output_to_operand_aliasing={{0}: (1, {}), {1}: (2, {})} | custom-call | bytes 1114112 | tf_op jit(solution)/shard_map/unpack_other/pallas_call | solution.py:480
  (4 shorter events, 0.1 us)
Async XLA Ops:
  2.0 1.4 %collective-permute-start = (bf16[3,8,1024]{2,1,0:T(8,128)(2,1)S(1)}, bf16[3,8,1024]{2,1,0:T(8,128)(2,1)S(1)}, u32[]{:S(2)}, u32[]{:S(2)}) collective-permute-start(bf16[3,8,1024]{2,1,0:T(8,128)(2,1)S(1)} %get-tuple-element.53), channel_id=1, source_target_pairs={{0,16},{16,0},{1,17},{17,1},{2,18},{18,2},{3,19},{19,3},{4,20},{20... | collective-permute-start | bytes 147464 | tf_op jit(solution)/shard_map/ppermute | solution.py:20
  3.4 1.6 %collective-permute-start.1 = (bf16[19,8,1024]{2,1,0:T(8,128)(2,1)S(1)}, bf16[19,8,1024]{2,1,0:T(8,128)(2,1)S(1)}, u32[]{:S(2)}, u32[]{:S(2)}) collective-permute-start(bf16[19,8,1024]{2,1,0:T(8,128)(2,1)S(1)} %get-tuple-element.55), channel_id=1, source_target_pairs={{0,16},{16,0},{1,17},{17,1},{2,18},{18,2},{3,19},{19,3},{4,20},{20... | collective-permute-start | bytes 933896 | tf_op jit(solution)/shard_map/ppermute | solution.py:20
  3.7 5.3 %collective-permute-start.2 = (bf16[3,16,1024]{2,1,0:T(8,128)(2,1)S(1)}, bf16[3,16,1024]{2,1,0:T(8,128)(2,1)S(1)}, u32[]{:S(2)}, u32[]{:S(2)}) collective-permute-start(bf16[3,16,1024]{2,1,0:T(8,128)(2,1)S(1)} %join_edges.1), channel_id=1, source_target_pairs={{16,4},{20,8},{24,12},{4,16},{8,20},{12,24},{17,5},{21,9},{25,13},... | collective-permute-start | bytes 294920 | tf_op jit(solution)/shard_map/ppermute | solution.py:532
  10.4 4.7 %collective-permute-start.3 = (bf16[896,128]{1,0:T(8,128)(2,1)S(1)}, bf16[896,128]{1,0:T(8,128)(2,1)S(1)}, u32[]{:S(2)}, u32[]{:S(2)}) collective-permute-start(bf16[896,128]{1,0:T(8,128)(2,1)S(1)} %get-tuple-element.66), channel_id=1, source_target_pairs={{0,16},{16,0},{1,17},{17,1},{2,18},{18,2},{3,19},{19,3},{4,20},{20... | collective-permute-start | bytes 688136 | tf_op jit(solution)/shard_map/ppermute | solution.py:20
  31.6 12.3 %all-to-all-start.1 = ((bf16[16,56,128]{2,1,0:T(8,128)(2,1)}), bf16[16,56,128]{2,1,0:T(8,128)(2,1)S(1)}, u32[]{:S(2)}, u32[]{:S(2)}) async-start(bf16[16,56,128]{2,1,0:T(8,128)(2,1)} %broadcast_in_dim.4), calls=%async_computation.1 | async-start | bytes 458752 | tf_op jit(solution)/shard_map/all_to_all | solution.py:568
  36.6 1.4 %collective-permute-start.4 = (bf16[8,8,1024]{2,1,0:T(8,128)(2,1)S(1)}, bf16[8,8,1024]{2,1,0:T(8,128)(2,1)S(1)}, u32[]{:S(2)}, u32[]{:S(2)}) collective-permute-start(bf16[8,8,1024]{2,1,0:T(8,128)(2,1)S(1)} %get-tuple-element.81), channel_id=1, source_target_pairs={{0,16},{16,0},{1,17},{17,1},{2,18},{18,2},{3,19},{19,3},{4,20},{20... | collective-permute-start | bytes 393224 | tf_op jit(solution)/shard_map/ppermute | solution.py:20
  43.9 1.5 %collective-permute-start.5 = (bf16[896,128]{1,0:T(8,128)(2,1)S(1)}, bf16[896,128]{1,0:T(8,128)(2,1)S(1)}, u32[]{:S(2)}, u32[]{:S(2)}) collective-permute-start(bf16[896,128]{1,0:T(8,128)(2,1)S(1)} %bitcast.10), channel_id=1, source_target_pairs={{0,16},{16,0},{1,17},{17,1},{2,18},{18,2},{3,19},{19,3},{4,20},{20... | collective-permute-start | bytes 688136 | tf_op jit(solution)/shard_map/ppermute | solution.py:20

commit v18 on v17

--- a/solution.py
+++ b/solution.py
@@ -208,9 +208,7 @@
     for scratch in (fs, cs, hs):
         blank_rows(scratch)
     blank_edges(fd)
-    blank_edges(cd)
     shift_rows(fs, fd, 2 - 2 * gx, lane, (0, 2))
-    shift_rows(cs, cd, 1 - gx, lane, (0, 2))
     for group in range(0, pairs + 1, 3):
         value = dot(jnp.concatenate([windows(fd, 2 - 2 * gx, count, p) for p in range(group, group + 3)], axis=0), w1b[...])
         for p in range(group, group + 3):
@@ -220,6 +218,8 @@
             hidden = (part * jax.nn.sigmoid(part) * inside_lanes(p)).reshape(count, across, lane)
             hs[pl.ds(2 - 2 * gx, count), 8:8 + across, here] = hidden
             hd[1, pl.ds(2 - 2 * gx, count), :, here] = hidden.astype(BF16)
+    blank_edges(cd)
+    shift_rows(cs, cd, 1 - gx, lane, (0, 2))
     cells = cells - across
     for group in range(0, pairs + 1, 3):
         value = dot_nt(jnp.concatenate([windows(cd, 1 - gx, count - 1, p) for p in range(group, group + 3)], axis=0), wfb[...])

time: 46.7 us -> 46.7 us (level)
  no operation moved by 1% of the time
where the time goes in v18:
time: 46.7 us; the launch traced here: 46.5 us
  blocking collectives  15.7 us (34%)
  Pallas kernels  13.1 us (28%)
  starting transfers between devices  8.68 us (19%)
  waiting for transfers between devices  7.56 us (16%)
  between operations  0.74 us (2%)
  local copies, waits for them, and re-layouts  0.72 us (2%)
    all_to_all x1, blocking collectives, shards(): lax.all_to_all(both.reshape(ranks, rows // ranks, lane), ('grp', 'gy'), 0...  15.7 us
    pallas_call x12, Pallas kernels, call(): pl.pallas_call(body, out_shape=list(outs), in_specs=[pl.BlockSpec(memory_...  13.1 us
    all_to_all x1, waiting for transfers between devices, shards(): sums = lax.all_to_all(spread, ('grp', 'gy'), 0, 0).reshape(rows, lane)  5.06 us
    ppermute x5, starting transfers between devices, swap(): return lax.ppermute(array, 'gx', [(0, 1), (1, 0)])  4.49 us
    all_to_all x1, starting transfers between devices, shards(): sums = lax.all_to_all(spread, ('grp', 'gy'), 0, 0).reshape(rows, lane)  3.53 us
    ppermute x5, waiting for transfers between devices, swap(): return lax.ppermute(array, 'gx', [(0, 1), (1, 0)])  2.51 us
  transfers between devices with their start and end apart: 7, of which 5 were waited for; matrix products, arithmetic and copies ran while one was open for 0% of the time, Pallas kernels for 20%

profile of v18, /device:TPU:0, one launch (start us, length us, event | category | flops | bytes accessed | tf_op | source)
XLA Modules:
  0.0 46.5 jit_solution(11572168598918072997)
XLA Ops:
  0.6 1.3 %pack_edges.1 = (bf16[8,16,1024]{2,1,0:T(8,128)(2,1)S(1)}, bf16[8,16,1024]{2,1,0:T(8,128)(2,1)S(1)}, bf16[3,8,1024]{2,1,0:T(8,128)(2,1)S(1)}, bf16[3,8,1024]{2,1...) custom-call(bf16[8,16,1024]{2,1,0:T(8,128)(2,1)} %bitcast.17, ...), custom_call_target="tpu_custom_call" | custom-call | bytes 966656 | tf_op jit(solution)/shard_map/pack_edges/pallas_call | solution.py:480
  2.0 0.5 %collective-permute-start = (bf16[3,8,1024]{2,1,0:T(8,128)(2,1)S(1)}, bf16[3,8,1024]{2,1,0:T(8,128)(2,1)S(1)}, u32[]{:S(2)}, u32[]{:S(2)}) collective-permute-start(bf16[3,8,1024]{2,1,0:T(8,128)(2,1)S(1)} %get-tuple-element.53), channel_id=1, source_target_pairs={{0,16},{16,0},{1,17},{17,1},{2,18},{18,2},{3,19},{19,3},{4,20},{20... | collective-permute-start | bytes 147464 | tf_op jit(solution)/shard_map/ppermute | solution.py:20
  2.5 0.7 %pack_halves.1 = (bf16[19,8,1024]{2,1,0:T(8,128)(2,1)S(1)}, bf16[19,8,1024]{2,1,0:T(8,128)(2,1)S(1)}, bf16[2304,128]{1,0:T(8,128)(2,1)S(1)}, bf16[128,2304]{1,0:T(8,128)(2,1)S(1)}) custom-call(bf16[8,16,1024]{2,1,0:T(8,128)(2,1)S(1)} %get-tuple-element.47.field, bf16[8,16,1024]{2,1,0:T(8,128)(2,1)S(1)} %get-tuple-element.48.cot, ...), custom_call_target="tpu_custom_call" | custom-call | flops 1000000000 | bytes 966656 | tf_op jit(solution)/shard_map/pack_halves/pallas_call | solution.py:480
  3.2 0.2 collective-permute-done.taken
  3.4 0.3 collective-permute-start.1
  3.7 0.7 %collective-permute-start.2 = (bf16[3,16,1024]{2,1,0:T(8,128)(2,1)S(1)}, bf16[3,16,1024]{2,1,0:T(8,128)(2,1)S(1)}, u32[]{:S(2)}, u32[]{:S(2)}) collective-permute-start(bf16[3,16,1024]{2,1,0:T(8,128)(2,1)S(1)} %join_edges.1), channel_id=1, source_target_pairs={{16,4},{20,8},{24,12},{4,16},{8,20},{12,24},{17,5},{21,9},{25,13},... | collective-permute-start | bytes 294920 | tf_op jit(solution)/shard_map/ppermute | solution.py:532
  4.4 0.6 %collective-permute-done.1.got = bf16[19,8,1024]{2,1,0:T(8,128)(2,1)S(1)} collective-permute-done((bf16[19,8,1024]{2,1,0:T(8,128)(2,1)S(1)}, bf16[19,8,1024]{2,1,0:T(8,128)(2,1)S(1)}, u32[]{:S(2)}, u32[]{:S(2)}) %collective-permute-start.1) | collective-permute-done | bytes 311328 | tf_op jit(solution)/shard_map/ppermute | solution.py:20
  5.0 4.0 %interior.1 = (bf16[3,12,16,1280]{3,2,1,0:T(8,128)(2,1)S(1)}, bf16[3,10,16,1280]{3,2,1,0:T(8,128)(2,1)S(1)}, bf16[3,10,16,1152]{3,2,1,0:T(8,128)(2,1)S(1)}, bf16...) custom-call(bf16[19,8,1024]{2,1,0:T(8,128)(2,1)S(1)} %get-tuple-element.51.own, ...), custom_call_target="tpu_custom_call" | custom-call | flops 4000000000 | bytes 1802240 | tf_op jit(solution)/shard_map/interior/pallas_call | solution.py:480
  9.0 1.4 %late_rows.1 = (bf16[3,12,16,1280]{3,2,1,0:T(8,128)(2,1)S(1)}, bf16[3,10,16,1280]{3,2,1,0:T(8,128)(2,1)S(1)}, bf16[3,10,16,1152]{3,2,1,0:T(8,128)(2,1)S(1)}, bf1...) custom-call(bf16[3,12,16,1280]{3,2,1,0:T(8,128)(2,1)S(1)} %get-tuple, ...), custom_call_target="tpu_custom_call", output_to_operand_aliasing={{0}: (0, {}), {1}: (1, {}), {2}: (2, {}), {3}: (3, {}), {4}... | custom-call | flops 1000000000 | bytes 8036352 | tf_op jit(solution)/shard_map/late_rows/pallas_call | solution.py:480
  10.4 3.5 %collective-permute-start.3 = (bf16[896,128]{1,0:T(8,128)(2,1)S(1)}, bf16[896,128]{1,0:T(8,128)(2,1)S(1)}, u32[]{:S(2)}, u32[]{:S(2)}) collective-permute-start(bf16[896,128]{1,0:T(8,128)(2,1)S(1)} %get-tuple-element.66), channel_id=1, source_target_pairs={{0,16},{16,0},{1,17},{17,1},{2,18},{18,2},{3,19},{19,3},{4,20},{20... | collective-permute-start | bytes 688136 | tf_op jit(solution)/shard_map/ppermute | solution.py:20
  13.9 1.1 %keep_sums.1 = (bf16[3,10,16,1152]{3,2,1,0:T(8,128)(2,1)S(1)}, f32[10,32,1152]{2,1,0:T(8,128)S(1)}, f32[896,128]{1,0:T(8,128)S(1)}) custom-call(bf16[3,12,16,1280]{3,2,1,0:T(8,128)(2,1)S(1)} %get-tuple-element.67.fd, bf16[3,10,16,1280]{3,2,1,0:T(8,128)(2,1)S(1)} %get-tuple-element.68.cd, ...), custom_call_target="tpu_custom_call", output_to_operand_aliasing={{0}: (2, {}), {1}: (4, {})} | custom-call | flops 2000000000 | bytes 6242304 | tf_op jit(solution)/shard_map/keep_sums/pallas_call | solution.py:480
  15.1 0.1 add_pair.1
  15.1 15.7 %all_to_all.10.terms = bf16[16,56,128]{2,1,0:T(8,128)(2,1)S(1)} all-to-all(bf16[16,56,128]{2,1,0:T(8,128)(2,1)S(1)} %bitcast.9), channel_id=1, replica_groups=mesh['gx'=2,'gy'=4,'grp'=4] {'grp','gy'}, dimensions={0} | all-to-all | bytes 458752 | tf_op jit(solution)/shard_map/all_to_all | solution.py:564
  30.9 0.7 %broadcast_in_dim.4 = bf16[16,56,128]{2,1,0:T(8,128)(2,1)} broadcast(bf16[56,128]{1,0:T(8,128)(2,1)S(1)} %add_terms.1), dimensions={1,2} | broadcast | bytes 243712 | tf_op jit(solution)/shard_map/broadcast_in_dim | solution.py:567
  31.6 3.5 %all-to-all-start.1 = ((bf16[16,56,128]{2,1,0:T(8,128)(2,1)}), bf16[16,56,128]{2,1,0:T(8,128)(2,1)S(1)}, u32[]{:S(2)}, u32[]{:S(2)}) async-start(bf16[16,56,128]{2,1,0:T(8,128)(2,1)} %broadcast_in_dim.4), calls=%async_computation.1 | async-start | bytes 458752 | tf_op jit(solution)/shard_map/all_to_all | solution.py:568
  35.1 1.5 %output_conv.1 = (bf16[8,8,1024]{2,1,0:T(8,128)(2,1)S(1)}, bf16[8,8,1024]{2,1,0:T(8,128)(2,1)S(1)}) custom-call(bf16[3,10,16,1152]{3,2,1,0:T(8,128)(2,1)S(1)} %get-tuple-element.78.hd, bf16[27,64,64]{2,1,0:T(8,128)(2,1)S(1)} %get-tuple-element.79.w2), custom_call_target="tpu_custom_call" | custom-call | flops 2000000000 | bytes 1327104 | tf_op jit(solution)/shard_map/output_conv/pallas_call | solution.py:480
  36.6 0.1 collective-permute-start.4
  36.7 1.3 %collective-permute-done.4.other = bf16[8,8,1024]{2,1,0:T(8,128)(2,1)S(1)} collective-permute-done((bf16[8,8,1024]{2,1,0:T(8,128)(2,1)S(1)}, bf16[8,8,1024]{2,1,0:T(8,128)(2,1)S(1)}, u32[]{:S(2)}, u32[]{:S(2)}) %collective-permute-start.4) | collective-permute-done | bytes 131104 | tf_op jit(solution)/shard_map/ppermute | solution.py:20
  38.0 0.8 %finish_output.1 = bf16[8,16,1024]{2,1,0:T(8,128)(2,1)} custom-call(bf16[8,8,1024]{2,1,0:T(8,128)(2,1)S(1)} %get-tuple-element.80.mine, bf16[8,8,1024]{2,1,0:T(8,128)(2,1)S(1)} %collective-permute-done.4.other), custom_call_target="tpu_custom_call" | custom-call | bytes 262144 | tf_op jit(solution)/shard_map/finish_output/pallas_call | solution.py:480
  38.9 5.1 %all-to-all-done.1 = bf16[16,56,128]{2,1,0:T(8,128)(2,1)S(1)} async-done(((bf16[16,56,128]{2,1,0:T(8,128)(2,1)}), bf16[16,56,128]{2,1,0:T(8,128)(2,1)S(1)}, u32[]{:S(2)}, u32[]{:S(2)}) %all-to-all-start.1) | async-done | bytes 229408 | tf_op jit(solution)/shard_map/all_to_all | solution.py:568
  43.9 0.0 collective-permute-start.5
  43.9 1.0 %unpack_own.1 = (f32[27,64,64]{2,1,0:T(8,128)}, f32[27,64,64]{2,1,0:T(8,128)}) custom-call(bf16[896,128]{1,0:T(8,128)(2,1)S(1)} %bitcast.11), custom_call_target="tpu_custom_call" | custom-call | bytes 229376 | tf_op jit(solution)/shard_map/unpack_own/pallas_call | solution.py:480
  45.0 0.4 collective-permute-done.5.rows
  45.4 1.0 %unpack_other.1 = (f32[27,64,64]{2,1,0:T(8,128)}, f32[27,64,64]{2,1,0:T(8,128)}) custom-call(bf16[896,128]{1,0:T(8,128)(2,1)S(1)} %collective-permute-done.5.rows, f32[27,64,64]{2,1,0:T(8,128)} %get-tuple-element.87.first_in, f32[27,64,64]{2,1,0:T(8,128)} %get-tuple-element.88.second_in), custom_call_target="tpu_custom_call", output_to_operand_aliasing={{0}: (1, {}), {1}: (2, {})} | custom-call | bytes 1114112 | tf_op jit(solution)/shard_map/unpack_other/pallas_call | solution.py:480
  (4 shorter events, 0.1 us)
Async XLA Ops:
  2.0 1.4 %collective-permute-start = (bf16[3,8,1024]{2,1,0:T(8,128)(2,1)S(1)}, bf16[3,8,1024]{2,1,0:T(8,128)(2,1)S(1)}, u32[]{:S(2)}, u32[]{:S(2)}) collective-permute-start(bf16[3,8,1024]{2,1,0:T(8,128)(2,1)S(1)} %get-tuple-element.53), channel_id=1, source_target_pairs={{0,16},{16,0},{1,17},{17,1},{2,18},{18,2},{3,19},{19,3},{4,20},{20... | collective-permute-start | bytes 147464 | tf_op jit(solution)/shard_map/ppermute | solution.py:20
  3.4 1.6 %collective-permute-start.1 = (bf16[19,8,1024]{2,1,0:T(8,128)(2,1)S(1)}, bf16[19,8,1024]{2,1,0:T(8,128)(2,1)S(1)}, u32[]{:S(2)}, u32[]{:S(2)}) collective-permute-start(bf16[19,8,1024]{2,1,0:T(8,128)(2,1)S(1)} %get-tuple-element.55), channel_id=1, source_target_pairs={{0,16},{16,0},{1,17},{17,1},{2,18},{18,2},{3,19},{19,3},{4,20},{20... | collective-permute-start | bytes 933896 | tf_op jit(solution)/shard_map/ppermute | solution.py:20
  3.7 5.3 %collective-permute-start.2 = (bf16[3,16,1024]{2,1,0:T(8,128)(2,1)S(1)}, bf16[3,16,1024]{2,1,0:T(8,128)(2,1)S(1)}, u32[]{:S(2)}, u32[]{:S(2)}) collective-permute-start(bf16[3,16,1024]{2,1,0:T(8,128)(2,1)S(1)} %join_edges.1), channel_id=1, source_target_pairs={{16,4},{20,8},{24,12},{4,16},{8,20},{12,24},{17,5},{21,9},{25,13},... | collective-permute-start | bytes 294920 | tf_op jit(solution)/shard_map/ppermute | solution.py:532
  10.4 4.7 %collective-permute-start.3 = (bf16[896,128]{1,0:T(8,128)(2,1)S(1)}, bf16[896,128]{1,0:T(8,128)(2,1)S(1)}, u32[]{:S(2)}, u32[]{:S(2)}) collective-permute-start(bf16[896,128]{1,0:T(8,128)(2,1)S(1)} %get-tuple-element.66), channel_id=1, source_target_pairs={{0,16},{16,0},{1,17},{17,1},{2,18},{18,2},{3,19},{19,3},{4,20},{20... | collective-permute-start | bytes 688136 | tf_op jit(solution)/shard_map/ppermute | solution.py:20
  31.6 12.3 %all-to-all-start.1 = ((bf16[16,56,128]{2,1,0:T(8,128)(2,1)}), bf16[16,56,128]{2,1,0:T(8,128)(2,1)S(1)}, u32[]{:S(2)}, u32[]{:S(2)}) async-start(bf16[16,56,128]{2,1,0:T(8,128)(2,1)} %broadcast_in_dim.4), calls=%async_computation.1 | async-start | bytes 458752 | tf_op jit(solution)/shard_map/all_to_all | solution.py:568
  36.6 1.4 %collective-permute-start.4 = (bf16[8,8,1024]{2,1,0:T(8,128)(2,1)S(1)}, bf16[8,8,1024]{2,1,0:T(8,128)(2,1)S(1)}, u32[]{:S(2)}, u32[]{:S(2)}) collective-permute-start(bf16[8,8,1024]{2,1,0:T(8,128)(2,1)S(1)} %get-tuple-element.81), channel_id=1, source_target_pairs={{0,16},{16,0},{1,17},{17,1},{2,18},{18,2},{3,19},{19,3},{4,20},{20... | collective-permute-start | bytes 393224 | tf_op jit(solution)/shard_map/ppermute | solution.py:20
  43.9 1.5 %collective-permute-start.5 = (bf16[896,128]{1,0:T(8,128)(2,1)S(1)}, bf16[896,128]{1,0:T(8,128)(2,1)S(1)}, u32[]{:S(2)}, u32[]{:S(2)}) collective-permute-start(bf16[896,128]{1,0:T(8,128)(2,1)S(1)} %bitcast.10), channel_id=1, source_target_pairs={{0,16},{16,0},{1,17},{17,1},{2,18},{18,2},{3,19},{19,3},{4,20},{20... | collective-permute-start | bytes 688136 | tf_op jit(solution)/shard_map/ppermute | solution.py:20

commit v19 on v17

--- a/solution.py
+++ b/solution.py
@@ -561,11 +561,8 @@
         flops=2 * 10 ** 9, aliases={2: 0, 4: 1})
     other, keep = lax.optimization_barrier((other, keep))
     both, = call(add_pair, "add_pair", [(keep, True), (other, True)], [near((rows, lane), BF16)])
+    both, hd, w2 = lax.optimization_barrier((both, hd, w2))
     terms = lax.all_to_all(both.reshape(ranks, rows // ranks, lane), ("grp", "gy"), 0, 0)
-    part, = call(add_terms, "add_terms", [(terms, True)], [near(terms.shape[1:], BF16)])
-    part, hd, w2 = lax.optimization_barrier((part, hd, w2))
-    spread = jnp.broadcast_to(part[None], terms.shape)
-    sums = lax.all_to_all(spread, ("grp", "gy"), 0, 0).reshape(rows, lane)
     mine, given = call(
         output_conv, "output_conv", [(hd, True), (w2, True)],
         [near((count, nx, width), BF16), near((count, nx, width), BF16)],
@@ -575,7 +572,10 @@
         finish_output, "finish_output", [(mine, True), (given, True)],
         [pltpu.HBM((nx, ny, width), BF16)],
         [pltpu.VMEM((nx, ny, width), BF16), pltpu.VMEM((width // lane, nx * ny, lane), F32), pltpu.SemaphoreType.DMA((nx // 2,))], far=True)
-    sums, out = lax.optimization_barrier((sums, out))
+    terms, out = lax.optimization_barrier((terms, out))
+    part, = call(add_terms, "add_terms", [(terms, True)], [near(terms.shape[1:], BF16)])
+    spread = jnp.broadcast_to(part[None], terms.shape)
+    sums = lax.all_to_all(spread, ("grp", "gy"), 0, 0).reshape(rows, lane)
     other = swap(sums)
     outs = [pltpu.HBM((27, C, C), F32)] * 2
     scratch = [pltpu.VMEM((27, C, C), F32), pltpu.SemaphoreType.DMA((3,))]

time: 46.7 us -> 46.7 us (level)
  blocking collectives: 15.7 us -> 12.1 us
  starting transfers between devices: 8.68 us -> 11.3 us
  waiting for transfers between devices: 7.56 us -> 8.45 us
  Pallas kernels: 13.1 us -> 13.8 us
  local copies, waits for them, and re-layouts: 0.72 us -> 0.03 us
    all_to_all x1, blocking collectives: 15.7 us -> 12.1 us  [shards(): sums = lax.all_to_all(spread, ('grp', 'gy'), 0, 0).reshape(rows, lane)]
    all_to_all x1, starting transfers between devices: 3.53 us -> 6.19 us  [shards(): lax.all_to_all(both.reshape(ranks, rows // ranks, lane), ('grp', 'gy'), 0...]
    all_to_all x1, waiting for transfers between devices: 5.06 us -> 5.94 us  [shards(): lax.all_to_all(both.reshape(ranks, rows // ranks, lane), ('grp', 'gy'), 0...]
    pallas_call x12, Pallas kernels: 13.1 us -> 13.8 us  [call(): pl.pallas_call(body, out_shape=list(outs), in_specs=[pl.BlockSpec(memory_...]
    broadcast_in_dim x1, local copies, waits for them, and re-layouts: 0.72 us -> 0.03 us  [shards(): spread = jnp.broadcast_to(part[None], terms.shape)]
where the time goes in v19:
time: 46.7 us; the launch traced here: 46.5 us
  Pallas kernels  13.8 us (30%)
  blocking collectives  12.1 us (26%)
  starting transfers between devices  11.3 us (24%)
  waiting for transfers between devices  8.45 us (18%)
  between operations  0.74 us (2%)
    pallas_call x12, Pallas kernels, call(): pl.pallas_call(body, out_shape=list(outs), in_specs=[pl.BlockSpec(memory_...  13.8 us
    all_to_all x1, blocking collectives, shards(): sums = lax.all_to_all(spread, ('grp', 'gy'), 0, 0).reshape(rows, lane)  12.1 us
    all_to_all x1, starting transfers between devices, shards(): lax.all_to_all(both.reshape(ranks, rows // ranks, lane), ('grp', 'gy'), 0...  6.19 us
    all_to_all x1, waiting for transfers between devices, shards(): lax.all_to_all(both.reshape(ranks, rows // ranks, lane), ('grp', 'gy'), 0...  5.94 us
    ppermute x5, starting transfers between devices, swap(): return lax.ppermute(array, 'gx', [(0, 1), (1, 0)])  4.49 us
    ppermute x5, waiting for transfers between devices, swap(): return lax.ppermute(array, 'gx', [(0, 1), (1, 0)])  2.51 us
  transfers between devices with their start and end apart: 7, of which 5 were waited for; matrix products, arithmetic and copies ran while one was open for 0% of the time, Pallas kernels for 20%

profile of v19, /device:TPU:0, one launch (start us, length us, event | category | flops | bytes accessed | tf_op | source)
XLA Modules:
  0.0 46.5 jit_solution(1002862968582030767)
XLA Ops:
  0.6 1.3 %pack_edges.1 = (bf16[8,16,1024]{2,1,0:T(8,128)(2,1)S(1)}, bf16[8,16,1024]{2,1,0:T(8,128)(2,1)S(1)}, bf16[3,8,1024]{2,1,0:T(8,128)(2,1)S(1)}, bf16[3,8,1024]{2,1...) custom-call(bf16[8,16,1024]{2,1,0:T(8,128)(2,1)} %bitcast.16, ...), custom_call_target="tpu_custom_call" | custom-call | bytes 966656 | tf_op jit(solution)/shard_map/pack_edges/pallas_call | solution.py:480
  2.0 0.5 %collective-permute-start = (bf16[3,8,1024]{2,1,0:T(8,128)(2,1)S(1)}, bf16[3,8,1024]{2,1,0:T(8,128)(2,1)S(1)}, u32[]{:S(2)}, u32[]{:S(2)}) collective-permute-start(bf16[3,8,1024]{2,1,0:T(8,128)(2,1)S(1)} %get-tuple-element.53), channel_id=1, source_target_pairs={{0,16},{16,0},{1,17},{17,1},{2,18},{18,2},{3,19},{19,3},{4,20},{20... | collective-permute-start | bytes 147464 | tf_op jit(solution)/shard_map/ppermute | solution.py:20
  2.5 0.7 %pack_halves.1 = (bf16[19,8,1024]{2,1,0:T(8,128)(2,1)S(1)}, bf16[19,8,1024]{2,1,0:T(8,128)(2,1)S(1)}, bf16[2304,128]{1,0:T(8,128)(2,1)S(1)}, bf16[128,2304]{1,0:T(8,128)(2,1)S(1)}) custom-call(bf16[8,16,1024]{2,1,0:T(8,128)(2,1)S(1)} %get-tuple-element.47.field, bf16[8,16,1024]{2,1,0:T(8,128)(2,1)S(1)} %get-tuple-element.48.cot, ...), custom_call_target="tpu_custom_call" | custom-call | flops 1000000000 | bytes 966656 | tf_op jit(solution)/shard_map/pack_halves/pallas_call | solution.py:480
  3.2 0.2 collective-permute-done.taken
  3.4 0.3 collective-permute-start.1
  3.7 0.7 %collective-permute-start.2 = (bf16[3,16,1024]{2,1,0:T(8,128)(2,1)S(1)}, bf16[3,16,1024]{2,1,0:T(8,128)(2,1)S(1)}, u32[]{:S(2)}, u32[]{:S(2)}) collective-permute-start(bf16[3,16,1024]{2,1,0:T(8,128)(2,1)S(1)} %join_edges.1), channel_id=1, source_target_pairs={{16,4},{20,8},{24,12},{4,16},{8,20},{12,24},{17,5},{21,9},{25,13},... | collective-permute-start | bytes 294920 | tf_op jit(solution)/shard_map/ppermute | solution.py:532
  4.4 0.6 %collective-permute-done.1.got = bf16[19,8,1024]{2,1,0:T(8,128)(2,1)S(1)} collective-permute-done((bf16[19,8,1024]{2,1,0:T(8,128)(2,1)S(1)}, bf16[19,8,1024]{2,1,0:T(8,128)(2,1)S(1)}, u32[]{:S(2)}, u32[]{:S(2)}) %collective-permute-start.1) | collective-permute-done | bytes 311328 | tf_op jit(solution)/shard_map/ppermute | solution.py:20
  5.0 4.0 %interior.1 = (bf16[3,12,16,1280]{3,2,1,0:T(8,128)(2,1)S(1)}, bf16[3,10,16,1280]{3,2,1,0:T(8,128)(2,1)S(1)}, bf16[3,10,16,1152]{3,2,1,0:T(8,128)(2,1)S(1)}, bf16...) custom-call(bf16[19,8,1024]{2,1,0:T(8,128)(2,1)S(1)} %get-tuple-element.51.own, ...), custom_call_target="tpu_custom_call" | custom-call | flops 4000000000 | bytes 1802240 | tf_op jit(solution)/shard_map/interior/pallas_call | solution.py:480
  9.0 0.0 collective-permute-done.2.rows
  9.0 1.4 %late_rows.1 = (bf16[3,12,16,1280]{3,2,1,0:T(8,128)(2,1)S(1)}, bf16[3,10,16,1280]{3,2,1,0:T(8,128)(2,1)S(1)}, bf16[3,10,16,1152]{3,2,1,0:T(8,128)(2,1)S(1)}, bf1...) custom-call(bf16[3,12,16,1280]{3,2,1,0:T(8,128)(2,1)S(1)} %get-tuple, ...), custom_call_target="tpu_custom_call", output_to_operand_aliasing={{0}: (0, {}), {1}: (1, {}), {2}: (2, {}), {3}: (3, {}), {4}... | custom-call | flops 1000000000 | bytes 8036352 | tf_op jit(solution)/shard_map/late_rows/pallas_call | solution.py:480
  10.4 3.5 %collective-permute-start.3 = (bf16[896,128]{1,0:T(8,128)(2,1)S(1)}, bf16[896,128]{1,0:T(8,128)(2,1)S(1)}, u32[]{:S(2)}, u32[]{:S(2)}) collective-permute-start(bf16[896,128]{1,0:T(8,128)(2,1)S(1)} %get-tuple-element.66), channel_id=1, source_target_pairs={{0,16},{16,0},{1,17},{17,1},{2,18},{18,2},{3,19},{19,3},{4,20},{20... | collective-permute-start | bytes 688136 | tf_op jit(solution)/shard_map/ppermute | solution.py:20
  13.9 1.1 %keep_sums.1 = (bf16[3,10,16,1152]{3,2,1,0:T(8,128)(2,1)S(1)}, f32[10,32,1152]{2,1,0:T(8,128)S(1)}, f32[896,128]{1,0:T(8,128)S(1)}) custom-call(bf16[3,12,16,1280]{3,2,1,0:T(8,128)(2,1)S(1)} %get-tuple-element.67.fd, bf16[3,10,16,1280]{3,2,1,0:T(8,128)(2,1)S(1)} %get-tuple-element.68.cd, ...), custom_call_target="tpu_custom_call", output_to_operand_aliasing={{0}: (2, {}), {1}: (4, {})} | custom-call | flops 2000000000 | bytes 6242304 | tf_op jit(solution)/shard_map/keep_sums/pallas_call | solution.py:480
  15.1 0.7 %add_pair.1 = bf16[896,128]{1,0:T(8,128)(2,1)} custom-call(f32[896,128]{1,0:T(8,128)S(1)} %get-tuple-element.74.keep, bf16[896,128]{1,0:T(8,128)(2,1)S(1)} %collective-permute-done.3.other), custom_call_target="tpu_custom_call" | custom-call | bytes 688128 | tf_op jit(solution)/shard_map/add_pair/pallas_call | solution.py:480
  15.8 6.2 %all-to-all-start = ((bf16[16,56,128]{2,1,0:T(8,128)(2,1)}), bf16[16,56,128]{2,1,0:T(8,128)(2,1)S(1)}, u32[]{:S(2)}, u32[]{:S(2)}) async-start(bf16[16,56,128]{2,1,0:T(8,128)(2,1)} %bitcast.4), calls=%async_computation | async-start | bytes 458752 | tf_op jit(solution)/shard_map/all_to_all | solution.py:565
  22.0 1.5 %output_conv.1 = (bf16[8,8,1024]{2,1,0:T(8,128)(2,1)S(1)}, bf16[8,8,1024]{2,1,0:T(8,128)(2,1)S(1)}) custom-call(bf16[3,10,16,1152]{3,2,1,0:T(8,128)(2,1)S(1)} %get-tuple-element.78.hd, bf16[27,64,64]{2,1,0:T(8,128)(2,1)S(1)} %get-tuple-element.79.w2), custom_call_target="tpu_custom_call" | custom-call | flops 2000000000 | bytes 1327104 | tf_op jit(solution)/shard_map/output_conv/pallas_call | solution.py:480
  23.5 0.1 collective-permute-start.4
  23.6 1.3 %collective-permute-done.4.other = bf16[8,8,1024]{2,1,0:T(8,128)(2,1)S(1)} collective-permute-done((bf16[8,8,1024]{2,1,0:T(8,128)(2,1)S(1)}, bf16[8,8,1024]{2,1,0:T(8,128)(2,1)S(1)}, u32[]{:S(2)}, u32[]{:S(2)}) %collective-permute-start.4) | collective-permute-done | bytes 131104 | tf_op jit(solution)/shard_map/ppermute | solution.py:20
  24.9 0.8 %finish_output.1 = bf16[8,16,1024]{2,1,0:T(8,128)(2,1)} custom-call(bf16[8,8,1024]{2,1,0:T(8,128)(2,1)S(1)} %get-tuple-element.80.mine, bf16[8,8,1024]{2,1,0:T(8,128)(2,1)S(1)} %collective-permute-done.4.other), custom_call_target="tpu_custom_call" | custom-call | bytes 262144 | tf_op jit(solution)/shard_map/finish_output/pallas_call | solution.py:480
  25.8 5.9 %all-to-all-done.terms = bf16[16,56,128]{2,1,0:T(8,128)(2,1)S(1)} async-done(((bf16[16,56,128]{2,1,0:T(8,128)(2,1)}), bf16[16,56,128]{2,1,0:T(8,128)(2,1)S(1)}, u32[]{:S(2)}, u32[]{:S(2)}) %all-to-all-start) | async-done | bytes 229408 | tf_op jit(solution)/shard_map/all_to_all | solution.py:565
  31.8 12.1 %all_to_all.10 = bf16[16,56,128]{2,1,0:T(8,128)(2,1)S(1)} all-to-all(bf16[16,56,128]{2,1,0:T(8,128)(2,1)S(1)} %broadcast_in_dim.10), channel_id=1, replica_groups=mesh['gx'=2,'gy'=4,'grp'=4] {'grp','gy'}, dimensions={0} | all-to-all | bytes 458752 | tf_op jit(solution)/shard_map/all_to_all | solution.py:578
  43.9 0.0 collective-permute-start.5
  43.9 1.0 %unpack_own.1 = (f32[27,64,64]{2,1,0:T(8,128)}, f32[27,64,64]{2,1,0:T(8,128)}) custom-call(bf16[896,128]{1,0:T(8,128)(2,1)S(1)} %bitcast.10), custom_call_target="tpu_custom_call" | custom-call | bytes 229376 | tf_op jit(solution)/shard_map/unpack_own/pallas_call | solution.py:480
  45.0 0.4 collective-permute-done.5.rows
  45.4 1.0 %unpack_other.1 = (f32[27,64,64]{2,1,0:T(8,128)}, f32[27,64,64]{2,1,0:T(8,128)}) custom-call(bf16[896,128]{1,0:T(8,128)(2,1)S(1)} %collective-permute-done.5.rows, f32[27,64,64]{2,1,0:T(8,128)} %get-tuple-element.87.first_in, f32[27,64,64]{2,1,0:T(8,128)} %get-tuple-element.88.second_in), custom_call_target="tpu_custom_call", output_to_operand_aliasing={{0}: (1, {}), {1}: (2, {})} | custom-call | bytes 1114112 | tf_op jit(solution)/shard_map/unpack_other/pallas_call | solution.py:480
  (4 shorter events, 0.1 us)
Async XLA Ops:
  2.0 1.4 %collective-permute-start = (bf16[3,8,1024]{2,1,0:T(8,128)(2,1)S(1)}, bf16[3,8,1024]{2,1,0:T(8,128)(2,1)S(1)}, u32[]{:S(2)}, u32[]{:S(2)}) collective-permute-start(bf16[3,8,1024]{2,1,0:T(8,128)(2,1)S(1)} %get-tuple-element.53), channel_id=1, source_target_pairs={{0,16},{16,0},{1,17},{17,1},{2,18},{18,2},{3,19},{19,3},{4,20},{20... | collective-permute-start | bytes 147464 | tf_op jit(solution)/shard_map/ppermute | solution.py:20
  3.4 1.6 %collective-permute-start.1 = (bf16[19,8,1024]{2,1,0:T(8,128)(2,1)S(1)}, bf16[19,8,1024]{2,1,0:T(8,128)(2,1)S(1)}, u32[]{:S(2)}, u32[]{:S(2)}) collective-permute-start(bf16[19,8,1024]{2,1,0:T(8,128)(2,1)S(1)} %get-tuple-element.55), channel_id=1, source_target_pairs={{0,16},{16,0},{1,17},{17,1},{2,18},{18,2},{3,19},{19,3},{4,20},{20... | collective-permute-start | bytes 933896 | tf_op jit(solution)/shard_map/ppermute | solution.py:20
  3.7 5.3 %collective-permute-start.2 = (bf16[3,16,1024]{2,1,0:T(8,128)(2,1)S(1)}, bf16[3,16,1024]{2,1,0:T(8,128)(2,1)S(1)}, u32[]{:S(2)}, u32[]{:S(2)}) collective-permute-start(bf16[3,16,1024]{2,1,0:T(8,128)(2,1)S(1)} %join_edges.1), channel_id=1, source_target_pairs={{16,4},{20,8},{24,12},{4,16},{8,20},{12,24},{17,5},{21,9},{25,13},... | collective-permute-start | bytes 294920 | tf_op jit(solution)/shard_map/ppermute | solution.py:532
  10.4 4.7 %collective-permute-start.3 = (bf16[896,128]{1,0:T(8,128)(2,1)S(1)}, bf16[896,128]{1,0:T(8,128)(2,1)S(1)}, u32[]{:S(2)}, u32[]{:S(2)}) collective-permute-start(bf16[896,128]{1,0:T(8,128)(2,1)S(1)} %get-tuple-element.66), channel_id=1, source_target_pairs={{0,16},{16,0},{1,17},{17,1},{2,18},{18,2},{3,19},{19,3},{4,20},{20... | collective-permute-start | bytes 688136 | tf_op jit(solution)/shard_map/ppermute | solution.py:20
  15.8 15.9 %all-to-all-start = ((bf16[16,56,128]{2,1,0:T(8,128)(2,1)}), bf16[16,56,128]{2,1,0:T(8,128)(2,1)S(1)}, u32[]{:S(2)}, u32[]{:S(2)}) async-start(bf16[16,56,128]{2,1,0:T(8,128)(2,1)} %bitcast.4), calls=%async_computation | async-start | bytes 458752 | tf_op jit(solution)/shard_map/all_to_all | solution.py:565
  23.5 1.4 %collective-permute-start.4 = (bf16[8,8,1024]{2,1,0:T(8,128)(2,1)S(1)}, bf16[8,8,1024]{2,1,0:T(8,128)(2,1)S(1)}, u32[]{:S(2)}, u32[]{:S(2)}) collective-permute-start(bf16[8,8,1024]{2,1,0:T(8,128)(2,1)S(1)} %get-tuple-element.81), channel_id=1, source_target_pairs={{0,16},{16,0},{1,17},{17,1},{2,18},{18,2},{3,19},{19,3},{4,20},{20... | collective-permute-start | bytes 393224 | tf_op jit(solution)/shard_map/ppermute | solution.py:20
  43.9 1.5 %collective-permute-start.5 = (bf16[896,128]{1,0:T(8,128)(2,1)S(1)}, bf16[896,128]{1,0:T(8,128)(2,1)S(1)}, u32[]{:S(2)}, u32[]{:S(2)}) collective-permute-start(bf16[896,128]{1,0:T(8,128)(2,1)S(1)} %bitcast.9), channel_id=1, source_target_pairs={{0,16},{16,0},{1,17},{17,1},{2,18},{18,2},{3,19},{19,3},{4,20},{20... | collective-permute-start | bytes 688136 | tf_op jit(solution)/shard_map/ppermute | solution.py:20

commit v20 on v19

--- a/solution.py
+++ b/solution.py
@@ -211,9 +211,9 @@
     blank_edges(cd)
     shift_rows(fs, fd, 2 - 2 * gx, lane, (0, 2))
     shift_rows(cs, cd, 1 - gx, lane, (0, 2))
-    for group in range(0, pairs + 1, 3):
-        value = dot(jnp.concatenate([windows(fd, 2 - 2 * gx, count, p) for p in range(group, group + 3)], axis=0), w1b[...])
-        for p in range(group, group + 3):
+    for group in range(0, pairs + 1, pairs + 1):
+        value = dot(jnp.concatenate([windows(fd, 2 - 2 * gx, count, p) for p in range(group, group + pairs + 1)], axis=0), w1b[...])
+        for p in range(group, group + pairs + 1):
             here = slice(lane * p, lane * (p + 1))
             part = value[cells * (p - group):cells * (p - group + 1)]
             pre[:, :, here] = part.reshape(count, across, lane)
@@ -221,9 +221,9 @@
             hs[pl.ds(2 - 2 * gx, count), 8:8 + across, here] = hidden
             hd[1, pl.ds(2 - 2 * gx, count), :, here] = hidden.astype(BF16)
     cells = cells - across
-    for group in range(0, pairs + 1, 3):
-        value = dot_nt(jnp.concatenate([windows(cd, 1 - gx, count - 1, p) for p in range(group, group + 3)], axis=0), wfb[...])
-        for p in range(group, group + 3):
+    for group in range(0, pairs + 1, pairs + 1):
+        value = dot_nt(jnp.concatenate([windows(cd, 1 - gx, count - 1, p) for p in range(group, group + pairs + 1)], axis=0), wfb[...])
+        for p in range(group, group + pairs + 1):
             here = slice(lane * p, lane * (p + 1))
             part = value[cells * (p - group):cells * (p - group + 1)]
             grad = pre_gradient(part, pre[pl.ds(gx, count - 1), :, here].reshape(cells, lane), p)

time: 46.7 us -> 46.7 us (level)
  no operation moved by 1% of the time
where the time goes in v20:
time: 46.7 us; the launch traced here: 46.5 us
  Pallas kernels  13.8 us (30%)
  blocking collectives  12.1 us (26%)
  starting transfers between devices  11.3 us (24%)
  waiting for transfers between devices  8.45 us (18%)
  between operations  0.74 us (2%)
    pallas_call x12, Pallas kernels, call(): pl.pallas_call(body, out_shape=list(outs), in_specs=[pl.BlockSpec(memory_...  13.8 us
    all_to_all x1, blocking collectives, shards(): sums = lax.all_to_all(spread, ('grp', 'gy'), 0, 0).reshape(rows, lane)  12.1 us
    all_to_all x1, starting transfers between devices, shards(): lax.all_to_all(both.reshape(ranks, rows // ranks, lane), ('grp', 'gy'), 0...  6.11 us
    all_to_all x1, waiting for transfers between devices, shards(): lax.all_to_all(both.reshape(ranks, rows // ranks, lane), ('grp', 'gy'), 0...  5.94 us
    ppermute x5, starting transfers between devices, swap(): return lax.ppermute(array, 'gx', [(0, 1), (1, 0)])  4.52 us
    ppermute x5, waiting for transfers between devices, swap(): return lax.ppermute(array, 'gx', [(0, 1), (1, 0)])  2.51 us
  transfers between devices with their start and end apart: 7, of which 5 were waited for; matrix products, arithmetic and copies ran while one was open for 0% of the time, Pallas kernels for 20%

profile of v20, /device:TPU:0, one launch (start us, length us, event | category | flops | bytes accessed | tf_op | source)
XLA Modules:
  0.0 46.5 jit_solution(4955330822047862874)
XLA Ops:
  0.6 1.3 %pack_edges.1 = (bf16[8,16,1024]{2,1,0:T(8,128)(2,1)S(1)}, bf16[8,16,1024]{2,1,0:T(8,128)(2,1)S(1)}, bf16[3,8,1024]{2,1,0:T(8,128)(2,1)S(1)}, bf16[3,8,1024]{2,1...) custom-call(bf16[8,16,1024]{2,1,0:T(8,128)(2,1)} %bitcast.16, ...), custom_call_target="tpu_custom_call" | custom-call | bytes 966656 | tf_op jit(solution)/shard_map/pack_edges/pallas_call | solution.py:480
  2.0 0.5 %collective-permute-start = (bf16[3,8,1024]{2,1,0:T(8,128)(2,1)S(1)}, bf16[3,8,1024]{2,1,0:T(8,128)(2,1)S(1)}, u32[]{:S(2)}, u32[]{:S(2)}) collective-permute-start(bf16[3,8,1024]{2,1,0:T(8,128)(2,1)S(1)} %get-tuple-element.53), channel_id=1, source_target_pairs={{0,16},{16,0},{1,17},{17,1},{2,18},{18,2},{3,19},{19,3},{4,20},{20... | collective-permute-start | bytes 147464 | tf_op jit(solution)/shard_map/ppermute | solution.py:20
  2.5 0.7 %pack_halves.1 = (bf16[19,8,1024]{2,1,0:T(8,128)(2,1)S(1)}, bf16[19,8,1024]{2,1,0:T(8,128)(2,1)S(1)}, bf16[2304,128]{1,0:T(8,128)(2,1)S(1)}, bf16[128,2304]{1,0:T(8,128)(2,1)S(1)}) custom-call(bf16[8,16,1024]{2,1,0:T(8,128)(2,1)S(1)} %get-tuple-element.47.field, bf16[8,16,1024]{2,1,0:T(8,128)(2,1)S(1)} %get-tuple-element.48.cot, ...), custom_call_target="tpu_custom_call" | custom-call | flops 1000000000 | bytes 966656 | tf_op jit(solution)/shard_map/pack_halves/pallas_call | solution.py:480
  3.2 0.2 collective-permute-done.taken
  3.4 0.3 collective-permute-start.1
  3.7 0.7 %collective-permute-start.2 = (bf16[3,16,1024]{2,1,0:T(8,128)(2,1)S(1)}, bf16[3,16,1024]{2,1,0:T(8,128)(2,1)S(1)}, u32[]{:S(2)}, u32[]{:S(2)}) collective-permute-start(bf16[3,16,1024]{2,1,0:T(8,128)(2,1)S(1)} %join_edges.1), channel_id=1, source_target_pairs={{16,4},{20,8},{24,12},{4,16},{8,20},{12,24},{17,5},{21,9},{25,13},... | collective-permute-start | bytes 294920 | tf_op jit(solution)/shard_map/ppermute | solution.py:532
  4.4 0.6 %collective-permute-done.1.got = bf16[19,8,1024]{2,1,0:T(8,128)(2,1)S(1)} collective-permute-done((bf16[19,8,1024]{2,1,0:T(8,128)(2,1)S(1)}, bf16[19,8,1024]{2,1,0:T(8,128)(2,1)S(1)}, u32[]{:S(2)}, u32[]{:S(2)}) %collective-permute-start.1) | collective-permute-done | bytes 311328 | tf_op jit(solution)/shard_map/ppermute | solution.py:20
  5.0 4.1 %interior.1 = (bf16[3,12,16,1280]{3,2,1,0:T(8,128)(2,1)S(1)}, bf16[3,10,16,1280]{3,2,1,0:T(8,128)(2,1)S(1)}, bf16[3,10,16,1152]{3,2,1,0:T(8,128)(2,1)S(1)}, bf16...) custom-call(bf16[19,8,1024]{2,1,0:T(8,128)(2,1)S(1)} %get-tuple-element.51.own, ...), custom_call_target="tpu_custom_call" | custom-call | flops 4000000000 | bytes 1802240 | tf_op jit(solution)/shard_map/interior/pallas_call | solution.py:480
  9.1 0.0 collective-permute-done.2.rows
  9.1 1.4 %late_rows.1 = (bf16[3,12,16,1280]{3,2,1,0:T(8,128)(2,1)S(1)}, bf16[3,10,16,1280]{3,2,1,0:T(8,128)(2,1)S(1)}, bf16[3,10,16,1152]{3,2,1,0:T(8,128)(2,1)S(1)}, bf1...) custom-call(bf16[3,12,16,1280]{3,2,1,0:T(8,128)(2,1)S(1)} %get-tuple, ...), custom_call_target="tpu_custom_call", output_to_operand_aliasing={{0}: (0, {}), {1}: (1, {}), {2}: (2, {}), {3}: (3, {}), {4}... | custom-call | flops 1000000000 | bytes 8036352 | tf_op jit(solution)/shard_map/late_rows/pallas_call | solution.py:480
  10.4 3.6 %collective-permute-start.3 = (bf16[896,128]{1,0:T(8,128)(2,1)S(1)}, bf16[896,128]{1,0:T(8,128)(2,1)S(1)}, u32[]{:S(2)}, u32[]{:S(2)}) collective-permute-start(bf16[896,128]{1,0:T(8,128)(2,1)S(1)} %get-tuple-element.66), channel_id=1, source_target_pairs={{0,16},{16,0},{1,17},{17,1},{2,18},{18,2},{3,19},{19,3},{4,20},{20... | collective-permute-start | bytes 688136 | tf_op jit(solution)/shard_map/ppermute | solution.py:20
  14.0 1.1 %keep_sums.1 = (bf16[3,10,16,1152]{3,2,1,0:T(8,128)(2,1)S(1)}, f32[10,32,1152]{2,1,0:T(8,128)S(1)}, f32[896,128]{1,0:T(8,128)S(1)}) custom-call(bf16[3,12,16,1280]{3,2,1,0:T(8,128)(2,1)S(1)} %get-tuple-element.67.fd, bf16[3,10,16,1280]{3,2,1,0:T(8,128)(2,1)S(1)} %get-tuple-element.68.cd, ...), custom_call_target="tpu_custom_call", output_to_operand_aliasing={{0}: (2, {}), {1}: (4, {})} | custom-call | flops 2000000000 | bytes 6242304 | tf_op jit(solution)/shard_map/keep_sums/pallas_call | solution.py:480
  15.1 0.7 %add_pair.1 = bf16[896,128]{1,0:T(8,128)(2,1)} custom-call(f32[896,128]{1,0:T(8,128)S(1)} %get-tuple-element.74.keep, bf16[896,128]{1,0:T(8,128)(2,1)S(1)} %collective-permute-done.3.other), custom_call_target="tpu_custom_call" | custom-call | bytes 688128 | tf_op jit(solution)/shard_map/add_pair/pallas_call | solution.py:480
  15.9 6.1 %all-to-all-start = ((bf16[16,56,128]{2,1,0:T(8,128)(2,1)}), bf16[16,56,128]{2,1,0:T(8,128)(2,1)S(1)}, u32[]{:S(2)}, u32[]{:S(2)}) async-start(bf16[16,56,128]{2,1,0:T(8,128)(2,1)} %bitcast.4), calls=%async_computation | async-start | bytes 458752 | tf_op jit(solution)/shard_map/all_to_all | solution.py:565
  22.0 1.5 %output_conv.1 = (bf16[8,8,1024]{2,1,0:T(8,128)(2,1)S(1)}, bf16[8,8,1024]{2,1,0:T(8,128)(2,1)S(1)}) custom-call(bf16[3,10,16,1152]{3,2,1,0:T(8,128)(2,1)S(1)} %get-tuple-element.78.hd, bf16[27,64,64]{2,1,0:T(8,128)(2,1)S(1)} %get-tuple-element.79.w2), custom_call_target="tpu_custom_call" | custom-call | flops 2000000000 | bytes 1327104 | tf_op jit(solution)/shard_map/output_conv/pallas_call | solution.py:480
  23.5 0.1 collective-permute-start.4
  23.6 1.3 %collective-permute-done.4.other = bf16[8,8,1024]{2,1,0:T(8,128)(2,1)S(1)} collective-permute-done((bf16[8,8,1024]{2,1,0:T(8,128)(2,1)S(1)}, bf16[8,8,1024]{2,1,0:T(8,128)(2,1)S(1)}, u32[]{:S(2)}, u32[]{:S(2)}) %collective-permute-start.4) | collective-permute-done | bytes 131104 | tf_op jit(solution)/shard_map/ppermute | solution.py:20
  24.9 0.8 %finish_output.1 = bf16[8,16,1024]{2,1,0:T(8,128)(2,1)} custom-call(bf16[8,8,1024]{2,1,0:T(8,128)(2,1)S(1)} %get-tuple-element.80.mine, bf16[8,8,1024]{2,1,0:T(8,128)(2,1)S(1)} %collective-permute-done.4.other), custom_call_target="tpu_custom_call" | custom-call | bytes 262144 | tf_op jit(solution)/shard_map/finish_output/pallas_call | solution.py:480
  25.8 5.9 %all-to-all-done.terms = bf16[16,56,128]{2,1,0:T(8,128)(2,1)S(1)} async-done(((bf16[16,56,128]{2,1,0:T(8,128)(2,1)}), bf16[16,56,128]{2,1,0:T(8,128)(2,1)S(1)}, u32[]{:S(2)}, u32[]{:S(2)}) %all-to-all-start) | async-done | bytes 229408 | tf_op jit(solution)/shard_map/all_to_all | solution.py:565
  31.8 12.1 %all_to_all.10 = bf16[16,56,128]{2,1,0:T(8,128)(2,1)S(1)} all-to-all(bf16[16,56,128]{2,1,0:T(8,128)(2,1)S(1)} %broadcast_in_dim.10), channel_id=1, replica_groups=mesh['gx'=2,'gy'=4,'grp'=4] {'grp','gy'}, dimensions={0} | all-to-all | bytes 458752 | tf_op jit(solution)/shard_map/all_to_all | solution.py:578
  43.9 0.0 collective-permute-start.5
  43.9 1.0 %unpack_own.1 = (f32[27,64,64]{2,1,0:T(8,128)}, f32[27,64,64]{2,1,0:T(8,128)}) custom-call(bf16[896,128]{1,0:T(8,128)(2,1)S(1)} %bitcast.10), custom_call_target="tpu_custom_call" | custom-call | bytes 229376 | tf_op jit(solution)/shard_map/unpack_own/pallas_call | solution.py:480
  45.0 0.4 collective-permute-done.5.rows
  45.4 1.0 %unpack_other.1 = (f32[27,64,64]{2,1,0:T(8,128)}, f32[27,64,64]{2,1,0:T(8,128)}) custom-call(bf16[896,128]{1,0:T(8,128)(2,1)S(1)} %collective-permute-done.5.rows, f32[27,64,64]{2,1,0:T(8,128)} %get-tuple-element.87.first_in, f32[27,64,64]{2,1,0:T(8,128)} %get-tuple-element.88.second_in), custom_call_target="tpu_custom_call", output_to_operand_aliasing={{0}: (1, {}), {1}: (2, {})} | custom-call | bytes 1114112 | tf_op jit(solution)/shard_map/unpack_other/pallas_call | solution.py:480
  (4 shorter events, 0.1 us)
Async XLA Ops:
  2.0 1.4 %collective-permute-start = (bf16[3,8,1024]{2,1,0:T(8,128)(2,1)S(1)}, bf16[3,8,1024]{2,1,0:T(8,128)(2,1)S(1)}, u32[]{:S(2)}, u32[]{:S(2)}) collective-permute-start(bf16[3,8,1024]{2,1,0:T(8,128)(2,1)S(1)} %get-tuple-element.53), channel_id=1, source_target_pairs={{0,16},{16,0},{1,17},{17,1},{2,18},{18,2},{3,19},{19,3},{4,20},{20... | collective-permute-start | bytes 147464 | tf_op jit(solution)/shard_map/ppermute | solution.py:20
  3.4 1.6 %collective-permute-start.1 = (bf16[19,8,1024]{2,1,0:T(8,128)(2,1)S(1)}, bf16[19,8,1024]{2,1,0:T(8,128)(2,1)S(1)}, u32[]{:S(2)}, u32[]{:S(2)}) collective-permute-start(bf16[19,8,1024]{2,1,0:T(8,128)(2,1)S(1)} %get-tuple-element.55), channel_id=1, source_target_pairs={{0,16},{16,0},{1,17},{17,1},{2,18},{18,2},{3,19},{19,3},{4,20},{20... | collective-permute-start | bytes 933896 | tf_op jit(solution)/shard_map/ppermute | solution.py:20
  3.7 5.3 %collective-permute-start.2 = (bf16[3,16,1024]{2,1,0:T(8,128)(2,1)S(1)}, bf16[3,16,1024]{2,1,0:T(8,128)(2,1)S(1)}, u32[]{:S(2)}, u32[]{:S(2)}) collective-permute-start(bf16[3,16,1024]{2,1,0:T(8,128)(2,1)S(1)} %join_edges.1), channel_id=1, source_target_pairs={{16,4},{20,8},{24,12},{4,16},{8,20},{12,24},{17,5},{21,9},{25,13},... | collective-permute-start | bytes 294920 | tf_op jit(solution)/shard_map/ppermute | solution.py:532
  10.4 4.7 %collective-permute-start.3 = (bf16[896,128]{1,0:T(8,128)(2,1)S(1)}, bf16[896,128]{1,0:T(8,128)(2,1)S(1)}, u32[]{:S(2)}, u32[]{:S(2)}) collective-permute-start(bf16[896,128]{1,0:T(8,128)(2,1)S(1)} %get-tuple-element.66), channel_id=1, source_target_pairs={{0,16},{16,0},{1,17},{17,1},{2,18},{18,2},{3,19},{19,3},{4,20},{20... | collective-permute-start | bytes 688136 | tf_op jit(solution)/shard_map/ppermute | solution.py:20
  15.9 15.8 %all-to-all-start = ((bf16[16,56,128]{2,1,0:T(8,128)(2,1)}), bf16[16,56,128]{2,1,0:T(8,128)(2,1)S(1)}, u32[]{:S(2)}, u32[]{:S(2)}) async-start(bf16[16,56,128]{2,1,0:T(8,128)(2,1)} %bitcast.4), calls=%async_computation | async-start | bytes 458752 | tf_op jit(solution)/shard_map/all_to_all | solution.py:565
  23.5 1.4 %collective-permute-start.4 = (bf16[8,8,1024]{2,1,0:T(8,128)(2,1)S(1)}, bf16[8,8,1024]{2,1,0:T(8,128)(2,1)S(1)}, u32[]{:S(2)}, u32[]{:S(2)}) collective-permute-start(bf16[8,8,1024]{2,1,0:T(8,128)(2,1)S(1)} %get-tuple-element.81), channel_id=1, source_target_pairs={{0,16},{16,0},{1,17},{17,1},{2,18},{18,2},{3,19},{19,3},{4,20},{20... | collective-permute-start | bytes 393224 | tf_op jit(solution)/shard_map/ppermute | solution.py:20
  43.9 1.5 %collective-permute-start.5 = (bf16[896,128]{1,0:T(8,128)(2,1)S(1)}, bf16[896,128]{1,0:T(8,128)(2,1)S(1)}, u32[]{:S(2)}, u32[]{:S(2)}) collective-permute-start(bf16[896,128]{1,0:T(8,128)(2,1)S(1)} %bitcast.9), channel_id=1, source_target_pairs={{0,16},{16,0},{1,17},{17,1},{2,18},{18,2},{3,19},{19,3},{4,20},{20... | collective-permute-start | bytes 688136 | tf_op jit(solution)/shard_map/ppermute | solution.py:20

commit v21 on v19

--- a/solution.py
+++ b/solution.py
@@ -181,7 +181,7 @@
     return grad * sigma * (1.0 + pre * (1.0 - sigma)) * inside_lanes(p)
 
 
-def interior(own, got, w1b, wfb, fd, cd, hd, pg, hs, acc, fs, cs, pre):
+def interior(own, got, w1b, wfb, fd, cd, hd, pg, hs, acc, fs, cs, slope):
     gx = lax.axis_index("gx")
     nx, width = own.shape[1:]
     across = 2 * nx
@@ -216,8 +216,9 @@
         for p in range(group, group + 3):
             here = slice(lane * p, lane * (p + 1))
             part = value[cells * (p - group):cells * (p - group + 1)]
-            pre[:, :, here] = part.reshape(count, across, lane)
-            hidden = (part * jax.nn.sigmoid(part) * inside_lanes(p)).reshape(count, across, lane)
+            sigma = jax.nn.sigmoid(part)
+            slope[:, :, here] = (sigma * (1.0 + part * (1.0 - sigma)) * inside_lanes(p)).reshape(count, across, lane)
+            hidden = (part * sigma * inside_lanes(p)).reshape(count, across, lane)
             hs[pl.ds(2 - 2 * gx, count), 8:8 + across, here] = hidden
             hd[1, pl.ds(2 - 2 * gx, count), :, here] = hidden.astype(BF16)
     cells = cells - across
@@ -226,7 +227,7 @@
         for p in range(group, group + 3):
             here = slice(lane * p, lane * (p + 1))
             part = value[cells * (p - group):cells * (p - group + 1)]
-            grad = pre_gradient(part, pre[pl.ds(gx, count - 1), :, here].reshape(cells, lane), p)
+            grad = part * slope[pl.ds(gx, count - 1), :, here].reshape(cells, lane)
             pg[pl.ds(1 - gx, count - 1), :, here] = grad.astype(BF16).reshape(count - 1, across, lane)
     pg[pl.ds((count - 1) * gx, 1)] = jnp.zeros((1,) + pg.shape[1:], BF16)
 

time: 46.7 us -> 46.7 us (level)
  no operation moved by 1% of the time
where the time goes in v21:
time: 46.7 us; the launch traced here: 46.5 us
  Pallas kernels  13.8 us (30%)
  blocking collectives  12.1 us (26%)
  starting transfers between devices  11.3 us (24%)
  waiting for transfers between devices  8.45 us (18%)
  between operations  0.74 us (2%)
    pallas_call x12, Pallas kernels, call(): pl.pallas_call(body, out_shape=list(outs), in_specs=[pl.BlockSpec(memory_...  13.8 us
    all_to_all x1, blocking collectives, shards(): sums = lax.all_to_all(spread, ('grp', 'gy'), 0, 0).reshape(rows, lane)  12.1 us
    all_to_all x1, starting transfers between devices, shards(): lax.all_to_all(both.reshape(ranks, rows // ranks, lane), ('grp', 'gy'), 0...  6.17 us
    all_to_all x1, waiting for transfers between devices, shards(): lax.all_to_all(both.reshape(ranks, rows // ranks, lane), ('grp', 'gy'), 0...  5.94 us
    ppermute x5, starting transfers between devices, swap(): return lax.ppermute(array, 'gx', [(0, 1), (1, 0)])  4.48 us
    ppermute x5, waiting for transfers between devices, swap(): return lax.ppermute(array, 'gx', [(0, 1), (1, 0)])  2.51 us
  transfers between devices with their start and end apart: 7, of which 5 were waited for; matrix products, arithmetic and copies ran while one was open for 0% of the time, Pallas kernels for 20%

profile of v21, /device:TPU:0, one launch (start us, length us, event | category | flops | bytes accessed | tf_op | source)
XLA Modules:
  0.0 46.5 jit_solution(10201281408247950515)
XLA Ops:
  0.6 1.3 %pack_edges.1 = (bf16[8,16,1024]{2,1,0:T(8,128)(2,1)S(1)}, bf16[8,16,1024]{2,1,0:T(8,128)(2,1)S(1)}, bf16[3,8,1024]{2,1,0:T(8,128)(2,1)S(1)}, bf16[3,8,1024]{2,1...) custom-call(bf16[8,16,1024]{2,1,0:T(8,128)(2,1)} %bitcast.16, ...), custom_call_target="tpu_custom_call" | custom-call | bytes 966656 | tf_op jit(solution)/shard_map/pack_edges/pallas_call | solution.py:481
  2.0 0.5 %collective-permute-start = (bf16[3,8,1024]{2,1,0:T(8,128)(2,1)S(1)}, bf16[3,8,1024]{2,1,0:T(8,128)(2,1)S(1)}, u32[]{:S(2)}, u32[]{:S(2)}) collective-permute-start(bf16[3,8,1024]{2,1,0:T(8,128)(2,1)S(1)} %get-tuple-element.53), channel_id=1, source_target_pairs={{0,16},{16,0},{1,17},{17,1},{2,18},{18,2},{3,19},{19,3},{4,20},{20... | collective-permute-start | bytes 147464 | tf_op jit(solution)/shard_map/ppermute | solution.py:20
  2.5 0.7 %pack_halves.1 = (bf16[19,8,1024]{2,1,0:T(8,128)(2,1)S(1)}, bf16[19,8,1024]{2,1,0:T(8,128)(2,1)S(1)}, bf16[2304,128]{1,0:T(8,128)(2,1)S(1)}, bf16[128,2304]{1,0:T(8,128)(2,1)S(1)}) custom-call(bf16[8,16,1024]{2,1,0:T(8,128)(2,1)S(1)} %get-tuple-element.47.field, bf16[8,16,1024]{2,1,0:T(8,128)(2,1)S(1)} %get-tuple-element.48.cot, ...), custom_call_target="tpu_custom_call" | custom-call | flops 1000000000 | bytes 966656 | tf_op jit(solution)/shard_map/pack_halves/pallas_call | solution.py:481
  3.2 0.2 collective-permute-done.taken
  3.4 0.3 collective-permute-start.1
  3.7 0.7 %collective-permute-start.2 = (bf16[3,16,1024]{2,1,0:T(8,128)(2,1)S(1)}, bf16[3,16,1024]{2,1,0:T(8,128)(2,1)S(1)}, u32[]{:S(2)}, u32[]{:S(2)}) collective-permute-start(bf16[3,16,1024]{2,1,0:T(8,128)(2,1)S(1)} %join_edges.1), channel_id=1, source_target_pairs={{16,4},{20,8},{24,12},{4,16},{8,20},{12,24},{17,5},{21,9},{25,13},... | collective-permute-start | bytes 294920 | tf_op jit(solution)/shard_map/ppermute | solution.py:533
  4.4 0.6 %collective-permute-done.1.got = bf16[19,8,1024]{2,1,0:T(8,128)(2,1)S(1)} collective-permute-done((bf16[19,8,1024]{2,1,0:T(8,128)(2,1)S(1)}, bf16[19,8,1024]{2,1,0:T(8,128)(2,1)S(1)}, u32[]{:S(2)}, u32[]{:S(2)}) %collective-permute-start.1) | collective-permute-done | bytes 311328 | tf_op jit(solution)/shard_map/ppermute | solution.py:20
  5.0 4.1 %interior.1 = (bf16[3,12,16,1280]{3,2,1,0:T(8,128)(2,1)S(1)}, bf16[3,10,16,1280]{3,2,1,0:T(8,128)(2,1)S(1)}, bf16[3,10,16,1152]{3,2,1,0:T(8,128)(2,1)S(1)}, bf16...) custom-call(bf16[19,8,1024]{2,1,0:T(8,128)(2,1)S(1)} %get-tuple-element.51.own, ...), custom_call_target="tpu_custom_call" | custom-call | flops 4000000000 | bytes 1802240 | tf_op jit(solution)/shard_map/interior/pallas_call | solution.py:481
  9.1 1.3 %late_rows.1 = (bf16[3,12,16,1280]{3,2,1,0:T(8,128)(2,1)S(1)}, bf16[3,10,16,1280]{3,2,1,0:T(8,128)(2,1)S(1)}, bf16[3,10,16,1152]{3,2,1,0:T(8,128)(2,1)S(1)}, bf1...) custom-call(bf16[3,12,16,1280]{3,2,1,0:T(8,128)(2,1)S(1)} %get-tuple, ...), custom_call_target="tpu_custom_call", output_to_operand_aliasing={{0}: (0, {}), {1}: (1, {}), {2}: (2, {}), {3}: (3, {}), {4}... | custom-call | flops 1000000000 | bytes 8036352 | tf_op jit(solution)/shard_map/late_rows/pallas_call | solution.py:481
  10.4 3.5 %collective-permute-start.3 = (bf16[896,128]{1,0:T(8,128)(2,1)S(1)}, bf16[896,128]{1,0:T(8,128)(2,1)S(1)}, u32[]{:S(2)}, u32[]{:S(2)}) collective-permute-start(bf16[896,128]{1,0:T(8,128)(2,1)S(1)} %get-tuple-element.66), channel_id=1, source_target_pairs={{0,16},{16,0},{1,17},{17,1},{2,18},{18,2},{3,19},{19,3},{4,20},{20... | collective-permute-start | bytes 688136 | tf_op jit(solution)/shard_map/ppermute | solution.py:20
  14.0 1.1 %keep_sums.1 = (bf16[3,10,16,1152]{3,2,1,0:T(8,128)(2,1)S(1)}, f32[10,32,1152]{2,1,0:T(8,128)S(1)}, f32[896,128]{1,0:T(8,128)S(1)}) custom-call(bf16[3,12,16,1280]{3,2,1,0:T(8,128)(2,1)S(1)} %get-tuple-element.67.fd, bf16[3,10,16,1280]{3,2,1,0:T(8,128)(2,1)S(1)} %get-tuple-element.68.cd, ...), custom_call_target="tpu_custom_call", output_to_operand_aliasing={{0}: (2, {}), {1}: (4, {})} | custom-call | flops 2000000000 | bytes 6242304 | tf_op jit(solution)/shard_map/keep_sums/pallas_call | solution.py:481
  15.1 0.0 collective-permute-done.3.other
  15.1 0.7 %add_pair.1 = bf16[896,128]{1,0:T(8,128)(2,1)} custom-call(f32[896,128]{1,0:T(8,128)S(1)} %get-tuple-element.74.keep, bf16[896,128]{1,0:T(8,128)(2,1)S(1)} %collective-permute-done.3.other), custom_call_target="tpu_custom_call" | custom-call | bytes 688128 | tf_op jit(solution)/shard_map/add_pair/pallas_call | solution.py:481
  15.8 6.2 %all-to-all-start = ((bf16[16,56,128]{2,1,0:T(8,128)(2,1)}), bf16[16,56,128]{2,1,0:T(8,128)(2,1)S(1)}, u32[]{:S(2)}, u32[]{:S(2)}) async-start(bf16[16,56,128]{2,1,0:T(8,128)(2,1)} %bitcast.4), calls=%async_computation | async-start | bytes 458752 | tf_op jit(solution)/shard_map/all_to_all | solution.py:566
  22.0 1.5 %output_conv.1 = (bf16[8,8,1024]{2,1,0:T(8,128)(2,1)S(1)}, bf16[8,8,1024]{2,1,0:T(8,128)(2,1)S(1)}) custom-call(bf16[3,10,16,1152]{3,2,1,0:T(8,128)(2,1)S(1)} %get-tuple-element.78.hd, bf16[27,64,64]{2,1,0:T(8,128)(2,1)S(1)} %get-tuple-element.79.w2), custom_call_target="tpu_custom_call" | custom-call | flops 2000000000 | bytes 1327104 | tf_op jit(solution)/shard_map/output_conv/pallas_call | solution.py:481
  23.5 0.1 collective-permute-start.4
  23.6 1.3 %collective-permute-done.4.other = bf16[8,8,1024]{2,1,0:T(8,128)(2,1)S(1)} collective-permute-done((bf16[8,8,1024]{2,1,0:T(8,128)(2,1)S(1)}, bf16[8,8,1024]{2,1,0:T(8,128)(2,1)S(1)}, u32[]{:S(2)}, u32[]{:S(2)}) %collective-permute-start.4) | collective-permute-done | bytes 131104 | tf_op jit(solution)/shard_map/ppermute | solution.py:20
  24.9 0.8 %finish_output.1 = bf16[8,16,1024]{2,1,0:T(8,128)(2,1)} custom-call(bf16[8,8,1024]{2,1,0:T(8,128)(2,1)S(1)} %get-tuple-element.80.mine, bf16[8,8,1024]{2,1,0:T(8,128)(2,1)S(1)} %collective-permute-done.4.other), custom_call_target="tpu_custom_call" | custom-call | bytes 262144 | tf_op jit(solution)/shard_map/finish_output/pallas_call | solution.py:481
  25.8 5.9 %all-to-all-done.terms = bf16[16,56,128]{2,1,0:T(8,128)(2,1)S(1)} async-done(((bf16[16,56,128]{2,1,0:T(8,128)(2,1)}), bf16[16,56,128]{2,1,0:T(8,128)(2,1)S(1)}, u32[]{:S(2)}, u32[]{:S(2)}) %all-to-all-start) | async-done | bytes 229408 | tf_op jit(solution)/shard_map/all_to_all | solution.py:566
  31.8 12.1 %all_to_all.10 = bf16[16,56,128]{2,1,0:T(8,128)(2,1)S(1)} all-to-all(bf16[16,56,128]{2,1,0:T(8,128)(2,1)S(1)} %broadcast_in_dim.10), channel_id=1, replica_groups=mesh['gx'=2,'gy'=4,'grp'=4] {'grp','gy'}, dimensions={0} | all-to-all | bytes 458752 | tf_op jit(solution)/shard_map/all_to_all | solution.py:579
  43.9 0.0 collective-permute-start.5
  43.9 1.0 %unpack_own.1 = (f32[27,64,64]{2,1,0:T(8,128)}, f32[27,64,64]{2,1,0:T(8,128)}) custom-call(bf16[896,128]{1,0:T(8,128)(2,1)S(1)} %bitcast.10), custom_call_target="tpu_custom_call" | custom-call | bytes 229376 | tf_op jit(solution)/shard_map/unpack_own/pallas_call | solution.py:481
  45.0 0.4 collective-permute-done.5.rows
  45.4 1.0 %unpack_other.1 = (f32[27,64,64]{2,1,0:T(8,128)}, f32[27,64,64]{2,1,0:T(8,128)}) custom-call(bf16[896,128]{1,0:T(8,128)(2,1)S(1)} %collective-permute-done.5.rows, f32[27,64,64]{2,1,0:T(8,128)} %get-tuple-element.87.first_in, f32[27,64,64]{2,1,0:T(8,128)} %get-tuple-element.88.second_in), custom_call_target="tpu_custom_call", output_to_operand_aliasing={{0}: (1, {}), {1}: (2, {})} | custom-call | bytes 1114112 | tf_op jit(solution)/shard_map/unpack_other/pallas_call | solution.py:481
  (4 shorter events, 0.1 us)
Async XLA Ops:
  2.0 1.4 %collective-permute-start = (bf16[3,8,1024]{2,1,0:T(8,128)(2,1)S(1)}, bf16[3,8,1024]{2,1,0:T(8,128)(2,1)S(1)}, u32[]{:S(2)}, u32[]{:S(2)}) collective-permute-start(bf16[3,8,1024]{2,1,0:T(8,128)(2,1)S(1)} %get-tuple-element.53), channel_id=1, source_target_pairs={{0,16},{16,0},{1,17},{17,1},{2,18},{18,2},{3,19},{19,3},{4,20},{20... | collective-permute-start | bytes 147464 | tf_op jit(solution)/shard_map/ppermute | solution.py:20
  3.4 1.6 %collective-permute-start.1 = (bf16[19,8,1024]{2,1,0:T(8,128)(2,1)S(1)}, bf16[19,8,1024]{2,1,0:T(8,128)(2,1)S(1)}, u32[]{:S(2)}, u32[]{:S(2)}) collective-permute-start(bf16[19,8,1024]{2,1,0:T(8,128)(2,1)S(1)} %get-tuple-element.55), channel_id=1, source_target_pairs={{0,16},{16,0},{1,17},{17,1},{2,18},{18,2},{3,19},{19,3},{4,20},{20... | collective-permute-start | bytes 933896 | tf_op jit(solution)/shard_map/ppermute | solution.py:20
  3.7 5.3 %collective-permute-start.2 = (bf16[3,16,1024]{2,1,0:T(8,128)(2,1)S(1)}, bf16[3,16,1024]{2,1,0:T(8,128)(2,1)S(1)}, u32[]{:S(2)}, u32[]{:S(2)}) collective-permute-start(bf16[3,16,1024]{2,1,0:T(8,128)(2,1)S(1)} %join_edges.1), channel_id=1, source_target_pairs={{16,4},{20,8},{24,12},{4,16},{8,20},{12,24},{17,5},{21,9},{25,13},... | collective-permute-start | bytes 294920 | tf_op jit(solution)/shard_map/ppermute | solution.py:533
  10.4 4.7 %collective-permute-start.3 = (bf16[896,128]{1,0:T(8,128)(2,1)S(1)}, bf16[896,128]{1,0:T(8,128)(2,1)S(1)}, u32[]{:S(2)}, u32[]{:S(2)}) collective-permute-start(bf16[896,128]{1,0:T(8,128)(2,1)S(1)} %get-tuple-element.66), channel_id=1, source_target_pairs={{0,16},{16,0},{1,17},{17,1},{2,18},{18,2},{3,19},{19,3},{4,20},{20... | collective-permute-start | bytes 688136 | tf_op jit(solution)/shard_map/ppermute | solution.py:20
  15.8 15.9 %all-to-all-start = ((bf16[16,56,128]{2,1,0:T(8,128)(2,1)}), bf16[16,56,128]{2,1,0:T(8,128)(2,1)S(1)}, u32[]{:S(2)}, u32[]{:S(2)}) async-start(bf16[16,56,128]{2,1,0:T(8,128)(2,1)} %bitcast.4), calls=%async_computation | async-start | bytes 458752 | tf_op jit(solution)/shard_map/all_to_all | solution.py:566
  23.5 1.4 %collective-permute-start.4 = (bf16[8,8,1024]{2,1,0:T(8,128)(2,1)S(1)}, bf16[8,8,1024]{2,1,0:T(8,128)(2,1)S(1)}, u32[]{:S(2)}, u32[]{:S(2)}) collective-permute-start(bf16[8,8,1024]{2,1,0:T(8,128)(2,1)S(1)} %get-tuple-element.81), channel_id=1, source_target_pairs={{0,16},{16,0},{1,17},{17,1},{2,18},{18,2},{3,19},{19,3},{4,20},{20... | collective-permute-start | bytes 393224 | tf_op jit(solution)/shard_map/ppermute | solution.py:20
  43.9 1.5 %collective-permute-start.5 = (bf16[896,128]{1,0:T(8,128)(2,1)S(1)}, bf16[896,128]{1,0:T(8,128)(2,1)S(1)}, u32[]{:S(2)}, u32[]{:S(2)}) collective-permute-start(bf16[896,128]{1,0:T(8,128)(2,1)S(1)} %bitcast.9), channel_id=1, source_target_pairs={{0,16},{16,0},{1,17},{17,1},{2,18},{18,2},{3,19},{19,3},{4,20},{20... | collective-permute-start | bytes 688136 | tf_op jit(solution)/shard_map/ppermute | solution.py:20
